TPU v7x, 512 devices: a whole 4x8x8 slice. The times are simulated.
512 devices in a mesh: ep: 128 (over z, y, core), edp: 4 (over x).
Axes of the slice: x: 4, y: 8, z: 8, core: 2. Of those that a mesh axis runs over, the one named last changes fastest.
Arguments:
- tokens: bfloat16 [12288, 2048], P(('ep', 'edp')), may hold values from -6 to 6
- out_grad: bfloat16 [12288, 2048], P(('ep', 'edp')), may hold values from -6 to 6
- expert_ids: int32 [12288, 8], P(('ep', 'edp')), may hold values from 0 to 127, all different within a row; in each aligned block of 24 rows (0 to 23, 24 to 47, ...) at most 2 rows name the same one
- gate_values: float32 [12288, 8], P(('ep', 'edp')), may hold values from 0.02 to 0.3
- gate_up_weight: bfloat16 [128, 2048, 1536], P('ep', 'edp'), may hold values from -0.125 to 0.125
- down_weight: bfloat16 [128, 768, 2048], P('ep', None, 'edp'), may hold values from -0.21875 to 0.21875
Outputs:
- token_grads: bfloat16 [12288, 2048], P(('ep', 'edp'))
- down_grad: bfloat16 [128, 768, 2048], P('ep', None, 'edp')
Inputs may be any that keep to these rules, and one draw needn't show every extreme that they name: `expert_ids`: A token names 8 different experts. Among the 24 tokens of one device no expert is named by more than 2 tokens, a bound that some block reaches.
All inputs are finite; a program needn't handle non-finite values. Where the computation divides by a largest or mean magnitude, that divisor is 1e-20 or more.
Results may differ from a plain program's by a relative error of at most 0.022.
Values may be sent and summed in bfloat16 or wider, within the bound.
No kernel may reach another device: no remote copies, remote signals or barrier semaphores. Data moves between devices by JAX's collectives and lax.ppermute only.
A program may use at most 64 MiB of HBM per device.

v0:
```python
import jax
import jax.numpy as jnp
from jax import lax
from jax.sharding import PartitionSpec as P

EPSILON = 1e-06


def quantize_rows(values):
    groups = values.reshape(values.shape[:-1] + (values.shape[-1] // 128, 128))
    scales = (jnp.max(jnp.abs(groups), axis=-1) + EPSILON).astype(jnp.bfloat16)
    quant = (groups / scales.astype(jnp.float32)[..., None]).astype(jnp.bfloat16)
    return (quant.reshape(values.shape), scales)


def restore_rows(quant, scales):
    groups = quant.astype(jnp.float32).reshape(scales.shape + (128,))
    restored = groups * scales.astype(jnp.float32)[..., None]
    return restored.astype(jnp.bfloat16).reshape(quant.shape)


def swiglu_backward(pre_gate, pre_up, grad_hidden):
    sigmoid = jax.nn.sigmoid(pre_gate)
    activ = pre_gate * sigmoid
    grad_gate = grad_hidden * pre_up * sigmoid * (1.0 + pre_gate * (1.0 - sigmoid))
    grad_up = grad_hidden * activ
    return jnp.concatenate([grad_gate, grad_up], axis=-1).astype(jnp.bfloat16)


def per_device(tokens, out_grad, expert_ids, gate_values, gate_up_weight, down_weight):
    experts = lax.axis_size("ep")
    tok_count, top_count = expert_ids.shape
    pair_count = tok_count * top_count
    model_width = tokens.shape[1]
    hidden_units = down_weight.shape[1]
    capacity = min(tok_count, max(2, 3 * tok_count * top_count // (2 * experts)))
    slot_count = experts * capacity
    flat_ids = expert_ids.reshape(pair_count)
    onehot = (flat_ids[:, None] == jnp.arange(experts, dtype=jnp.int32)[None, :]).astype(jnp.int32)
    slot_rank = jnp.sum((jnp.cumsum(onehot, axis=0) - 1) * onehot, axis=1)
    target = flat_ids * capacity + slot_rank
    matches = jnp.arange(slot_count, dtype=jnp.int32)[:, None] == target[None, :]
    pick_bf = jnp.any(matches.reshape(slot_count, tok_count, top_count), axis=2).astype(
        jnp.bfloat16
    )
    slot_gate = jnp.sum(jnp.where(matches, gate_values.reshape(pair_count)[None, :], 0.0), axis=1)
    sent_tokens = jnp.dot(pick_bf, tokens, preferred_element_type=jnp.float32)
    sent_grads = jnp.dot(pick_bf, out_grad, preferred_element_type=jnp.float32) * slot_gate[:, None]
    quant_x, scale_x = quantize_rows(sent_tokens)
    quant_g, scale_g = quantize_rows(sent_grads)
    quant_x = quant_x.reshape(experts, capacity, model_width)
    scale_x = scale_x.reshape(experts, capacity, model_width // 128)
    quant_g = quant_g.reshape(experts, capacity, model_width)
    scale_g = scale_g.reshape(experts, capacity, model_width // 128)
    gate_up_all, down_all = (
        lax.all_gather(gate_up_weight, "edp", axis=1, tiled=True),
        lax.all_gather(down_weight, "edp", axis=2, tiled=True),
    )
    recv_x, recv_sx, recv_g, recv_sg = (
        lax.all_to_all(quant_x, "ep", split_axis=0, concat_axis=0, tiled=True),
        lax.all_to_all(scale_x, "ep", split_axis=0, concat_axis=0, tiled=True),
        lax.all_to_all(quant_g, "ep", split_axis=0, concat_axis=0, tiled=True),
        lax.all_to_all(scale_g, "ep", split_axis=0, concat_axis=0, tiled=True),
    )
    rows_x = restore_rows(recv_x, recv_sx).reshape(slot_count, model_width)
    gate_up_mat = gate_up_all[0]
    pre = jnp.dot(rows_x, gate_up_mat, preferred_element_type=jnp.float32)
    pre_gate = pre[:, :hidden_units]
    pre_up = pre[:, hidden_units:]
    hidden = (jax.nn.silu(pre_gate) * pre_up).astype(jnp.bfloat16)
    rows_g = restore_rows(recv_g, recv_sg).reshape(slot_count, model_width)
    grad_hidden = lax.dot_general(
        rows_g, down_all[0], (((1,), (1,)), ((), ())), preferred_element_type=jnp.float32
    )
    partial_value = lax.dot_general(
        hidden, rows_g, (((0,), (0,)), ((), ())), preferred_element_type=jnp.float32
    )
    rounded = lax.optimization_barrier(partial_value.astype(jnp.bfloat16)).astype(jnp.float32)
    summed = lax.psum_scatter(rounded.astype(jnp.bfloat16), "edp", scatter_dimension=1, tiled=True)
    down_grad = summed[None]
    grad_pre = swiglu_backward(pre_gate, pre_up, grad_hidden)
    back = lax.dot_general(
        grad_pre, gate_up_mat, (((1,), (1,)), ((), ())), preferred_element_type=jnp.float32
    )
    back = back.astype(jnp.bfloat16).reshape(experts, capacity, model_width)
    returned = lax.all_to_all(back, "ep", split_axis=0, concat_axis=0, tiled=True).reshape(
        slot_count, model_width
    )
    token_grads = lax.dot_general(
        pick_bf, returned, (((0,), (0,)), ((), ())), preferred_element_type=jnp.float32
    )
    return (token_grads.astype(jnp.bfloat16), down_grad)


def solution(mesh):
    return jax.shard_map(
        per_device,
        mesh=mesh,
        in_specs=(
            P(("ep", "edp"), None),
            P(("ep", "edp"), None),
            P(("ep", "edp"), None),
            P(("ep", "edp"), None),
            P("ep", "edp", None),
            P("ep", None, "edp"),
        ),
        out_specs=(P(("ep", "edp"), None), P("ep", None, "edp")),
        check_vma=False,
    )
```

profile of v0, /device:TPU:1, one launch (start us, length us, event | category | flops | bytes accessed | tf_op | source)
XLA Modules:
  0.0 201.3 jit_solution(129299203498786674)
XLA Ops:
  7.2 0.7 all-gather.5.cloned.1.call-update
  7.9 0.8 copy.50
  8.9 0.1 fusion.16
  9.1 0.2 fusion.22
  9.4 0.1 fusion.15
  9.6 0.5 abs_reduce_fusion
  10.1 0.7 copy.60
  10.8 18.4 %all-to-all-start.3 = ((bf16[128,2,16]{2,1,0:T(2,128)(2,1)}), bf16[128,2,16]{2,1,0:T(2,128)(2,1)S(1)}, u32[]{:S(2)}, u32[]{:S(2)}) async-start(bf16[128,2,16]{2,1,0:T(2,128)(2,1)} %bitcast.8), calls=%async_computation.3 | async-start | bytes 131072 | tf_op jit(solution)/shard_map/all_to_all | solution.py:61
  29.3 0.2 divide_convert_fusion
  29.5 1.1 copy.59
  30.6 1.1 reshape_reshape.2
  31.7 8.9 %all-to-all-done.3 = bf16[128,2,16]{2,1,0:T(2,128)(2,1)S(1)} async-done(((bf16[128,2,16]{2,1,0:T(2,128)(2,1)}), bf16[128,2,16]{2,1,0:T(2,128)(2,1)S(1)}, u32[]{:S(2)}, u32[]{:S(2)}) %all-to-all-start.3) | async-done | bytes 8224 | tf_op jit(solution)/shard_map/all_to_all | solution.py:61
  40.6 5.8 %all-to-all-start.2 = ((bf16[128,2,2048]{2,1,0:T(2,128)(2,1)}), bf16[128,2,2048]{2,1,0:T(2,128)(2,1)S(1)}, u32[]{:S(2)}, u32[]{:S(2)}) async-start(bf16[128,2,2048]{2,1,0:T(2,128)(2,1)} %reshape_reshape.2), calls=%async_computation.2 | async-start | bytes 2097152 | tf_op jit(solution)/shard_map/all_to_all | solution.py:60
  46.5 0.7 all-gather.3.cloned.1.call-update
  47.3 0.1 select_reduce_fusion
  47.5 0.5 convolution_multiply_fusion
  48.0 2.2 %reshape.87 = f32[128,2,2048]{2,1,0:T(2,128)} reshape(f32[256,2048]{1,0:T(8,128)S(1)} %convolution_multiply_fusion) | data formatting | bytes 4194304 | tf_op jit(solution)/shard_map/reshape | solution.py:10
  50.2 0.2 abs_bitcast_fusion
  50.4 0.4 copy.62
  50.8 0.6 reduce_max.18
  51.5 0.1 copy.56
  51.6 1.9 div.24
  53.5 3.5 %div.25 = f32[128,2,2048]{2,1,0:T(2,128)} reshape(f32[256,16,128]{2,1,0:T(8,128)} %div.24) | data formatting | bytes 4194304 | tf_op jit(solution)/shard_map/div | solution.py:12
  57.1 4.5 %divide_convert_fusion.1 = bf16[128,2,2048]{2,1,0:T(2,128)(2,1)} fusion(f32[128,2,2048]{2,1,0:T(2,128)S(1)} %copy-done.1, f32[128,2,2048]{2,1,0:T(2,128)} %div.25), kind=kLoop, calls=%fused_computation.17 | loop fusion | flops 1048576 | bytes 5242880 | tf_op jit(solution)/shard_map/convert_element_type | solution.py:12
  61.6 15.8 %all-to-all-done.2 = bf16[128,2,2048]{2,1,0:T(2,128)(2,1)S(1)} async-done(((bf16[128,2,2048]{2,1,0:T(2,128)(2,1)}), bf16[128,2,2048]{2,1,0:T(2,128)(2,1)S(1)}, u32[]{:S(2)}, u32[]{:S(2)}) %all-to-all-start.2) | async-done | bytes 1048608 | tf_op jit(solution)/shard_map/all_to_all | solution.py:60
  77.4 6.7 %all-to-all-start = ((bf16[128,2,2048]{2,1,0:T(2,128)(2,1)}), bf16[128,2,2048]{2,1,0:T(2,128)(2,1)S(1)}, u32[]{:S(2)}, u32[]{:S(2)}) async-start(bf16[128,2,2048]{2,1,0:T(2,128)(2,1)} %divide_convert_fusion.1), calls=%async_computation | async-start | bytes 2097152 | tf_op jit(solution)/shard_map/all_to_all | solution.py:62
  84.1 0.7 copy.57
  84.8 1.9 mul.87
  86.8 2.3 %mul.88 = f32[128,2,2048]{2,1,0:T(2,128)S(1)} reshape(f32[128,2,16,128]{3,2,1,0:T(8,128)} %mul.87) | data formatting | bytes 4194304 | tf_op jit(solution)/shard_map/mul | solution.py:18
  89.1 3.4 %multiply_convert_fusion = bf16[128,2,2048]{2,1,0:T(2,128)(2,1)} fusion(f32[128,2,2048]{2,1,0:T(2,128)S(1)} %mul.88, bf16[128,2,2048]{2,1,0:T(2,128)(2,1)} %copy-done.3), kind=kLoop, calls=%fused_computation.12 | loop fusion | flops 1572864 | bytes 4194304 | tf_op jit(solution)/shard_map/convert_element_type | solution.py:19
  92.5 1.5 convert_element_type.104
  94.0 21.0 %all-to-all-done = bf16[128,2,2048]{2,1,0:T(2,128)(2,1)S(1)} async-done(((bf16[128,2,2048]{2,1,0:T(2,128)(2,1)}), bf16[128,2,2048]{2,1,0:T(2,128)(2,1)S(1)}, u32[]{:S(2)}, u32[]{:S(2)}) %all-to-all-start) | async-done | bytes 1048608 | tf_op jit(solution)/shard_map/all_to_all | solution.py:62
  115.0 6.5 %all-to-all-start.1 = ((bf16[128,2,16]{2,1,0:T(2,128)(2,1)}), bf16[128,2,16]{2,1,0:T(2,128)(2,1)S(1)}, u32[]{:S(2)}, u32[]{:S(2)}) async-start(bf16[128,2,16]{2,1,0:T(2,128)(2,1)} %bitcast.4), calls=%async_computation.1 | async-start | bytes 131072 | tf_op jit(solution)/shard_map/all_to_all | solution.py:63
  121.5 1.5 reshape.90
  123.0 5.8 %fusion.2 = f32[256,1536]{1,0:T(8,128)} fusion(bf16[256,2048]{1,0:T(8,128)(2,1)S(1)} %convert_element_type.104, bf16[1,2048,1536]{2,1,0:T(8,128)(2,1)} %all-gather.5.cloned.1.call-done), kind=kOutput, calls=%fused_computation.2 | convolution fusion | flops 1610612736 | bytes 8912896 | tf_op jit(solution)/shard_map/dot_general | solution.py:67
  128.8 4.0 %all-to-all-done.1 = bf16[128,2,16]{2,1,0:T(2,128)(2,1)S(1)} async-done(((bf16[128,2,16]{2,1,0:T(2,128)(2,1)}), bf16[128,2,16]{2,1,0:T(2,128)(2,1)S(1)}, u32[]{:S(2)}, u32[]{:S(2)}) %all-to-all-start.1) | async-done | bytes 8224 | tf_op jit(solution)/shard_map/all_to_all | solution.py:63
  132.9 0.6 mul.84
  133.5 1.0 copy-done.2
  134.5 4.4 %convolution_convert_fusion = bf16[768,2048]{1,0:T(8,128)(2,1)} fusion(f32[256,2048]{1,0:T(8,128)S(1)} %copy-done.2, f32[32,8,16,128]{3,2,1,0:T(8,128)S(1)} %bitcast.59, f32[256,1536]{1,0:T(8,128)} %fusion.2), kind=kOutput, calls=%fused_computation.4 | convolution fusion | flops 809107456 | bytes 8912896 | tf_op jit(solution)/shard_map/dot_general | solution.py:75
  138.9 2.1 %mul.85 = f32[128,2,2048]{2,1,0:T(2,128)} reshape(f32[128,2,16,128]{3,2,1,0:T(8,128)S(1)} %mul.84) | data formatting | bytes 4194304 | tf_op jit(solution)/shard_map/mul | solution.py:18
  141.0 2.7 %multiply_convert_fusion.1 = bf16[128,2,2048]{2,1,0:T(2,128)(2,1)S(1)} fusion(f32[128,2,2048]{2,1,0:T(2,128)} %mul.85, bf16[128,2,2048]{2,1,0:T(2,128)(2,1)S(1)} %all-to-all-done), kind=kLoop, calls=%fused_computation.15 | loop fusion | flops 1572864 | bytes 4194304 | tf_op jit(solution)/shard_map/convert_element_type | solution.py:19
  143.7 0.4 convert_element_type.96
  144.2 3.5 %multiply_convert_fusion.4 = (bf16[256,768]{1,0:T(8,128)(2,1)S(1)}, bf16[256,768]{1,0:T(8,128)(2,1)S(1)}) fusion(f32[256,1536]{1,0:T(8,128)} %fusion.2, bf16[256,2048]{1,0:T(8,128)(2,1)S(1)} %convert_element_type.96, bf16[1,768,2048]{2,1,0:T(8,128)(2,1)} %all-gather.3.cloned.1.call-done), kind=kOutput, calls=%fused_computation.23 | convolution fusion | flops 807862272 | bytes 6553600 | tf_op jit(solution)/shard_map/dot_general | solution.py:72
  147.7 4.6 %fusion.6 = bf16[256,2048]{1,0:T(8,128)(2,1)S(1)} fusion(bf16[1,2048,1536]{2,1,0:T(8,128)(2,1)} %all-gather.5.cloned.1.call-done, bf16[256,768]{1,0:T(8,128)(2,1)S(1)} %get-tuple-element.5, bf16[256,768]{1,0:T(8,128)(2,1)S(1)} %get-tuple-element.4), kind=kOutput, calls=%fused_computation.8 | convolution fusion | flops 1612709888 | bytes 8126464 | tf_op jit(solution)/shard_map/dot_general | solution.py:82
  152.3 0.7 reshape.88
  153.0 40.4 %all_to_all.25 = bf16[128,2,2048]{2,1,0:T(2,128)(2,1)S(1)} all-to-all(bf16[128,2,2048]{2,1,0:T(2,128)(2,1)S(1)} %reshape.88), channel_id=1, replica_groups=mesh['ep'=128,'edp'=4] {'ep'}, dimensions={0} | all-to-all | bytes 2097152 | tf_op jit(solution)/shard_map/all_to_all | solution.py:86
  193.4 0.4 reshape.89
  193.8 0.9 convolution_convert_fusion.1
  (35 shorter events, 0.8 us)
Async XLA Ops:
  7.2 2.4 %copy-start = (bf16[24,2048]{1,0:T(8,128)(2,1)S(1)}, bf16[24,2048]{1,0:T(8,128)(2,1)}, u32[]{:S(2)}) copy-start(bf16[24,2048]{1,0:T(8,128)(2,1)} %param.6) | copy-start | bytes 294916
  7.2 115.9 %all-gather.5.cloned.1.call-start = ((), (), s32[]{:S(2)}) async-start(), calls=%async_computation.7 | async-start | bytes 7864320 | tf_op jit(solution)/shard_map/all_gather | solution.py:56
  10.8 29.8 %all-to-all-start.3 = ((bf16[128,2,16]{2,1,0:T(2,128)(2,1)}), bf16[128,2,16]{2,1,0:T(2,128)(2,1)S(1)}, u32[]{:S(2)}, u32[]{:S(2)}) async-start(bf16[128,2,16]{2,1,0:T(2,128)(2,1)} %bitcast.8), calls=%async_computation.3 | async-start | bytes 131072 | tf_op jit(solution)/shard_map/all_to_all | solution.py:61
  30.6 16.6 %copy-start.5 = (f32[24,8]{0,1:T(8,128)S(1)}, f32[24,8]{0,1:T(8,128)}, u32[]{:S(2)}) copy-start(f32[24,8]{0,1:T(8,128)} %param.9) | copy-start | bytes 2308
  30.6 16.9 %copy-start.4 = (bf16[24,2048]{1,0:T(8,128)(2,1)S(1)}, bf16[24,2048]{1,0:T(8,128)(2,1)}, u32[]{:S(2)}) copy-start(bf16[24,2048]{1,0:T(8,128)(2,1)} %param.7) | copy-start | bytes 294916
  40.6 36.8 %all-to-all-start.2 = ((bf16[128,2,2048]{2,1,0:T(2,128)(2,1)}), bf16[128,2,2048]{2,1,0:T(2,128)(2,1)S(1)}, u32[]{:S(2)}, u32[]{:S(2)}) async-start(bf16[128,2,2048]{2,1,0:T(2,128)(2,1)} %reshape_reshape.2), calls=%async_computation.2 | async-start | bytes 2097152 | tf_op jit(solution)/shard_map/all_to_all | solution.py:60
  46.4 97.8 %all-gather.3.cloned.1.call-start = ((), (), s32[]{:S(2)}) async-start(), calls=%async_computation.6 | async-start | bytes 3932160 | tf_op jit(solution)/shard_map/all_gather | solution.py:57
  53.5 3.5 %copy-start.1 = (f32[128,2,2048]{2,1,0:T(2,128)S(1)}, f32[128,2,2048]{2,1,0:T(2,128)}, u32[]{:S(2)}) copy-start(f32[128,2,2048]{2,1,0:T(2,128)} %reshape.87) | copy-start | bytes 6291460
  77.4 7.4 %copy-start.3 = (bf16[128,2,2048]{2,1,0:T(2,128)(2,1)}, bf16[128,2,2048]{2,1,0:T(2,128)(2,1)S(1)}, u32[]{:S(2)}) copy-start(bf16[128,2,2048]{2,1,0:T(2,128)(2,1)S(1)} %all-to-all-done.2) | copy-start | bytes 3145732
  77.4 37.6 %all-to-all-start = ((bf16[128,2,2048]{2,1,0:T(2,128)(2,1)}), bf16[128,2,2048]{2,1,0:T(2,128)(2,1)S(1)}, u32[]{:S(2)}, u32[]{:S(2)}) async-start(bf16[128,2,2048]{2,1,0:T(2,128)(2,1)} %divide_convert_fusion.1), calls=%async_computation | async-start | bytes 2097152 | tf_op jit(solution)/shard_map/all_to_all | solution.py:62
  115.0 17.9 %all-to-all-start.1 = ((bf16[128,2,16]{2,1,0:T(2,128)(2,1)}), bf16[128,2,16]{2,1,0:T(2,128)(2,1)S(1)}, u32[]{:S(2)}, u32[]{:S(2)}) async-start(bf16[128,2,16]{2,1,0:T(2,128)(2,1)} %bitcast.4), calls=%async_computation.1 | async-start | bytes 131072 | tf_op jit(solution)/shard_map/all_to_all | solution.py:63
  121.5 73.2 %reduce-scatter.2.cloned.1.call-start = ((), (), s32[]{:S(2)}) async-start(), calls=%async_computation.8 | async-start | bytes 3932160 | tf_op jit(solution)/shard_map/reduce_scatter | solution.py:79
  132.9 1.6 copy-start.2
Sparse Core Ops, SparseCore 0:
  10.1 76.4 all-gather.4
  88.7 45.5 all-gather.2
  139.0 42.6 reduce-scatter.1
where the time goes:
time: 202 us; the launch traced here: 201 us
  waiting for transfers between devices  51.2 us (25%)
  blocking collectives  40.4 us (20%)
  starting transfers between devices  37.5 us (19%)
  local copies, waits for them, and re-layouts  25.5 us (13%)
  matrix products  20.2 us (10%)
  between operations  14 us (7%)
  other arithmetic  12.5 us (6%)
    all_to_all x1, blocking collectives, per_device(): lax.all_to_all(back, 'ep', split_axis=0, concat_axis=0, tiled=True)  40.4 us
    all_to_all x1, waiting for transfers between devices, per_device(): lax.all_to_all(quant_g, 'ep', split_axis=0, concat_axis=0, tiled=True)  21 us
    all_to_all x1, starting transfers between devices, per_device(): lax.all_to_all(scale_x, 'ep', split_axis=0, concat_axis=0, tiled=True)  18.4 us
    all_to_all x1, waiting for transfers between devices, per_device(): lax.all_to_all(quant_x, 'ep', split_axis=0, concat_axis=0, tiled=True)  15.8 us
    all_to_all x1, waiting for transfers between devices, per_device(): lax.all_to_all(scale_x, 'ep', split_axis=0, concat_axis=0, tiled=True)  8.92 us
    mul x4, local copies, waits for them, and re-layouts, restore_rows(): restored = groups * scales.astype(jnp.float32)[..., None]  6.96 us
    all_to_all x1, starting transfers between devices, per_device(): lax.all_to_all(quant_g, 'ep', split_axis=0, concat_axis=0, tiled=True)  6.67 us
    all_to_all x1, starting transfers between devices, per_device(): lax.all_to_all(scale_g, 'ep', split_axis=0, concat_axis=0, tiled=True)  6.48 us
  transfers between devices with their start and end apart: 7, of which 4 were waited for; matrix products, arithmetic and copies ran while one was open for 28% of the time, Pallas kernels for 0%

commit v1 on v0

v1 whole, which is shorter than its diff:
```python
import functools

import jax
import jax.numpy as jnp
from jax import lax
from jax.experimental import pallas as pl
from jax.experimental.pallas import tpu as pltpu
from jax.sharding import PartitionSpec as P

EPSILON = 1e-06
F32, BF16 = jnp.float32, jnp.bfloat16
NT = (((1,), (1,)), ((), ()))
TN = (((0,), (0,)), ((), ()))
VMEM_LIMIT = 56 * 1024 * 1024


def whole(memory_space=pltpu.VMEM):
    return pl.BlockSpec(memory_space=memory_space)


def send_kernel(parts, toks, me_ref, ids_ref, gate_ref, tok_ref, grad_ref, send_ref, pick_ref, stack):
    block = pl.program_id(0)
    rows = send_ref.shape[0]
    lanes = parts * toks
    feat = tok_ref.shape[1] // parts

    @pl.when(block == 0)
    def _():
        for side, ref in enumerate((tok_ref, grad_ref)):
            for k in range(parts):
                first = pl.multiple_of(lax.rem(me_ref[0] + k, parts) * feat, feat)
                stack[pl.ds((side * 2 + k // 2) * toks, toks), pl.ds((k % 2) * feat, feat)] = ref[
                    :, pl.ds(first, feat)
                ].astype(F32)

    row = lax.broadcasted_iota(jnp.int32, (rows, lanes), 0) + block * rows
    lane = lax.broadcasted_iota(jnp.int32, (rows, lanes), 1)
    expert, slot, quarter = row >> 3, (row >> 2) & 1, row & 3
    named = jnp.zeros((rows, lanes), F32)
    weight = jnp.zeros((rows, lanes), F32)
    for k in range(ids_ref.shape[0]):
        hit = ids_ref[k : k + 1, :] == expert
        named = jnp.where(hit, 1.0, named)
        weight = jnp.where(hit, gate_ref[k : k + 1, :], weight)
    above = lax.broadcasted_iota(jnp.int32, (lanes, lanes), 0)
    below = lax.broadcasted_iota(jnp.int32, (lanes, lanes), 1)
    earlier = (above < below) & (above // toks == below // toks)
    rank = jnp.dot(named.astype(BF16), earlier.astype(BF16), preferred_element_type=F32)
    chosen = (named > 0.5) & (rank == slot.astype(F32)) & (lane // toks == quarter)
    pick = jnp.where(chosen, 1.0, 0.0).astype(BF16)
    pick_ref[...] = pick
    scale_row = jnp.sum(jnp.where(chosen, weight, 0.0), axis=1, keepdims=True)
    scale_row = jnp.where(quarter[:, :1] < 2, 1.0, scale_row)
    for g in range(send_ref.shape[1] // 128):
        cols = slice(g * 128, g * 128 + 128)
        value = jnp.dot(pick, stack[:, cols].astype(BF16), preferred_element_type=F32) * scale_row
        top = jnp.max(jnp.abs(value), axis=1, keepdims=True)
        scale = (top + EPSILON).astype(BF16).astype(F32)
        quant = (value / scale).astype(BF16).astype(F32)
        send_ref[:, cols] = (quant * scale).astype(BF16)


def order_matrix(rows, parts):
    out = lax.broadcasted_iota(jnp.int32, (rows, rows), 0)
    src = lax.broadcasted_iota(jnp.int32, (rows, rows), 1)
    per = rows // parts
    return ((out % per) * parts + out // per == src).astype(BF16)


def hidden_kernel(parts, recv_ref, *refs):
    weights, (pre_ref, g_ref), downs, (x_ref, hid_ref) = refs[:7], refs[7:9], refs[9:13], refs[13:]
    rows = 256
    per = rows // parts
    order = order_matrix(rows, parts)
    width = recv_ref.shape[1]
    for b in range(recv_ref.shape[0] // rows):
        got = jnp.dot(order, recv_ref[b * rows : b * rows + rows, :], preferred_element_type=F32).astype(BF16)
        at = slice(b * per, b * per + per)
        x_ref[at, :width] = got[:per]
        x_ref[at, width:] = got[per : 2 * per]
        g_ref[at, :width] = got[2 * per : 3 * per]
        g_ref[at, width:] = got[3 * per :]
    hidden_units = pre_ref.shape[1] // 2
    tile = 256
    for n in range(pre_ref.shape[1] // tile):
        cols = slice(n * tile, n * tile + tile)
        total, at = None, 0
        for w in weights:
            depth = w.shape[0]
            term = jnp.dot(x_ref[:, at : at + depth], w[:, cols], preferred_element_type=F32)
            total, at = term if total is None else total + term, at + depth
        pre_ref[:, cols] = total
    for n in range(hidden_units // tile):
        cols = slice(n * tile, n * tile + tile)
        gate = pre_ref[:, cols]
        up = pre_ref[:, hidden_units + n * tile : hidden_units + n * tile + tile]
        hid_ref[:, cols] = (gate * jax.nn.sigmoid(gate) * up).astype(BF16)
    for k, down in enumerate(downs):
        feat = down.shape[1]
        for n in range(hidden_units // tile):
            cols = slice(n * tile, n * tile + tile)
            down[cols, :] = lax.dot_general(
                hid_ref[:, cols], g_ref[:, k * feat : k * feat + feat], TN, preferred_element_type=F32
            ).astype(BF16)


def back_kernel(parts, pre_ref, g_ref, *refs):
    ups, downs, (back_ref, gp_ref) = refs[:7], refs[7:14], refs[14:]
    hidden_units = pre_ref.shape[1] // 2
    half = hidden_units // 2
    feat = g_ref.shape[1] // parts
    gs = [g_ref[:, k * feat : k * feat + feat] for k in range(parts)]
    own, right_a, right_b, far_a, far_b, left_a, left_b = downs
    for h in range(2):
        picks = (own[h * half : h * half + half, :], (right_a, right_b)[h][...], (far_a, far_b)[h][...], (left_a, left_b)[h][...])
        total = None
        for g, w in zip(gs, picks):
            term = lax.dot_general(g, w, NT, preferred_element_type=F32)
            total = term if total is None else total + term
        cols = slice(h * half, h * half + half)
        up_cols = slice(hidden_units + h * half, hidden_units + h * half + half)
        gate, up = pre_ref[:, cols], pre_ref[:, up_cols]
        sig = jax.nn.sigmoid(gate)
        gp_ref[:, cols] = (total * up * sig * (1.0 + gate * (1.0 - sig))).astype(BF16)
        gp_ref[:, up_cols] = (total * (gate * sig)).astype(BF16)
    blocks = []
    pieces = [ups[0]], [ups[1], ups[2]], [ups[3], ups[4]], [ups[5], ups[6]]
    for group in pieces:
        outs = [lax.dot_general(gp_ref[...], w[...], NT, preferred_element_type=F32).astype(BF16) for w in group]
        blocks.append(outs[0] if len(outs) == 1 else jnp.concatenate(outs, axis=1))
    rows = 256
    per = rows // parts
    order = order_matrix(rows, parts)
    for b in range(back_ref.shape[0] // rows):
        stacked = jnp.concatenate([blk[b * per : b * per + per] for blk in blocks], axis=0)
        back_ref[b * rows : b * rows + rows, :] = lax.dot_general(
            order, stacked, TN, preferred_element_type=F32
        ).astype(BF16)


def combine_kernel(parts, toks, me_ref, pick_ref, ret_ref, out_ref):
    feat = ret_ref.shape[1]
    total = lax.dot_general(pick_ref[...], ret_ref[...], TN, preferred_element_type=F32)
    for k in range(parts):
        first = pl.multiple_of(lax.rem(me_ref[0] + k, parts) * feat, feat)
        out_ref[:, pl.ds(first, feat)] = total[k * toks : k * toks + toks].astype(BF16)


def gather_pieces(w, size):
    half = w.shape[0] // 2
    top, bottom = w[:half], w[half:]
    fwd = [(i, (i + 1) % size) for i in range(size)]
    bwd = [(i, (i - 1) % size) for i in range(size)]
    left_top = lax.ppermute(top, "edp", fwd)
    right_bottom = lax.ppermute(bottom, "edp", bwd)
    left_bottom = lax.ppermute(bottom, "edp", fwd)
    right_top = lax.ppermute(top, "edp", bwd)
    far_top = lax.ppermute(left_top, "edp", fwd)
    far_bottom = lax.ppermute(right_bottom, "edp", bwd)
    return [w, right_top, right_bottom, far_top, far_bottom, left_top, left_bottom]


def per_device(tokens, out_grad, expert_ids, gate_values, gate_up_weight, down_weight):
    experts, parts = lax.axis_size("ep"), lax.axis_size("edp")
    toks, width = tokens.shape
    hidden_units = down_weight.shape[1]
    feat = width // parts
    slots = experts * 2
    params = pltpu.CompilerParams(vmem_limit_bytes=VMEM_LIMIT)
    me = lax.axis_index("edp").astype(jnp.int32).reshape(1)
    ids = jnp.tile(expert_ids.T, (1, parts))
    gates = jnp.tile(gate_values.T, (1, parts))

    ups = gather_pieces(gate_up_weight[0], parts)
    downs = gather_pieces(down_weight[0], parts)

    rows = slots * parts
    tile = 128
    sent, pick = pl.pallas_call(
        functools.partial(send_kernel, parts, toks),
        grid=(rows // tile,),
        in_specs=[whole(pltpu.SMEM)] + [whole()] * 4,
        out_specs=[
            pl.BlockSpec((tile, width // 2), lambda b: (b, 0)),
            pl.BlockSpec((tile, parts * toks), lambda b: (b, 0)),
        ],
        out_shape=[
            jax.ShapeDtypeStruct((rows, width // 2), BF16),
            jax.ShapeDtypeStruct((rows, parts * toks), BF16),
        ],
        scratch_shapes=[pltpu.VMEM((parts * toks, width // 2), F32)],
        compiler_params=params,
        name="send_rows",
    )(me, ids, gates, tokens, out_grad)
    recv = lax.all_to_all(sent, "ep", split_axis=0, concat_axis=0, tiled=True)

    pre, rows_g, *partial = pl.pallas_call(
        functools.partial(hidden_kernel, parts),
        in_specs=[whole()] * 8,
        out_specs=[whole()] * 6,
        out_shape=[
            jax.ShapeDtypeStruct((slots, 2 * hidden_units), F32),
            jax.ShapeDtypeStruct((slots, width), BF16),
        ]
        + [jax.ShapeDtypeStruct((hidden_units, feat), BF16)] * parts,
        scratch_shapes=[pltpu.VMEM((slots, width), BF16), pltpu.VMEM((slots, hidden_units), BF16)],
        compiler_params=params,
        name="hidden_rows",
    )(recv, *ups)

    sums = partial[0].astype(F32)
    for k in range(1, parts):
        perm = [(i, (i + k) % parts) for i in range(parts)]
        sums = sums + lax.ppermute(partial[k], "edp", perm).astype(F32)
    down_grad = sums.astype(BF16)[None]

    back = pl.pallas_call(
        functools.partial(back_kernel, parts),
        in_specs=[whole()] * 16,
        out_specs=whole(),
        out_shape=jax.ShapeDtypeStruct((rows, feat), BF16),
        scratch_shapes=[pltpu.VMEM((slots, 2 * hidden_units), BF16)],
        compiler_params=params,
        name="back_rows",
    )(pre, rows_g, *ups, *downs)
    returned = lax.all_to_all(back, "ep", split_axis=0, concat_axis=0, tiled=True)
    token_grads = pl.pallas_call(
        functools.partial(combine_kernel, parts, toks),
        in_specs=[whole(pltpu.SMEM), whole(), whole()],
        out_specs=whole(),
        out_shape=jax.ShapeDtypeStruct((toks, width), BF16),
        compiler_params=params,
        name="combine_rows",
    )(me, pick, returned)
    return (token_grads, down_grad)


def solution(mesh):
    return jax.shard_map(
        per_device,
        mesh=mesh,
        in_specs=(
            P(("ep", "edp"), None),
            P(("ep", "edp"), None),
            P(("ep", "edp"), None),
            P(("ep", "edp"), None),
            P("ep", "edp", None),
            P("ep", None, "edp"),
        ),
        out_specs=(P(("ep", "edp"), None), P("ep", None, "edp")),
        check_vma=False,
    )
```

time: 202 us -> 187 us (0.926)
  starting transfers between devices: 37.5 us -> 83.2 us
  blocking collectives: 40.4 us -> 0 us
  Pallas kernels: 0 us -> 25.5 us
  matrix products: 20.2 us -> 0 us
  local copies, waits for them, and re-layouts: 25.5 us -> 5.7 us
  waiting for transfers between devices: 51.2 us -> 69.8 us
  between operations: 14 us -> 0.95 us
  other arithmetic: 12.5 us -> 1.31 us
    ppermute x0 -> x15, waiting for transfers between devices: none -> 69.8 us  [the longest x2 34.3 us: gather_pieces(): left_top = lax.ppermute(top, 'edp', fwd)]
    all_to_all x4 -> x2, waiting for transfers between devices: 49.8 us -> 0.01 us  [the longest x1 0.01 us: per_device(): lax.all_to_all(back, 'ep', split_axis=0, concat_axis=0, tiled=True)]
    ppermute x0 -> x15, starting transfers between devices: none -> 46.9 us  [the longest x3 10.4 us: per_device(): sums = sums + lax.ppermute(partial[k], 'edp', perm).astype(F32)]
    all_to_all x1 -> x0, blocking collectives: 40.4 us -> none  [per_device(): lax.all_to_all(back, 'ep', split_axis=0, concat_axis=0, tiled=True)]
    pallas_call x0 -> x4, Pallas kernels: none -> 25.5 us  [the longest x1 8.76 us: per_device(): pl.pallas_call(functools.partial(back_kernel, parts), in_specs=[whole()]...]
    dot_general x7 -> x0, matrix products: 20.2 us -> none  [the longest x1 5.8 us: per_device(): pre = jnp.dot(rows_x, gate_up_mat, preferred_element_type=jnp.float32)]
    convert_element_type x6 -> x0, other arithmetic: 10.9 us -> none  [the longest x2 6.14 us: restore_rows(): return restored.astype(jnp.bfloat16).reshape(quant.shape)]
    mul x4 -> x0, local copies, waits for them, and re-layouts: 6.96 us -> none  [restore_rows(): restored = groups * scales.astype(jnp.float32)[..., None]]
  transfers between devices with their start and end apart: 7 -> 17, of which waited for: 4 -> 7; matrix products, arithmetic and copies ran while one was open for 28% -> 1% of each run, Pallas kernels for 0% -> 4%
where the time goes in v1:
time: 187 us; the launch traced here: 186 us
  starting transfers between devices  83.2 us (44%)
  waiting for transfers between devices  69.8 us (37%)
  Pallas kernels  25.5 us (14%)
  local copies, waits for them, and re-layouts  5.7 us (3%)
    ppermute x2, waiting for transfers between devices, gather_pieces(): left_top = lax.ppermute(top, 'edp', fwd)  34.3 us
    ppermute x3, waiting for transfers between devices, per_device(): sums = sums + lax.ppermute(partial[k], 'edp', perm).astype(F32)  31.3 us
    all_to_all x1, starting transfers between devices, per_device(): recv = lax.all_to_all(sent, 'ep', split_axis=0, concat_axis=0, tiled=True)  19 us
    all_to_all x1, starting transfers between devices, per_device(): lax.all_to_all(back, 'ep', split_axis=0, concat_axis=0, tiled=True)  17.3 us
    ppermute x3, starting transfers between devices, per_device(): sums = sums + lax.ppermute(partial[k], 'edp', perm).astype(F32)  10.4 us
    pallas_call x1, Pallas kernels, per_device(): pl.pallas_call(functools.partial(back_kernel, parts), in_specs=[whole()]...  8.76 us
    pallas_call x1, Pallas kernels, per_device(): pl.pallas_call(functools.partial(hidden_kernel, parts), in_specs=[whole()...  7.87 us
    ppermute x2, starting transfers between devices, gather_pieces(): right_top = lax.ppermute(top, 'edp', bwd)  7.03 us
  transfers between devices with their start and end apart: 17, of which 7 were waited for; matrix products, arithmetic and copies ran while one was open for 1% of the time, Pallas kernels for 4%

profile of v1, /device:TPU:1, one launch (start us, length us, event | category | flops | bytes accessed | tf_op | source)
XLA Modules:
  0.0 186.4 jit_solution(3520868161973654198)
XLA Ops:
  0.6 0.7 tile.20
  1.3 0.7 tile.21.gate_ref
  2.0 0.7 tile.8
  2.7 0.7 tile.9.ids_ref
  3.4 6.6 %send_rows.1 = (bf16[1024,1024]{1,0:T(8,128)(2,1)}, bf16[1024,96]{1,0:T(8,128)(2,1)}) custom-call(s32[1]{0:T(128)} %bitcast.me_ref, s32[8,96]{1,0:T(8,128)} %tile.9.ids_ref, f32[8,96]{1,0:T(8,128)} %tile.21.gate_ref, bf16[24,2048]{1,0:T(8,128)(2,1)} %tok_ref.1, bf16[24,2048]{1,0:T(8,128)(2,1)} %grad_ref.1), custom_call_target="tpu_custom_call" | custom-call | tf_op jit(solution)/shard_map/send_rows/pallas_call | solution.py:179
  9.9 19.0 %all-to-all-start = ((bf16[128,8,1024]{2,1,0:T(8,128)(2,1)}), bf16[128,8,1024]{2,1,0:T(8,128)(2,1)}, u32[]{:S(2)}, u32[]{:S(2)}) async-start(bf16[128,8,1024]{2,1,0:T(8,128)(2,1)} %bitcast.24), calls=%async_computation | async-start | bytes 4194304 | tf_op jit(solution)/shard_map/all_to_all | solution.py:195
  29.0 0.0 copy-start.7
  29.0 0.1 slice_bitcast_fusion
  29.1 3.3 %collective-permute-start.2 = (bf16[256,1536]{1,0:T(8,128)(2,1)S(1)}, bf16[256,1536]{1,0:T(8,128)(2,1)S(1)}, u32[]{:S(2)}, u32[]{:S(2)}) collective-permute-start(bf16[256,1536]{1,0:T(8,128)(2,1)S(1)} %get-tuple-element.19), channel_id=1, source_target_pairs={{0,1},{1,2},{2,3},{3,0},{4,5},{5,6},{6,7},{7,4},{8,9},{9,10},{10,1... | collective-permute-start | bytes 2359304 | tf_op jit(solution)/shard_map/ppermute | solution.py:154
  32.3 3.4 %collective-permute-start.1 = (bf16[256,1536]{1,0:T(8,128)(2,1)S(1)}, bf16[256,1536]{1,0:T(8,128)(2,1)S(1)}, u32[]{:S(2)}, u32[]{:S(2)}) collective-permute-start(bf16[256,1536]{1,0:T(8,128)(2,1)S(1)} %get-tuple-element.18), channel_id=1, source_target_pairs={{0,3},{1,0},{2,1},{3,2},{4,7},{5,4},{6,5},{7,6},{8,11},{9,8},{10,9... | collective-permute-start | bytes 2359304 | tf_op jit(solution)/shard_map/ppermute | solution.py:155
  35.7 0.9 slice_bitcast_fusion.2
  36.7 3.2 %collective-permute-start.7 = (bf16[384,512]{1,0:T(8,128)(2,1)}, bf16[384,512]{1,0:T(8,128)(2,1)S(1)}, u32[]{:S(2)}, u32[]{:S(2)}) collective-permute-start(bf16[384,512]{1,0:T(8,128)(2,1)} %get-tuple-element.20), channel_id=1, source_target_pairs={{0,3},{1,0},{2,1},{3,2},{4,7},{5,4},{6,5},{7,6},{8,11},{9,8},{10,9... | collective-permute-start | bytes 1179656 | tf_op jit(solution)/shard_map/ppermute | solution.py:155
  39.9 2.5 %collective-permute-start = (bf16[256,1536]{1,0:T(8,128)(2,1)S(1)}, bf16[256,1536]{1,0:T(8,128)(2,1)S(1)}, u32[]{:S(2)}, u32[]{:S(2)}) collective-permute-start(bf16[256,1536]{1,0:T(8,128)(2,1)S(1)} %get-tuple-element.19), channel_id=1, source_target_pairs={{0,3},{1,0},{2,1},{3,2},{4,7},{5,4},{6,5},{7,6},{8,11},{9,8},{10,9... | collective-permute-start | bytes 2359304 | tf_op jit(solution)/shard_map/ppermute | solution.py:157
  42.3 2.8 %collective-permute-start.5 = (bf16[256,1536]{1,0:T(8,128)(2,1)S(1)}, bf16[256,1536]{1,0:T(8,128)(2,1)S(1)}, u32[]{:S(2)}, u32[]{:S(2)}) collective-permute-start(bf16[256,1536]{1,0:T(8,128)(2,1)S(1)} %get-tuple-element.18), channel_id=1, source_target_pairs={{0,1},{1,2},{2,3},{3,0},{4,5},{5,6},{6,7},{7,4},{8,9},{9,10},{10,1... | collective-permute-start | bytes 2359304 | tf_op jit(solution)/shard_map/ppermute | solution.py:156
  45.1 5.4 %collective-permute-done.2.refs_5_ = bf16[256,1536]{1,0:T(8,128)(2,1)S(1)} collective-permute-done((bf16[256,1536]{1,0:T(8,128)(2,1)S(1)}, bf16[256,1536]{1,0:T(8,128)(2,1)S(1)}, u32[]{:S(2)}, u32[]{:S(2)}) %collective-permute-start.2) | collective-permute-done | bytes 786464 | tf_op jit(solution)/shard_map/ppermute | solution.py:154
  50.5 1.9 %collective-permute-start.3 = (bf16[256,1536]{1,0:T(8,128)(2,1)S(1)}, bf16[256,1536]{1,0:T(8,128)(2,1)S(1)}, u32[]{:S(2)}, u32[]{:S(2)}) collective-permute-start(bf16[256,1536]{1,0:T(8,128)(2,1)S(1)} %collective-permute-done.2.refs_5_), channel_id=1, source_target_pairs={{0,1},{1,2},{2,3},{3,0},{4,5},{5,6},{6,7},{7,4},{8,9},{9,10},{10,1... | collective-permute-start | bytes 2359304 | tf_op jit(solution)/shard_map/ppermute | solution.py:158
  52.4 0.0 collective-permute-done.1.refs_2_
  52.4 4.6 %collective-permute-start.4 = (bf16[256,1536]{1,0:T(8,128)(2,1)S(1)}, bf16[256,1536]{1,0:T(8,128)(2,1)}, u32[]{:S(2)}, u32[]{:S(2)}) collective-permute-start(bf16[256,1536]{1,0:T(8,128)(2,1)S(1)} %collective-permute-done.1.refs_2_), channel_id=1, source_target_pairs={{0,3},{1,0},{2,1},{3,2},{4,7},{5,4},{6,5},{7,6},{8,11},{9,8},{10,9... | collective-permute-start | bytes 2359304 | tf_op jit(solution)/shard_map/ppermute | solution.py:159
  57.0 3.5 %collective-permute-done.7.refs_9_ = bf16[384,512]{1,0:T(8,128)(2,1)S(1)} collective-permute-done((bf16[384,512]{1,0:T(8,128)(2,1)}, bf16[384,512]{1,0:T(8,128)(2,1)S(1)}, u32[]{:S(2)}, u32[]{:S(2)}) %collective-permute-start.7) | collective-permute-done | bytes 393248 | tf_op jit(solution)/shard_map/ppermute | solution.py:155
  60.6 3.1 %collective-permute-start.8 = (bf16[384,512]{1,0:T(8,128)(2,1)}, bf16[384,512]{1,0:T(8,128)(2,1)}, u32[]{:S(2)}, u32[]{:S(2)}) collective-permute-start(bf16[384,512]{1,0:T(8,128)(2,1)} %get-tuple-element.21), channel_id=1, source_target_pairs={{0,1},{1,2},{2,3},{3,0},{4,5},{5,6},{6,7},{7,4},{8,9},{9,10},{10,1... | collective-permute-start | bytes 1179656 | tf_op jit(solution)/shard_map/ppermute | solution.py:154
  63.7 29.0 %collective-permute-done.8.refs_12_ = bf16[384,512]{1,0:T(8,128)(2,1)} collective-permute-done((bf16[384,512]{1,0:T(8,128)(2,1)}, bf16[384,512]{1,0:T(8,128)(2,1)}, u32[]{:S(2)}, u32[]{:S(2)}) %collective-permute-start.8) | collective-permute-done | bytes 393248 | tf_op jit(solution)/shard_map/ppermute | solution.py:154
  92.6 1.9 %collective-permute-start.11 = (bf16[384,512]{1,0:T(8,128)(2,1)}, bf16[384,512]{1,0:T(8,128)(2,1)}, u32[]{:S(2)}, u32[]{:S(2)}) collective-permute-start(bf16[384,512]{1,0:T(8,128)(2,1)} %get-tuple-element.20), channel_id=1, source_target_pairs={{0,1},{1,2},{2,3},{3,0},{4,5},{5,6},{6,7},{7,4},{8,9},{9,10},{10,1... | collective-permute-start | bytes 1179656 | tf_op jit(solution)/shard_map/ppermute | solution.py:156
  94.6 0.0 collective-permute-done.refs_1_
  94.6 0.0 copy-start.4
  94.6 4.6 %collective-permute-start.6 = (bf16[384,512]{1,0:T(8,128)(2,1)}, bf16[384,512]{1,0:T(8,128)(2,1)}, u32[]{:S(2)}, u32[]{:S(2)}) collective-permute-start(bf16[384,512]{1,0:T(8,128)(2,1)} %get-tuple-element.21), channel_id=1, source_target_pairs={{0,3},{1,0},{2,1},{3,2},{4,7},{5,4},{6,5},{7,6},{8,11},{9,8},{10,9... | collective-permute-start | bytes 1179656 | tf_op jit(solution)/shard_map/ppermute | solution.py:157
  99.2 0.0 collective-permute-done.5.refs_6_
  99.2 2.0 %collective-permute-start.10 = (bf16[384,512]{1,0:T(8,128)(2,1)S(1)}, bf16[384,512]{1,0:T(8,128)(2,1)}, u32[]{:S(2)}, u32[]{:S(2)}) collective-permute-start(bf16[384,512]{1,0:T(8,128)(2,1)S(1)} %collective-permute-done.7.refs_9_), channel_id=1, source_target_pairs={{0,3},{1,0},{2,1},{3,2},{4,7},{5,4},{6,5},{7,6},{8,11},{9,8},{10,9... | collective-permute-start | bytes 1179656 | tf_op jit(solution)/shard_map/ppermute | solution.py:159
  101.2 0.0 collective-permute-done.3.refs_3_
  101.2 0.9 copy-done.6
  102.1 3.3 %collective-permute-start.9 = (bf16[384,512]{1,0:T(8,128)(2,1)}, bf16[384,512]{1,0:T(8,128)(2,1)}, u32[]{:S(2)}, u32[]{:S(2)}) collective-permute-start(bf16[384,512]{1,0:T(8,128)(2,1)} %collective-permute-done.8.refs_12_), channel_id=1, source_target_pairs={{0,1},{1,2},{2,3},{3,0},{4,5},{5,6},{6,7},{7,4},{8,9},{9,10},{10,1... | collective-permute-start | bytes 1179656 | tf_op jit(solution)/shard_map/ppermute | solution.py:158
  105.4 0.0 collective-permute-done.4.refs_4_
  105.4 7.9 %hidden_rows.1 = (f32[256,1536]{1,0:T(8,128)}, bf16[256,2048]{1,0:T(8,128)(2,1)}, bf16[768,512]{1,0:T(8,128)(2,1)}, bf16[768,512]{1,0:T(8,128)(2,1)}, bf16[768,5...) custom-call(bf16[1024,1024]{1,0:T(8,128)(2,1)} %bitcast.4.recv_ref, bf16[512,1536]{1,0:T(8,128)(2,1)} %bitcast.19, ...), custom_call_target="tpu_custom_call" | custom-call | tf_op jit(solution)/shard_map/hidden_rows/pallas_call | solution.py:197
  113.3 0.0 collective-permute-done.11.refs_13_
  113.3 0.0 collective-permute-done.6.refs_8_
  113.3 0.7 collective-permute-done.10.refs_11_
  114.0 0.0 collective-permute-done.9.refs_10_
  114.0 8.8 %back_rows.1 = bf16[1024,512]{1,0:T(8,128)(2,1)} custom-call(f32[256,1536]{1,0:T(8,128)} %get-tuple-element.12.pre_ref, bf16[256,2048]{1,0:T(8,128)(2,1)} %get-tuple-element.13.g_ref, bf16[512,1536]{1,0:T(8,128)(2,1)} %bitcast.20, bf16[256,1536]{1,0:T(8,128)(2,1)} %copy-done.4, bf16[256,1536]{1,0:T(8,128)(2,1)} %copy-done.3, bf16[256,1536]{1,0:T(8,128)(2,1)} %copy-done.6, ...), custom_call_target="tpu_custom_call" | custom-call | tf_op jit(solution)/shard_map/back_rows/pallas_call | solution.py:217
  122.8 17.3 %all-to-all-start.1 = ((bf16[128,8,512]{2,1,0:T(8,128)(2,1)}), bf16[128,8,512]{2,1,0:T(8,128)(2,1)S(1)}, u32[]{:S(2)}, u32[]{:S(2)}) async-start(bf16[128,8,512]{2,1,0:T(8,128)(2,1)} %bitcast.21), calls=%async_computation.1 | async-start | bytes 2097152 | tf_op jit(solution)/shard_map/all_to_all | solution.py:226
  140.1 2.8 %collective-permute-start.12 = (bf16[768,512]{1,0:T(8,128)(2,1)}, bf16[768,512]{1,0:T(8,128)(2,1)S(1)}, u32[]{:S(2)}, u32[]{:S(2)}) collective-permute-start(bf16[768,512]{1,0:T(8,128)(2,1)} %get-tuple-element.15), channel_id=1, source_target_pairs={{0,1},{1,2},{2,3},{3,0},{4,5},{5,6},{6,7},{7,4},{8,9},{9,10},{10,1... | collective-permute-start | bytes 2359304 | tf_op jit(solution)/shard_map/ppermute | solution.py:214
  142.9 5.8 %collective-permute-start.13 = (bf16[768,512]{1,0:T(8,128)(2,1)S(1)}, bf16[768,512]{1,0:T(8,128)(2,1)S(1)}, u32[]{:S(2)}, u32[]{:S(2)}) collective-permute-start(bf16[768,512]{1,0:T(8,128)(2,1)S(1)} %copy-done.11), channel_id=1, source_target_pairs={{0,2},{1,3},{2,0},{3,1},{4,6},{5,7},{6,4},{7,5},{8,10},{9,11},{10,... | collective-permute-start | bytes 2359304 | tf_op jit(solution)/shard_map/ppermute | solution.py:214
  148.6 1.9 %collective-permute-start.14 = (bf16[768,512]{1,0:T(8,128)(2,1)S(1)}, bf16[768,512]{1,0:T(8,128)(2,1)S(1)}, u32[]{:S(2)}, u32[]{:S(2)}) collective-permute-start(bf16[768,512]{1,0:T(8,128)(2,1)S(1)} %copy-done.10), channel_id=1, source_target_pairs={{0,3},{1,0},{2,1},{3,2},{4,7},{5,4},{6,5},{7,6},{8,11},{9,8},{10,9... | collective-permute-start | bytes 2359304 | tf_op jit(solution)/shard_map/ppermute | solution.py:214
  150.6 12.2 %collective-permute-done.12 = bf16[768,512]{1,0:T(8,128)(2,1)S(1)} collective-permute-done((bf16[768,512]{1,0:T(8,128)(2,1)}, bf16[768,512]{1,0:T(8,128)(2,1)S(1)}, u32[]{:S(2)}, u32[]{:S(2)}) %collective-permute-start.12) | collective-permute-done | bytes 786464 | tf_op jit(solution)/shard_map/ppermute | solution.py:214
  162.7 17.7 %collective-permute-done.13 = bf16[768,512]{1,0:T(8,128)(2,1)S(1)} collective-permute-done((bf16[768,512]{1,0:T(8,128)(2,1)S(1)}, bf16[768,512]{1,0:T(8,128)(2,1)S(1)}, u32[]{:S(2)}, u32[]{:S(2)}) %collective-permute-start.13) | collective-permute-done | bytes 786464 | tf_op jit(solution)/shard_map/ppermute | solution.py:214
  180.4 1.4 collective-permute-done.14
  181.9 1.3 fusion
  183.2 0.0 all-to-all-done.1
  183.2 1.0 copy-done.1
  184.2 2.3 %combine_rows.1 = bf16[24,2048]{1,0:T(8,128)(2,1)} custom-call(s32[1]{0:T(128)} %bitcast.me_ref, bf16[1024,96]{1,0:T(8,128)(2,1)} %get-tuple-element.10.pick_ref, bf16[1024,512]{1,0:T(8,128)(2,1)} %bitcast.22), custom_call_target="tpu_custom_call" | custom-call | tf_op jit(solution)/shard_map/combine_rows/pallas_call | solution.py:227
  (21 shorter events, 0.0 us)
Async XLA Ops:
  9.9 19.0 %copy-start = (bf16[1,512,1536]{2,1,0:T(8,128)(2,1)S(1)}, bf16[1,512,1536]{2,1,0:T(8,128)(2,1)}, u32[]{:S(2)}) copy-start(bf16[1,512,1536]{2,1,0:T(8,128)(2,1)} %param.10) | copy-start | bytes 4718596
  9.9 95.5 %all-to-all-start = ((bf16[128,8,1024]{2,1,0:T(8,128)(2,1)}), bf16[128,8,1024]{2,1,0:T(8,128)(2,1)}, u32[]{:S(2)}, u32[]{:S(2)}) async-start(bf16[128,8,1024]{2,1,0:T(8,128)(2,1)} %bitcast.24), calls=%async_computation | async-start | bytes 4194304 | tf_op jit(solution)/shard_map/all_to_all | solution.py:195
  29.0 6.8 %copy-start.7 = (bf16[1,768,512]{2,1,0:T(8,128)(2,1)S(1)}, bf16[1,768,512]{2,1,0:T(8,128)(2,1)}, u32[]{:S(2)}) copy-start(bf16[1,768,512]{2,1,0:T(8,128)(2,1)} %param.11) | copy-start | bytes 2359300
  29.1 21.4 %collective-permute-start.2 = (bf16[256,1536]{1,0:T(8,128)(2,1)S(1)}, bf16[256,1536]{1,0:T(8,128)(2,1)S(1)}, u32[]{:S(2)}, u32[]{:S(2)}) collective-permute-start(bf16[256,1536]{1,0:T(8,128)(2,1)S(1)} %get-tuple-element.19), channel_id=1, source_target_pairs={{0,1},{1,2},{2,3},{3,0},{4,5},{5,6},{6,7},{7,4},{8,9},{9,10},{10,1... | collective-permute-start | bytes 2359304 | tf_op jit(solution)/shard_map/ppermute | solution.py:154
  32.3 20.1 %collective-permute-start.1 = (bf16[256,1536]{1,0:T(8,128)(2,1)S(1)}, bf16[256,1536]{1,0:T(8,128)(2,1)S(1)}, u32[]{:S(2)}, u32[]{:S(2)}) collective-permute-start(bf16[256,1536]{1,0:T(8,128)(2,1)S(1)} %get-tuple-element.18), channel_id=1, source_target_pairs={{0,3},{1,0},{2,1},{3,2},{4,7},{5,4},{6,5},{7,6},{8,11},{9,8},{10,9... | collective-permute-start | bytes 2359304 | tf_op jit(solution)/shard_map/ppermute | solution.py:155
  36.7 23.9 %collective-permute-start.7 = (bf16[384,512]{1,0:T(8,128)(2,1)}, bf16[384,512]{1,0:T(8,128)(2,1)S(1)}, u32[]{:S(2)}, u32[]{:S(2)}) collective-permute-start(bf16[384,512]{1,0:T(8,128)(2,1)} %get-tuple-element.20), channel_id=1, source_target_pairs={{0,3},{1,0},{2,1},{3,2},{4,7},{5,4},{6,5},{7,6},{8,11},{9,8},{10,9... | collective-permute-start | bytes 1179656 | tf_op jit(solution)/shard_map/ppermute | solution.py:155
  39.9 54.7 %collective-permute-start = (bf16[256,1536]{1,0:T(8,128)(2,1)S(1)}, bf16[256,1536]{1,0:T(8,128)(2,1)S(1)}, u32[]{:S(2)}, u32[]{:S(2)}) collective-permute-start(bf16[256,1536]{1,0:T(8,128)(2,1)S(1)} %get-tuple-element.19), channel_id=1, source_target_pairs={{0,3},{1,0},{2,1},{3,2},{4,7},{5,4},{6,5},{7,6},{8,11},{9,8},{10,9... | collective-permute-start | bytes 2359304 | tf_op jit(solution)/shard_map/ppermute | solution.py:157
  42.3 56.8 %collective-permute-start.5 = (bf16[256,1536]{1,0:T(8,128)(2,1)S(1)}, bf16[256,1536]{1,0:T(8,128)(2,1)S(1)}, u32[]{:S(2)}, u32[]{:S(2)}) collective-permute-start(bf16[256,1536]{1,0:T(8,128)(2,1)S(1)} %get-tuple-element.18), channel_id=1, source_target_pairs={{0,1},{1,2},{2,3},{3,0},{4,5},{5,6},{6,7},{7,4},{8,9},{9,10},{10,1... | collective-permute-start | bytes 2359304 | tf_op jit(solution)/shard_map/ppermute | solution.py:156
  50.5 54.9 %copy-start.2 = (bf16[256,1536]{1,0:T(8,128)(2,1)}, bf16[256,1536]{1,0:T(8,128)(2,1)S(1)}, u32[]{:S(2)}) copy-start(bf16[256,1536]{1,0:T(8,128)(2,1)S(1)} %collective-permute-done.2.refs_5_) | copy-start | bytes 2359300
  50.5 50.7 %collective-permute-start.3 = (bf16[256,1536]{1,0:T(8,128)(2,1)S(1)}, bf16[256,1536]{1,0:T(8,128)(2,1)S(1)}, u32[]{:S(2)}, u32[]{:S(2)}) collective-permute-start(bf16[256,1536]{1,0:T(8,128)(2,1)S(1)} %collective-permute-done.2.refs_5_), channel_id=1, source_target_pairs={{0,1},{1,2},{2,3},{3,0},{4,5},{5,6},{6,7},{7,4},{8,9},{9,10},{10,1... | collective-permute-start | bytes 2359304 | tf_op jit(solution)/shard_map/ppermute | solution.py:158
  52.4 53.0 %copy-start.3 = (bf16[256,1536]{1,0:T(8,128)(2,1)}, bf16[256,1536]{1,0:T(8,128)(2,1)S(1)}, u32[]{:S(2)}) copy-start(bf16[256,1536]{1,0:T(8,128)(2,1)S(1)} %collective-permute-done.1.refs_2_) | copy-start | bytes 2359300
  52.4 52.9 %collective-permute-start.4 = (bf16[256,1536]{1,0:T(8,128)(2,1)S(1)}, bf16[256,1536]{1,0:T(8,128)(2,1)}, u32[]{:S(2)}, u32[]{:S(2)}) collective-permute-start(bf16[256,1536]{1,0:T(8,128)(2,1)S(1)} %collective-permute-done.1.refs_2_), channel_id=1, source_target_pairs={{0,3},{1,0},{2,1},{3,2},{4,7},{5,4},{6,5},{7,6},{8,11},{9,8},{10,9... | collective-permute-start | bytes 2359304 | tf_op jit(solution)/shard_map/ppermute | solution.py:159
  60.6 53.5 %copy-start.9 = (bf16[384,512]{1,0:T(8,128)(2,1)}, bf16[384,512]{1,0:T(8,128)(2,1)S(1)}, u32[]{:S(2)}) copy-start(bf16[384,512]{1,0:T(8,128)(2,1)S(1)} %collective-permute-done.7.refs_9_) | copy-start | bytes 1179652
  60.6 32.1 %collective-permute-start.8 = (bf16[384,512]{1,0:T(8,128)(2,1)}, bf16[384,512]{1,0:T(8,128)(2,1)}, u32[]{:S(2)}, u32[]{:S(2)}) collective-permute-start(bf16[384,512]{1,0:T(8,128)(2,1)} %get-tuple-element.21), channel_id=1, source_target_pairs={{0,1},{1,2},{2,3},{3,0},{4,5},{5,6},{6,7},{7,4},{8,9},{9,10},{10,1... | collective-permute-start | bytes 1179656 | tf_op jit(solution)/shard_map/ppermute | solution.py:154
  92.6 20.7 %collective-permute-start.11 = (bf16[384,512]{1,0:T(8,128)(2,1)}, bf16[384,512]{1,0:T(8,128)(2,1)}, u32[]{:S(2)}, u32[]{:S(2)}) collective-permute-start(bf16[384,512]{1,0:T(8,128)(2,1)} %get-tuple-element.20), channel_id=1, source_target_pairs={{0,1},{1,2},{2,3},{3,0},{4,5},{5,6},{6,7},{7,4},{8,9},{9,10},{10,1... | collective-permute-start | bytes 1179656 | tf_op jit(solution)/shard_map/ppermute | solution.py:156
  94.6 10.9 %copy-start.4 = (bf16[256,1536]{1,0:T(8,128)(2,1)}, bf16[256,1536]{1,0:T(8,128)(2,1)S(1)}, u32[]{:S(2)}) copy-start(bf16[256,1536]{1,0:T(8,128)(2,1)S(1)} %collective-permute-done.refs_1_) | copy-start | bytes 2359300
  94.6 18.7 %collective-permute-start.6 = (bf16[384,512]{1,0:T(8,128)(2,1)}, bf16[384,512]{1,0:T(8,128)(2,1)}, u32[]{:S(2)}, u32[]{:S(2)}) collective-permute-start(bf16[384,512]{1,0:T(8,128)(2,1)} %get-tuple-element.21), channel_id=1, source_target_pairs={{0,3},{1,0},{2,1},{3,2},{4,7},{5,4},{6,5},{7,6},{8,11},{9,8},{10,9... | collective-permute-start | bytes 1179656 | tf_op jit(solution)/shard_map/ppermute | solution.py:157
  99.2 6.3 %copy-start.5 = (bf16[256,1536]{1,0:T(8,128)(2,1)}, bf16[256,1536]{1,0:T(8,128)(2,1)S(1)}, u32[]{:S(2)}) copy-start(bf16[256,1536]{1,0:T(8,128)(2,1)S(1)} %collective-permute-done.5.refs_6_) | copy-start | bytes 2359300
  99.2 14.8 %collective-permute-start.10 = (bf16[384,512]{1,0:T(8,128)(2,1)S(1)}, bf16[384,512]{1,0:T(8,128)(2,1)}, u32[]{:S(2)}, u32[]{:S(2)}) collective-permute-start(bf16[384,512]{1,0:T(8,128)(2,1)S(1)} %collective-permute-done.7.refs_9_), channel_id=1, source_target_pairs={{0,3},{1,0},{2,1},{3,2},{4,7},{5,4},{6,5},{7,6},{8,11},{9,8},{10,9... | collective-permute-start | bytes 1179656 | tf_op jit(solution)/shard_map/ppermute | solution.py:159
  101.2 0.9 copy-start.6
  102.1 12.0 %collective-permute-start.9 = (bf16[384,512]{1,0:T(8,128)(2,1)}, bf16[384,512]{1,0:T(8,128)(2,1)}, u32[]{:S(2)}, u32[]{:S(2)}) collective-permute-start(bf16[384,512]{1,0:T(8,128)(2,1)} %collective-permute-done.8.refs_12_), channel_id=1, source_target_pairs={{0,1},{1,2},{2,3},{3,0},{4,5},{5,6},{6,7},{7,4},{8,9},{9,10},{10,1... | collective-permute-start | bytes 1179656 | tf_op jit(solution)/shard_map/ppermute | solution.py:158
  114.0 28.8 %copy-start.11 = (bf16[768,512]{1,0:T(8,128)(2,1)S(1)}, bf16[768,512]{1,0:T(8,128)(2,1)}, u32[]{:S(2)}) copy-start(bf16[768,512]{1,0:T(8,128)(2,1)} %get-tuple-element.16) | copy-start | bytes 2359300
  122.8 25.8 %copy-start.10 = (bf16[768,512]{1,0:T(8,128)(2,1)S(1)}, bf16[768,512]{1,0:T(8,128)(2,1)}, u32[]{:S(2)}) copy-start(bf16[768,512]{1,0:T(8,128)(2,1)} %get-tuple-element.17) | copy-start | bytes 2359300
  122.8 59.1 %copy-start.8 = (bf16[768,512]{1,0:T(8,128)(2,1)S(1)}, bf16[768,512]{1,0:T(8,128)(2,1)}, u32[]{:S(2)}) copy-start(bf16[768,512]{1,0:T(8,128)(2,1)} %get-tuple-element.14) | copy-start | bytes 2359300
  122.8 60.4 %all-to-all-start.1 = ((bf16[128,8,512]{2,1,0:T(8,128)(2,1)}), bf16[128,8,512]{2,1,0:T(8,128)(2,1)S(1)}, u32[]{:S(2)}, u32[]{:S(2)}) async-start(bf16[128,8,512]{2,1,0:T(8,128)(2,1)} %bitcast.21), calls=%async_computation.1 | async-start | bytes 2097152 | tf_op jit(solution)/shard_map/all_to_all | solution.py:226
  140.1 22.7 %collective-permute-start.12 = (bf16[768,512]{1,0:T(8,128)(2,1)}, bf16[768,512]{1,0:T(8,128)(2,1)S(1)}, u32[]{:S(2)}, u32[]{:S(2)}) collective-permute-start(bf16[768,512]{1,0:T(8,128)(2,1)} %get-tuple-element.15), channel_id=1, source_target_pairs={{0,1},{1,2},{2,3},{3,0},{4,5},{5,6},{6,7},{7,4},{8,9},{9,10},{10,1... | collective-permute-start | bytes 2359304 | tf_op jit(solution)/shard_map/ppermute | solution.py:214
  142.9 37.6 %collective-permute-start.13 = (bf16[768,512]{1,0:T(8,128)(2,1)S(1)}, bf16[768,512]{1,0:T(8,128)(2,1)S(1)}, u32[]{:S(2)}, u32[]{:S(2)}) collective-permute-start(bf16[768,512]{1,0:T(8,128)(2,1)S(1)} %copy-done.11), channel_id=1, source_target_pairs={{0,2},{1,3},{2,0},{3,1},{4,6},{5,7},{6,4},{7,5},{8,10},{9,11},{10,... | collective-permute-start | bytes 2359304 | tf_op jit(solution)/shard_map/ppermute | solution.py:214
  148.6 33.2 %collective-permute-start.14 = (bf16[768,512]{1,0:T(8,128)(2,1)S(1)}, bf16[768,512]{1,0:T(8,128)(2,1)S(1)}, u32[]{:S(2)}, u32[]{:S(2)}) collective-permute-start(bf16[768,512]{1,0:T(8,128)(2,1)S(1)} %copy-done.10), channel_id=1, source_target_pairs={{0,3},{1,0},{2,1},{3,2},{4,7},{5,4},{6,5},{7,6},{8,11},{9,8},{10,9... | collective-permute-start | bytes 2359304 | tf_op jit(solution)/shard_map/ppermute | solution.py:214
  183.2 1.0 copy-start.1

commit v2 on v1

v2 whole, which is shorter than its diff:
```python
import functools

import jax
import jax.numpy as jnp
from jax import lax
from jax.experimental import pallas as pl
from jax.experimental.pallas import tpu as pltpu
from jax.sharding import PartitionSpec as P

EPSILON = 1e-06
F32, BF16 = jnp.float32, jnp.bfloat16
NT = (((1,), (1,)), ((), ()))
TN = (((0,), (0,)), ((), ()))
VMEM_LIMIT = 56 * 1024 * 1024


def whole(memory_space=pltpu.VMEM):
    return pl.BlockSpec(memory_space=memory_space)


def quantize(value):
    top = jnp.max(jnp.abs(value), axis=1, keepdims=True)
    scale = (top + EPSILON).astype(BF16).astype(F32)
    return ((value / scale).astype(BF16).astype(F32) * scale).astype(BF16)


def send_kernel(quarters, ids_ref, gate_ref, tok_ref, grad_ref, send_ref, pick_ref, stack):
    block = pl.program_id(0)
    rows = send_ref.shape[0]
    toks, width = tok_ref.shape
    lanes = quarters * toks
    feat = width // quarters

    @pl.when(block == 0)
    def _():
        for q in range(quarters):
            here = pl.ds(q * toks, toks)
            for g in range(feat // 128):
                cols = slice(q * feat + g * 128, q * feat + g * 128 + 128)
                stack[here, pl.ds(g * 128, 128)] = quantize(tok_ref[:, cols].astype(F32)).astype(F32)
            stack[here, pl.ds(feat, feat)] = grad_ref[:, q * feat : q * feat + feat].astype(F32)

    row = lax.broadcasted_iota(jnp.int32, (rows, lanes), 0) + block * rows
    lane = lax.broadcasted_iota(jnp.int32, (rows, lanes), 1)
    expert, slot, quarter = row >> 3, (row >> 2) & 1, row & 3
    ids = jnp.concatenate([ids_ref[...]] * quarters, axis=1)
    gates = jnp.concatenate([gate_ref[...]] * quarters, axis=1)
    named = jnp.zeros((rows, lanes), F32)
    weight = jnp.zeros((rows, lanes), F32)
    for k in range(ids_ref.shape[0]):
        hit = ids[k : k + 1, :] == expert
        named = jnp.where(hit, 1.0, named)
        weight = jnp.where(hit, gates[k : k + 1, :], weight)
    above = lax.broadcasted_iota(jnp.int32, (lanes, lanes), 0)
    below = lax.broadcasted_iota(jnp.int32, (lanes, lanes), 1)
    earlier = (above < below) & (above // toks == below // toks)
    rank = jnp.dot(named.astype(BF16), earlier.astype(BF16), preferred_element_type=F32)
    chosen = (named > 0.5) & (rank == slot.astype(F32)) & (lane // toks == quarter)
    pick = jnp.where(chosen, 1.0, 0.0).astype(BF16)
    pick_ref[...] = pick
    send_ref[:, :feat] = jnp.dot(pick, stack[:, :feat].astype(BF16), preferred_element_type=F32).astype(BF16)
    gate = jnp.sum(jnp.where(chosen, weight, 0.0), axis=1, keepdims=True)
    grads = jnp.dot(pick, stack[:, feat:].astype(BF16), preferred_element_type=F32) * gate
    for g in range(feat // 128):
        cols = slice(g * 128, g * 128 + 128)
        send_ref[:, feat + g * 128 : feat + g * 128 + 128] = quantize(grads[:, cols])


def order_matrix(rows, quarters):
    out = lax.broadcasted_iota(jnp.int32, (rows, rows), 0)
    src = lax.broadcasted_iota(jnp.int32, (rows, rows), 1)
    per = rows // quarters
    return ((out % per) * quarters + out // per == src).astype(BF16)


def hidden_kernel(quarters, recv_ref, gate_w, up_w, *refs):
    to_gate_ref, to_up_ref, g_ref, down_ref, x_ref = refs[-5:]
    rows = 256
    per = rows // quarters
    feat = recv_ref.shape[1] // 2

    @pl.when(pl.program_id(0) == 0)
    def _():
        order = order_matrix(rows, quarters)
        for b in range(recv_ref.shape[0] // rows):
            block = recv_ref[b * rows : b * rows + rows, :]
            got = jnp.dot(order, block, preferred_element_type=F32).astype(BF16)
            for q in range(quarters):
                here, cols = slice(b * per, b * per + per), slice(q * feat, q * feat + feat)
                x_ref[here, cols] = got[q * per : q * per + per, :feat]
                g_ref[here, cols] = got[q * per : q * per + per, feat:]

    x = x_ref[...]
    gate = jnp.dot(x, gate_w[...], preferred_element_type=F32)
    up = jnp.dot(x, up_w[...], preferred_element_type=F32)
    sig = jax.nn.sigmoid(gate)
    activ = gate * sig
    to_gate_ref[...] = up * sig * (1.0 + gate * (1.0 - sig))
    to_up_ref[...] = activ
    hidden = (activ * up).astype(BF16)
    down_ref[...] = lax.dot_general(hidden, g_ref[...], TN, preferred_element_type=F32).astype(BF16)


def back_kernel(quarters, me_ref, to_gate_ref, to_up_ref, g_ref, *refs):
    downs, (up_ref, back_ref, gp_ref, hold) = refs[:7], refs[7:]
    step = pl.program_id(0)
    hidden_units = to_gate_ref.shape[1]
    half = hidden_units // 2
    feat = g_ref.shape[1] // quarters

    @pl.when(step == 0)
    def _():
        gs = []
        for k in range(quarters):
            first = pl.multiple_of(lax.rem(me_ref[0] + k, quarters) * feat, feat)
            gs.append(g_ref[:, pl.ds(first, feat)])
        own, right_a, right_b, far_a, far_b, left_a, left_b = downs
        for h, others in enumerate(((right_a, far_a, left_a), (right_b, far_b, left_b))):
            total = lax.dot_general(gs[0], own[h * half : h * half + half, :], NT, preferred_element_type=F32)
            for g, w in zip(gs[1:], others):
                total = total + lax.dot_general(g, w[...], NT, preferred_element_type=F32)
            cols = slice(h * half, h * half + half)
            up_cols = slice(hidden_units + h * half, hidden_units + h * half + half)
            gp_ref[:, cols] = (total * to_gate_ref[:, cols]).astype(BF16)
            gp_ref[:, up_cols] = (total * to_up_ref[:, cols]).astype(BF16)

    hold[step] = lax.dot_general(gp_ref[...], up_ref[...], NT, preferred_element_type=F32).astype(BF16)

    @pl.when(step == quarters - 1)
    def _():
        rows = 256
        per = rows // quarters
        order = order_matrix(rows, quarters)
        for b in range(back_ref.shape[0] // rows):
            stacked = jnp.concatenate([hold[q, b * per : b * per + per, :] for q in range(quarters)], axis=0)
            back_ref[b * rows : b * rows + rows, :] = lax.dot_general(
                order, stacked, TN, preferred_element_type=F32
            ).astype(BF16)


def combine_kernel(toks, pick_ref, ret_ref, out_ref):
    feat = ret_ref.shape[1]
    total = lax.dot_general(pick_ref[...], ret_ref[...], TN, preferred_element_type=F32)
    for q in range(out_ref.shape[1] // feat):
        out_ref[:, q * feat : q * feat + feat] = total[q * toks : q * toks + toks].astype(BF16)


def gather_pieces(w, size):
    half = w.shape[0] // 2
    top, bottom = w[:half], w[half:]
    fwd = [(i, (i + 1) % size) for i in range(size)]
    bwd = [(i, (i - 1) % size) for i in range(size)]
    left_top = lax.ppermute(top, "edp", fwd)
    right_bottom = lax.ppermute(bottom, "edp", bwd)
    left_bottom = lax.ppermute(bottom, "edp", fwd)
    right_top = lax.ppermute(top, "edp", bwd)
    far_top = lax.ppermute(left_top, "edp", fwd)
    far_bottom = lax.ppermute(right_bottom, "edp", bwd)
    return [w, right_top, right_bottom, far_top, far_bottom, left_top, left_bottom]


def per_device(tokens, out_grad, expert_ids, gate_values, gate_up_weight, down_weight):
    experts, parts = lax.axis_size("ep"), lax.axis_size("edp")
    toks, width = tokens.shape
    hidden_units = down_weight.shape[1]
    quarters = 4
    feat = width // quarters
    slots = experts * 2
    rows = slots * quarters
    params = pltpu.CompilerParams(vmem_limit_bytes=VMEM_LIMIT)
    me = lax.axis_index("edp").astype(jnp.int32).reshape(1)

    gate_up = lax.all_gather(gate_up_weight[0], "edp", axis=0, tiled=True)
    downs = gather_pieces(down_weight[0], parts)

    tile = 128
    sent, pick = pl.pallas_call(
        functools.partial(send_kernel, quarters),
        grid=(rows // tile,),
        in_specs=[whole()] * 4,
        out_specs=[
            pl.BlockSpec((tile, 2 * feat), lambda b: (b, 0)),
            pl.BlockSpec((tile, quarters * toks), lambda b: (b, 0)),
        ],
        out_shape=[
            jax.ShapeDtypeStruct((rows, 2 * feat), BF16),
            jax.ShapeDtypeStruct((rows, quarters * toks), BF16),
        ],
        scratch_shapes=[pltpu.VMEM((quarters * toks, 2 * feat), F32)],
        compiler_params=params,
        name="send_rows",
    )(expert_ids.T, gate_values.T, tokens, out_grad)
    recv = lax.all_to_all(sent, "ep", split_axis=0, concat_axis=0, tiled=True)

    tile = 256
    blocks = hidden_units // tile
    to_gate, to_up, rows_g, partial = pl.pallas_call(
        functools.partial(hidden_kernel, quarters),
        grid=(blocks,),
        in_specs=[
            whole(),
            pl.BlockSpec((width, tile), lambda n: (0, n)),
            pl.BlockSpec((width, tile), lambda n: (0, n + blocks)),
        ]
        + [whole(pl.ANY)] * len(downs),
        out_specs=[
            pl.BlockSpec((slots, tile), lambda n: (0, n)),
            pl.BlockSpec((slots, tile), lambda n: (0, n)),
            whole(),
            pl.BlockSpec((tile, width), lambda n: (n, 0)),
        ],
        out_shape=[
            jax.ShapeDtypeStruct((slots, hidden_units), F32),
            jax.ShapeDtypeStruct((slots, hidden_units), F32),
            jax.ShapeDtypeStruct((slots, width), BF16),
            jax.ShapeDtypeStruct((hidden_units, width), BF16),
        ],
        scratch_shapes=[pltpu.VMEM((slots, width), BF16)],
        compiler_params=params,
        name="hidden_rows",
    )(recv, gate_up, gate_up, *downs)
    down_grad = lax.psum_scatter(partial, "edp", scatter_dimension=1, tiled=True)[None]

    back = pl.pallas_call(
        functools.partial(back_kernel, quarters),
        grid=(quarters,),
        in_specs=[whole(pltpu.SMEM)] + [whole()] * 10 + [pl.BlockSpec((feat, 2 * hidden_units), lambda k: (k, 0))],
        out_specs=whole(),
        out_shape=jax.ShapeDtypeStruct((rows, feat), BF16),
        scratch_shapes=[
            pltpu.VMEM((slots, 2 * hidden_units), BF16),
            pltpu.VMEM((quarters, slots, feat), BF16),
        ],
        compiler_params=params,
        name="back_rows",
    )(me, to_gate, to_up, rows_g, *downs, gate_up)
    returned = lax.all_to_all(back, "ep", split_axis=0, concat_axis=0, tiled=True)
    token_grads = pl.pallas_call(
        functools.partial(combine_kernel, toks),
        in_specs=[whole(), whole()],
        out_specs=whole(),
        out_shape=jax.ShapeDtypeStruct((toks, width), BF16),
        compiler_params=params,
        name="combine_rows",
    )(pick, returned)
    return (token_grads, down_grad)


def solution(mesh):
    return jax.shard_map(
        per_device,
        mesh=mesh,
        in_specs=(
            P(("ep", "edp"), None),
            P(("ep", "edp"), None),
            P(("ep", "edp"), None),
            P(("ep", "edp"), None),
            P("ep", "edp", None),
            P("ep", None, "edp"),
        ),
        out_specs=(P(("ep", "edp"), None), P("ep", None, "edp")),
        check_vma=False,
    )
```

time: 187 us -> 185 us (0.989)
  starting transfers between devices: 83.2 us -> 36.9 us
  blocking collectives: 0 us -> 45.3 us
  between operations: 0.95 us -> 14.1 us
  waiting for transfers between devices: 69.8 us -> 60.2 us
  local copies, waits for them, and re-layouts: 5.7 us -> 0.84 us
    all_to_all x0 -> x1, blocking collectives: none -> 45.3 us  [per_device(): lax.all_to_all(back, 'ep', split_axis=0, concat_axis=0, tiled=True)]
    ppermute x3 -> x0, waiting for transfers between devices: 31.3 us -> none  [per_device(): sums = sums + lax.ppermute(partial[k], 'edp', perm).astype(F32)]
    ppermute x2 -> x1, waiting for transfers between devices: 34.3 us -> 10.5 us  [gather_pieces(): left_top = lax.ppermute(top, 'edp', fwd)]
    all_gather x0 -> x1, waiting for transfers between devices: none -> 20.8 us  [per_device(): gate_up = lax.all_gather(gate_up_weight[0], 'edp', axis=0, tiled=True)]
    all_to_all x1 -> x0, starting transfers between devices: 17.3 us -> none  [per_device(): lax.all_to_all(back, 'ep', split_axis=0, concat_axis=0, tiled=True)]
    ppermute x2 -> x1, waiting for transfers between devices: 0.01 us -> 15 us  [gather_pieces(): far_top = lax.ppermute(left_top, 'edp', fwd)]
    ppermute x2 -> x1, waiting for transfers between devices: 0.01 us -> 12.2 us  [gather_pieces(): right_top = lax.ppermute(top, 'edp', bwd)]
    ppermute x3 -> x0, starting transfers between devices: 10.4 us -> none  [per_device(): sums = sums + lax.ppermute(partial[k], 'edp', perm).astype(F32)]
  transfers between devices with their start and end apart: 17 -> 9, of which waited for: 7 -> 5; matrix products, arithmetic and copies ran while one was open for 1% -> 0% of each run, Pallas kernels for 4% -> 10%
where the time goes in v2:
time: 185 us; the launch traced here: 184 us
  waiting for transfers between devices  60.2 us (33%)
  blocking collectives  45.3 us (24%)
  starting transfers between devices  36.9 us (20%)
  Pallas kernels  26.9 us (15%)
  between operations  14.1 us (8%)
    all_to_all x1, blocking collectives, per_device(): lax.all_to_all(back, 'ep', split_axis=0, concat_axis=0, tiled=True)  45.3 us
    all_gather x1, waiting for transfers between devices, per_device(): gate_up = lax.all_gather(gate_up_weight[0], 'edp', axis=0, tiled=True)  20.8 us
    all_to_all x1, starting transfers between devices, per_device(): recv = lax.all_to_all(sent, 'ep', split_axis=0, concat_axis=0, tiled=True)  18.6 us
    ppermute x1, waiting for transfers between devices, gather_pieces(): far_top = lax.ppermute(left_top, 'edp', fwd)  15 us
    ppermute x1, waiting for transfers between devices, gather_pieces(): right_top = lax.ppermute(top, 'edp', bwd)  12.2 us
    ppermute x1, waiting for transfers between devices, gather_pieces(): left_top = lax.ppermute(top, 'edp', fwd)  10.5 us
    pallas_call x1, Pallas kernels, per_device(): pl.pallas_call(functools.partial(back_kernel, quarters), grid=(quarters,)...  9.27 us
    pallas_call x1, Pallas kernels, per_device(): pl.pallas_call(functools.partial(hidden_kernel, quarters), grid=(blocks,)...  8.69 us
  transfers between devices with their start and end apart: 9, of which 5 were waited for; matrix products, arithmetic and copies ran while one was open for 0% of the time, Pallas kernels for 10%

profile of v2, /device:TPU:1, one launch (start us, length us, event | category | flops | bytes accessed | tf_op | source)
XLA Modules:
  0.0 184.3 jit_solution(2835425911240296048)
XLA Ops:
  7.2 0.0 all-gather.3.cloned.1.call-start
  7.2 0.7 all-gather.3.cloned.1.call-update
  7.9 6.7 %send_rows.1 = (bf16[1024,1024]{1,0:T(8,128)(2,1)}, bf16[1024,96]{1,0:T(8,128)(2,1)}) custom-call(s32[8,24]{1,0:T(8,128)} %bitcast.23, f32[8,24]{1,0:T(8,128)} %bitcast.24, bf16[24,2048]{1,0:T(8,128)(2,1)} %tok_ref.1, bf16[24,2048]{1,0:T(8,128)(2,1)} %grad_ref.1), custom_call_target="tpu_custom_call" | custom-call | tf_op jit(solution)/shard_map/send_rows/pallas_call | solution.py:177
  14.6 0.0 copy-start.1
  14.6 18.6 %all-to-all-start = ((bf16[128,8,1024]{2,1,0:T(8,128)(2,1)}), bf16[128,8,1024]{2,1,0:T(8,128)(2,1)S(1)}, u32[]{:S(2)}, u32[]{:S(2)}) async-start(bf16[128,8,1024]{2,1,0:T(8,128)(2,1)} %bitcast.22), calls=%async_computation | async-start | bytes 4194304 | tf_op jit(solution)/shard_map/all_to_all | solution.py:193
  33.2 0.0 reduce-scatter.2.cloned.1.call-start
  33.2 0.0 copy-done.1
  33.2 0.1 slice_bitcast_fusion
  33.3 3.1 %collective-permute-start.2 = (bf16[384,512]{1,0:T(8,128)(2,1)S(1)}, bf16[384,512]{1,0:T(8,128)(2,1)S(1)}, u32[]{:S(2)}, u32[]{:S(2)}) collective-permute-start(bf16[384,512]{1,0:T(8,128)(2,1)S(1)} %get-tuple-element.15), channel_id=1, source_target_pairs={{0,1},{1,2},{2,3},{3,0},{4,5},{5,6},{6,7},{7,4},{8,9},{9,10},{10,1... | collective-permute-start | bytes 1179656 | tf_op jit(solution)/shard_map/ppermute | solution.py:153
  36.4 3.4 %collective-permute-start.1 = (bf16[384,512]{1,0:T(8,128)(2,1)S(1)}, bf16[384,512]{1,0:T(8,128)(2,1)S(1)}, u32[]{:S(2)}, u32[]{:S(2)}) collective-permute-start(bf16[384,512]{1,0:T(8,128)(2,1)S(1)} %get-tuple-element.14), channel_id=1, source_target_pairs={{0,3},{1,0},{2,1},{3,2},{4,7},{5,4},{6,5},{7,6},{8,11},{9,8},{10,9... | collective-permute-start | bytes 1179656 | tf_op jit(solution)/shard_map/ppermute | solution.py:154
  39.8 3.2 %collective-permute-start = (bf16[384,512]{1,0:T(8,128)(2,1)S(1)}, bf16[384,512]{1,0:T(8,128)(2,1)S(1)}, u32[]{:S(2)}, u32[]{:S(2)}) collective-permute-start(bf16[384,512]{1,0:T(8,128)(2,1)S(1)} %get-tuple-element.15), channel_id=1, source_target_pairs={{0,3},{1,0},{2,1},{3,2},{4,7},{5,4},{6,5},{7,6},{8,11},{9,8},{10,9... | collective-permute-start | bytes 1179656 | tf_op jit(solution)/shard_map/ppermute | solution.py:156
  43.0 2.1 %collective-permute-start.5 = (bf16[384,512]{1,0:T(8,128)(2,1)S(1)}, bf16[384,512]{1,0:T(8,128)(2,1)S(1)}, u32[]{:S(2)}, u32[]{:S(2)}) collective-permute-start(bf16[384,512]{1,0:T(8,128)(2,1)S(1)} %get-tuple-element.14), channel_id=1, source_target_pairs={{0,1},{1,2},{2,3},{3,0},{4,5},{5,6},{6,7},{7,4},{8,9},{9,10},{10,1... | collective-permute-start | bytes 1179656 | tf_op jit(solution)/shard_map/ppermute | solution.py:155
  45.1 10.5 %collective-permute-done.2.refs_5_ = bf16[384,512]{1,0:T(8,128)(2,1)S(1)} collective-permute-done((bf16[384,512]{1,0:T(8,128)(2,1)S(1)}, bf16[384,512]{1,0:T(8,128)(2,1)S(1)}, u32[]{:S(2)}, u32[]{:S(2)}) %collective-permute-start.2) | collective-permute-done | bytes 393248 | tf_op jit(solution)/shard_map/ppermute | solution.py:153
  55.6 0.0 copy-start.2
  55.6 1.9 %collective-permute-start.3 = (bf16[384,512]{1,0:T(8,128)(2,1)S(1)}, bf16[384,512]{1,0:T(8,128)(2,1)S(1)}, u32[]{:S(2)}, u32[]{:S(2)}) collective-permute-start(bf16[384,512]{1,0:T(8,128)(2,1)S(1)} %collective-permute-done.2.refs_5_), channel_id=1, source_target_pairs={{0,1},{1,2},{2,3},{3,0},{4,5},{5,6},{6,7},{7,4},{8,9},{9,10},{10,1... | collective-permute-start | bytes 1179656 | tf_op jit(solution)/shard_map/ppermute | solution.py:157
  57.5 0.0 collective-permute-done.1.refs_2_
  57.5 0.0 copy-start.3
  57.5 4.6 %collective-permute-start.4 = (bf16[384,512]{1,0:T(8,128)(2,1)S(1)}, bf16[384,512]{1,0:T(8,128)(2,1)}, u32[]{:S(2)}, u32[]{:S(2)}) collective-permute-start(bf16[384,512]{1,0:T(8,128)(2,1)S(1)} %collective-permute-done.1.refs_2_), channel_id=1, source_target_pairs={{0,3},{1,0},{2,1},{3,2},{4,7},{5,4},{6,5},{7,6},{8,11},{9,8},{10,9... | collective-permute-start | bytes 1179656 | tf_op jit(solution)/shard_map/ppermute | solution.py:158
  62.1 12.2 %collective-permute-done.refs_1_ = bf16[384,512]{1,0:T(8,128)(2,1)S(1)} collective-permute-done((bf16[384,512]{1,0:T(8,128)(2,1)S(1)}, bf16[384,512]{1,0:T(8,128)(2,1)S(1)}, u32[]{:S(2)}, u32[]{:S(2)}) %collective-permute-start) | collective-permute-done | bytes 393248 | tf_op jit(solution)/shard_map/ppermute | solution.py:156
  74.3 0.0 copy-start.4
  74.3 0.0 collective-permute-done.5.refs_6_
  74.3 0.0 copy-start.5
  74.3 15.0 %collective-permute-done.3.refs_3_ = bf16[384,512]{1,0:T(8,128)(2,1)S(1)} collective-permute-done((bf16[384,512]{1,0:T(8,128)(2,1)S(1)}, bf16[384,512]{1,0:T(8,128)(2,1)S(1)}, u32[]{:S(2)}, u32[]{:S(2)}) %collective-permute-start.3) | collective-permute-done | bytes 393248 | tf_op jit(solution)/shard_map/ppermute | solution.py:157
  89.3 0.0 copy-done.5
  89.3 0.0 copy-start.6
  89.3 0.8 copy-done.6
  90.1 1.1 collective-permute-done.4.refs_4_
  91.1 0.0 all-to-all-done
  91.1 0.0 copy-start
  91.1 20.8 %all-gather.3.cloned.1.call-done = bf16[1,2048,1536]{2,1,0:T(8,128)(2,1)} async-done(((bf16[1,512,1536]{2,1,0:T(8,128)(2,1)}), bf16[1,2048,1536]{2,1,0:T(8,128)(2,1)}) %all-gather.3.cloned.1.call-update) | async-done | bytes 6291472 | tf_op jit(solution)/shard_map/all_gather | solution.py:173
  111.9 0.0 copy-done.2
  111.9 0.0 copy-done.3
  111.9 0.0 copy-done.4
  111.9 0.0 copy-done
  111.9 8.7 %hidden_rows.1 = (f32[256,768]{1,0:T(8,128)}, f32[256,768]{1,0:T(8,128)}, bf16[256,2048]{1,0:T(8,128)(2,1)}, bf16[768,2048]{1,0:T(8,128)(2,1)}) custom-call(bf16[1024,1024]{1,0:T(8,128)(2,1)} %bitcast.17, bf16[2048,1536]{1,0:T(8,128)(2,1)} %bitcast.14, bf16[2048,1536]{1,0:T(8,128)(2,1)} %bitcast.15, bf16[768,512]{1,0:T(8,128)(2,1)} %bitcast.18, ...), custom_call_target="tpu_custom_call" | custom-call | tf_op jit(solution)/shard_map/hidden_rows/pallas_call | solution.py:197
  120.6 0.0 reduce-scatter.2.cloned.1.call-update
  120.6 9.3 %back_rows.1 = bf16[1024,512]{1,0:T(8,128)(2,1)} custom-call(s32[1]{0:T(128)} %bitcast.2.me_ref, f32[256,768]{1,0:T(8,128)} %get-tuple-element.10.to_gate_ref, f32[256,768]{1,0:T(8,128)} %get-tuple-element.11.to_up_ref, bf16[256,2048]{1,0:T(8,128)(2,1)} %get-tuple-element.12.g_ref, bf16[768,512]{1,0:T(8,128)(2,1)} %bitcast.19, bf16[384,512]{1,0:T(8,128)(2,1)} %copy-done.4, ...), custom_call_target="tpu_custom_call" | custom-call | tf_op jit(solution)/shard_map/back_rows/pallas_call | solution.py:224
  129.9 45.3 %all_to_all.22 = bf16[128,8,512]{2,1,0:T(8,128)(2,1)} all-to-all(bf16[128,8,512]{2,1,0:T(8,128)(2,1)} %bitcast.20), channel_id=1, replica_groups=mesh['ep'=128,'edp'=4] {'ep'}, dimensions={0} | all-to-all | bytes 2097152 | tf_op jit(solution)/shard_map/all_to_all | solution.py:237
  175.2 2.3 %combine_rows.1 = bf16[24,2048]{1,0:T(8,128)(2,1)} custom-call(bf16[1024,96]{1,0:T(8,128)(2,1)} %get-tuple-element.8.pick_ref, bf16[1024,512]{1,0:T(8,128)(2,1)} %bitcast.21), custom_call_target="tpu_custom_call" | custom-call | tf_op jit(solution)/shard_map/combine_rows/pallas_call | solution.py:238
  177.5 0.0 reduce-scatter.2.cloned.1.call-done
Async XLA Ops:
  7.2 104.7 %all-gather.3.cloned.1.call-start = ((), (), s32[]{:S(2)}) async-start(), calls=%async_computation.4 | async-start | bytes 7864320 | tf_op jit(solution)/shard_map/all_gather | solution.py:173
  14.6 18.6 %copy-start.1 = (bf16[1,768,512]{2,1,0:T(8,128)(2,1)S(1)}, bf16[1,768,512]{2,1,0:T(8,128)(2,1)}, u32[]{:S(2)}) copy-start(bf16[1,768,512]{2,1,0:T(8,128)(2,1)} %param.11) | copy-start | bytes 2359300
  14.6 76.5 %all-to-all-start = ((bf16[128,8,1024]{2,1,0:T(8,128)(2,1)}), bf16[128,8,1024]{2,1,0:T(8,128)(2,1)S(1)}, u32[]{:S(2)}, u32[]{:S(2)}) async-start(bf16[128,8,1024]{2,1,0:T(8,128)(2,1)} %bitcast.22), calls=%async_computation | async-start | bytes 4194304 | tf_op jit(solution)/shard_map/all_to_all | solution.py:193
  33.2 144.3 %reduce-scatter.2.cloned.1.call-start = ((), (), s32[]{:S(2)}) async-start(), calls=%async_computation.3 | async-start | bytes 3932160 | tf_op jit(solution)/shard_map/reduce_scatter | solution.py:222
  33.3 22.3 %collective-permute-start.2 = (bf16[384,512]{1,0:T(8,128)(2,1)S(1)}, bf16[384,512]{1,0:T(8,128)(2,1)S(1)}, u32[]{:S(2)}, u32[]{:S(2)}) collective-permute-start(bf16[384,512]{1,0:T(8,128)(2,1)S(1)} %get-tuple-element.15), channel_id=1, source_target_pairs={{0,1},{1,2},{2,3},{3,0},{4,5},{5,6},{6,7},{7,4},{8,9},{9,10},{10,1... | collective-permute-start | bytes 1179656 | tf_op jit(solution)/shard_map/ppermute | solution.py:153
  36.4 21.1 %collective-permute-start.1 = (bf16[384,512]{1,0:T(8,128)(2,1)S(1)}, bf16[384,512]{1,0:T(8,128)(2,1)S(1)}, u32[]{:S(2)}, u32[]{:S(2)}) collective-permute-start(bf16[384,512]{1,0:T(8,128)(2,1)S(1)} %get-tuple-element.14), channel_id=1, source_target_pairs={{0,3},{1,0},{2,1},{3,2},{4,7},{5,4},{6,5},{7,6},{8,11},{9,8},{10,9... | collective-permute-start | bytes 1179656 | tf_op jit(solution)/shard_map/ppermute | solution.py:154
  39.8 34.5 %collective-permute-start = (bf16[384,512]{1,0:T(8,128)(2,1)S(1)}, bf16[384,512]{1,0:T(8,128)(2,1)S(1)}, u32[]{:S(2)}, u32[]{:S(2)}) collective-permute-start(bf16[384,512]{1,0:T(8,128)(2,1)S(1)} %get-tuple-element.15), channel_id=1, source_target_pairs={{0,3},{1,0},{2,1},{3,2},{4,7},{5,4},{6,5},{7,6},{8,11},{9,8},{10,9... | collective-permute-start | bytes 1179656 | tf_op jit(solution)/shard_map/ppermute | solution.py:156
  43.0 31.3 %collective-permute-start.5 = (bf16[384,512]{1,0:T(8,128)(2,1)S(1)}, bf16[384,512]{1,0:T(8,128)(2,1)S(1)}, u32[]{:S(2)}, u32[]{:S(2)}) collective-permute-start(bf16[384,512]{1,0:T(8,128)(2,1)S(1)} %get-tuple-element.14), channel_id=1, source_target_pairs={{0,1},{1,2},{2,3},{3,0},{4,5},{5,6},{6,7},{7,4},{8,9},{9,10},{10,1... | collective-permute-start | bytes 1179656 | tf_op jit(solution)/shard_map/ppermute | solution.py:155
  55.6 56.3 %copy-start.2 = (bf16[384,512]{1,0:T(8,128)(2,1)}, bf16[384,512]{1,0:T(8,128)(2,1)S(1)}, u32[]{:S(2)}) copy-start(bf16[384,512]{1,0:T(8,128)(2,1)S(1)} %collective-permute-done.2.refs_5_) | copy-start | bytes 1179652
  55.6 33.7 %collective-permute-start.3 = (bf16[384,512]{1,0:T(8,128)(2,1)S(1)}, bf16[384,512]{1,0:T(8,128)(2,1)S(1)}, u32[]{:S(2)}, u32[]{:S(2)}) collective-permute-start(bf16[384,512]{1,0:T(8,128)(2,1)S(1)} %collective-permute-done.2.refs_5_), channel_id=1, source_target_pairs={{0,1},{1,2},{2,3},{3,0},{4,5},{5,6},{6,7},{7,4},{8,9},{9,10},{10,1... | collective-permute-start | bytes 1179656 | tf_op jit(solution)/shard_map/ppermute | solution.py:157
  57.5 54.4 %copy-start.3 = (bf16[384,512]{1,0:T(8,128)(2,1)}, bf16[384,512]{1,0:T(8,128)(2,1)S(1)}, u32[]{:S(2)}) copy-start(bf16[384,512]{1,0:T(8,128)(2,1)S(1)} %collective-permute-done.1.refs_2_) | copy-start | bytes 1179652
  57.5 33.6 %collective-permute-start.4 = (bf16[384,512]{1,0:T(8,128)(2,1)S(1)}, bf16[384,512]{1,0:T(8,128)(2,1)}, u32[]{:S(2)}, u32[]{:S(2)}) collective-permute-start(bf16[384,512]{1,0:T(8,128)(2,1)S(1)} %collective-permute-done.1.refs_2_), channel_id=1, source_target_pairs={{0,3},{1,0},{2,1},{3,2},{4,7},{5,4},{6,5},{7,6},{8,11},{9,8},{10,9... | collective-permute-start | bytes 1179656 | tf_op jit(solution)/shard_map/ppermute | solution.py:158
  74.3 37.6 %copy-start.4 = (bf16[384,512]{1,0:T(8,128)(2,1)}, bf16[384,512]{1,0:T(8,128)(2,1)S(1)}, u32[]{:S(2)}) copy-start(bf16[384,512]{1,0:T(8,128)(2,1)S(1)} %collective-permute-done.refs_1_) | copy-start | bytes 1179652
  74.3 15.0 %copy-start.5 = (bf16[384,512]{1,0:T(8,128)(2,1)}, bf16[384,512]{1,0:T(8,128)(2,1)S(1)}, u32[]{:S(2)}) copy-start(bf16[384,512]{1,0:T(8,128)(2,1)S(1)} %collective-permute-done.5.refs_6_) | copy-start | bytes 1179652
  89.3 0.8 copy-start.6
  91.1 20.8 %copy-start = (bf16[128,8,1024]{2,1,0:T(8,128)(2,1)}, bf16[128,8,1024]{2,1,0:T(8,128)(2,1)S(1)}, u32[]{:S(2)}) copy-start(bf16[128,8,1024]{2,1,0:T(8,128)(2,1)S(1)} %all-to-all-done) | copy-start | bytes 6291460
Sparse Core Ops, SparseCore 0:
  10.1 101.7 all-gather.2
  120.7 44.3 reduce-scatter.1

commit v3 on v2

v3 whole, which is shorter than its diff:
```python
import functools

import jax
import jax.numpy as jnp
from jax import lax
from jax.experimental import pallas as pl
from jax.experimental.pallas import tpu as pltpu
from jax.sharding import PartitionSpec as P

EPSILON = 1e-06
F32, BF16 = jnp.float32, jnp.bfloat16
NT = (((1,), (1,)), ((), ()))
TN = (((0,), (0,)), ((), ()))
VMEM_LIMIT = 56 * 1024 * 1024
COST = 20 * 10**9
PASS = (0,)


def whole(memory_space=pltpu.VMEM):
    return pl.BlockSpec(memory_space=memory_space)


def quantize(value):
    top = jnp.max(jnp.abs(value), axis=1, keepdims=True)
    scale = (top + EPSILON).astype(BF16).astype(F32)
    return ((value / scale).astype(BF16).astype(F32) * scale).astype(BF16)


def send_kernel(quarters, ids_ref, gate_ref, tok_ref, grad_ref, send_ref, pick_ref, stack):
    block = pl.program_id(0)
    rows = send_ref.shape[0]
    toks, width = tok_ref.shape
    lanes = quarters * toks
    feat = width // quarters

    @pl.when(block == 0)
    def _():
        for q in range(quarters):
            here = pl.ds(q * toks, toks)
            for g in range(feat // 128):
                cols = slice(q * feat + g * 128, q * feat + g * 128 + 128)
                stack[here, pl.ds(g * 128, 128)] = quantize(tok_ref[:, cols].astype(F32)).astype(F32)
            stack[here, pl.ds(feat, feat)] = grad_ref[:, q * feat : q * feat + feat].astype(F32)

    row = lax.broadcasted_iota(jnp.int32, (rows, lanes), 0) + block * rows
    lane = lax.broadcasted_iota(jnp.int32, (rows, lanes), 1)
    expert, slot, quarter = row >> 3, (row >> 2) & 1, row & 3
    ids = jnp.concatenate([ids_ref[...]] * quarters, axis=1)
    gates = jnp.concatenate([gate_ref[...]] * quarters, axis=1)
    named = jnp.zeros((rows, lanes), F32)
    weight = jnp.zeros((rows, lanes), F32)
    for k in range(ids_ref.shape[0]):
        hit = ids[k : k + 1, :] == expert
        named = jnp.where(hit, 1.0, named)
        weight = jnp.where(hit, gates[k : k + 1, :], weight)
    above = lax.broadcasted_iota(jnp.int32, (lanes, lanes), 0)
    below = lax.broadcasted_iota(jnp.int32, (lanes, lanes), 1)
    earlier = (above < below) & (above // toks == below // toks)
    rank = jnp.dot(named.astype(BF16), earlier.astype(BF16), preferred_element_type=F32)
    chosen = (named > 0.5) & (rank == slot.astype(F32)) & (lane // toks == quarter)
    pick = jnp.where(chosen, 1.0, 0.0).astype(BF16)
    pick_ref[...] = pick
    send_ref[:, :feat] = jnp.dot(pick, stack[:, :feat].astype(BF16), preferred_element_type=F32).astype(BF16)
    gate = jnp.sum(jnp.where(chosen, weight, 0.0), axis=1, keepdims=True)
    grads = jnp.dot(pick, stack[:, feat:].astype(BF16), preferred_element_type=F32) * gate
    for g in range(feat // 128):
        cols = slice(g * 128, g * 128 + 128)
        send_ref[:, feat + g * 128 : feat + g * 128 + 128] = quantize(grads[:, cols])


def order_matrix(rows, quarters):
    out = lax.broadcasted_iota(jnp.int32, (rows, rows), 0)
    src = lax.broadcasted_iota(jnp.int32, (rows, rows), 1)
    per = rows // quarters
    return ((out % per) * quarters + out // per == src).astype(BF16)


def start_all(copies, sems, first=0):
    out = []
    for n, (src, dst) in enumerate(copies):
        copy = pltpu.make_async_copy(src, dst, sems.at[first + n])
        copy.start()
        out.append(copy)
    return out


def up_rows(own, others, cols):
    feat = own.shape[0]
    half = feat // 2
    (left_a, far_a, right_a), (right_b, far_b, left_b) = others[:3], others[3:]
    out = [(own.at[:, cols], 0, feat)]
    for k, (a, b) in enumerate(((right_a, right_b), (far_a, far_b), (left_a, left_b)), 1):
        out.append((a.at[pl.ds(0, half), cols], k * feat, half))
        out.append((b.at[pl.ds(0, half), cols], k * feat + half, half))
    return out


def hidden_kernel(quarters, me_ref, recv_ref, own, *refs):
    others, refs = refs[:6], refs[6:]
    to_gate_ref, to_up_ref, g_ref, first_a, first_b, down_ref, recv, w, x_ref, sems = refs
    rows = 256
    per = rows // quarters
    feat = recv_ref.shape[1] // 2
    hidden_units = to_gate_ref.shape[1]
    tile = 256
    (got_rows,) = start_all([(recv_ref, recv)], sems)
    waits = []
    for n in range(hidden_units // tile):
        copies = []
        for at in (n * tile, hidden_units + n * tile):
            cols = pl.ds(at, tile)
            copies += [(src, w.at[pl.ds(row, size), cols]) for src, row, size in up_rows(own, others, cols)]
        waits.append(start_all(copies, sems, 1 + n * len(copies)))
    got_rows.wait()
    order = order_matrix(rows, quarters)
    for b in range(recv_ref.shape[0] // rows):
        got = jnp.dot(order, recv[b * rows : b * rows + rows, :], preferred_element_type=F32).astype(BF16)
        here = slice(b * per, b * per + per)
        for q in range(quarters):
            at = pl.multiple_of(lax.rem(q + quarters - me_ref[0], quarters) * feat, feat)
            x_ref[here, pl.ds(at, feat)] = got[q * per : q * per + per, :feat]
            g_ref[here, pl.ds(at, feat)] = got[q * per : q * per + per, feat:]
    half = hidden_units // 2
    for n in range(hidden_units // tile):
        for copy in waits[n]:
            copy.wait()
        cols = slice(n * tile, n * tile + tile)
        gate = jnp.dot(x_ref[...], w[:, cols], preferred_element_type=F32)
        up = jnp.dot(x_ref[...], w[:, hidden_units + n * tile : hidden_units + n * tile + tile], preferred_element_type=F32)
        sig = jax.nn.sigmoid(gate)
        activ = gate * sig
        to_gate_ref[:, cols] = up * sig * (1.0 + gate * (1.0 - sig))
        to_up_ref[:, cols] = activ
        hidden = (activ * up).astype(BF16)
        part = lax.dot_general(hidden, g_ref[...], TN, preferred_element_type=F32).astype(BF16)
        for k in range(quarters):
            down_ref[k, cols, :] = part[:, k * feat : k * feat + feat]
        lo, hi = n * tile, n * tile + tile
        if lo < half:
            end = min(hi, half)
            first_a[lo:end, :] = part[: end - lo, (quarters - 1) * feat :]
        if hi > half:
            start = max(lo, half)
            first_b[start - half : hi - half, :] = part[start - lo :, feat : 2 * feat]


def back_kernel(quarters, me_ref, to_gate_ref, to_up_ref, g_ref, own_down, own, *refs):
    others, refs = refs[:6], refs[6:]
    back_ref, to_gate, to_up, g, wd, w, gp_ref, hold, sems = refs
    slots, hidden_units = to_gate.shape
    feat = own.shape[0]
    half = feat // 2
    third = hidden_units // 6
    (left_a, far_a, right_a), (right_b, far_b, left_b) = others[:3], others[3:]
    copies = [(g_ref, g), (own_down, wd.at[:, pl.ds(0, feat)])]
    for k, pair in enumerate(((right_a, right_b), (far_a, far_b), (left_a, left_b)), 1):
        for h, piece in enumerate(pair):
            for m in range(3):
                src = piece.at[pl.ds(half, third), pl.ds(m * feat, feat)]
                copies.append((src, wd.at[pl.ds((h * 3 + m) * third, third), pl.ds(k * feat, feat)]))
    copies += [(to_gate_ref, to_gate), (to_up_ref, to_up)]
    early = start_all(copies, sems)
    late = start_all(
        [(src, w.at[pl.ds(row, size), :]) for src, row, size in up_rows(own, others, slice(None))], sems, len(copies)
    )
    for copy in early:
        copy.wait()
    tile = 256
    for n in range(hidden_units // tile):
        cols = slice(n * tile, n * tile + tile)
        total = lax.dot_general(g[...], wd[cols, :], NT, preferred_element_type=F32)
        gp_ref[:, cols] = (total * to_gate[:, cols]).astype(BF16)
        gp_ref[:, hidden_units + n * tile : hidden_units + n * tile + tile] = (total * to_up[:, cols]).astype(BF16)
    for k in range(quarters):
        for copy in late[:1] if k == 0 else late[2 * k - 1 : 2 * k + 1]:
            copy.wait()
        hold[lax.rem(me_ref[0] + k, quarters)] = lax.dot_general(
            gp_ref[...], w[k * feat : k * feat + feat, :], NT, preferred_element_type=F32
        ).astype(BF16)
    rows = 256
    per = rows // quarters
    order = order_matrix(rows, quarters)
    for b in range(back_ref.shape[0] // rows):
        stacked = jnp.concatenate([hold[q, b * per : b * per + per, :] for q in range(quarters)], axis=0)
        back_ref[b * rows : b * rows + rows, :] = lax.dot_general(
            order, stacked, TN, preferred_element_type=F32
        ).astype(BF16)


def combine_kernel(toks, pick_ref, ret_ref, out_ref):
    feat = ret_ref.shape[1]
    total = lax.dot_general(pick_ref[...], ret_ref[...], TN, preferred_element_type=F32)
    for q in range(out_ref.shape[1] // feat):
        out_ref[:, q * feat : q * feat + feat] = total[q * toks : q * toks + toks].astype(BF16)


def ring(size, step):
    return [(i, (i + step) % size) for i in range(size)]


def pack_kernel(up, down, a_ref, b_ref, sems):
    half, third, feat = up.shape[0] // 2, down.shape[0] // 6, down.shape[1]
    copies = []
    for h, ref in enumerate((a_ref, b_ref)):
        copies.append((up.at[pl.ds(h * half, half), :], ref.at[pl.ds(0, half), :]))
        for m in range(3):
            copies.append(
                (down.at[pl.ds((h * 3 + m) * third, third), :], ref.at[pl.ds(half, third), pl.ds(m * feat, feat)])
            )
    for copy in start_all(copies, sems):
        copy.wait()


def halves(up, down):
    shape = jax.ShapeDtypeStruct((up.shape[0] // 2 + down.shape[0] // 6, up.shape[1]), BF16)
    return pl.pallas_call(
        pack_kernel,
        in_specs=[whole(pl.ANY)] * 2,
        out_specs=[whole(pl.ANY)] * 2,
        out_shape=[shape] * 2,
        scratch_shapes=[pltpu.SemaphoreType.DMA((8,))],
        compiler_params=pltpu.CompilerParams(vmem_limit_bytes=VMEM_LIMIT),
        name="pack_weights",
    )(up, down)


def pass_on(a, b):
    return pl.pallas_call(
        lambda *refs: None,
        in_specs=[whole(pl.ANY)] * 2,
        out_specs=[whole(pl.ANY)] * 2,
        out_shape=[jax.ShapeDtypeStruct(a.shape, a.dtype)] * 2,
        input_output_aliases={0: 0, 1: 1},
        compiler_params=pltpu.CompilerParams(vmem_limit_bytes=VMEM_LIMIT),
        cost_estimate=pl.CostEstimate(flops=COST, bytes_accessed=0, transcendentals=0),
        name="pass_on",
    )(a, b)


def gather_rings(up, down, size):
    a, b = halves(up, down)
    came_a, came_b = [], []
    for step in range(size - 1):
        a, b = lax.ppermute(a, "edp", ring(size, 1)), lax.ppermute(b, "edp", ring(size, -1))
        if step in PASS:
            a, b = pass_on(a, b)
        came_a.append(a)
        came_b.append(b)
    return came_a + came_b


def scatter_rings(first_a, first_b, partial, size):
    half = partial.shape[1] // 2
    a, b = first_a, first_b
    for step in range(size - 1):
        a, b = lax.ppermute(a, "edp", ring(size, 1)), lax.ppermute(b, "edp", ring(size, -1))
        a = (a.astype(F32) + partial[(size - 2 - step) % size, :half].astype(F32)).astype(BF16)
        b = (b.astype(F32) + partial[(step + 2) % size, half:].astype(F32)).astype(BF16)
    return jnp.concatenate([a, b], axis=0)


def per_device(tokens, out_grad, expert_ids, gate_values, gate_up_weight, down_weight):
    experts, parts = lax.axis_size("ep"), lax.axis_size("edp")
    toks, width = tokens.shape
    hidden_units = down_weight.shape[1]
    quarters = 4
    feat = width // quarters
    slots = experts * 2
    rows = slots * quarters
    params = pltpu.CompilerParams(vmem_limit_bytes=VMEM_LIMIT)
    me = lax.axis_index("edp").astype(jnp.int32).reshape(1)

    others = gather_rings(gate_up_weight[0], down_weight[0], parts)

    tile = 128
    sent, pick = pl.pallas_call(
        functools.partial(send_kernel, quarters),
        grid=(rows // tile,),
        in_specs=[whole()] * 4,
        out_specs=[
            pl.BlockSpec((tile, 2 * feat), lambda b: (b, 0)),
            pl.BlockSpec((tile, quarters * toks), lambda b: (b, 0)),
        ],
        out_shape=[
            jax.ShapeDtypeStruct((rows, 2 * feat), BF16),
            jax.ShapeDtypeStruct((rows, quarters * toks), BF16),
        ],
        scratch_shapes=[pltpu.VMEM((quarters * toks, 2 * feat), F32)],
        compiler_params=params,
        name="send_rows",
    )(expert_ids.T, gate_values.T, tokens, out_grad)
    recv = lax.all_to_all(sent, "ep", split_axis=0, concat_axis=0, tiled=True)

    half = hidden_units // 2
    to_gate, to_up, rows_g, first_a, first_b, partial = pl.pallas_call(
        functools.partial(hidden_kernel, quarters),
        in_specs=[whole(pltpu.SMEM)] + [whole(pl.ANY)] * 8,
        out_specs=[whole()] * 6,
        out_shape=[
            jax.ShapeDtypeStruct((slots, hidden_units), F32),
            jax.ShapeDtypeStruct((slots, hidden_units), F32),
            jax.ShapeDtypeStruct((slots, width), BF16),
            jax.ShapeDtypeStruct((half, feat), BF16),
            jax.ShapeDtypeStruct((half, feat), BF16),
            jax.ShapeDtypeStruct((parts, hidden_units, feat), BF16),
        ],
        scratch_shapes=[
            pltpu.VMEM((rows, 2 * feat), BF16),
            pltpu.VMEM((width, 2 * hidden_units), BF16),
            pltpu.VMEM((slots, width), BF16),
            pltpu.SemaphoreType.DMA((64,)),
        ],
        compiler_params=params,
        name="hidden_rows",
    )(me, recv, gate_up_weight[0], *others)
    down_grad = scatter_rings(first_a, first_b, partial, parts)[None]

    back = pl.pallas_call(
        functools.partial(back_kernel, quarters),
        in_specs=[whole(pltpu.SMEM)] + [whole(pl.ANY)] * 11,
        out_specs=whole(),
        out_shape=jax.ShapeDtypeStruct((rows, feat), BF16),
        scratch_shapes=[
            pltpu.VMEM((slots, hidden_units), F32),
            pltpu.VMEM((slots, hidden_units), F32),
            pltpu.VMEM((slots, width), BF16),
            pltpu.VMEM((hidden_units, width), BF16),
            pltpu.VMEM((width, 2 * hidden_units), BF16),
            pltpu.VMEM((slots, 2 * hidden_units), BF16),
            pltpu.VMEM((quarters, slots, feat), BF16),
            pltpu.SemaphoreType.DMA((32,)),
        ],
        compiler_params=params,
        name="back_rows",
    )(me, to_gate, to_up, rows_g, down_weight[0], gate_up_weight[0], *others)
    returned = lax.all_to_all(back, "ep", split_axis=0, concat_axis=0, tiled=True)
    token_grads = pl.pallas_call(
        functools.partial(combine_kernel, toks),
        in_specs=[whole(), whole()],
        out_specs=whole(),
        out_shape=jax.ShapeDtypeStruct((toks, width), BF16),
        compiler_params=params,
        name="combine_rows",
    )(pick, returned)
    return (token_grads, down_grad)


def solution(mesh):
    return jax.shard_map(
        per_device,
        mesh=mesh,
        in_specs=(
            P(("ep", "edp"), None),
            P(("ep", "edp"), None),
            P(("ep", "edp"), None),
            P(("ep", "edp"), None),
            P("ep", "edp", None),
            P("ep", None, "edp"),
        ),
        out_specs=(P(("ep", "edp"), None), P("ep", None, "edp")),
        check_vma=False,
    )
```

time: 185 us -> 250 us (1.35); the launches traced: 184 us -> 247 us
  Pallas kernels: 26.9 us -> 98.9 us
  blocking collectives: 45.3 us -> 0 us
  starting transfers between devices: 36.9 us -> 79 us
  between operations: 14.1 us -> 0.83 us
  other arithmetic: 0 us -> 4.9 us
  local copies, waits for them, and re-layouts: 0.84 us -> 3.42 us
    pallas_call x2 -> x4, Pallas kernels: 18 us -> 89.9 us  [the longest x1 72.6 us: halves(): pl.pallas_call(pack_kernel, in_specs=[whole(pl.ANY)] * 2, out_specs=[whol...]
    all_to_all x1 -> x0, blocking collectives: 45.3 us -> none  [per_device(): lax.all_to_all(back, 'ep', split_axis=0, concat_axis=0, tiled=True)]
    ppermute x6 -> x12, starting transfers between devices: 18.3 us -> 41.1 us  [the longest x3 14.3 us: scatter_rings(): lax.ppermute(b, 'edp', ring(size, -1))]
    all_gather x1 -> x0, waiting for transfers between devices: 20.8 us -> none  [per_device(): gate_up = lax.all_gather(gate_up_weight[0], 'edp', axis=0, tiled=True)]
    ppermute x6 -> x12, waiting for transfers between devices: 38.7 us -> 59.5 us  [the longest x3 44.8 us: gather_rings(): lax.ppermute(a, 'edp', ring(size, 1))]
    all_to_all x0 -> x1, starting transfers between devices: none -> 19.6 us  [per_device(): lax.all_to_all(back, 'ep', split_axis=0, concat_axis=0, tiled=True)]
    convert_element_type x0 -> x3, other arithmetic: none -> 3.97 us  [scatter_rings(): (a.astype(F32) + partial[(size - 2 - step) % size, :half].astype(F32)).as...]
    unnamed x14 -> x8, local copies, waits for them, and re-layouts: 0.79 us -> 3.42 us
  transfers between devices with their start and end apart: 9 -> 14, of which waited for: 5 -> 7; matrix products, arithmetic and copies ran while one was open for 0% -> 2% of each run, Pallas kernels for 10% -> 6%
where the time goes in v3:
time: 250 us; the launch traced here: 247 us
  Pallas kernels  98.9 us (40%)
  starting transfers between devices  79 us (32%)
  waiting for transfers between devices  59.5 us (24%)
  other arithmetic  4.9 us (2%)
  local copies, waits for them, and re-layouts  3.42 us (1%)
    pallas_call x1, Pallas kernels, halves(): pl.pallas_call(pack_kernel, in_specs=[whole(pl.ANY)] * 2, out_specs=[whol...  72.6 us
    ppermute x3, waiting for transfers between devices, gather_rings(): lax.ppermute(a, 'edp', ring(size, 1))  44.8 us
    all_to_all x1, starting transfers between devices, per_device(): lax.all_to_all(back, 'ep', split_axis=0, concat_axis=0, tiled=True)  19.6 us
    all_to_all x1, starting transfers between devices, per_device(): recv = lax.all_to_all(sent, 'ep', split_axis=0, concat_axis=0, tiled=True)  18.3 us
    ppermute x3, starting transfers between devices, scatter_rings(): lax.ppermute(b, 'edp', ring(size, -1))  14.3 us
    ppermute x3, waiting for transfers between devices, scatter_rings(): lax.ppermute(a, 'edp', ring(size, 1))  11.7 us
    ppermute x3, starting transfers between devices, gather_rings(): lax.ppermute(b, 'edp', ring(size, -1))  11.7 us
    pallas_call x1, Pallas kernels, per_device(): pl.pallas_call(functools.partial(hidden_kernel, quarters), in_specs=[whol...  8.76 us
  transfers between devices with their start and end apart: 14, of which 7 were waited for; matrix products, arithmetic and copies ran while one was open for 2% of the time, Pallas kernels for 6%

profile of v3, /device:TPU:1, one launch (start us, length us, event | category | flops | bytes accessed | tf_op | source)
XLA Modules:
  0.0 246.5 jit_solution(16620607146561482045)
XLA Ops:
  0.6 72.6 %pack_weights.1 = (bf16[384,1536]{1,0:T(8,128)(2,1)}, bf16[384,1536]{1,0:T(8,128)(2,1)}) custom-call(bf16[512,1536]{1,0:T(8,128)(2,1)} %bitcast.29, bf16[768,512]{1,0:T(8,128)(2,1)} %bitcast.35), custom_call_target="tpu_custom_call" | custom-call | tf_op jit(solution)/shard_map/pack_weights/pallas_call | solution.py:216
  73.3 3.9 %collective-permute-start = (bf16[384,1536]{1,0:T(8,128)(2,1)}, bf16[384,1536]{1,0:T(8,128)(2,1)S(1)}, u32[]{:S(2)}, u32[]{:S(2)}) collective-permute-start(bf16[384,1536]{1,0:T(8,128)(2,1)} %get-tuple-element.16), channel_id=1, source_target_pairs={{0,1},{1,2},{2,3},{3,0},{4,5},{5,6},{6,7},{7,4},{8,9},{9,10},{10,1... | collective-permute-start | bytes 3538952 | tf_op jit(solution)/shard_map/ppermute | solution.py:244
  77.2 3.2 %collective-permute-start.1 = (bf16[384,1536]{1,0:T(8,128)(2,1)}, bf16[384,1536]{1,0:T(8,128)(2,1)}, u32[]{:S(2)}, u32[]{:S(2)}) collective-permute-start(bf16[384,1536]{1,0:T(8,128)(2,1)} %get-tuple-element.17), channel_id=1, source_target_pairs={{0,3},{1,0},{2,1},{3,2},{4,7},{5,4},{6,5},{7,6},{8,11},{9,8},{10,9... | collective-permute-start | bytes 3538952 | tf_op jit(solution)/shard_map/ppermute | solution.py:244
  80.4 6.7 %send_rows.1 = (bf16[1024,1024]{1,0:T(8,128)(2,1)}, bf16[1024,96]{1,0:T(8,128)(2,1)}) custom-call(s32[8,24]{1,0:T(8,128)} %bitcast.38, f32[8,24]{1,0:T(8,128)} %bitcast.39, bf16[24,2048]{1,0:T(8,128)(2,1)} %tok_ref.1, bf16[24,2048]{1,0:T(8,128)(2,1)} %grad_ref.1), custom_call_target="tpu_custom_call" | custom-call | tf_op jit(solution)/shard_map/send_rows/pallas_call | solution.py:276
  87.1 18.3 %all-to-all-start = ((bf16[128,8,1024]{2,1,0:T(8,128)(2,1)}), bf16[128,8,1024]{2,1,0:T(8,128)(2,1)S(1)}, u32[]{:S(2)}, u32[]{:S(2)}) async-start(bf16[128,8,1024]{2,1,0:T(8,128)(2,1)} %bitcast.37), calls=%async_computation | async-start | bytes 4194304 | tf_op jit(solution)/shard_map/all_to_all | solution.py:292
  105.5 0.0 collective-permute-done.refs_0_
  105.5 0.0 copy-start.2
  105.5 0.0 collective-permute-done.1.refs_1_
  105.5 1.0 copy-done.2
  106.5 2.6 %collective-permute-start.2 = (bf16[384,1536]{1,0:T(8,128)(2,1)}, bf16[384,1536]{1,0:T(8,128)(2,1)S(1)}, u32[]{:S(2)}, u32[]{:S(2)}) collective-permute-start(bf16[384,1536]{1,0:T(8,128)(2,1)} %get-tuple-element.18.refs_0_), channel_id=1, source_target_pairs={{0,1},{1,2},{2,3},{3,0},{4,5},{5,6},{6,7},{7,4},{8,9},{9,10},{10,1... | collective-permute-start | bytes 3538952 | tf_op jit(solution)/shard_map/ppermute | solution.py:244
  109.1 3.9 %collective-permute-start.4 = (bf16[384,1536]{1,0:T(8,128)(2,1)}, bf16[384,1536]{1,0:T(8,128)(2,1)}, u32[]{:S(2)}, u32[]{:S(2)}) collective-permute-start(bf16[384,1536]{1,0:T(8,128)(2,1)} %get-tuple-element.19.refs_3_), channel_id=1, source_target_pairs={{0,3},{1,0},{2,1},{3,2},{4,7},{5,4},{6,5},{7,6},{8,11},{9,8},{10,9... | collective-permute-start | bytes 3538952 | tf_op jit(solution)/shard_map/ppermute | solution.py:244
  113.0 22.9 %collective-permute-done.2.refs_1_ = bf16[384,1536]{1,0:T(8,128)(2,1)S(1)} collective-permute-done((bf16[384,1536]{1,0:T(8,128)(2,1)}, bf16[384,1536]{1,0:T(8,128)(2,1)S(1)}, u32[]{:S(2)}, u32[]{:S(2)}) %collective-permute-start.2) | collective-permute-done | bytes 1179680 | tf_op jit(solution)/shard_map/ppermute | solution.py:244
  135.9 0.0 copy-start.1
  135.9 1.9 collective-permute-start.3
  137.9 0.0 collective-permute-done.4.refs_4_
  137.9 4.6 %collective-permute-start.5 = (bf16[384,1536]{1,0:T(8,128)(2,1)}, bf16[384,1536]{1,0:T(8,128)(2,1)}, u32[]{:S(2)}, u32[]{:S(2)}) collective-permute-start(bf16[384,1536]{1,0:T(8,128)(2,1)} %collective-permute-done.4.refs_4_), channel_id=1, source_target_pairs={{0,3},{1,0},{2,1},{3,2},{4,7},{5,4},{6,5},{7,6},{8,11},{9,8},{10,9... | collective-permute-start | bytes 3538952 | tf_op jit(solution)/shard_map/ppermute | solution.py:244
  142.5 21.9 %collective-permute-done.3.refs_2_ = bf16[384,1536]{1,0:T(8,128)(2,1)} collective-permute-done((bf16[384,1536]{1,0:T(8,128)(2,1)S(1)}, bf16[384,1536]{1,0:T(8,128)(2,1)}, u32[]{:S(2)}, u32[]{:S(2)}) %collective-permute-start.3) | collective-permute-done | bytes 1179680 | tf_op jit(solution)/shard_map/ppermute | solution.py:244
  164.3 1.1 collective-permute-done.5.refs_5_
  165.5 0.0 all-to-all-done
  165.5 0.0 copy-start
  165.5 0.0 copy-done.1
  165.5 1.4 copy-done
  166.9 8.8 %hidden_rows.1 = (f32[256,768]{1,0:T(8,128)}, f32[256,768]{1,0:T(8,128)}, bf16[256,2048]{1,0:T(8,128)(2,1)}, bf16[384,512]{1,0:T(8,128)(2,1)}, bf16[384,512]{1,0:T(8,128)(2,1)}, /*index=5*/bf16[4,768,512]{2,1,0:T(8,128)(2,1)}) custom-call(s32[1]{0:T(128)} %bitcast.2.me_ref, bf16[1024,1024]{1,0:T(8,128)(2,1)} %bitcast.32, bf16[512,1536]{1,0:T(8,128)(2,1)} %bitcast.30, ...), custom_call_target="tpu_custom_call" | custom-call | tf_op jit(solution)/shard_map/hidden_rows/pallas_call | solution.py:295
  175.6 1.9 collective-permute-start.6
  177.5 5.3 %collective-permute-start.9 = (bf16[384,512]{1,0:T(8,128)(2,1)}, bf16[384,512]{1,0:T(8,128)(2,1)S(1)}, u32[]{:S(2)}, u32[]{:S(2)}) collective-permute-start(bf16[384,512]{1,0:T(8,128)(2,1)} %get-tuple-element.25), channel_id=1, source_target_pairs={{0,3},{1,0},{2,1},{3,2},{4,7},{5,4},{6,5},{7,6},{8,11},{9,8},{10,9... | collective-permute-start | bytes 1179656 | tf_op jit(solution)/shard_map/ppermute | solution.py:256
  182.9 8.5 %back_rows.1 = bf16[1024,512]{1,0:T(8,128)(2,1)} custom-call(s32[1]{0:T(128)} %bitcast.2.me_ref, f32[256,768]{1,0:T(8,128)} %get-tuple-element.20.to_gate_ref, f32[256,768]{1,0:T(8,128)} %get-tuple-element.21.to_up_ref, bf16[256,2048]{1,0:T(8,128)(2,1)} %get-tuple-element.22.g_ref, bf16[768,512]{1,0:T(8,128)(2,1)} %bitcast.36, bf16[512,1536]{1,0:T(8,128)(2,1)} %bitcast.31, ...), custom_call_target="tpu_custom_call" | custom-call | tf_op jit(solution)/shard_map/back_rows/pallas_call | solution.py:318
  191.4 19.6 %all-to-all-start.1 = ((bf16[128,8,512]{2,1,0:T(8,128)(2,1)}), bf16[128,8,512]{2,1,0:T(8,128)(2,1)S(1)}, u32[]{:S(2)}, u32[]{:S(2)}) async-start(bf16[128,8,512]{2,1,0:T(8,128)(2,1)} %bitcast.33), calls=%async_computation.1 | async-start | bytes 2097152 | tf_op jit(solution)/shard_map/all_to_all | solution.py:336
  211.0 0.0 collective-permute-done.6
  211.0 0.0 collective-permute-done.9
  211.0 1.3 fusion.5
  212.4 1.9 collective-permute-start.7
  214.3 4.6 %collective-permute-start.10 = (bf16[384,512]{1,0:T(8,128)(2,1)S(1)}, bf16[384,512]{1,0:T(8,128)(2,1)S(1)}, u32[]{:S(2)}, u32[]{:S(2)}) collective-permute-start(bf16[384,512]{1,0:T(8,128)(2,1)S(1)} %get-tuple-element.31), channel_id=1, source_target_pairs={{0,3},{1,0},{2,1},{3,2},{4,7},{5,4},{6,5},{7,6},{8,11},{9,8},{10,9... | collective-permute-start | bytes 1179656 | tf_op jit(solution)/shard_map/ppermute | solution.py:256
  218.9 6.3 %collective-permute-done.7 = bf16[384,512]{1,0:T(8,128)(2,1)S(1)} collective-permute-done((bf16[384,512]{1,0:T(8,128)(2,1)S(1)}, bf16[384,512]{1,0:T(8,128)(2,1)S(1)}, u32[]{:S(2)}, u32[]{:S(2)}) %collective-permute-start.7) | collective-permute-done | bytes 393248 | tf_op jit(solution)/shard_map/ppermute | solution.py:256
  225.2 0.9 collective-permute-done.10
  226.1 1.3 fusion.4
  227.4 2.9 %collective-permute-start.8 = (bf16[384,512]{1,0:T(8,128)(2,1)S(1)}, bf16[384,512]{1,0:T(8,128)(2,1)S(1)}, u32[]{:S(2)}, u32[]{:S(2)}) collective-permute-start(bf16[384,512]{1,0:T(8,128)(2,1)S(1)} %get-tuple-element.28), channel_id=1, source_target_pairs={{0,1},{1,2},{2,3},{3,0},{4,5},{5,6},{6,7},{7,4},{8,9},{9,10},{10,1... | collective-permute-start | bytes 1179656 | tf_op jit(solution)/shard_map/ppermute | solution.py:256
  230.3 4.4 %collective-permute-start.11 = (bf16[384,512]{1,0:T(8,128)(2,1)S(1)}, bf16[384,512]{1,0:T(8,128)(2,1)S(1)}, u32[]{:S(2)}, u32[]{:S(2)}) collective-permute-start(bf16[384,512]{1,0:T(8,128)(2,1)S(1)} %get-tuple-element.29), channel_id=1, source_target_pairs={{0,3},{1,0},{2,1},{3,2},{4,7},{5,4},{6,5},{7,6},{8,11},{9,8},{10,9... | collective-permute-start | bytes 1179656 | tf_op jit(solution)/shard_map/ppermute | solution.py:256
  234.7 5.4 %collective-permute-done.8 = bf16[384,512]{1,0:T(8,128)(2,1)S(1)} collective-permute-done((bf16[384,512]{1,0:T(8,128)(2,1)S(1)}, bf16[384,512]{1,0:T(8,128)(2,1)S(1)}, u32[]{:S(2)}, u32[]{:S(2)}) %collective-permute-start.8) | collective-permute-done | bytes 393248 | tf_op jit(solution)/shard_map/ppermute | solution.py:256
  240.1 0.9 collective-permute-done.11
  241.0 1.3 fusion.3
  242.3 0.9 maximum_bitcast_fusion
  243.2 0.0 all-to-all-done.1
  243.2 0.0 copy-start.3
  243.2 1.0 copy-done.3
  244.2 2.3 combine_rows.1
  (1 shorter events, 0.0 us)
Async XLA Ops:
  73.3 32.2 %collective-permute-start = (bf16[384,1536]{1,0:T(8,128)(2,1)}, bf16[384,1536]{1,0:T(8,128)(2,1)S(1)}, u32[]{:S(2)}, u32[]{:S(2)}) collective-permute-start(bf16[384,1536]{1,0:T(8,128)(2,1)} %get-tuple-element.16), channel_id=1, source_target_pairs={{0,1},{1,2},{2,3},{3,0},{4,5},{5,6},{6,7},{7,4},{8,9},{9,10},{10,1... | collective-permute-start | bytes 3538952 | tf_op jit(solution)/shard_map/ppermute | solution.py:244
  77.2 28.2 %collective-permute-start.1 = (bf16[384,1536]{1,0:T(8,128)(2,1)}, bf16[384,1536]{1,0:T(8,128)(2,1)}, u32[]{:S(2)}, u32[]{:S(2)}) collective-permute-start(bf16[384,1536]{1,0:T(8,128)(2,1)} %get-tuple-element.17), channel_id=1, source_target_pairs={{0,3},{1,0},{2,1},{3,2},{4,7},{5,4},{6,5},{7,6},{8,11},{9,8},{10,9... | collective-permute-start | bytes 3538952 | tf_op jit(solution)/shard_map/ppermute | solution.py:244
  87.1 78.4 %all-to-all-start = ((bf16[128,8,1024]{2,1,0:T(8,128)(2,1)}), bf16[128,8,1024]{2,1,0:T(8,128)(2,1)S(1)}, u32[]{:S(2)}, u32[]{:S(2)}) async-start(bf16[128,8,1024]{2,1,0:T(8,128)(2,1)} %bitcast.37), calls=%async_computation | async-start | bytes 4194304 | tf_op jit(solution)/shard_map/all_to_all | solution.py:292
  105.5 1.0 copy-start.2
  106.5 29.4 %collective-permute-start.2 = (bf16[384,1536]{1,0:T(8,128)(2,1)}, bf16[384,1536]{1,0:T(8,128)(2,1)S(1)}, u32[]{:S(2)}, u32[]{:S(2)}) collective-permute-start(bf16[384,1536]{1,0:T(8,128)(2,1)} %get-tuple-element.18.refs_0_), channel_id=1, source_target_pairs={{0,1},{1,2},{2,3},{3,0},{4,5},{5,6},{6,7},{7,4},{8,9},{9,10},{10,1... | collective-permute-start | bytes 3538952 | tf_op jit(solution)/shard_map/ppermute | solution.py:244
  109.1 28.8 %collective-permute-start.4 = (bf16[384,1536]{1,0:T(8,128)(2,1)}, bf16[384,1536]{1,0:T(8,128)(2,1)}, u32[]{:S(2)}, u32[]{:S(2)}) collective-permute-start(bf16[384,1536]{1,0:T(8,128)(2,1)} %get-tuple-element.19.refs_3_), channel_id=1, source_target_pairs={{0,3},{1,0},{2,1},{3,2},{4,7},{5,4},{6,5},{7,6},{8,11},{9,8},{10,9... | collective-permute-start | bytes 3538952 | tf_op jit(solution)/shard_map/ppermute | solution.py:244
  135.9 29.5 %copy-start.1 = (bf16[384,1536]{1,0:T(8,128)(2,1)}, bf16[384,1536]{1,0:T(8,128)(2,1)S(1)}, u32[]{:S(2)}) copy-start(bf16[384,1536]{1,0:T(8,128)(2,1)S(1)} %collective-permute-done.2.refs_1_) | copy-start | bytes 3538948
  135.9 28.4 %collective-permute-start.3 = (bf16[384,1536]{1,0:T(8,128)(2,1)S(1)}, bf16[384,1536]{1,0:T(8,128)(2,1)}, u32[]{:S(2)}, u32[]{:S(2)}) collective-permute-start(bf16[384,1536]{1,0:T(8,128)(2,1)S(1)} %collective-permute-done.2.refs_1_), channel_id=1, source_target_pairs={{0,1},{1,2},{2,3},{3,0},{4,5},{5,6},{6,7},{7,4},{8,9},{9,10},{10,1... | collective-permute-start | bytes 3538952 | tf_op jit(solution)/shard_map/ppermute | solution.py:244
  137.9 27.6 %collective-permute-start.5 = (bf16[384,1536]{1,0:T(8,128)(2,1)}, bf16[384,1536]{1,0:T(8,128)(2,1)}, u32[]{:S(2)}, u32[]{:S(2)}) collective-permute-start(bf16[384,1536]{1,0:T(8,128)(2,1)} %collective-permute-done.4.refs_4_), channel_id=1, source_target_pairs={{0,3},{1,0},{2,1},{3,2},{4,7},{5,4},{6,5},{7,6},{8,11},{9,8},{10,9... | collective-permute-start | bytes 3538952 | tf_op jit(solution)/shard_map/ppermute | solution.py:244
  165.5 1.4 copy-start
  175.6 35.4 %collective-permute-start.6 = (bf16[384,512]{1,0:T(8,128)(2,1)}, bf16[384,512]{1,0:T(8,128)(2,1)S(1)}, u32[]{:S(2)}, u32[]{:S(2)}) collective-permute-start(bf16[384,512]{1,0:T(8,128)(2,1)} %get-tuple-element.23), channel_id=1, source_target_pairs={{0,1},{1,2},{2,3},{3,0},{4,5},{5,6},{6,7},{7,4},{8,9},{9,10},{10,1... | collective-permute-start | bytes 1179656 | tf_op jit(solution)/shard_map/ppermute | solution.py:256
  177.5 33.5 %collective-permute-start.9 = (bf16[384,512]{1,0:T(8,128)(2,1)}, bf16[384,512]{1,0:T(8,128)(2,1)S(1)}, u32[]{:S(2)}, u32[]{:S(2)}) collective-permute-start(bf16[384,512]{1,0:T(8,128)(2,1)} %get-tuple-element.25), channel_id=1, source_target_pairs={{0,3},{1,0},{2,1},{3,2},{4,7},{5,4},{6,5},{7,6},{8,11},{9,8},{10,9... | collective-permute-start | bytes 1179656 | tf_op jit(solution)/shard_map/ppermute | solution.py:256
  191.4 51.8 %all-to-all-start.1 = ((bf16[128,8,512]{2,1,0:T(8,128)(2,1)}), bf16[128,8,512]{2,1,0:T(8,128)(2,1)S(1)}, u32[]{:S(2)}, u32[]{:S(2)}) async-start(bf16[128,8,512]{2,1,0:T(8,128)(2,1)} %bitcast.33), calls=%async_computation.1 | async-start | bytes 2097152 | tf_op jit(solution)/shard_map/all_to_all | solution.py:336
  212.4 12.8 %collective-permute-start.7 = (bf16[384,512]{1,0:T(8,128)(2,1)S(1)}, bf16[384,512]{1,0:T(8,128)(2,1)S(1)}, u32[]{:S(2)}, u32[]{:S(2)}) collective-permute-start(bf16[384,512]{1,0:T(8,128)(2,1)S(1)} %get-tuple-element.30), channel_id=1, source_target_pairs={{0,1},{1,2},{2,3},{3,0},{4,5},{5,6},{6,7},{7,4},{8,9},{9,10},{10,1... | collective-permute-start | bytes 1179656 | tf_op jit(solution)/shard_map/ppermute | solution.py:256
  214.3 11.8 %collective-permute-start.10 = (bf16[384,512]{1,0:T(8,128)(2,1)S(1)}, bf16[384,512]{1,0:T(8,128)(2,1)S(1)}, u32[]{:S(2)}, u32[]{:S(2)}) collective-permute-start(bf16[384,512]{1,0:T(8,128)(2,1)S(1)} %get-tuple-element.31), channel_id=1, source_target_pairs={{0,3},{1,0},{2,1},{3,2},{4,7},{5,4},{6,5},{7,6},{8,11},{9,8},{10,9... | collective-permute-start | bytes 1179656 | tf_op jit(solution)/shard_map/ppermute | solution.py:256
  227.4 12.6 %collective-permute-start.8 = (bf16[384,512]{1,0:T(8,128)(2,1)S(1)}, bf16[384,512]{1,0:T(8,128)(2,1)S(1)}, u32[]{:S(2)}, u32[]{:S(2)}) collective-permute-start(bf16[384,512]{1,0:T(8,128)(2,1)S(1)} %get-tuple-element.28), channel_id=1, source_target_pairs={{0,1},{1,2},{2,3},{3,0},{4,5},{5,6},{6,7},{7,4},{8,9},{9,10},{10,1... | collective-permute-start | bytes 1179656 | tf_op jit(solution)/shard_map/ppermute | solution.py:256
  230.3 10.7 %collective-permute-start.11 = (bf16[384,512]{1,0:T(8,128)(2,1)S(1)}, bf16[384,512]{1,0:T(8,128)(2,1)S(1)}, u32[]{:S(2)}, u32[]{:S(2)}) collective-permute-start(bf16[384,512]{1,0:T(8,128)(2,1)S(1)} %get-tuple-element.29), channel_id=1, source_target_pairs={{0,3},{1,0},{2,1},{3,2},{4,7},{5,4},{6,5},{7,6},{8,11},{9,8},{10,9... | collective-permute-start | bytes 1179656 | tf_op jit(solution)/shard_map/ppermute | solution.py:256
  243.2 1.0 copy-start.3

commit v4 on v3

--- a/solution.py
+++ b/solution.py
@@ -13,15 +13,13 @@
 TN = (((0,), (0,)), ((), ()))
 VMEM_LIMIT = 56 * 1024 * 1024
 COST = 20 * 10**9
-PASS = (0,)
 
 
 def whole(memory_space=pltpu.VMEM):
     return pl.BlockSpec(memory_space=memory_space)
 
 
-def quantize(value):
-    top = jnp.max(jnp.abs(value), axis=1, keepdims=True)
+def rebuild(value, top):
     scale = (top + EPSILON).astype(BF16).astype(F32)
     return ((value / scale).astype(BF16).astype(F32) * scale).astype(BF16)
 
@@ -39,8 +37,14 @@
             here = pl.ds(q * toks, toks)
             for g in range(feat // 128):
                 cols = slice(q * feat + g * 128, q * feat + g * 128 + 128)
-                stack[here, pl.ds(g * 128, 128)] = quantize(tok_ref[:, cols].astype(F32)).astype(F32)
-            stack[here, pl.ds(feat, feat)] = grad_ref[:, q * feat : q * feat + feat].astype(F32)
+                value = tok_ref[:, cols].astype(F32)
+                top = jnp.max(jnp.abs(value), axis=1, keepdims=True)
+                stack[here, pl.ds(g * 128, 128)] = rebuild(value, top).astype(F32)
+            grads = grad_ref[:, q * feat : q * feat + feat].astype(F32)
+            stack[here, pl.ds(feat, feat)] = grads
+            for g in range(feat // 128):
+                top = jnp.max(jnp.abs(grads[:, g * 128 : g * 128 + 128]), axis=1, keepdims=True)
+                stack[here, pl.ds(2 * feat + g * 128, 128)] = jnp.broadcast_to(top, (toks, 128))
 
     row = lax.broadcasted_iota(jnp.int32, (rows, lanes), 0) + block * rows
     lane = lax.broadcasted_iota(jnp.int32, (rows, lanes), 1)
@@ -62,10 +66,9 @@
     pick_ref[...] = pick
     send_ref[:, :feat] = jnp.dot(pick, stack[:, :feat].astype(BF16), preferred_element_type=F32).astype(BF16)
     gate = jnp.sum(jnp.where(chosen, weight, 0.0), axis=1, keepdims=True)
-    grads = jnp.dot(pick, stack[:, feat:].astype(BF16), preferred_element_type=F32) * gate
-    for g in range(feat // 128):
-        cols = slice(g * 128, g * 128 + 128)
-        send_ref[:, feat + g * 128 : feat + g * 128 + 128] = quantize(grads[:, cols])
+    grads = jnp.dot(pick, stack[:, feat : 2 * feat].astype(BF16), preferred_element_type=F32) * gate
+    top = jnp.dot(pick, stack[:, 2 * feat :].astype(BF16), preferred_element_type=F32) * gate
+    send_ref[:, feat:] = rebuild(grads, top)
 
 
 def order_matrix(rows, quarters):
@@ -84,20 +87,23 @@
     return out
 
 
-def up_rows(own, others, cols):
-    feat = own.shape[0]
-    half = feat // 2
-    (left_a, far_a, right_a), (right_b, far_b, left_b) = others[:3], others[3:]
-    out = [(own.at[:, cols], 0, feat)]
-    for k, (a, b) in enumerate(((right_a, right_b), (far_a, far_b), (left_a, left_b)), 1):
-        out.append((a.at[pl.ds(0, half), cols], k * feat, half))
-        out.append((b.at[pl.ds(0, half), cols], k * feat + half, half))
-    return out
+def pieces(own, others, axis):
+    right, far_a, far_b, left = others
+    rows = own.shape[0]
+    step = rows if axis == 0 else 0
+    half = rows // 2
+    return [
+        (own, 0, rows, 0),
+        (right, step, rows, 1),
+        (far_a, 2 * step, half, 2),
+        (far_b, 2 * step + half, half, 2),
+        (left, 3 * step, rows, 3),
+    ]
 
 
 def hidden_kernel(quarters, me_ref, recv_ref, own, *refs):
-    others, refs = refs[:6], refs[6:]
-    to_gate_ref, to_up_ref, g_ref, first_a, first_b, down_ref, recv, w, x_ref, sems = refs
+    others, refs = refs[:4], refs[4:]
+    to_gate_ref, to_up_ref, g_ref, down_own, down_right, far_top, far_bottom, down_left, recv, w, x_ref, sems = refs
     rows = 256
     per = rows // quarters
     feat = recv_ref.shape[1] // 2
@@ -109,7 +115,8 @@
         copies = []
         for at in (n * tile, hidden_units + n * tile):
             cols = pl.ds(at, tile)
-            copies += [(src, w.at[pl.ds(row, size), cols]) for src, row, size in up_rows(own, others, cols)]
+            for src, row, size, _ in pieces(own, others, 0):
+                copies.append((src.at[:, cols], w.at[pl.ds(row, size), cols]))
         waits.append(start_all(copies, sems, 1 + n * len(copies)))
     got_rows.wait()
     order = order_matrix(rows, quarters)
@@ -133,35 +140,28 @@
         to_up_ref[:, cols] = activ
         hidden = (activ * up).astype(BF16)
         part = lax.dot_general(hidden, g_ref[...], TN, preferred_element_type=F32).astype(BF16)
-        for k in range(quarters):
-            down_ref[k, cols, :] = part[:, k * feat : k * feat + feat]
+        for k, ref in ((0, down_own), (1, down_right), (3, down_left)):
+            ref[cols, :] = part[:, k * feat : k * feat + feat]
         lo, hi = n * tile, n * tile + tile
-        if lo < half:
-            end = min(hi, half)
-            first_a[lo:end, :] = part[: end - lo, (quarters - 1) * feat :]
-        if hi > half:
-            start = max(lo, half)
-            first_b[start - half : hi - half, :] = part[start - lo :, feat : 2 * feat]
+        mid = min(max(half, lo), hi)
+        if lo < mid:
+            far_top[lo:mid, :] = part[: mid - lo, 2 * feat : 3 * feat]
+        if mid < hi:
+            far_bottom[mid - half : hi - half, :] = part[mid - lo :, 2 * feat : 3 * feat]
 
 
 def back_kernel(quarters, me_ref, to_gate_ref, to_up_ref, g_ref, own_down, own, *refs):
-    others, refs = refs[:6], refs[6:]
+    others, other_downs, refs = refs[:4], refs[4:8], refs[8:]
     back_ref, to_gate, to_up, g, wd, w, gp_ref, hold, sems = refs
     slots, hidden_units = to_gate.shape
     feat = own.shape[0]
-    half = feat // 2
-    third = hidden_units // 6
-    (left_a, far_a, right_a), (right_b, far_b, left_b) = others[:3], others[3:]
-    copies = [(g_ref, g), (own_down, wd.at[:, pl.ds(0, feat)])]
-    for k, pair in enumerate(((right_a, right_b), (far_a, far_b), (left_a, left_b)), 1):
-        for h, piece in enumerate(pair):
-            for m in range(3):
-                src = piece.at[pl.ds(half, third), pl.ds(m * feat, feat)]
-                copies.append((src, wd.at[pl.ds((h * 3 + m) * third, third), pl.ds(k * feat, feat)]))
+    copies = [(g_ref, g)]
+    for src, row, size, k in pieces(own_down, other_downs, 1):
+        copies.append((src, wd.at[pl.ds(row, size), pl.ds(k * feat, feat)]))
     copies += [(to_gate_ref, to_gate), (to_up_ref, to_up)]
     early = start_all(copies, sems)
     late = start_all(
-        [(src, w.at[pl.ds(row, size), :]) for src, row, size in up_rows(own, others, slice(None))], sems, len(copies)
+        [(src, w.at[pl.ds(row, size), :]) for src, row, size, _ in pieces(own, others, 0)], sems, len(copies)
     )
     for copy in early:
         copy.wait()
@@ -172,7 +172,7 @@
         gp_ref[:, cols] = (total * to_gate[:, cols]).astype(BF16)
         gp_ref[:, hidden_units + n * tile : hidden_units + n * tile + tile] = (total * to_up[:, cols]).astype(BF16)
     for k in range(quarters):
-        for copy in late[:1] if k == 0 else late[2 * k - 1 : 2 * k + 1]:
+        for copy in (late[:1], late[1:2], late[2:4], late[4:])[k]:
             copy.wait()
         hold[lax.rem(me_ref[0] + k, quarters)] = lax.dot_general(
             gp_ref[...], w[k * feat : k * feat + feat, :], NT, preferred_element_type=F32
@@ -198,32 +198,6 @@
     return [(i, (i + step) % size) for i in range(size)]
 
 
-def pack_kernel(up, down, a_ref, b_ref, sems):
-    half, third, feat = up.shape[0] // 2, down.shape[0] // 6, down.shape[1]
-    copies = []
-    for h, ref in enumerate((a_ref, b_ref)):
-        copies.append((up.at[pl.ds(h * half, half), :], ref.at[pl.ds(0, half), :]))
-        for m in range(3):
-            copies.append(
-                (down.at[pl.ds((h * 3 + m) * third, third), :], ref.at[pl.ds(half, third), pl.ds(m * feat, feat)])
-            )
-    for copy in start_all(copies, sems):
-        copy.wait()
-
-
-def halves(up, down):
-    shape = jax.ShapeDtypeStruct((up.shape[0] // 2 + down.shape[0] // 6, up.shape[1]), BF16)
-    return pl.pallas_call(
-        pack_kernel,
-        in_specs=[whole(pl.ANY)] * 2,
-        out_specs=[whole(pl.ANY)] * 2,
-        out_shape=[shape] * 2,
-        scratch_shapes=[pltpu.SemaphoreType.DMA((8,))],
-        compiler_params=pltpu.CompilerParams(vmem_limit_bytes=VMEM_LIMIT),
-        name="pack_weights",
-    )(up, down)
-
-
 def pass_on(a, b):
     return pl.pallas_call(
         lambda *refs: None,
@@ -237,26 +211,40 @@
     )(a, b)
 
 
-def gather_rings(up, down, size):
-    a, b = halves(up, down)
-    came_a, came_b = [], []
-    for step in range(size - 1):
-        a, b = lax.ppermute(a, "edp", ring(size, 1)), lax.ppermute(b, "edp", ring(size, -1))
-        if step in PASS:
-            a, b = pass_on(a, b)
-        came_a.append(a)
-        came_b.append(b)
-    return came_a + came_b
-
-
-def scatter_rings(first_a, first_b, partial, size):
-    half = partial.shape[1] // 2
-    a, b = first_a, first_b
-    for step in range(size - 1):
-        a, b = lax.ppermute(a, "edp", ring(size, 1)), lax.ppermute(b, "edp", ring(size, -1))
-        a = (a.astype(F32) + partial[(size - 2 - step) % size, :half].astype(F32)).astype(BF16)
-        b = (b.astype(F32) + partial[(step + 2) % size, half:].astype(F32)).astype(BF16)
-    return jnp.concatenate([a, b], axis=0)
+def gather_two_steps(up, down, size):
+    fwd, bwd = ring(size, 1), ring(size, -1)
+    left_up, right_up = pass_on(lax.ppermute(up, "edp", fwd), lax.ppermute(up, "edp", bwd))
+    left_down, right_down = lax.ppermute(down, "edp", fwd), lax.ppermute(down, "edp", bwd)
+    out = []
+    for left, right in ((left_up, right_up), (left_down, right_down)):
+        half = left.shape[0] // 2
+        out += [right, lax.ppermute(left[:half], "edp", fwd), lax.ppermute(right[half:], "edp", bwd), left]
+    return out
+
+
+def add_kernel(right, left, top, bottom, right_out, left_out):
+    half = top.shape[0]
+    right_out[:half, :] = (right[:half, :].astype(F32) + top[...].astype(F32)).astype(BF16)
+    right_out[half:, :] = right[half:, :]
+    left_out[:half, :] = left[:half, :]
+    left_out[half:, :] = (left[half:, :].astype(F32) + bottom[...].astype(F32)).astype(BF16)
+
+
+def scatter_two_steps(blocks, size):
+    fwd, bwd = ring(size, 1), ring(size, -1)
+    own, right, far_top, far_bottom, left = blocks
+    top, bottom = lax.ppermute(far_top, "edp", fwd), lax.ppermute(far_bottom, "edp", bwd)
+    right, left = pl.pallas_call(
+        add_kernel,
+        in_specs=[whole()] * 4,
+        out_specs=[whole()] * 2,
+        out_shape=[jax.ShapeDtypeStruct(right.shape, BF16)] * 2,
+        compiler_params=pltpu.CompilerParams(vmem_limit_bytes=VMEM_LIMIT),
+        cost_estimate=pl.CostEstimate(flops=COST, bytes_accessed=0, transcendentals=0),
+        name="add_far",
+    )(right, left, top, bottom)
+    from_left, from_right = lax.ppermute(right, "edp", fwd), lax.ppermute(left, "edp", bwd)
+    return (own.astype(F32) + from_left.astype(F32) + from_right.astype(F32)).astype(BF16)
 
 
 def per_device(tokens, out_grad, expert_ids, gate_values, gate_up_weight, down_weight):
@@ -270,7 +258,7 @@
     params = pltpu.CompilerParams(vmem_limit_bytes=VMEM_LIMIT)
     me = lax.axis_index("edp").astype(jnp.int32).reshape(1)
 
-    others = gather_rings(gate_up_weight[0], down_weight[0], parts)
+    others = gather_two_steps(gate_up_weight[0], down_weight[0], parts)
 
     tile = 128
     sent, pick = pl.pallas_call(
@@ -285,25 +273,23 @@
             jax.ShapeDtypeStruct((rows, 2 * feat), BF16),
             jax.ShapeDtypeStruct((rows, quarters * toks), BF16),
         ],
-        scratch_shapes=[pltpu.VMEM((quarters * toks, 2 * feat), F32)],
+        scratch_shapes=[pltpu.VMEM((quarters * toks, 3 * feat), F32)],
         compiler_params=params,
         name="send_rows",
     )(expert_ids.T, gate_values.T, tokens, out_grad)
     recv = lax.all_to_all(sent, "ep", split_axis=0, concat_axis=0, tiled=True)
 
     half = hidden_units // 2
-    to_gate, to_up, rows_g, first_a, first_b, partial = pl.pallas_call(
+    to_gate, to_up, rows_g, *blocks = pl.pallas_call(
         functools.partial(hidden_kernel, quarters),
-        in_specs=[whole(pltpu.SMEM)] + [whole(pl.ANY)] * 8,
-        out_specs=[whole()] * 6,
+        in_specs=[whole(pltpu.SMEM)] + [whole(pl.ANY)] * 6,
+        out_specs=[whole()] * 8,
         out_shape=[
             jax.ShapeDtypeStruct((slots, hidden_units), F32),
             jax.ShapeDtypeStruct((slots, hidden_units), F32),
             jax.ShapeDtypeStruct((slots, width), BF16),
-            jax.ShapeDtypeStruct((half, feat), BF16),
-            jax.ShapeDtypeStruct((half, feat), BF16),
-            jax.ShapeDtypeStruct((parts, hidden_units, feat), BF16),
-        ],
+        ]
+        + [jax.ShapeDtypeStruct((size, feat), BF16) for size in (hidden_units, hidden_units, half, half, hidden_units)],
         scratch_shapes=[
             pltpu.VMEM((rows, 2 * feat), BF16),
             pltpu.VMEM((width, 2 * hidden_units), BF16),
@@ -312,12 +298,12 @@
         ],
         compiler_params=params,
         name="hidden_rows",
-    )(me, recv, gate_up_weight[0], *others)
-    down_grad = scatter_rings(first_a, first_b, partial, parts)[None]
+    )(me, recv, gate_up_weight[0], *others[:4])
+    down_grad = scatter_two_steps(blocks, parts)[None]
 
     back = pl.pallas_call(
         functools.partial(back_kernel, quarters),
-        in_specs=[whole(pltpu.SMEM)] + [whole(pl.ANY)] * 11,
+        in_specs=[whole(pltpu.SMEM)] + [whole(pl.ANY)] * 13,
         out_specs=whole(),
         out_shape=jax.ShapeDtypeStruct((rows, feat), BF16),
         scratch_shapes=[

time: 250 us -> 157 us (0.63)
  Pallas kernels: 98.9 us -> 28.9 us
  waiting for transfers between devices: 59.5 us -> 43.5 us
  starting transfers between devices: 79 us -> 71.4 us
  local copies, waits for them, and re-layouts: 3.42 us -> 9.93 us
  other arithmetic: 4.9 us -> 1.19 us
    pallas_call x1, Pallas kernels: 72.6 us -> 2.92 us  [scatter_two_steps(): pl.pallas_call(add_kernel, in_specs=[whole()] * 4, out_specs=[whole()] *...]
    ppermute x12, waiting for transfers between devices: 59.5 us -> 30.2 us  [the longest x1 15 us: scatter_two_steps(): lax.ppermute(right, 'edp', fwd)]
    all_to_all x1, waiting for transfers between devices: 0.01 us -> 9.93 us  [per_device(): recv = lax.all_to_all(sent, 'ep', split_axis=0, concat_axis=0, tiled=True)]
    all_to_all x1, starting transfers between devices: 19.6 us -> 13 us  [per_device(): lax.all_to_all(back, 'ep', split_axis=0, concat_axis=0, tiled=True)]
    slice x0 -> x4, local copies, waits for them, and re-layouts: none -> 4.9 us  [the longest x2 3.08 us: gather_two_steps(): left[:half]]
    convert_element_type x3 -> x0, other arithmetic: 3.97 us -> none  [scatter_rings(): (a.astype(F32) + partial[(size - 2 - step) % size, :half].astype(F32)).as...]
    all_to_all x1, waiting for transfers between devices: 0.01 us -> 3.39 us  [per_device(): lax.all_to_all(back, 'ep', split_axis=0, concat_axis=0, tiled=True)]
    unnamed x8 -> x20, local copies, waits for them, and re-layouts: 3.42 us -> 5.03 us
  transfers between devices with their start and end apart: 14 -> 14, of which waited for: 7 -> 7; matrix products, arithmetic and copies ran while one was open for 2% -> 4% of each run, Pallas kernels for 6% -> 17%
where the time goes in v4:
time: 157 us; the launch traced here: 156 us
  starting transfers between devices  71.4 us (45%)
  waiting for transfers between devices  43.5 us (28%)
  Pallas kernels  28.9 us (18%)
  local copies, waits for them, and re-layouts  9.93 us (6%)
    all_to_all x1, starting transfers between devices, per_device(): recv = lax.all_to_all(sent, 'ep', split_axis=0, concat_axis=0, tiled=True)  18.8 us
    ppermute x1, waiting for transfers between devices, scatter_two_steps(): lax.ppermute(right, 'edp', fwd)  15 us
    all_to_all x1, starting transfers between devices, per_device(): lax.all_to_all(back, 'ep', split_axis=0, concat_axis=0, tiled=True)  13 us
    all_to_all x1, waiting for transfers between devices, per_device(): recv = lax.all_to_all(sent, 'ep', split_axis=0, concat_axis=0, tiled=True)  9.93 us
    pallas_call x1, Pallas kernels, per_device(): pl.pallas_call(functools.partial(back_kernel, quarters), in_specs=[whole(...  8.61 us
    pallas_call x1, Pallas kernels, per_device(): pl.pallas_call(functools.partial(hidden_kernel, quarters), in_specs=[whol...  8.52 us
    ppermute x2, starting transfers between devices, gather_two_steps(): lax.ppermute(right[half:], 'edp', bwd)  7.01 us
    ppermute x2, waiting for transfers between devices, gather_two_steps(): lax.ppermute(left[:half], 'edp', fwd)  6.82 us
  transfers between devices with their start and end apart: 14, of which 7 were waited for; matrix products, arithmetic and copies ran while one was open for 4% of the time, Pallas kernels for 17%

profile of v4, /device:TPU:1, one launch (start us, length us, event | category | flops | bytes accessed | tf_op | source)
XLA Modules:
  0.0 155.7 jit_solution(7903904293991995177)
XLA Ops:
  0.6 4.0 %collective-permute-start = (bf16[512,1536]{1,0:T(8,128)(2,1)}, bf16[512,1536]{1,0:T(8,128)(2,1)S(1)}, u32[]{:S(2)}, u32[]{:S(2)}) collective-permute-start(bf16[512,1536]{1,0:T(8,128)(2,1)} %bitcast.11), channel_id=1, source_target_pairs={{0,1},{1,2},{2,3},{3,0},{4,5},{5,6},{6,7},{7,4},{8,9},{9,10},{10,1... | collective-permute-start | bytes 4718600 | tf_op jit(solution)/shard_map/ppermute | solution.py:216
  4.6 3.2 %collective-permute-start.1 = (bf16[512,1536]{1,0:T(8,128)(2,1)}, bf16[512,1536]{1,0:T(8,128)(2,1)S(1)}, u32[]{:S(2)}, u32[]{:S(2)}) collective-permute-start(bf16[512,1536]{1,0:T(8,128)(2,1)} %bitcast.12), channel_id=1, source_target_pairs={{0,3},{1,0},{2,1},{3,2},{4,7},{5,4},{6,5},{7,6},{8,11},{9,8},{10,9... | collective-permute-start | bytes 4718600 | tf_op jit(solution)/shard_map/ppermute | solution.py:216
  7.8 6.5 %send_rows.1 = (bf16[1024,1024]{1,0:T(8,128)(2,1)}, bf16[1024,96]{1,0:T(8,128)(2,1)}) custom-call(s32[8,24]{1,0:T(8,128)} %bitcast.21, f32[8,24]{1,0:T(8,128)} %bitcast.22, bf16[24,2048]{1,0:T(8,128)(2,1)} %tok_ref.1, bf16[24,2048]{1,0:T(8,128)(2,1)} %grad_ref.1), custom_call_target="tpu_custom_call" | custom-call | tf_op jit(solution)/shard_map/send_rows/pallas_call | solution.py:264
  14.3 18.8 %all-to-all-start = ((bf16[128,8,1024]{2,1,0:T(8,128)(2,1)}), bf16[128,8,1024]{2,1,0:T(8,128)(2,1)}, u32[]{:S(2)}, u32[]{:S(2)}) async-start(bf16[128,8,1024]{2,1,0:T(8,128)(2,1)} %bitcast.17), calls=%async_computation | async-start | bytes 4194304 | tf_op jit(solution)/shard_map/all_to_all | solution.py:280
  33.1 1.9 %collective-permute-start.5 = (bf16[768,512]{1,0:T(8,128)(2,1)}, bf16[768,512]{1,0:T(8,128)(2,1)}, u32[]{:S(2)}, u32[]{:S(2)}) collective-permute-start(bf16[768,512]{1,0:T(8,128)(2,1)} %bitcast.18), channel_id=1, source_target_pairs={{0,1},{1,2},{2,3},{3,0},{4,5},{5,6},{6,7},{7,4},{8,9},{9,10},{10,1... | collective-permute-start | bytes 2359304 | tf_op jit(solution)/shard_map/ppermute | solution.py:217
  35.1 4.6 %collective-permute-start.4 = (bf16[768,512]{1,0:T(8,128)(2,1)}, bf16[768,512]{1,0:T(8,128)(2,1)}, u32[]{:S(2)}, u32[]{:S(2)}) collective-permute-start(bf16[768,512]{1,0:T(8,128)(2,1)} %bitcast.19), channel_id=1, source_target_pairs={{0,3},{1,0},{2,1},{3,2},{4,7},{5,4},{6,5},{7,6},{8,11},{9,8},{10,9... | collective-permute-start | bytes 2359304 | tf_op jit(solution)/shard_map/ppermute | solution.py:217
  39.6 0.0 collective-permute-done.refs_0_
  39.7 0.0 copy-start
  39.7 0.0 collective-permute-done.1.refs_1_
  39.7 1.1 copy-done
  40.8 1.2 copy-done.1
  42.0 1.3 slice.12
  43.3 4.0 %collective-permute-start.2 = (bf16[256,1536]{1,0:T(8,128)(2,1)S(1)}, bf16[256,1536]{1,0:T(8,128)(2,1)S(1)}, u32[]{:S(2)}, u32[]{:S(2)}) collective-permute-start(bf16[256,1536]{1,0:T(8,128)(2,1)S(1)} %slice.12), channel_id=1, source_target_pairs={{0,1},{1,2},{2,3},{3,0},{4,5},{5,6},{6,7},{7,4},{8,9},{9,10},{10,1... | collective-permute-start | bytes 2359304 | tf_op jit(solution)/shard_map/ppermute | solution.py:221
  47.4 0.0 copy-done.2
  47.4 0.1 slice.13
  47.4 2.4 %collective-permute-start.3 = (bf16[256,1536]{1,0:T(8,128)(2,1)S(1)}, bf16[256,1536]{1,0:T(8,128)(2,1)S(1)}, u32[]{:S(2)}, u32[]{:S(2)}) collective-permute-start(bf16[256,1536]{1,0:T(8,128)(2,1)S(1)} %slice.13), channel_id=1, source_target_pairs={{0,3},{1,0},{2,1},{3,2},{4,7},{5,4},{6,5},{7,6},{8,11},{9,8},{10,9... | collective-permute-start | bytes 2359304 | tf_op jit(solution)/shard_map/ppermute | solution.py:221
  49.9 6.3 %collective-permute-done.5.refs_7_ = bf16[768,512]{1,0:T(8,128)(2,1)} collective-permute-done((bf16[768,512]{1,0:T(8,128)(2,1)}, bf16[768,512]{1,0:T(8,128)(2,1)}, u32[]{:S(2)}, u32[]{:S(2)}) %collective-permute-start.5) | collective-permute-done | bytes 786464 | tf_op jit(solution)/shard_map/ppermute | solution.py:217
  56.2 1.8 %slice.16 = bf16[384,512]{1,0:T(8,128)(2,1)} slice(bf16[768,512]{1,0:T(8,128)(2,1)} %collective-permute-done.5.refs_7_), slice={[0:384], [0:512]} | slice | bytes 786432 | tf_op jit(solution)/shard_map/slice | solution.py:221
  58.0 1.9 %collective-permute-start.6 = (bf16[384,512]{1,0:T(8,128)(2,1)}, bf16[384,512]{1,0:T(8,128)(2,1)S(1)}, u32[]{:S(2)}, u32[]{:S(2)}) collective-permute-start(bf16[384,512]{1,0:T(8,128)(2,1)} %slice.16), channel_id=1, source_target_pairs={{0,1},{1,2},{2,3},{3,0},{4,5},{5,6},{6,7},{7,4},{8,9},{9,10},{10,1... | collective-permute-start | bytes 1179656 | tf_op jit(solution)/shard_map/ppermute | solution.py:221
  59.9 0.0 collective-permute-done.4.refs_4_
  59.9 1.8 %slice.17 = bf16[384,512]{1,0:T(8,128)(2,1)} slice(bf16[768,512]{1,0:T(8,128)(2,1)} %collective-permute-done.4.refs_4_), slice={[384:768], [0:512]} | slice | bytes 786432 | tf_op jit(solution)/shard_map/slice | solution.py:221
  61.6 4.6 %collective-permute-start.7 = (bf16[384,512]{1,0:T(8,128)(2,1)}, bf16[384,512]{1,0:T(8,128)(2,1)}, u32[]{:S(2)}, u32[]{:S(2)}) collective-permute-start(bf16[384,512]{1,0:T(8,128)(2,1)} %slice.17), channel_id=1, source_target_pairs={{0,3},{1,0},{2,1},{3,2},{4,7},{5,4},{6,5},{7,6},{8,11},{9,8},{10,9... | collective-permute-start | bytes 1179656 | tf_op jit(solution)/shard_map/ppermute | solution.py:221
  66.2 6.8 %collective-permute-done.2.refs_1_ = bf16[256,1536]{1,0:T(8,128)(2,1)S(1)} collective-permute-done((bf16[256,1536]{1,0:T(8,128)(2,1)S(1)}, bf16[256,1536]{1,0:T(8,128)(2,1)S(1)}, u32[]{:S(2)}, u32[]{:S(2)}) %collective-permute-start.2) | collective-permute-done | bytes 786464 | tf_op jit(solution)/shard_map/ppermute | solution.py:221
  73.0 1.1 collective-permute-done.3.refs_2_
  74.1 9.9 %all-to-all-done = bf16[128,8,1024]{2,1,0:T(8,128)(2,1)} async-done(((bf16[128,8,1024]{2,1,0:T(8,128)(2,1)}), bf16[128,8,1024]{2,1,0:T(8,128)(2,1)}, u32[]{:S(2)}, u32[]{:S(2)}) %all-to-all-start) | async-done | bytes 2097184 | tf_op jit(solution)/shard_map/all_to_all | solution.py:280
  84.0 0.0 copy-done.4
  84.0 0.0 copy-done.5
  84.0 8.5 %hidden_rows.1 = (f32[256,768]{1,0:T(8,128)}, f32[256,768]{1,0:T(8,128)}, bf16[256,2048]{1,0:T(8,128)(2,1)}, bf16[768,512]{1,0:T(8,128)(2,1)}, bf16[768,512]{1,0...) custom-call(s32[1]{0:T(128)} %bitcast.2.me_ref, ...), custom_call_target="tpu_custom_call" | custom-call | tf_op jit(solution)/shard_map/hidden_rows/pallas_call | solution.py:283
  92.6 1.9 %collective-permute-start.8 = (bf16[384,512]{1,0:T(8,128)(2,1)}, bf16[384,512]{1,0:T(8,128)(2,1)S(1)}, u32[]{:S(2)}, u32[]{:S(2)}) collective-permute-start(bf16[384,512]{1,0:T(8,128)(2,1)} %get-tuple-element.26), channel_id=1, source_target_pairs={{0,1},{1,2},{2,3},{3,0},{4,5},{5,6},{6,7},{7,4},{8,9},{9,10},{10,1... | collective-permute-start | bytes 1179656 | tf_op jit(solution)/shard_map/ppermute | solution.py:236
  94.5 4.6 %collective-permute-start.9 = (bf16[384,512]{1,0:T(8,128)(2,1)}, bf16[384,512]{1,0:T(8,128)(2,1)S(1)}, u32[]{:S(2)}, u32[]{:S(2)}) collective-permute-start(bf16[384,512]{1,0:T(8,128)(2,1)} %get-tuple-element.27), channel_id=1, source_target_pairs={{0,3},{1,0},{2,1},{3,2},{4,7},{5,4},{6,5},{7,6},{8,11},{9,8},{10,9... | collective-permute-start | bytes 1179656 | tf_op jit(solution)/shard_map/ppermute | solution.py:236
  99.1 0.0 collective-permute-done.6.refs_5_
  99.1 0.0 collective-permute-done.7.refs_6_
  99.1 0.8 copy-done.7
  99.9 8.6 %back_rows.1 = bf16[1024,512]{1,0:T(8,128)(2,1)} custom-call(s32[1]{0:T(128)} %bitcast.2.me_ref, f32[256,768]{1,0:T(8,128)} %get-tuple-element.20.to_gate_ref, f32[256,768]{1,0:T(8,128)} %get-tuple-element.21.to_up_ref, bf16[256,2048]{1,0:T(8,128)(2,1)} %get-tuple-element.22.g_ref, bf16[768,512]{1,0:T(8,128)(2,1)} %bitcast.20, bf16[512,1536]{1,0:T(8,128)(2,1)} %bitcast.14, ...), custom_call_target="tpu_custom_call" | custom-call | tf_op jit(solution)/shard_map/back_rows/pallas_call | solution.py:304
  108.5 13.0 %all-to-all-start.1 = ((bf16[128,8,512]{2,1,0:T(8,128)(2,1)}), bf16[128,8,512]{2,1,0:T(8,128)(2,1)S(1)}, u32[]{:S(2)}, u32[]{:S(2)}) async-start(bf16[128,8,512]{2,1,0:T(8,128)(2,1)} %bitcast.15), calls=%async_computation.1 | async-start | bytes 2097152 | tf_op jit(solution)/shard_map/all_to_all | solution.py:322
  121.5 0.0 collective-permute-done.8.top
  121.6 0.0 collective-permute-done.9.bottom
  121.6 0.8 copy-done.8
  122.4 0.1 copy-done.9
  122.5 2.9 %add_far.1 = (bf16[768,512]{1,0:T(8,128)(2,1)}, bf16[768,512]{1,0:T(8,128)(2,1)}) custom-call(bf16[768,512]{1,0:T(8,128)(2,1)} %get-tuple-element.24.right, bf16[768,512]{1,0:T(8,128)(2,1)} %get-tuple-element.25.left, bf16[384,512]{1,0:T(8,128)(2,1)} %copy-done.8, bf16[384,512]{1,0:T(8,128)(2,1)} %copy-done.9), custom_call_target="tpu_custom_call" | custom-call | flops 20000000000 | tf_op jit(solution)/shard_map/add_far/pallas_call | solution.py:237
  125.4 1.9 %collective-permute-start.10 = (bf16[768,512]{1,0:T(8,128)(2,1)}, bf16[768,512]{1,0:T(8,128)(2,1)S(1)}, u32[]{:S(2)}, u32[]{:S(2)}) collective-permute-start(bf16[768,512]{1,0:T(8,128)(2,1)} %get-tuple-element.28), channel_id=1, source_target_pairs={{0,1},{1,2},{2,3},{3,0},{4,5},{5,6},{6,7},{7,4},{8,9},{9,10},{10,1... | collective-permute-start | bytes 2359304 | tf_op jit(solution)/shard_map/ppermute | solution.py:246
  127.3 4.6 %collective-permute-start.11 = (bf16[768,512]{1,0:T(8,128)(2,1)}, bf16[768,512]{1,0:T(8,128)(2,1)S(1)}, u32[]{:S(2)}, u32[]{:S(2)}) collective-permute-start(bf16[768,512]{1,0:T(8,128)(2,1)} %get-tuple-element.29), channel_id=1, source_target_pairs={{0,3},{1,0},{2,1},{3,2},{4,7},{5,4},{6,5},{7,6},{8,11},{9,8},{10,9... | collective-permute-start | bytes 2359304 | tf_op jit(solution)/shard_map/ppermute | solution.py:246
  131.9 15.0 %collective-permute-done.10 = bf16[768,512]{1,0:T(8,128)(2,1)S(1)} collective-permute-done((bf16[768,512]{1,0:T(8,128)(2,1)}, bf16[768,512]{1,0:T(8,128)(2,1)S(1)}, u32[]{:S(2)}, u32[]{:S(2)}) %collective-permute-start.10) | collective-permute-done | bytes 786464 | tf_op jit(solution)/shard_map/ppermute | solution.py:246
  146.9 1.0 collective-permute-done.11
  147.9 1.2 fusion
  149.1 3.4 %all-to-all-done.1 = bf16[128,8,512]{2,1,0:T(8,128)(2,1)S(1)} async-done(((bf16[128,8,512]{2,1,0:T(8,128)(2,1)}), bf16[128,8,512]{2,1,0:T(8,128)(2,1)S(1)}, u32[]{:S(2)}, u32[]{:S(2)}) %all-to-all-start.1) | async-done | bytes 1048608 | tf_op jit(solution)/shard_map/all_to_all | solution.py:322
  152.5 1.0 copy-done.3
  153.5 2.3 %combine_rows.1 = bf16[24,2048]{1,0:T(8,128)(2,1)} custom-call(bf16[1024,96]{1,0:T(8,128)(2,1)} %get-tuple-element.16.pick_ref, bf16[1024,512]{1,0:T(8,128)(2,1)} %bitcast.16), custom_call_target="tpu_custom_call" | custom-call | tf_op jit(solution)/shard_map/combine_rows/pallas_call | solution.py:323
  (11 shorter events, 0.0 us)
Async XLA Ops:
  0.6 39.0 %collective-permute-start = (bf16[512,1536]{1,0:T(8,128)(2,1)}, bf16[512,1536]{1,0:T(8,128)(2,1)S(1)}, u32[]{:S(2)}, u32[]{:S(2)}) collective-permute-start(bf16[512,1536]{1,0:T(8,128)(2,1)} %bitcast.11), channel_id=1, source_target_pairs={{0,1},{1,2},{2,3},{3,0},{4,5},{5,6},{6,7},{7,4},{8,9},{9,10},{10,1... | collective-permute-start | bytes 4718600 | tf_op jit(solution)/shard_map/ppermute | solution.py:216
  4.6 35.1 %collective-permute-start.1 = (bf16[512,1536]{1,0:T(8,128)(2,1)}, bf16[512,1536]{1,0:T(8,128)(2,1)S(1)}, u32[]{:S(2)}, u32[]{:S(2)}) collective-permute-start(bf16[512,1536]{1,0:T(8,128)(2,1)} %bitcast.12), channel_id=1, source_target_pairs={{0,3},{1,0},{2,1},{3,2},{4,7},{5,4},{6,5},{7,6},{8,11},{9,8},{10,9... | collective-permute-start | bytes 4718600 | tf_op jit(solution)/shard_map/ppermute | solution.py:216
  14.3 69.7 %all-to-all-start = ((bf16[128,8,1024]{2,1,0:T(8,128)(2,1)}), bf16[128,8,1024]{2,1,0:T(8,128)(2,1)}, u32[]{:S(2)}, u32[]{:S(2)}) async-start(bf16[128,8,1024]{2,1,0:T(8,128)(2,1)} %bitcast.17), calls=%async_computation | async-start | bytes 4194304 | tf_op jit(solution)/shard_map/all_to_all | solution.py:280
  33.1 23.1 %collective-permute-start.5 = (bf16[768,512]{1,0:T(8,128)(2,1)}, bf16[768,512]{1,0:T(8,128)(2,1)}, u32[]{:S(2)}, u32[]{:S(2)}) collective-permute-start(bf16[768,512]{1,0:T(8,128)(2,1)} %bitcast.18), channel_id=1, source_target_pairs={{0,1},{1,2},{2,3},{3,0},{4,5},{5,6},{6,7},{7,4},{8,9},{9,10},{10,1... | collective-permute-start | bytes 2359304 | tf_op jit(solution)/shard_map/ppermute | solution.py:217
  35.1 24.8 %collective-permute-start.4 = (bf16[768,512]{1,0:T(8,128)(2,1)}, bf16[768,512]{1,0:T(8,128)(2,1)}, u32[]{:S(2)}, u32[]{:S(2)}) collective-permute-start(bf16[768,512]{1,0:T(8,128)(2,1)} %bitcast.19), channel_id=1, source_target_pairs={{0,3},{1,0},{2,1},{3,2},{4,7},{5,4},{6,5},{7,6},{8,11},{9,8},{10,9... | collective-permute-start | bytes 2359304 | tf_op jit(solution)/shard_map/ppermute | solution.py:217
  39.7 1.2 copy-start
  40.8 1.2 copy-start.1
  42.0 5.4 %copy-start.2 = (bf16[512,1536]{1,0:T(8,128)(2,1)S(1)}, bf16[512,1536]{1,0:T(8,128)(2,1)}, u32[]{:S(2)}) copy-start(bf16[512,1536]{1,0:T(8,128)(2,1)} %get-tuple-element.18.refs_0_) | copy-start | bytes 4718596
  43.3 29.7 %collective-permute-start.2 = (bf16[256,1536]{1,0:T(8,128)(2,1)S(1)}, bf16[256,1536]{1,0:T(8,128)(2,1)S(1)}, u32[]{:S(2)}, u32[]{:S(2)}) collective-permute-start(bf16[256,1536]{1,0:T(8,128)(2,1)S(1)} %slice.12), channel_id=1, source_target_pairs={{0,1},{1,2},{2,3},{3,0},{4,5},{5,6},{6,7},{7,4},{8,9},{9,10},{10,1... | collective-permute-start | bytes 2359304 | tf_op jit(solution)/shard_map/ppermute | solution.py:221
  47.4 26.7 %collective-permute-start.3 = (bf16[256,1536]{1,0:T(8,128)(2,1)S(1)}, bf16[256,1536]{1,0:T(8,128)(2,1)S(1)}, u32[]{:S(2)}, u32[]{:S(2)}) collective-permute-start(bf16[256,1536]{1,0:T(8,128)(2,1)S(1)} %slice.13), channel_id=1, source_target_pairs={{0,3},{1,0},{2,1},{3,2},{4,7},{5,4},{6,5},{7,6},{8,11},{9,8},{10,9... | collective-permute-start | bytes 2359304 | tf_op jit(solution)/shard_map/ppermute | solution.py:221
  58.0 41.1 %collective-permute-start.6 = (bf16[384,512]{1,0:T(8,128)(2,1)}, bf16[384,512]{1,0:T(8,128)(2,1)S(1)}, u32[]{:S(2)}, u32[]{:S(2)}) collective-permute-start(bf16[384,512]{1,0:T(8,128)(2,1)} %slice.16), channel_id=1, source_target_pairs={{0,1},{1,2},{2,3},{3,0},{4,5},{5,6},{6,7},{7,4},{8,9},{9,10},{10,1... | collective-permute-start | bytes 1179656 | tf_op jit(solution)/shard_map/ppermute | solution.py:221
  61.6 37.5 %collective-permute-start.7 = (bf16[384,512]{1,0:T(8,128)(2,1)}, bf16[384,512]{1,0:T(8,128)(2,1)}, u32[]{:S(2)}, u32[]{:S(2)}) collective-permute-start(bf16[384,512]{1,0:T(8,128)(2,1)} %slice.17), channel_id=1, source_target_pairs={{0,3},{1,0},{2,1},{3,2},{4,7},{5,4},{6,5},{7,6},{8,11},{9,8},{10,9... | collective-permute-start | bytes 1179656 | tf_op jit(solution)/shard_map/ppermute | solution.py:221
  73.0 11.0 %copy-start.4 = (bf16[256,1536]{1,0:T(8,128)(2,1)}, bf16[256,1536]{1,0:T(8,128)(2,1)S(1)}, u32[]{:S(2)}) copy-start(bf16[256,1536]{1,0:T(8,128)(2,1)S(1)} %collective-permute-done.2.refs_1_) | copy-start | bytes 2359300
  74.1 9.9 %copy-start.5 = (bf16[256,1536]{1,0:T(8,128)(2,1)}, bf16[256,1536]{1,0:T(8,128)(2,1)S(1)}, u32[]{:S(2)}) copy-start(bf16[256,1536]{1,0:T(8,128)(2,1)S(1)} %collective-permute-done.3.refs_2_) | copy-start | bytes 2359300
  92.6 29.0 %collective-permute-start.8 = (bf16[384,512]{1,0:T(8,128)(2,1)}, bf16[384,512]{1,0:T(8,128)(2,1)S(1)}, u32[]{:S(2)}, u32[]{:S(2)}) collective-permute-start(bf16[384,512]{1,0:T(8,128)(2,1)} %get-tuple-element.26), channel_id=1, source_target_pairs={{0,1},{1,2},{2,3},{3,0},{4,5},{5,6},{6,7},{7,4},{8,9},{9,10},{10,1... | collective-permute-start | bytes 1179656 | tf_op jit(solution)/shard_map/ppermute | solution.py:236
  94.5 27.1 %collective-permute-start.9 = (bf16[384,512]{1,0:T(8,128)(2,1)}, bf16[384,512]{1,0:T(8,128)(2,1)S(1)}, u32[]{:S(2)}, u32[]{:S(2)}) collective-permute-start(bf16[384,512]{1,0:T(8,128)(2,1)} %get-tuple-element.27), channel_id=1, source_target_pairs={{0,3},{1,0},{2,1},{3,2},{4,7},{5,4},{6,5},{7,6},{8,11},{9,8},{10,9... | collective-permute-start | bytes 1179656 | tf_op jit(solution)/shard_map/ppermute | solution.py:236
  99.1 0.8 copy-start.7
  108.5 43.9 %all-to-all-start.1 = ((bf16[128,8,512]{2,1,0:T(8,128)(2,1)}), bf16[128,8,512]{2,1,0:T(8,128)(2,1)S(1)}, u32[]{:S(2)}, u32[]{:S(2)}) async-start(bf16[128,8,512]{2,1,0:T(8,128)(2,1)} %bitcast.15), calls=%async_computation.1 | async-start | bytes 2097152 | tf_op jit(solution)/shard_map/all_to_all | solution.py:322
  121.6 0.8 copy-start.8
  121.6 0.9 copy-start.9
  122.5 25.4 %copy-start.6 = (bf16[768,512]{1,0:T(8,128)(2,1)S(1)}, bf16[768,512]{1,0:T(8,128)(2,1)}, u32[]{:S(2)}) copy-start(bf16[768,512]{1,0:T(8,128)(2,1)} %get-tuple-element.23) | copy-start | bytes 2359300
  125.4 21.5 %collective-permute-start.10 = (bf16[768,512]{1,0:T(8,128)(2,1)}, bf16[768,512]{1,0:T(8,128)(2,1)S(1)}, u32[]{:S(2)}, u32[]{:S(2)}) collective-permute-start(bf16[768,512]{1,0:T(8,128)(2,1)} %get-tuple-element.28), channel_id=1, source_target_pairs={{0,1},{1,2},{2,3},{3,0},{4,5},{5,6},{6,7},{7,4},{8,9},{9,10},{10,1... | collective-permute-start | bytes 2359304 | tf_op jit(solution)/shard_map/ppermute | solution.py:246
  127.3 20.5 %collective-permute-start.11 = (bf16[768,512]{1,0:T(8,128)(2,1)}, bf16[768,512]{1,0:T(8,128)(2,1)S(1)}, u32[]{:S(2)}, u32[]{:S(2)}) collective-permute-start(bf16[768,512]{1,0:T(8,128)(2,1)} %get-tuple-element.29), channel_id=1, source_target_pairs={{0,3},{1,0},{2,1},{3,2},{4,7},{5,4},{6,5},{7,6},{8,11},{9,8},{10,9... | collective-permute-start | bytes 2359304 | tf_op jit(solution)/shard_map/ppermute | solution.py:246
  152.5 1.0 copy-start.3

commit v5 on v4

--- a/solution.py
+++ b/solution.py
@@ -11,7 +11,8 @@
 F32, BF16 = jnp.float32, jnp.bfloat16
 NT = (((1,), (1,)), ((), ()))
 TN = (((0,), (0,)), ((), ()))
-VMEM_LIMIT = 56 * 1024 * 1024
+VMEM_LIMIT = 16 * 1024 * 1024
+SEND_LIMIT = 56 * 1024 * 1024
 COST = 20 * 10**9
 
 
@@ -78,113 +79,87 @@
     return ((out % per) * quarters + out // per == src).astype(BF16)
 
 
-def start_all(copies, sems, first=0):
-    out = []
-    for n, (src, dst) in enumerate(copies):
-        copy = pltpu.make_async_copy(src, dst, sems.at[first + n])
-        copy.start()
-        out.append(copy)
-    return out
-
-
-def pieces(own, others, axis):
-    right, far_a, far_b, left = others
-    rows = own.shape[0]
-    step = rows if axis == 0 else 0
-    half = rows // 2
-    return [
-        (own, 0, rows, 0),
-        (right, step, rows, 1),
-        (far_a, 2 * step, half, 2),
-        (far_b, 2 * step + half, half, 2),
-        (left, 3 * step, rows, 3),
-    ]
-
-
-def hidden_kernel(quarters, me_ref, recv_ref, own, *refs):
-    others, refs = refs[:4], refs[4:]
-    to_gate_ref, to_up_ref, g_ref, down_own, down_right, far_top, far_bottom, down_left, recv, w, x_ref, sems = refs
+def hidden_kernel(quarters, me_ref, recv, own_ref, right, far_a, far_b, left, *refs):
+    to_gate_ref, to_up_ref, g_ref, *downs, x_ref, own, sem = refs[2:]
+    fetch = pltpu.make_async_copy(own_ref, own, sem)
+    fetch.start()
     rows = 256
     per = rows // quarters
-    feat = recv_ref.shape[1] // 2
+    feat = recv.shape[1] // 2
     hidden_units = to_gate_ref.shape[1]
     tile = 256
-    (got_rows,) = start_all([(recv_ref, recv)], sems)
-    waits = []
-    for n in range(hidden_units // tile):
-        copies = []
-        for at in (n * tile, hidden_units + n * tile):
-            cols = pl.ds(at, tile)
-            for src, row, size, _ in pieces(own, others, 0):
-                copies.append((src.at[:, cols], w.at[pl.ds(row, size), cols]))
-        waits.append(start_all(copies, sems, 1 + n * len(copies)))
-    got_rows.wait()
     order = order_matrix(rows, quarters)
-    for b in range(recv_ref.shape[0] // rows):
+    for b in range(recv.shape[0] // rows):
         got = jnp.dot(order, recv[b * rows : b * rows + rows, :], preferred_element_type=F32).astype(BF16)
         here = slice(b * per, b * per + per)
         for q in range(quarters):
             at = pl.multiple_of(lax.rem(q + quarters - me_ref[0], quarters) * feat, feat)
             x_ref[here, pl.ds(at, feat)] = got[q * per : q * per + per, :feat]
             g_ref[here, pl.ds(at, feat)] = got[q * per : q * per + per, feat:]
-    half = hidden_units // 2
+
+    fetch.wait()
+
+    def pre(cols):
+        total, row = None, 0
+        for w in (own, right, far_a, far_b, left):
+            term = jnp.dot(x_ref[:, row : row + w.shape[0]], w[:, cols], preferred_element_type=F32)
+            total, row = term if total is None else total + term, row + w.shape[0]
+        return total
+
     for n in range(hidden_units // tile):
-        for copy in waits[n]:
-            copy.wait()
         cols = slice(n * tile, n * tile + tile)
-        gate = jnp.dot(x_ref[...], w[:, cols], preferred_element_type=F32)
-        up = jnp.dot(x_ref[...], w[:, hidden_units + n * tile : hidden_units + n * tile + tile], preferred_element_type=F32)
+        gate = pre(cols)
+        up = pre(slice(hidden_units + n * tile, hidden_units + n * tile + tile))
         sig = jax.nn.sigmoid(gate)
         activ = gate * sig
         to_gate_ref[:, cols] = up * sig * (1.0 + gate * (1.0 - sig))
         to_up_ref[:, cols] = activ
         hidden = (activ * up).astype(BF16)
-        part = lax.dot_general(hidden, g_ref[...], TN, preferred_element_type=F32).astype(BF16)
-        for k, ref in ((0, down_own), (1, down_right), (3, down_left)):
-            ref[cols, :] = part[:, k * feat : k * feat + feat]
-        lo, hi = n * tile, n * tile + tile
-        mid = min(max(half, lo), hi)
-        if lo < mid:
-            far_top[lo:mid, :] = part[: mid - lo, 2 * feat : 3 * feat]
-        if mid < hi:
-            far_bottom[mid - half : hi - half, :] = part[mid - lo :, 2 * feat : 3 * feat]
-
-
-def back_kernel(quarters, me_ref, to_gate_ref, to_up_ref, g_ref, own_down, own, *refs):
-    others, other_downs, refs = refs[:4], refs[4:8], refs[8:]
-    back_ref, to_gate, to_up, g, wd, w, gp_ref, hold, sems = refs
-    slots, hidden_units = to_gate.shape
-    feat = own.shape[0]
-    copies = [(g_ref, g)]
-    for src, row, size, k in pieces(own_down, other_downs, 1):
-        copies.append((src, wd.at[pl.ds(row, size), pl.ds(k * feat, feat)]))
-    copies += [(to_gate_ref, to_gate), (to_up_ref, to_up)]
-    early = start_all(copies, sems)
-    late = start_all(
-        [(src, w.at[pl.ds(row, size), :]) for src, row, size, _ in pieces(own, others, 0)], sems, len(copies)
-    )
-    for copy in early:
-        copy.wait()
-    tile = 256
-    for n in range(hidden_units // tile):
-        cols = slice(n * tile, n * tile + tile)
-        total = lax.dot_general(g[...], wd[cols, :], NT, preferred_element_type=F32)
+        for k, ref in enumerate(downs):
+            ref[cols, :] = lax.dot_general(
+                hidden, g_ref[:, k * feat : k * feat + feat], TN, preferred_element_type=F32
+            ).astype(BF16)
+
+
+def back_kernel(quarters, me_ref, to_gate, to_up, g, *refs):
+    (own_up_ref, *ups), (own_ref, right, far_a, far_b, left), refs = refs[:5], refs[5:10], refs[10:]
+    back_ref, gp_ref, hold, own_up, own, out, sems = refs
+    fetch_down = pltpu.make_async_copy(own_ref, own, sems.at[0])
+    fetch_down.start()
+    fetch_up = pltpu.make_async_copy(own_up_ref, own_up, sems.at[1])
+    fetch_up.start()
+    hidden_units = to_gate.shape[1]
+    feat = g.shape[1] // quarters
+    half = hidden_units // 2
+    fetch_down.wait()
+    for h, far in enumerate((far_a, far_b)):
+        cols = slice(h * half, h * half + half)
+        total = None
+        for k, w in enumerate((own[cols, :], right[cols, :], far[...], left[cols, :])):
+            term = lax.dot_general(g[:, k * feat : k * feat + feat], w, NT, preferred_element_type=F32)
+            total = term if total is None else total + term
         gp_ref[:, cols] = (total * to_gate[:, cols]).astype(BF16)
-        gp_ref[:, hidden_units + n * tile : hidden_units + n * tile + tile] = (total * to_up[:, cols]).astype(BF16)
-    for k in range(quarters):
-        for copy in (late[:1], late[1:2], late[2:4], late[4:])[k]:
-            copy.wait()
-        hold[lax.rem(me_ref[0] + k, quarters)] = lax.dot_general(
-            gp_ref[...], w[k * feat : k * feat + feat, :], NT, preferred_element_type=F32
+        gp_ref[:, hidden_units + h * half : hidden_units + h * half + half] = (total * to_up[:, cols]).astype(BF16)
+    fetch_up.wait()
+    at = 0
+    for w in (own_up, *ups):
+        rows = w.shape[0]
+        hold[lax.rem(me_ref[0] + at // feat, quarters), :, at % feat : at % feat + rows] = lax.dot_general(
+            gp_ref[...], w[...], NT, preferred_element_type=F32
         ).astype(BF16)
+        at += rows
     rows = 256
     per = rows // quarters
     order = order_matrix(rows, quarters)
+    copies = []
     for b in range(back_ref.shape[0] // rows):
+        here = pl.ds(b * rows, rows)
         stacked = jnp.concatenate([hold[q, b * per : b * per + per, :] for q in range(quarters)], axis=0)
-        back_ref[b * rows : b * rows + rows, :] = lax.dot_general(
-            order, stacked, TN, preferred_element_type=F32
-        ).astype(BF16)
+        out[here, :] = lax.dot_general(order, stacked, TN, preferred_element_type=F32).astype(BF16)
+        copies.append(pltpu.make_async_copy(out.at[here, :], back_ref.at[here, :], sems.at[2 + b]))
+        copies[-1].start()
+    for copy in copies:
+        copy.wait()
 
 
 def combine_kernel(toks, pick_ref, ret_ref, out_ref):
@@ -222,28 +197,23 @@
     return out
 
 
-def add_kernel(right, left, top, bottom, right_out, left_out):
-    half = top.shape[0]
-    right_out[:half, :] = (right[:half, :].astype(F32) + top[...].astype(F32)).astype(BF16)
-    right_out[half:, :] = right[half:, :]
-    left_out[:half, :] = left[:half, :]
-    left_out[half:, :] = (left[half:, :].astype(F32) + bottom[...].astype(F32)).astype(BF16)
+def add_kernel(block, came, out):
+    out[...] = (block[...].astype(F32) + came[...].astype(F32)).astype(BF16)
 
 
 def scatter_two_steps(blocks, size):
-    fwd, bwd = ring(size, 1), ring(size, -1)
-    own, right, far_top, far_bottom, left = blocks
-    top, bottom = lax.ppermute(far_top, "edp", fwd), lax.ppermute(far_bottom, "edp", bwd)
-    right, left = pl.pallas_call(
+    own, right, far, left = blocks
+    came = lax.ppermute(far, "edp", ring(size, 1))
+    right = pl.pallas_call(
         add_kernel,
-        in_specs=[whole()] * 4,
-        out_specs=[whole()] * 2,
-        out_shape=[jax.ShapeDtypeStruct(right.shape, BF16)] * 2,
+        in_specs=[whole()] * 2,
+        out_specs=whole(),
+        out_shape=jax.ShapeDtypeStruct(right.shape, BF16),
         compiler_params=pltpu.CompilerParams(vmem_limit_bytes=VMEM_LIMIT),
         cost_estimate=pl.CostEstimate(flops=COST, bytes_accessed=0, transcendentals=0),
         name="add_far",
-    )(right, left, top, bottom)
-    from_left, from_right = lax.ppermute(right, "edp", fwd), lax.ppermute(left, "edp", bwd)
+    )(right, came)
+    from_left, from_right = lax.ppermute(right, "edp", ring(size, 1)), lax.ppermute(left, "edp", ring(size, -1))
     return (own.astype(F32) + from_left.astype(F32) + from_right.astype(F32)).astype(BF16)
 
 
@@ -260,7 +230,7 @@
 
     others = gather_two_steps(gate_up_weight[0], down_weight[0], parts)
 
-    tile = 128
+    tile = 512
     sent, pick = pl.pallas_call(
         functools.partial(send_kernel, quarters),
         grid=(rows // tile,),
@@ -274,51 +244,52 @@
             jax.ShapeDtypeStruct((rows, quarters * toks), BF16),
         ],
         scratch_shapes=[pltpu.VMEM((quarters * toks, 3 * feat), F32)],
-        compiler_params=params,
+        compiler_params=pltpu.CompilerParams(vmem_limit_bytes=SEND_LIMIT),
         name="send_rows",
     )(expert_ids.T, gate_values.T, tokens, out_grad)
     recv = lax.all_to_all(sent, "ep", split_axis=0, concat_axis=0, tiled=True)
 
-    half = hidden_units // 2
     to_gate, to_up, rows_g, *blocks = pl.pallas_call(
         functools.partial(hidden_kernel, quarters),
-        in_specs=[whole(pltpu.SMEM)] + [whole(pl.ANY)] * 6,
-        out_specs=[whole()] * 8,
+        in_specs=[whole(pltpu.SMEM), whole(), whole(pltpu.HBM)] + [whole()] * 6,
+        out_specs=[whole()] * 7,
         out_shape=[
             jax.ShapeDtypeStruct((slots, hidden_units), F32),
             jax.ShapeDtypeStruct((slots, hidden_units), F32),
             jax.ShapeDtypeStruct((slots, width), BF16),
         ]
-        + [jax.ShapeDtypeStruct((size, feat), BF16) for size in (hidden_units, hidden_units, half, half, hidden_units)],
+        + [jax.ShapeDtypeStruct((hidden_units, feat), BF16)] * parts,
         scratch_shapes=[
-            pltpu.VMEM((rows, 2 * feat), BF16),
-            pltpu.VMEM((width, 2 * hidden_units), BF16),
             pltpu.VMEM((slots, width), BF16),
-            pltpu.SemaphoreType.DMA((64,)),
+            pltpu.VMEM((feat, 2 * hidden_units), BF16),
+            pltpu.SemaphoreType.DMA,
         ],
         compiler_params=params,
         name="hidden_rows",
-    )(me, recv, gate_up_weight[0], *others[:4])
+    )(me, recv, gate_up_weight[0], *others[:4], *others[5:7])
     down_grad = scatter_two_steps(blocks, parts)[None]
 
     back = pl.pallas_call(
         functools.partial(back_kernel, quarters),
-        in_specs=[whole(pltpu.SMEM)] + [whole(pl.ANY)] * 13,
-        out_specs=whole(),
+        in_specs=[whole(pltpu.SMEM)]
+        + [whole()] * 3
+        + [whole(pltpu.HBM)]
+        + [whole()] * 4
+        + [whole(pltpu.HBM)]
+        + [whole()] * 4,
+        out_specs=whole(pltpu.HBM),
         out_shape=jax.ShapeDtypeStruct((rows, feat), BF16),
         scratch_shapes=[
-            pltpu.VMEM((slots, hidden_units), F32),
-            pltpu.VMEM((slots, hidden_units), F32),
-            pltpu.VMEM((slots, width), BF16),
-            pltpu.VMEM((hidden_units, width), BF16),
-            pltpu.VMEM((width, 2 * hidden_units), BF16),
             pltpu.VMEM((slots, 2 * hidden_units), BF16),
             pltpu.VMEM((quarters, slots, feat), BF16),
-            pltpu.SemaphoreType.DMA((32,)),
+            pltpu.VMEM((feat, 2 * hidden_units), BF16),
+            pltpu.VMEM((hidden_units, feat), BF16),
+            pltpu.VMEM((rows, feat), BF16),
+            pltpu.SemaphoreType.DMA((8,)),
         ],
         compiler_params=params,
         name="back_rows",
-    )(me, to_gate, to_up, rows_g, down_weight[0], gate_up_weight[0], *others)
+    )(me, to_gate, to_up, rows_g, gate_up_weight[0], *others[:4], down_weight[0], *others[4:])
     returned = lax.all_to_all(back, "ep", split_axis=0, concat_axis=0, tiled=True)
     token_grads = pl.pallas_call(
         functools.partial(combine_kernel, toks),

time: 157 us -> 157 us (level)
  Pallas kernels: 28.9 us -> 21.4 us
  starting transfers between devices: 71.4 us -> 76.6 us
  waiting for transfers between devices: 43.5 us -> 48.3 us
  local copies, waits for them, and re-layouts: 9.93 us -> 7.67 us
    ppermute x2, waiting for transfers between devices: 1.08 us -> 14.5 us  [gather_two_steps(): lax.ppermute(right[half:], 'edp', bwd)]
    all_to_all x1, waiting for transfers between devices: 9.93 us -> 0.01 us  [per_device(): recv = lax.all_to_all(sent, 'ep', split_axis=0, concat_axis=0, tiled=True)]
    all_to_all x1, starting transfers between devices: 13 us -> 21.8 us  [per_device(): lax.all_to_all(back, 'ep', split_axis=0, concat_axis=0, tiled=True)]
    ppermute x1, waiting for transfers between devices: 6.29 us -> 0.01 us  [gather_two_steps(): lax.ppermute(down, 'edp', fwd)]
    ppermute x4 -> x3, starting transfers between devices: 13 us -> 8.7 us  [the longest x1 4.85 us: scatter_two_steps(): lax.ppermute(left, 'edp', ring(size, -1))]
    ppermute x1, waiting for transfers between devices: 0.01 us -> 4.03 us  [gather_two_steps(): lax.ppermute(up, 'edp', fwd)]
    ppermute x1, waiting for transfers between devices: 0.01 us -> 3.39 us  [gather_two_steps(): lax.ppermute(down, 'edp', bwd)]
    ppermute x4 -> x3, waiting for transfers between devices: 16 us -> 19.1 us  [the longest x1 12.8 us: scatter_two_steps(): lax.ppermute(left, 'edp', ring(size, -1))]
  transfers between devices with their start and end apart: 14 -> 13, of which waited for: 7 -> 7; matrix products, arithmetic and copies ran while one was open for 4% -> 3% of each run, Pallas kernels for 17% -> 8%
where the time goes in v5:
time: 157 us; the launch traced here: 156 us
  starting transfers between devices  76.6 us (49%)
  waiting for transfers between devices  48.3 us (31%)
  Pallas kernels  21.4 us (14%)
  local copies, waits for them, and re-layouts  7.67 us (5%)
    all_to_all x1, starting transfers between devices, per_device(): lax.all_to_all(back, 'ep', split_axis=0, concat_axis=0, tiled=True)  21.8 us
    all_to_all x1, starting transfers between devices, per_device(): recv = lax.all_to_all(sent, 'ep', split_axis=0, concat_axis=0, tiled=True)  18.3 us
    ppermute x2, waiting for transfers between devices, gather_two_steps(): lax.ppermute(right[half:], 'edp', bwd)  14.5 us
    ppermute x1, waiting for transfers between devices, scatter_two_steps(): lax.ppermute(left, 'edp', ring(size, -1))  12.8 us
    ppermute x2, starting transfers between devices, gather_two_steps(): lax.ppermute(right[half:], 'edp', bwd)  9.88 us
    pallas_call x1, Pallas kernels, per_device(): pl.pallas_call(functools.partial(hidden_kernel, quarters), in_specs=[whol...  7.39 us
    ppermute x1, waiting for transfers between devices, scatter_two_steps(): lax.ppermute(right, 'edp', ring(size, 1))  6.24 us
    pallas_call x1, Pallas kernels, per_device(): pl.pallas_call(functools.partial(back_kernel, quarters), in_specs=[whole(...  5.77 us
  transfers between devices with their start and end apart: 13, of which 7 were waited for; matrix products, arithmetic and copies ran while one was open for 3% of the time, Pallas kernels for 8%

profile of v5, /device:TPU:1, one launch (start us, length us, event | category | flops | bytes accessed | tf_op | source)
XLA Modules:
  0.0 156.1 jit_solution(1483949857194540396)
XLA Ops:
  0.6 5.2 %collective-permute-start.1 = (bf16[512,1536]{1,0:T(8,128)(2,1)}, bf16[512,1536]{1,0:T(8,128)(2,1)S(1)}, u32[]{:S(2)}, u32[]{:S(2)}) collective-permute-start(bf16[512,1536]{1,0:T(8,128)(2,1)} %bitcast.11), channel_id=1, source_target_pairs={{0,3},{1,0},{2,1},{3,2},{4,7},{5,4},{6,5},{7,6},{8,11},{9,8},{10,9... | collective-permute-start | bytes 4718600 | tf_op jit(solution)/shard_map/ppermute | solution.py:191
  5.9 1.9 %collective-permute-start = (bf16[512,1536]{1,0:T(8,128)(2,1)}, bf16[512,1536]{1,0:T(8,128)(2,1)S(1)}, u32[]{:S(2)}, u32[]{:S(2)}) collective-permute-start(bf16[512,1536]{1,0:T(8,128)(2,1)} %bitcast.12), channel_id=1, source_target_pairs={{0,1},{1,2},{2,3},{3,0},{4,5},{5,6},{6,7},{7,4},{8,9},{9,10},{10,1... | collective-permute-start | bytes 4718600 | tf_op jit(solution)/shard_map/ppermute | solution.py:191
  7.8 4.6 %send_rows.1 = (bf16[1024,1024]{1,0:T(8,128)(2,1)}, bf16[1024,96]{1,0:T(8,128)(2,1)}) custom-call(s32[8,24]{1,0:T(8,128)} %bitcast.20, f32[8,24]{1,0:T(8,128)} %bitcast.21, bf16[24,2048]{1,0:T(8,128)(2,1)} %tok_ref.1, bf16[24,2048]{1,0:T(8,128)(2,1)} %grad_ref.1), custom_call_target="tpu_custom_call" | custom-call | tf_op jit(solution)/shard_map/send_rows/pallas_call | solution.py:234
  12.4 18.3 %all-to-all-start = ((bf16[128,8,1024]{2,1,0:T(8,128)(2,1)}), bf16[128,8,1024]{2,1,0:T(8,128)(2,1)}, u32[]{:S(2)}, u32[]{:S(2)}) async-start(bf16[128,8,1024]{2,1,0:T(8,128)(2,1)} %bitcast.19), calls=%async_computation | async-start | bytes 4194304 | tf_op jit(solution)/shard_map/all_to_all | solution.py:250
  30.8 4.9 %collective-permute-start.6 = (bf16[768,512]{1,0:T(8,128)(2,1)}, bf16[768,512]{1,0:T(8,128)(2,1)S(1)}, u32[]{:S(2)}, u32[]{:S(2)}) collective-permute-start(bf16[768,512]{1,0:T(8,128)(2,1)} %bitcast.16), channel_id=1, source_target_pairs={{0,3},{1,0},{2,1},{3,2},{4,7},{5,4},{6,5},{7,6},{8,11},{9,8},{10,9... | collective-permute-start | bytes 2359304 | tf_op jit(solution)/shard_map/ppermute | solution.py:192
  35.6 1.9 %collective-permute-start.4 = (bf16[768,512]{1,0:T(8,128)(2,1)}, bf16[768,512]{1,0:T(8,128)(2,1)S(1)}, u32[]{:S(2)}, u32[]{:S(2)}) collective-permute-start(bf16[768,512]{1,0:T(8,128)(2,1)} %bitcast.17), channel_id=1, source_target_pairs={{0,1},{1,2},{2,3},{3,0},{4,5},{5,6},{6,7},{7,4},{8,9},{9,10},{10,1... | collective-permute-start | bytes 2359304 | tf_op jit(solution)/shard_map/ppermute | solution.py:192
  37.5 0.0 collective-permute-done.1.refs_1_
  37.6 4.0 %collective-permute-done.refs_0_ = bf16[512,1536]{1,0:T(8,128)(2,1)S(1)} collective-permute-done((bf16[512,1536]{1,0:T(8,128)(2,1)}, bf16[512,1536]{1,0:T(8,128)(2,1)S(1)}, u32[]{:S(2)}, u32[]{:S(2)}) %collective-permute-start) | collective-permute-done | bytes 1572896 | tf_op jit(solution)/shard_map/ppermute | solution.py:191
  41.6 1.0 slice.13
  42.6 0.9 slice.12
  43.5 1.9 %collective-permute-start.2 = (bf16[256,1536]{1,0:T(8,128)(2,1)}, bf16[256,1536]{1,0:T(8,128)(2,1)}, u32[]{:S(2)}, u32[]{:S(2)}) collective-permute-start(bf16[256,1536]{1,0:T(8,128)(2,1)} %slice.12), channel_id=1, source_target_pairs={{0,1},{1,2},{2,3},{3,0},{4,5},{5,6},{6,7},{7,4},{8,9},{9,10},{10,1... | collective-permute-start | bytes 2359304 | tf_op jit(solution)/shard_map/ppermute | solution.py:196
  45.4 4.6 %collective-permute-start.3 = (bf16[256,1536]{1,0:T(8,128)(2,1)}, bf16[256,1536]{1,0:T(8,128)(2,1)}, u32[]{:S(2)}, u32[]{:S(2)}) collective-permute-start(bf16[256,1536]{1,0:T(8,128)(2,1)} %slice.13), channel_id=1, source_target_pairs={{0,3},{1,0},{2,1},{3,2},{4,7},{5,4},{6,5},{7,6},{8,11},{9,8},{10,9... | collective-permute-start | bytes 2359304 | tf_op jit(solution)/shard_map/ppermute | solution.py:196
  50.0 3.4 %collective-permute-done.6.refs_6_ = bf16[768,512]{1,0:T(8,128)(2,1)S(1)} collective-permute-done((bf16[768,512]{1,0:T(8,128)(2,1)}, bf16[768,512]{1,0:T(8,128)(2,1)S(1)}, u32[]{:S(2)}, u32[]{:S(2)}) %collective-permute-start.6) | collective-permute-done | bytes 786464 | tf_op jit(solution)/shard_map/ppermute | solution.py:192
  53.4 0.8 slice.17
  54.2 0.9 copy-done.3
  55.1 5.3 %collective-permute-start.7 = (bf16[384,512]{1,0:T(8,128)(2,1)}, bf16[384,512]{1,0:T(8,128)(2,1)S(1)}, u32[]{:S(2)}, u32[]{:S(2)}) collective-permute-start(bf16[384,512]{1,0:T(8,128)(2,1)} %slice.17), channel_id=1, source_target_pairs={{0,3},{1,0},{2,1},{3,2},{4,7},{5,4},{6,5},{7,6},{8,11},{9,8},{10,9... | collective-permute-start | bytes 1179656 | tf_op jit(solution)/shard_map/ppermute | solution.py:196
  60.4 0.0 collective-permute-done.4.refs_9_
  60.4 0.8 slice.16
  61.2 0.9 copy-done.5
  62.1 2.1 %collective-permute-start.5 = (bf16[384,512]{1,0:T(8,128)(2,1)}, bf16[384,512]{1,0:T(8,128)(2,1)}, u32[]{:S(2)}, u32[]{:S(2)}) collective-permute-start(bf16[384,512]{1,0:T(8,128)(2,1)} %slice.16), channel_id=1, source_target_pairs={{0,1},{1,2},{2,3},{3,0},{4,5},{5,6},{6,7},{7,4},{8,9},{9,10},{10,1... | collective-permute-start | bytes 1179656 | tf_op jit(solution)/shard_map/ppermute | solution.py:196
  64.2 14.5 %collective-permute-done.7.refs_1_.refs_8_ = bf16[384,512]{1,0:T(8,128)(2,1)S(1)} collective-permute-done((bf16[384,512]{1,0:T(8,128)(2,1)}, bf16[384,512]{1,0:T(8,128)(2,1)S(1)}, u32[]{:S(2)}, u32[]{:S(2)}) %collective-permute-start.7) | collective-permute-done | bytes 393248 | tf_op jit(solution)/shard_map/ppermute | solution.py:196
  78.7 5.3 %collective-permute-done.5.refs_0_.refs_7_ = bf16[384,512]{1,0:T(8,128)(2,1)} collective-permute-done((bf16[384,512]{1,0:T(8,128)(2,1)}, bf16[384,512]{1,0:T(8,128)(2,1)}, u32[]{:S(2)}, u32[]{:S(2)}) %collective-permute-start.5) | collective-permute-done | bytes 393248 | tf_op jit(solution)/shard_map/ppermute | solution.py:196
  83.9 0.0 collective-permute-done.2.far_a.refs_2_
  83.9 0.0 collective-permute-done.3.far_b.refs_3_
  83.9 0.0 all-to-all-done
  84.0 0.0 copy-start
  84.0 1.4 copy-done
  85.4 7.4 %hidden_rows.1 = (f32[256,768]{1,0:T(8,128)S(1)}, f32[256,768]{1,0:T(8,128)S(1)}, bf16[256,2048]{1,0:T(8,128)(2,1)S(1)}, bf16[768,512]{1,0:T(8,128)(2,1)S(1)}, b...) custom-call(s32[1]{0:T(128)} %bitcast.2.me_ref, bf16[1024,1024]{1,0:T(8,128)(2,1)} %bitcast.4.recv, ...), custom_call_target="tpu_custom_call" | custom-call | tf_op jit(solution)/shard_map/hidden_rows/pallas_call | solution.py:252
  92.8 0.0 copy-start.8
  92.8 0.0 copy-start.11
  92.8 1.9 %collective-permute-start.8 = (bf16[768,512]{1,0:T(8,128)(2,1)}, bf16[768,512]{1,0:T(8,128)(2,1)}, u32[]{:S(2)}, u32[]{:S(2)}) collective-permute-start(bf16[768,512]{1,0:T(8,128)(2,1)} %get-tuple-element.22), channel_id=1, source_target_pairs={{0,1},{1,2},{2,3},{3,0},{4,5},{5,6},{6,7},{7,4},{8,9},{9,10},{10,1... | collective-permute-start | bytes 2359304 | tf_op jit(solution)/shard_map/ppermute | solution.py:206
  94.7 0.0 copy-done.1
  94.7 0.0 copy-done.4
  94.7 0.0 copy-done.6
  94.8 5.8 %back_rows.1 = bf16[1024,512]{1,0:T(8,128)(2,1)S(1)} custom-call(s32[1]{0:T(128)} %bitcast.2.me_ref, f32[256,768]{1,0:T(8,128)S(1)} %get-tuple-element.17.to_gate, f32[256,768]{1,0:T(8,128)S(1)} %get-tuple-element.18.to_up, bf16[256,2048]{1,0:T(8,128)(2,1)S(1)} %get-tuple-element.19.g, bf16[512,1536]{1,0:T(8,128)(2,1)S(1)} %bitcast.14, ...), custom_call_target="tpu_custom_call" | custom-call | tf_op jit(solution)/shard_map/back_rows/pallas_call | solution.py:272
  100.6 1.0 copy-done.2
  101.5 21.8 %all-to-all-start.1 = ((bf16[128,8,512]{2,1,0:T(8,128)(2,1)}), bf16[128,8,512]{2,1,0:T(8,128)(2,1)}, u32[]{:S(2)}, u32[]{:S(2)}) async-start(bf16[128,8,512]{2,1,0:T(8,128)(2,1)} %bitcast.15), calls=%async_computation.1 | async-start | bytes 2097152 | tf_op jit(solution)/shard_map/all_to_all | solution.py:293
  123.3 4.9 %collective-permute-start.10 = (bf16[768,512]{1,0:T(8,128)(2,1)}, bf16[768,512]{1,0:T(8,128)(2,1)S(1)}, u32[]{:S(2)}, u32[]{:S(2)}) collective-permute-start(bf16[768,512]{1,0:T(8,128)(2,1)} %get-tuple-element.23), channel_id=1, source_target_pairs={{0,3},{1,0},{2,1},{3,2},{4,7},{5,4},{6,5},{7,6},{8,11},{9,8},{10,9... | collective-permute-start | bytes 2359304 | tf_op jit(solution)/shard_map/ppermute | solution.py:216
  128.2 0.0 collective-permute-done.8.came
  128.2 0.0 copy-done.12
  128.2 0.0 copy-start.9
  128.2 1.4 add_far.1
  129.6 1.9 %collective-permute-start.9 = (bf16[768,512]{1,0:T(8,128)(2,1)S(1)}, bf16[768,512]{1,0:T(8,128)(2,1)S(1)}, u32[]{:S(2)}, u32[]{:S(2)}) collective-permute-start(bf16[768,512]{1,0:T(8,128)(2,1)S(1)} %add_far.1), channel_id=1, source_target_pairs={{0,1},{1,2},{2,3},{3,0},{4,5},{5,6},{6,7},{7,4},{8,9},{9,10},{10,1... | collective-permute-start | bytes 2359304 | tf_op jit(solution)/shard_map/ppermute | solution.py:216
  131.5 12.8 %collective-permute-done.10 = bf16[768,512]{1,0:T(8,128)(2,1)S(1)} collective-permute-done((bf16[768,512]{1,0:T(8,128)(2,1)}, bf16[768,512]{1,0:T(8,128)(2,1)S(1)}, u32[]{:S(2)}, u32[]{:S(2)}) %collective-permute-start.10) | collective-permute-done | bytes 786464 | tf_op jit(solution)/shard_map/ppermute | solution.py:216
  144.4 6.2 %collective-permute-done.9 = bf16[768,512]{1,0:T(8,128)(2,1)S(1)} collective-permute-done((bf16[768,512]{1,0:T(8,128)(2,1)S(1)}, bf16[768,512]{1,0:T(8,128)(2,1)S(1)}, u32[]{:S(2)}, u32[]{:S(2)}) %collective-permute-start.9) | collective-permute-done | bytes 786464 | tf_op jit(solution)/shard_map/ppermute | solution.py:216
  150.6 1.2 fusion
  151.8 2.1 %all-to-all-done.1 = bf16[128,8,512]{2,1,0:T(8,128)(2,1)} async-done(((bf16[128,8,512]{2,1,0:T(8,128)(2,1)}), bf16[128,8,512]{2,1,0:T(8,128)(2,1)}, u32[]{:S(2)}, u32[]{:S(2)}) %all-to-all-start.1) | async-done | bytes 1048608 | tf_op jit(solution)/shard_map/all_to_all | solution.py:293
  153.9 2.2 %combine_rows.1 = bf16[24,2048]{1,0:T(8,128)(2,1)} custom-call(bf16[1024,96]{1,0:T(8,128)(2,1)S(1)} %copy-done.10, bf16[1024,512]{1,0:T(8,128)(2,1)} %bitcast.8.ret_ref), custom_call_target="tpu_custom_call" | custom-call | tf_op jit(solution)/shard_map/combine_rows/pallas_call | solution.py:294
  (15 shorter events, 0.0 us)
Async XLA Ops:
  0.6 36.9 %collective-permute-start.1 = (bf16[512,1536]{1,0:T(8,128)(2,1)}, bf16[512,1536]{1,0:T(8,128)(2,1)S(1)}, u32[]{:S(2)}, u32[]{:S(2)}) collective-permute-start(bf16[512,1536]{1,0:T(8,128)(2,1)} %bitcast.11), channel_id=1, source_target_pairs={{0,3},{1,0},{2,1},{3,2},{4,7},{5,4},{6,5},{7,6},{8,11},{9,8},{10,9... | collective-permute-start | bytes 4718600 | tf_op jit(solution)/shard_map/ppermute | solution.py:191
  5.9 35.7 %collective-permute-start = (bf16[512,1536]{1,0:T(8,128)(2,1)}, bf16[512,1536]{1,0:T(8,128)(2,1)S(1)}, u32[]{:S(2)}, u32[]{:S(2)}) collective-permute-start(bf16[512,1536]{1,0:T(8,128)(2,1)} %bitcast.12), channel_id=1, source_target_pairs={{0,1},{1,2},{2,3},{3,0},{4,5},{5,6},{6,7},{7,4},{8,9},{9,10},{10,1... | collective-permute-start | bytes 4718600 | tf_op jit(solution)/shard_map/ppermute | solution.py:191
  12.4 71.5 %all-to-all-start = ((bf16[128,8,1024]{2,1,0:T(8,128)(2,1)}), bf16[128,8,1024]{2,1,0:T(8,128)(2,1)}, u32[]{:S(2)}, u32[]{:S(2)}) async-start(bf16[128,8,1024]{2,1,0:T(8,128)(2,1)} %bitcast.19), calls=%async_computation | async-start | bytes 4194304 | tf_op jit(solution)/shard_map/all_to_all | solution.py:250
  30.8 22.6 %collective-permute-start.6 = (bf16[768,512]{1,0:T(8,128)(2,1)}, bf16[768,512]{1,0:T(8,128)(2,1)S(1)}, u32[]{:S(2)}, u32[]{:S(2)}) collective-permute-start(bf16[768,512]{1,0:T(8,128)(2,1)} %bitcast.16), channel_id=1, source_target_pairs={{0,3},{1,0},{2,1},{3,2},{4,7},{5,4},{6,5},{7,6},{8,11},{9,8},{10,9... | collective-permute-start | bytes 2359304 | tf_op jit(solution)/shard_map/ppermute | solution.py:192
  35.6 24.8 %collective-permute-start.4 = (bf16[768,512]{1,0:T(8,128)(2,1)}, bf16[768,512]{1,0:T(8,128)(2,1)S(1)}, u32[]{:S(2)}, u32[]{:S(2)}) collective-permute-start(bf16[768,512]{1,0:T(8,128)(2,1)} %bitcast.17), channel_id=1, source_target_pairs={{0,1},{1,2},{2,3},{3,0},{4,5},{5,6},{6,7},{7,4},{8,9},{9,10},{10,1... | collective-permute-start | bytes 2359304 | tf_op jit(solution)/shard_map/ppermute | solution.py:192
  43.5 40.4 %collective-permute-start.2 = (bf16[256,1536]{1,0:T(8,128)(2,1)}, bf16[256,1536]{1,0:T(8,128)(2,1)}, u32[]{:S(2)}, u32[]{:S(2)}) collective-permute-start(bf16[256,1536]{1,0:T(8,128)(2,1)} %slice.12), channel_id=1, source_target_pairs={{0,1},{1,2},{2,3},{3,0},{4,5},{5,6},{6,7},{7,4},{8,9},{9,10},{10,1... | collective-permute-start | bytes 2359304 | tf_op jit(solution)/shard_map/ppermute | solution.py:196
  45.4 38.5 %collective-permute-start.3 = (bf16[256,1536]{1,0:T(8,128)(2,1)}, bf16[256,1536]{1,0:T(8,128)(2,1)}, u32[]{:S(2)}, u32[]{:S(2)}) collective-permute-start(bf16[256,1536]{1,0:T(8,128)(2,1)} %slice.13), channel_id=1, source_target_pairs={{0,3},{1,0},{2,1},{3,2},{4,7},{5,4},{6,5},{7,6},{8,11},{9,8},{10,9... | collective-permute-start | bytes 2359304 | tf_op jit(solution)/shard_map/ppermute | solution.py:196
  54.2 0.9 copy-start.3
  55.1 23.6 %collective-permute-start.7 = (bf16[384,512]{1,0:T(8,128)(2,1)}, bf16[384,512]{1,0:T(8,128)(2,1)S(1)}, u32[]{:S(2)}, u32[]{:S(2)}) collective-permute-start(bf16[384,512]{1,0:T(8,128)(2,1)} %slice.17), channel_id=1, source_target_pairs={{0,3},{1,0},{2,1},{3,2},{4,7},{5,4},{6,5},{7,6},{8,11},{9,8},{10,9... | collective-permute-start | bytes 1179656 | tf_op jit(solution)/shard_map/ppermute | solution.py:196
  61.2 0.9 copy-start.5
  62.1 21.9 %collective-permute-start.5 = (bf16[384,512]{1,0:T(8,128)(2,1)}, bf16[384,512]{1,0:T(8,128)(2,1)}, u32[]{:S(2)}, u32[]{:S(2)}) collective-permute-start(bf16[384,512]{1,0:T(8,128)(2,1)} %slice.16), channel_id=1, source_target_pairs={{0,1},{1,2},{2,3},{3,0},{4,5},{5,6},{6,7},{7,4},{8,9},{9,10},{10,1... | collective-permute-start | bytes 1179656 | tf_op jit(solution)/shard_map/ppermute | solution.py:196
  84.0 1.4 copy-start
  85.4 9.4 %copy-start.1 = (bf16[1,512,1536]{2,1,0:T(8,128)(2,1)S(1)}, bf16[1,512,1536]{2,1,0:T(8,128)(2,1)}, u32[]{:S(2)}) copy-start(bf16[1,512,1536]{2,1,0:T(8,128)(2,1)} %param.10) | copy-start | bytes 4718596
  85.4 9.4 %copy-start.4 = (bf16[768,512]{1,0:T(8,128)(2,1)S(1)}, bf16[768,512]{1,0:T(8,128)(2,1)}, u32[]{:S(2)}) copy-start(bf16[768,512]{1,0:T(8,128)(2,1)} %copy-done.3) | copy-start | bytes 2359300
  85.4 9.4 %copy-start.6 = (bf16[768,512]{1,0:T(8,128)(2,1)S(1)}, bf16[768,512]{1,0:T(8,128)(2,1)}, u32[]{:S(2)}) copy-start(bf16[768,512]{1,0:T(8,128)(2,1)} %copy-done.5) | copy-start | bytes 2359300
  85.4 9.4 %copy-start.7 = (bf16[1,768,512]{2,1,0:T(8,128)(2,1)S(1)}, bf16[1,768,512]{2,1,0:T(8,128)(2,1)}, u32[]{:S(2)}) copy-start(bf16[1,768,512]{2,1,0:T(8,128)(2,1)} %param.11) | copy-start | bytes 2359300
  92.8 7.8 %copy-start.8 = (bf16[768,512]{1,0:T(8,128)(2,1)}, bf16[768,512]{1,0:T(8,128)(2,1)S(1)}, u32[]{:S(2)}) copy-start(bf16[768,512]{1,0:T(8,128)(2,1)S(1)} %get-tuple-element.20) | copy-start | bytes 2359300
  92.8 7.8 %copy-start.11 = (bf16[768,512]{1,0:T(8,128)(2,1)}, bf16[768,512]{1,0:T(8,128)(2,1)S(1)}, u32[]{:S(2)}) copy-start(bf16[768,512]{1,0:T(8,128)(2,1)S(1)} %get-tuple-element.21.block) | copy-start | bytes 2359300
  92.8 35.4 %collective-permute-start.8 = (bf16[768,512]{1,0:T(8,128)(2,1)}, bf16[768,512]{1,0:T(8,128)(2,1)}, u32[]{:S(2)}, u32[]{:S(2)}) collective-permute-start(bf16[768,512]{1,0:T(8,128)(2,1)} %get-tuple-element.22), channel_id=1, source_target_pairs={{0,1},{1,2},{2,3},{3,0},{4,5},{5,6},{6,7},{7,4},{8,9},{9,10},{10,1... | collective-permute-start | bytes 2359304 | tf_op jit(solution)/shard_map/ppermute | solution.py:206
  100.6 1.0 copy-start.2
  101.5 26.7 %copy-start.12 = (bf16[768,512]{1,0:T(8,128)(2,1)S(1)}, bf16[768,512]{1,0:T(8,128)(2,1)}, u32[]{:S(2)}) copy-start(bf16[768,512]{1,0:T(8,128)(2,1)} %copy-done.11) | copy-start | bytes 2359300
  101.5 52.3 %all-to-all-start.1 = ((bf16[128,8,512]{2,1,0:T(8,128)(2,1)}), bf16[128,8,512]{2,1,0:T(8,128)(2,1)}, u32[]{:S(2)}, u32[]{:S(2)}) async-start(bf16[128,8,512]{2,1,0:T(8,128)(2,1)} %bitcast.15), calls=%async_computation.1 | async-start | bytes 2097152 | tf_op jit(solution)/shard_map/all_to_all | solution.py:293
  123.3 21.0 %collective-permute-start.10 = (bf16[768,512]{1,0:T(8,128)(2,1)}, bf16[768,512]{1,0:T(8,128)(2,1)S(1)}, u32[]{:S(2)}, u32[]{:S(2)}) collective-permute-start(bf16[768,512]{1,0:T(8,128)(2,1)} %get-tuple-element.23), channel_id=1, source_target_pairs={{0,3},{1,0},{2,1},{3,2},{4,7},{5,4},{6,5},{7,6},{8,11},{9,8},{10,9... | collective-permute-start | bytes 2359304 | tf_op jit(solution)/shard_map/ppermute | solution.py:216
  128.2 22.4 %copy-start.9 = (bf16[768,512]{1,0:T(8,128)(2,1)S(1)}, bf16[768,512]{1,0:T(8,128)(2,1)}, u32[]{:S(2)}) copy-start(bf16[768,512]{1,0:T(8,128)(2,1)} %copy-done.8) | copy-start | bytes 2359300
  129.6 21.0 %collective-permute-start.9 = (bf16[768,512]{1,0:T(8,128)(2,1)S(1)}, bf16[768,512]{1,0:T(8,128)(2,1)S(1)}, u32[]{:S(2)}, u32[]{:S(2)}) collective-permute-start(bf16[768,512]{1,0:T(8,128)(2,1)S(1)} %add_far.1), channel_id=1, source_target_pairs={{0,1},{1,2},{2,3},{3,0},{4,5},{5,6},{6,7},{7,4},{8,9},{9,10},{10,1... | collective-permute-start | bytes 2359304 | tf_op jit(solution)/shard_map/ppermute | solution.py:216
  150.6 3.3 %copy-start.10 = (bf16[1024,96]{1,0:T(8,128)(2,1)S(1)}, bf16[1024,96]{1,0:T(8,128)(2,1)}, u32[]{:S(2)}) copy-start(bf16[1024,96]{1,0:T(8,128)(2,1)} %get-tuple-element.13.pick_ref) | copy-start | bytes 589828

commit v6 on v5

--- a/solution.py
+++ b/solution.py
@@ -80,7 +80,7 @@
 
 
 def hidden_kernel(quarters, me_ref, recv, own_ref, right, far_a, far_b, left, *refs):
-    to_gate_ref, to_up_ref, g_ref, *downs, x_ref, own, sem = refs[2:]
+    to_gate_ref, to_up_ref, g_ref, *downs, x_ref, own, sem = refs
     fetch = pltpu.make_async_copy(own_ref, own, sem)
     fetch.start()
     rows = 256
@@ -197,22 +197,23 @@
     return out
 
 
-def add_kernel(block, came, out):
+def add_kernel(block, came, left, out, left_out):
     out[...] = (block[...].astype(F32) + came[...].astype(F32)).astype(BF16)
 
 
 def scatter_two_steps(blocks, size):
     own, right, far, left = blocks
     came = lax.ppermute(far, "edp", ring(size, 1))
-    right = pl.pallas_call(
+    right, left = pl.pallas_call(
         add_kernel,
-        in_specs=[whole()] * 2,
-        out_specs=whole(),
-        out_shape=jax.ShapeDtypeStruct(right.shape, BF16),
+        in_specs=[whole()] * 2 + [whole(pl.ANY)],
+        out_specs=[whole(), whole(pl.ANY)],
+        out_shape=[jax.ShapeDtypeStruct(right.shape, BF16)] * 2,
+        input_output_aliases={2: 1},
         compiler_params=pltpu.CompilerParams(vmem_limit_bytes=VMEM_LIMIT),
         cost_estimate=pl.CostEstimate(flops=COST, bytes_accessed=0, transcendentals=0),
         name="add_far",
-    )(right, came)
+    )(right, came, left)
     from_left, from_right = lax.ppermute(right, "edp", ring(size, 1)), lax.ppermute(left, "edp", ring(size, -1))
     return (own.astype(F32) + from_left.astype(F32) + from_right.astype(F32)).astype(BF16)
 
@@ -251,7 +252,7 @@
 
     to_gate, to_up, rows_g, *blocks = pl.pallas_call(
         functools.partial(hidden_kernel, quarters),
-        in_specs=[whole(pltpu.SMEM), whole(), whole(pltpu.HBM)] + [whole()] * 6,
+        in_specs=[whole(pltpu.SMEM), whole(), whole(pltpu.HBM)] + [whole()] * 4,
         out_specs=[whole()] * 7,
         out_shape=[
             jax.ShapeDtypeStruct((slots, hidden_units), F32),
@@ -265,8 +266,9 @@
             pltpu.SemaphoreType.DMA,
         ],
         compiler_params=params,
+        cost_estimate=pl.CostEstimate(flops=1, bytes_accessed=1, transcendentals=0),
         name="hidden_rows",
-    )(me, recv, gate_up_weight[0], *others[:4], *others[5:7])
+    )(me, recv, gate_up_weight[0], *others[:4])
     down_grad = scatter_two_steps(blocks, parts)[None]
 
     back = pl.pallas_call(
@@ -288,6 +290,7 @@
             pltpu.SemaphoreType.DMA((8,)),
         ],
         compiler_params=params,
+        cost_estimate=pl.CostEstimate(flops=COST, bytes_accessed=0, transcendentals=0),
         name="back_rows",
     )(me, to_gate, to_up, rows_g, gate_up_weight[0], *others[:4], down_weight[0], *others[4:])
     returned = lax.all_to_all(back, "ep", split_axis=0, concat_axis=0, tiled=True)

time: 157 us -> 150 us (0.955)
  waiting for transfers between devices: 48.3 us -> 42.9 us
  starting transfers between devices: 76.6 us -> 71.7 us
  local copies, waits for them, and re-layouts: 7.67 us -> 10.8 us
    ppermute x2, waiting for transfers between devices: 14.5 us -> 1.29 us  [gather_two_steps(): lax.ppermute(right[half:], 'edp', bwd)]
    all_to_all x1, waiting for transfers between devices: 0.01 us -> 10.2 us  [per_device(): recv = lax.all_to_all(sent, 'ep', split_axis=0, concat_axis=0, tiled=True)]
    ppermute x2, starting transfers between devices: 4.02 us -> 11.2 us  [gather_two_steps(): lax.ppermute(left[:half], 'edp', fwd)]
    all_to_all x1, starting transfers between devices: 21.8 us -> 15.3 us  [per_device(): lax.all_to_all(back, 'ep', split_axis=0, concat_axis=0, tiled=True)]
    ppermute x1, waiting for transfers between devices: 4.03 us -> 0.01 us  [gather_two_steps(): lax.ppermute(up, 'edp', fwd)]
    ppermute x2, starting transfers between devices: 9.88 us -> 5.97 us  [gather_two_steps(): lax.ppermute(right[half:], 'edp', bwd)]
    ppermute x1, waiting for transfers between devices: 3.39 us -> 0.01 us  [gather_two_steps(): lax.ppermute(down, 'edp', bwd)]
    ppermute x1, waiting for transfers between devices: 0.01 us -> 2.77 us  [gather_two_steps(): lax.ppermute(down, 'edp', fwd)]
  transfers between devices with their start and end apart: 13 -> 13, of which waited for: 7 -> 8; matrix products, arithmetic and copies ran while one was open for 3% -> 5% of each run, Pallas kernels for 8% -> 14%
where the time goes in v6:
time: 150 us; the launch traced here: 149 us
  starting transfers between devices  71.7 us (48%)
  waiting for transfers between devices  42.9 us (29%)
  Pallas kernels  21.8 us (15%)
  local copies, waits for them, and re-layouts  10.8 us (7%)
    all_to_all x1, starting transfers between devices, per_device(): recv = lax.all_to_all(sent, 'ep', split_axis=0, concat_axis=0, tiled=True)  18.3 us
    all_to_all x1, starting transfers between devices, per_device(): lax.all_to_all(back, 'ep', split_axis=0, concat_axis=0, tiled=True)  15.3 us
    ppermute x1, waiting for transfers between devices, scatter_two_steps(): lax.ppermute(left, 'edp', ring(size, -1))  14.7 us
    ppermute x2, starting transfers between devices, gather_two_steps(): lax.ppermute(left[:half], 'edp', fwd)  11.2 us
    all_to_all x1, waiting for transfers between devices, per_device(): recv = lax.all_to_all(sent, 'ep', split_axis=0, concat_axis=0, tiled=True)  10.2 us
    pallas_call x1, Pallas kernels, per_device(): pl.pallas_call(functools.partial(back_kernel, quarters), in_specs=[whole(...  7.7 us
    pallas_call x1, Pallas kernels, per_device(): pl.pallas_call(functools.partial(hidden_kernel, quarters), in_specs=[whol...  7.1 us
    ppermute x2, starting transfers between devices, gather_two_steps(): lax.ppermute(right[half:], 'edp', bwd)  5.97 us
  transfers between devices with their start and end apart: 13, of which 8 were waited for; matrix products, arithmetic and copies ran while one was open for 5% of the time, Pallas kernels for 14%

profile of v6, /device:TPU:1, one launch (start us, length us, event | category | flops | bytes accessed | tf_op | source)
XLA Modules:
  0.0 149.2 jit_solution(12982294388226317808)
XLA Ops:
  0.6 4.0 %collective-permute-start = (bf16[512,1536]{1,0:T(8,128)(2,1)}, bf16[512,1536]{1,0:T(8,128)(2,1)}, u32[]{:S(2)}, u32[]{:S(2)}) collective-permute-start(bf16[512,1536]{1,0:T(8,128)(2,1)} %bitcast.13), channel_id=1, source_target_pairs={{0,1},{1,2},{2,3},{3,0},{4,5},{5,6},{6,7},{7,4},{8,9},{9,10},{10,1... | collective-permute-start | bytes 4718600 | tf_op jit(solution)/shard_map/ppermute | solution.py:191
  4.6 3.2 %collective-permute-start.1 = (bf16[512,1536]{1,0:T(8,128)(2,1)}, bf16[512,1536]{1,0:T(8,128)(2,1)}, u32[]{:S(2)}, u32[]{:S(2)}) collective-permute-start(bf16[512,1536]{1,0:T(8,128)(2,1)} %bitcast.14), channel_id=1, source_target_pairs={{0,3},{1,0},{2,1},{3,2},{4,7},{5,4},{6,5},{7,6},{8,11},{9,8},{10,9... | collective-permute-start | bytes 4718600 | tf_op jit(solution)/shard_map/ppermute | solution.py:191
  7.8 4.6 %send_rows.1 = (bf16[1024,1024]{1,0:T(8,128)(2,1)}, bf16[1024,96]{1,0:T(8,128)(2,1)}) custom-call(s32[8,24]{1,0:T(8,128)} %bitcast.18, f32[8,24]{1,0:T(8,128)} %bitcast.19, bf16[24,2048]{1,0:T(8,128)(2,1)} %tok_ref.1, bf16[24,2048]{1,0:T(8,128)(2,1)} %grad_ref.1), custom_call_target="tpu_custom_call" | custom-call | tf_op jit(solution)/shard_map/send_rows/pallas_call | solution.py:235
  12.4 18.3 %all-to-all-start = ((bf16[128,8,1024]{2,1,0:T(8,128)(2,1)}), bf16[128,8,1024]{2,1,0:T(8,128)(2,1)S(1)}, u32[]{:S(2)}, u32[]{:S(2)}) async-start(bf16[128,8,1024]{2,1,0:T(8,128)(2,1)} %bitcast.17), calls=%async_computation | async-start | bytes 4194304 | tf_op jit(solution)/shard_map/all_to_all | solution.py:251
  30.8 1.9 %collective-permute-start.5 = (bf16[768,512]{1,0:T(8,128)(2,1)}, bf16[768,512]{1,0:T(8,128)(2,1)S(1)}, u32[]{:S(2)}, u32[]{:S(2)}) collective-permute-start(bf16[768,512]{1,0:T(8,128)(2,1)} %bitcast.6.refs_5_), channel_id=1, source_target_pairs={{0,1},{1,2},{2,3},{3,0},{4,5},{5,6},{6,7},{7,4},{8,9},{9,10},{10,1... | collective-permute-start | bytes 2359304 | tf_op jit(solution)/shard_map/ppermute | solution.py:192
  32.7 4.6 %collective-permute-start.4 = (bf16[768,512]{1,0:T(8,128)(2,1)}, bf16[768,512]{1,0:T(8,128)(2,1)S(1)}, u32[]{:S(2)}, u32[]{:S(2)}) collective-permute-start(bf16[768,512]{1,0:T(8,128)(2,1)} %bitcast.6.refs_5_), channel_id=1, source_target_pairs={{0,3},{1,0},{2,1},{3,2},{4,7},{5,4},{6,5},{7,6},{8,11},{9,8},{10,9... | collective-permute-start | bytes 2359304 | tf_op jit(solution)/shard_map/ppermute | solution.py:192
  37.3 0.0 collective-permute-done.refs_0_
  37.3 0.6 collective-permute-done.1.refs_1_
  37.8 2.1 %slice.12 = bf16[256,1536]{1,0:T(8,128)(2,1)} slice(bf16[512,1536]{1,0:T(8,128)(2,1)} %get-tuple-element.18.left.refs_4_), slice={[0:256], [0:1536]} | slice | bytes 1572864 | tf_op jit(solution)/shard_map/slice | solution.py:196
  39.9 7.0 %collective-permute-start.2 = (bf16[256,1536]{1,0:T(8,128)(2,1)}, bf16[256,1536]{1,0:T(8,128)(2,1)S(1)}, u32[]{:S(2)}, u32[]{:S(2)}) collective-permute-start(bf16[256,1536]{1,0:T(8,128)(2,1)} %slice.12), channel_id=1, source_target_pairs={{0,1},{1,2},{2,3},{3,0},{4,5},{5,6},{6,7},{7,4},{8,9},{9,10},{10,1... | collective-permute-start | bytes 2359304 | tf_op jit(solution)/shard_map/ppermute | solution.py:196
  46.9 2.1 %slice.13 = bf16[256,1536]{1,0:T(8,128)(2,1)} slice(bf16[512,1536]{1,0:T(8,128)(2,1)} %get-tuple-element.17.right.refs_1_), slice={[256:512], [0:1536]} | slice | bytes 1572864 | tf_op jit(solution)/shard_map/slice | solution.py:196
  49.0 1.9 %collective-permute-start.3 = (bf16[256,1536]{1,0:T(8,128)(2,1)}, bf16[256,1536]{1,0:T(8,128)(2,1)}, u32[]{:S(2)}, u32[]{:S(2)}) collective-permute-start(bf16[256,1536]{1,0:T(8,128)(2,1)} %slice.13), channel_id=1, source_target_pairs={{0,3},{1,0},{2,1},{3,2},{4,7},{5,4},{6,5},{7,6},{8,11},{9,8},{10,9... | collective-permute-start | bytes 2359304 | tf_op jit(solution)/shard_map/ppermute | solution.py:196
  50.9 2.8 %collective-permute-done.5.refs_9_ = bf16[768,512]{1,0:T(8,128)(2,1)S(1)} collective-permute-done((bf16[768,512]{1,0:T(8,128)(2,1)}, bf16[768,512]{1,0:T(8,128)(2,1)S(1)}, u32[]{:S(2)}, u32[]{:S(2)}) %collective-permute-start.5) | collective-permute-done | bytes 786464 | tf_op jit(solution)/shard_map/ppermute | solution.py:192
  53.7 0.8 slice.16
  54.5 1.0 copy-done.4
  55.4 4.2 %collective-permute-start.6 = (bf16[384,512]{1,0:T(8,128)(2,1)}, bf16[384,512]{1,0:T(8,128)(2,1)S(1)}, u32[]{:S(2)}, u32[]{:S(2)}) collective-permute-start(bf16[384,512]{1,0:T(8,128)(2,1)} %slice.16), channel_id=1, source_target_pairs={{0,1},{1,2},{2,3},{3,0},{4,5},{5,6},{6,7},{7,4},{8,9},{9,10},{10,1... | collective-permute-start | bytes 1179656 | tf_op jit(solution)/shard_map/ppermute | solution.py:196
  59.7 0.0 collective-permute-done.4.refs_6_
  59.7 0.8 slice.17
  60.5 0.9 copy-done.6
  61.4 4.1 %collective-permute-start.7 = (bf16[384,512]{1,0:T(8,128)(2,1)}, bf16[384,512]{1,0:T(8,128)(2,1)}, u32[]{:S(2)}, u32[]{:S(2)}) collective-permute-start(bf16[384,512]{1,0:T(8,128)(2,1)} %slice.17), channel_id=1, source_target_pairs={{0,3},{1,0},{2,1},{3,2},{4,7},{5,4},{6,5},{7,6},{8,11},{9,8},{10,9... | collective-permute-start | bytes 1179656 | tf_op jit(solution)/shard_map/ppermute | solution.py:196
  65.4 5.1 %collective-permute-done.2.far_a.refs_2_ = bf16[256,1536]{1,0:T(8,128)(2,1)S(1)} collective-permute-done((bf16[256,1536]{1,0:T(8,128)(2,1)}, bf16[256,1536]{1,0:T(8,128)(2,1)S(1)}, u32[]{:S(2)}, u32[]{:S(2)}) %collective-permute-start.2) | collective-permute-done | bytes 786464 | tf_op jit(solution)/shard_map/ppermute | solution.py:196
  70.5 1.3 collective-permute-done.3.far_b.refs_3_
  71.8 10.2 %all-to-all-done = bf16[128,8,1024]{2,1,0:T(8,128)(2,1)S(1)} async-done(((bf16[128,8,1024]{2,1,0:T(8,128)(2,1)}), bf16[128,8,1024]{2,1,0:T(8,128)(2,1)S(1)}, u32[]{:S(2)}, u32[]{:S(2)}) %all-to-all-start) | async-done | bytes 2097184 | tf_op jit(solution)/shard_map/all_to_all | solution.py:251
  82.0 1.4 copy-done
  83.4 7.1 %hidden_rows.1 = (f32[256,768]{1,0:T(8,128)S(1)}, f32[256,768]{1,0:T(8,128)S(1)}, bf16[256,2048]{1,0:T(8,128)(2,1)S(1)}, bf16[768,512]{1,0:T(8,128)(2,1)S(1)}, b...) custom-call(s32[1]{0:T(128)} %bitcast.2.me_ref, ...), custom_call_target="tpu_custom_call" | custom-call | flops 1 | bytes 1 | tf_op jit(solution)/shard_map/hidden_rows/pallas_call | solution.py:253
  90.5 0.0 copy-start.1
  90.6 0.9 copy-done.1
  91.4 0.9 copy-done.8
  92.3 1.9 %collective-permute-start.8 = (bf16[768,512]{1,0:T(8,128)(2,1)}, bf16[768,512]{1,0:T(8,128)(2,1)}, u32[]{:S(2)}, u32[]{:S(2)}) collective-permute-start(bf16[768,512]{1,0:T(8,128)(2,1)} %get-tuple-element.24), channel_id=1, source_target_pairs={{0,1},{1,2},{2,3},{3,0},{4,5},{5,6},{6,7},{7,4},{8,9},{9,10},{10,1... | collective-permute-start | bytes 2359304 | tf_op jit(solution)/shard_map/ppermute | solution.py:206
  94.2 0.0 collective-permute-done.6.refs_7_
  94.3 0.0 collective-permute-done.7.refs_8_
  94.3 0.0 copy-done.5
  94.3 0.0 copy-done.7
  94.3 7.7 %back_rows.1 = bf16[1024,512]{1,0:T(8,128)(2,1)} custom-call(s32[1]{0:T(128)} %bitcast.2.me_ref, f32[256,768]{1,0:T(8,128)S(1)} %get-tuple-element.19.to_gate, f32[256,768]{1,0:T(8,128)S(1)} %get-tuple-element.20.to_up, bf16[256,2048]{1,0:T(8,128)(2,1)S(1)} %get-tuple-element.21.g, bf16[512,1536]{1,0:T(8,128)(2,1)S(1)} %bitcast.16, ...), custom_call_target="tpu_custom_call" | custom-call | flops 20000000000 | tf_op jit(solution)/shard_map/back_rows/pallas_call | solution.py:274
  102.0 0.0 copy-done.10
  102.0 0.0 copy-start.9
  102.0 0.0 copy-start.11
  102.0 15.3 %all-to-all-start.1 = ((bf16[128,8,512]{2,1,0:T(8,128)(2,1)}), bf16[128,8,512]{2,1,0:T(8,128)(2,1)S(1)}, u32[]{:S(2)}, u32[]{:S(2)}) async-start(bf16[128,8,512]{2,1,0:T(8,128)(2,1)} %bitcast.7), calls=%async_computation.1 | async-start | bytes 2097152 | tf_op jit(solution)/shard_map/all_to_all | solution.py:296
  117.3 0.0 collective-permute-done.8.came
  117.3 0.0 copy-done.9
  117.4 1.4 add_far.1
  118.8 3.4 %collective-permute-start.10 = (bf16[768,512]{1,0:T(8,128)(2,1)S(1)}, bf16[768,512]{1,0:T(8,128)(2,1)S(1)}, u32[]{:S(2)}, u32[]{:S(2)}) collective-permute-start(bf16[768,512]{1,0:T(8,128)(2,1)S(1)} %get-tuple-element.27), channel_id=1, source_target_pairs={{0,3},{1,0},{2,1},{3,2},{4,7},{5,4},{6,5},{7,6},{8,11},{9,8},{10,9... | collective-permute-start | bytes 2359304 | tf_op jit(solution)/shard_map/ppermute | solution.py:217
  122.1 1.9 %collective-permute-start.9 = (bf16[768,512]{1,0:T(8,128)(2,1)S(1)}, bf16[768,512]{1,0:T(8,128)(2,1)S(1)}, u32[]{:S(2)}, u32[]{:S(2)}) collective-permute-start(bf16[768,512]{1,0:T(8,128)(2,1)S(1)} %get-tuple-element.26), channel_id=1, source_target_pairs={{0,1},{1,2},{2,3},{3,0},{4,5},{5,6},{6,7},{7,4},{8,9},{9,10},{10,1... | collective-permute-start | bytes 2359304 | tf_op jit(solution)/shard_map/ppermute | solution.py:217
  124.1 14.7 %collective-permute-done.10 = bf16[768,512]{1,0:T(8,128)(2,1)S(1)} collective-permute-done((bf16[768,512]{1,0:T(8,128)(2,1)S(1)}, bf16[768,512]{1,0:T(8,128)(2,1)S(1)}, u32[]{:S(2)}, u32[]{:S(2)}) %collective-permute-start.10) | collective-permute-done | bytes 786464 | tf_op jit(solution)/shard_map/ppermute | solution.py:217
  138.8 4.3 %collective-permute-done.9 = bf16[768,512]{1,0:T(8,128)(2,1)S(1)} collective-permute-done((bf16[768,512]{1,0:T(8,128)(2,1)S(1)}, bf16[768,512]{1,0:T(8,128)(2,1)S(1)}, u32[]{:S(2)}, u32[]{:S(2)}) %collective-permute-start.9) | collective-permute-done | bytes 786464 | tf_op jit(solution)/shard_map/ppermute | solution.py:217
  143.1 1.2 fusion
  144.3 3.9 %all-to-all-done.1 = bf16[128,8,512]{2,1,0:T(8,128)(2,1)S(1)} async-done(((bf16[128,8,512]{2,1,0:T(8,128)(2,1)}), bf16[128,8,512]{2,1,0:T(8,128)(2,1)S(1)}, u32[]{:S(2)}, u32[]{:S(2)}) %all-to-all-start.1) | async-done | bytes 1048608 | tf_op jit(solution)/shard_map/all_to_all | solution.py:296
  148.2 1.0 combine_rows.1
  (13 shorter events, 0.0 us)
Async XLA Ops:
  0.6 36.6 %collective-permute-start = (bf16[512,1536]{1,0:T(8,128)(2,1)}, bf16[512,1536]{1,0:T(8,128)(2,1)}, u32[]{:S(2)}, u32[]{:S(2)}) collective-permute-start(bf16[512,1536]{1,0:T(8,128)(2,1)} %bitcast.13), channel_id=1, source_target_pairs={{0,1},{1,2},{2,3},{3,0},{4,5},{5,6},{6,7},{7,4},{8,9},{9,10},{10,1... | collective-permute-start | bytes 4718600 | tf_op jit(solution)/shard_map/ppermute | solution.py:191
  4.6 33.3 %collective-permute-start.1 = (bf16[512,1536]{1,0:T(8,128)(2,1)}, bf16[512,1536]{1,0:T(8,128)(2,1)}, u32[]{:S(2)}, u32[]{:S(2)}) collective-permute-start(bf16[512,1536]{1,0:T(8,128)(2,1)} %bitcast.14), channel_id=1, source_target_pairs={{0,3},{1,0},{2,1},{3,2},{4,7},{5,4},{6,5},{7,6},{8,11},{9,8},{10,9... | collective-permute-start | bytes 4718600 | tf_op jit(solution)/shard_map/ppermute | solution.py:191
  12.4 69.6 %all-to-all-start = ((bf16[128,8,1024]{2,1,0:T(8,128)(2,1)}), bf16[128,8,1024]{2,1,0:T(8,128)(2,1)S(1)}, u32[]{:S(2)}, u32[]{:S(2)}) async-start(bf16[128,8,1024]{2,1,0:T(8,128)(2,1)} %bitcast.17), calls=%async_computation | async-start | bytes 4194304 | tf_op jit(solution)/shard_map/all_to_all | solution.py:251
  30.8 22.9 %collective-permute-start.5 = (bf16[768,512]{1,0:T(8,128)(2,1)}, bf16[768,512]{1,0:T(8,128)(2,1)S(1)}, u32[]{:S(2)}, u32[]{:S(2)}) collective-permute-start(bf16[768,512]{1,0:T(8,128)(2,1)} %bitcast.6.refs_5_), channel_id=1, source_target_pairs={{0,1},{1,2},{2,3},{3,0},{4,5},{5,6},{6,7},{7,4},{8,9},{9,10},{10,1... | collective-permute-start | bytes 2359304 | tf_op jit(solution)/shard_map/ppermute | solution.py:192
  32.7 27.0 %collective-permute-start.4 = (bf16[768,512]{1,0:T(8,128)(2,1)}, bf16[768,512]{1,0:T(8,128)(2,1)S(1)}, u32[]{:S(2)}, u32[]{:S(2)}) collective-permute-start(bf16[768,512]{1,0:T(8,128)(2,1)} %bitcast.6.refs_5_), channel_id=1, source_target_pairs={{0,3},{1,0},{2,1},{3,2},{4,7},{5,4},{6,5},{7,6},{8,11},{9,8},{10,9... | collective-permute-start | bytes 2359304 | tf_op jit(solution)/shard_map/ppermute | solution.py:192
  39.9 30.6 %collective-permute-start.2 = (bf16[256,1536]{1,0:T(8,128)(2,1)}, bf16[256,1536]{1,0:T(8,128)(2,1)S(1)}, u32[]{:S(2)}, u32[]{:S(2)}) collective-permute-start(bf16[256,1536]{1,0:T(8,128)(2,1)} %slice.12), channel_id=1, source_target_pairs={{0,1},{1,2},{2,3},{3,0},{4,5},{5,6},{6,7},{7,4},{8,9},{9,10},{10,1... | collective-permute-start | bytes 2359304 | tf_op jit(solution)/shard_map/ppermute | solution.py:196
  49.0 22.8 %collective-permute-start.3 = (bf16[256,1536]{1,0:T(8,128)(2,1)}, bf16[256,1536]{1,0:T(8,128)(2,1)}, u32[]{:S(2)}, u32[]{:S(2)}) collective-permute-start(bf16[256,1536]{1,0:T(8,128)(2,1)} %slice.13), channel_id=1, source_target_pairs={{0,3},{1,0},{2,1},{3,2},{4,7},{5,4},{6,5},{7,6},{8,11},{9,8},{10,9... | collective-permute-start | bytes 2359304 | tf_op jit(solution)/shard_map/ppermute | solution.py:196
  54.5 1.0 copy-start.4
  55.4 38.8 %collective-permute-start.6 = (bf16[384,512]{1,0:T(8,128)(2,1)}, bf16[384,512]{1,0:T(8,128)(2,1)S(1)}, u32[]{:S(2)}, u32[]{:S(2)}) collective-permute-start(bf16[384,512]{1,0:T(8,128)(2,1)} %slice.16), channel_id=1, source_target_pairs={{0,1},{1,2},{2,3},{3,0},{4,5},{5,6},{6,7},{7,4},{8,9},{9,10},{10,1... | collective-permute-start | bytes 1179656 | tf_op jit(solution)/shard_map/ppermute | solution.py:196
  60.5 0.9 copy-start.6
  61.4 32.9 %collective-permute-start.7 = (bf16[384,512]{1,0:T(8,128)(2,1)}, bf16[384,512]{1,0:T(8,128)(2,1)}, u32[]{:S(2)}, u32[]{:S(2)}) collective-permute-start(bf16[384,512]{1,0:T(8,128)(2,1)} %slice.17), channel_id=1, source_target_pairs={{0,3},{1,0},{2,1},{3,2},{4,7},{5,4},{6,5},{7,6},{8,11},{9,8},{10,9... | collective-permute-start | bytes 1179656 | tf_op jit(solution)/shard_map/ppermute | solution.py:196
  82.0 1.4 copy-start
  83.4 10.8 %copy-start.5 = (bf16[768,512]{1,0:T(8,128)(2,1)S(1)}, bf16[768,512]{1,0:T(8,128)(2,1)}, u32[]{:S(2)}) copy-start(bf16[768,512]{1,0:T(8,128)(2,1)} %copy-done.4) | copy-start | bytes 2359300
  83.4 10.8 %copy-start.7 = (bf16[768,512]{1,0:T(8,128)(2,1)S(1)}, bf16[768,512]{1,0:T(8,128)(2,1)}, u32[]{:S(2)}) copy-start(bf16[768,512]{1,0:T(8,128)(2,1)} %copy-done.6) | copy-start | bytes 2359300
  90.5 0.9 copy-start.1
  91.4 0.9 copy-start.8
  92.3 9.7 %copy-start.10 = (bf16[768,512]{1,0:T(8,128)(2,1)}, bf16[768,512]{1,0:T(8,128)(2,1)S(1)}, u32[]{:S(2)}) copy-start(bf16[768,512]{1,0:T(8,128)(2,1)S(1)} %get-tuple-element.25.left) | copy-start | bytes 2359300
  92.3 25.0 %collective-permute-start.8 = (bf16[768,512]{1,0:T(8,128)(2,1)}, bf16[768,512]{1,0:T(8,128)(2,1)}, u32[]{:S(2)}, u32[]{:S(2)}) collective-permute-start(bf16[768,512]{1,0:T(8,128)(2,1)} %get-tuple-element.24), channel_id=1, source_target_pairs={{0,1},{1,2},{2,3},{3,0},{4,5},{5,6},{6,7},{7,4},{8,9},{9,10},{10,1... | collective-permute-start | bytes 2359304 | tf_op jit(solution)/shard_map/ppermute | solution.py:206
  102.0 15.3 %copy-start.9 = (bf16[768,512]{1,0:T(8,128)(2,1)S(1)}, bf16[768,512]{1,0:T(8,128)(2,1)}, u32[]{:S(2)}) copy-start(bf16[768,512]{1,0:T(8,128)(2,1)} %copy-done.8) | copy-start | bytes 2359300
  102.0 15.3 %copy-start.11 = (bf16[768,512]{1,0:T(8,128)(2,1)S(1)}, bf16[768,512]{1,0:T(8,128)(2,1)}, u32[]{:S(2)}) copy-start(bf16[768,512]{1,0:T(8,128)(2,1)} %copy-done.10) | copy-start | bytes 2359300
  102.0 46.2 %all-to-all-start.1 = ((bf16[128,8,512]{2,1,0:T(8,128)(2,1)}), bf16[128,8,512]{2,1,0:T(8,128)(2,1)S(1)}, u32[]{:S(2)}, u32[]{:S(2)}) async-start(bf16[128,8,512]{2,1,0:T(8,128)(2,1)} %bitcast.7), calls=%async_computation.1 | async-start | bytes 2097152 | tf_op jit(solution)/shard_map/all_to_all | solution.py:296
  117.4 25.7 %copy-start.2 = (bf16[768,512]{1,0:T(8,128)(2,1)S(1)}, bf16[768,512]{1,0:T(8,128)(2,1)}, u32[]{:S(2)}) copy-start(bf16[768,512]{1,0:T(8,128)(2,1)} %copy-done.1) | copy-start | bytes 2359300
  118.8 20.1 %collective-permute-start.10 = (bf16[768,512]{1,0:T(8,128)(2,1)S(1)}, bf16[768,512]{1,0:T(8,128)(2,1)S(1)}, u32[]{:S(2)}, u32[]{:S(2)}) collective-permute-start(bf16[768,512]{1,0:T(8,128)(2,1)S(1)} %get-tuple-element.27), channel_id=1, source_target_pairs={{0,3},{1,0},{2,1},{3,2},{4,7},{5,4},{6,5},{7,6},{8,11},{9,8},{10,9... | collective-permute-start | bytes 2359304 | tf_op jit(solution)/shard_map/ppermute | solution.py:217
  122.1 21.0 %collective-permute-start.9 = (bf16[768,512]{1,0:T(8,128)(2,1)S(1)}, bf16[768,512]{1,0:T(8,128)(2,1)S(1)}, u32[]{:S(2)}, u32[]{:S(2)}) collective-permute-start(bf16[768,512]{1,0:T(8,128)(2,1)S(1)} %get-tuple-element.26), channel_id=1, source_target_pairs={{0,1},{1,2},{2,3},{3,0},{4,5},{5,6},{6,7},{7,4},{8,9},{9,10},{10,1... | collective-permute-start | bytes 2359304 | tf_op jit(solution)/shard_map/ppermute | solution.py:217
  143.1 5.1 %copy-start.3 = (bf16[1024,96]{1,0:T(8,128)(2,1)S(1)}, bf16[1024,96]{1,0:T(8,128)(2,1)}, u32[]{:S(2)}) copy-start(bf16[1024,96]{1,0:T(8,128)(2,1)} %get-tuple-element.15.pick_ref) | copy-start | bytes 589828

commit v7 on v5

--- a/solution.py
+++ b/solution.py
@@ -12,6 +12,7 @@
 NT = (((1,), (1,)), ((), ()))
 TN = (((0,), (0,)), ((), ()))
 VMEM_LIMIT = 16 * 1024 * 1024
+EXPERT_LIMIT = 50 * 1024 * 1024
 SEND_LIMIT = 56 * 1024 * 1024
 COST = 20 * 10**9
 
@@ -79,17 +80,45 @@
     return ((out % per) * quarters + out // per == src).astype(BF16)
 
 
-def hidden_kernel(quarters, me_ref, recv, own_ref, right, far_a, far_b, left, *refs):
-    to_gate_ref, to_up_ref, g_ref, *downs, x_ref, own, sem = refs[2:]
-    fetch = pltpu.make_async_copy(own_ref, own, sem)
-    fetch.start()
+def start(copies, src, dst, sems):
+    copies.append(pltpu.make_async_copy(src, dst, sems.at[len(copies)]))
+    copies[-1].start()
+    return copies[-1]
+
+
+def pieces(own, others):
+    right, far_a, far_b, left = others
+    rows = own.shape[0]
+    half = rows // 2
+    return [(own, 0, 0, rows), (right, 1, 0, rows), (far_a, 2, 0, half), (far_b, 2, half, half), (left, 3, 0, rows)]
+
+
+def expert_kernel(quarters, me_ref, recv_ref, *refs):
+    ups, downs, refs = pieces(refs[0], refs[1:5]), pieces(refs[5], refs[6:10]), refs[10:]
+    back_ref, *blocks, recv, w, wd, x_ref, g_ref, hid_ref, to_gate, to_up, gp_ref, hold, out, sems = refs
     rows = 256
     per = rows // quarters
     feat = recv.shape[1] // 2
-    hidden_units = to_gate_ref.shape[1]
+    hidden_units = hid_ref.shape[1]
     tile = 256
+    started = []
+    came, columns = [], []
+    for b in range(recv.shape[0] // rows):
+        here = pl.ds(b * rows, rows)
+        came.append(start(started, recv_ref.at[here, :], recv.at[here, :], sems))
+    for n in range(hidden_units // tile):
+        some = []
+        for at in (n * tile, hidden_units + n * tile):
+            for ref, block, row, size in ups:
+                to = w.at[pl.ds(block * feat + row, size), pl.ds(at, tile)]
+                some.append(start(started, ref.at[:, pl.ds(at, tile)], to, sems))
+        columns.append(some)
+    down_came = [
+        start(started, ref, wd.at[pl.ds(row, size), pl.ds(block * feat, feat)], sems) for ref, block, row, size in downs
+    ]
     order = order_matrix(rows, quarters)
     for b in range(recv.shape[0] // rows):
+        came[b].wait()
         got = jnp.dot(order, recv[b * rows : b * rows + rows, :], preferred_element_type=F32).astype(BF16)
         here = slice(b * per, b * per + per)
         for q in range(quarters):
@@ -97,67 +126,43 @@
             x_ref[here, pl.ds(at, feat)] = got[q * per : q * per + per, :feat]
             g_ref[here, pl.ds(at, feat)] = got[q * per : q * per + per, feat:]
 
-    fetch.wait()
-
     def pre(cols):
-        total, row = None, 0
-        for w in (own, right, far_a, far_b, left):
-            term = jnp.dot(x_ref[:, row : row + w.shape[0]], w[:, cols], preferred_element_type=F32)
-            total, row = term if total is None else total + term, row + w.shape[0]
-        return total
-
+        return jnp.dot(x_ref[...], w[:, cols], preferred_element_type=F32)
+
+    tile = 256
     for n in range(hidden_units // tile):
+        for copy in columns[n]:
+            copy.wait()
         cols = slice(n * tile, n * tile + tile)
         gate = pre(cols)
         up = pre(slice(hidden_units + n * tile, hidden_units + n * tile + tile))
         sig = jax.nn.sigmoid(gate)
         activ = gate * sig
-        to_gate_ref[:, cols] = up * sig * (1.0 + gate * (1.0 - sig))
-        to_up_ref[:, cols] = activ
-        hidden = (activ * up).astype(BF16)
-        for k, ref in enumerate(downs):
-            ref[cols, :] = lax.dot_general(
-                hidden, g_ref[:, k * feat : k * feat + feat], TN, preferred_element_type=F32
-            ).astype(BF16)
-
-
-def back_kernel(quarters, me_ref, to_gate, to_up, g, *refs):
-    (own_up_ref, *ups), (own_ref, right, far_a, far_b, left), refs = refs[:5], refs[5:10], refs[10:]
-    back_ref, gp_ref, hold, own_up, own, out, sems = refs
-    fetch_down = pltpu.make_async_copy(own_ref, own, sems.at[0])
-    fetch_down.start()
-    fetch_up = pltpu.make_async_copy(own_up_ref, own_up, sems.at[1])
-    fetch_up.start()
-    hidden_units = to_gate.shape[1]
-    feat = g.shape[1] // quarters
-    half = hidden_units // 2
-    fetch_down.wait()
-    for h, far in enumerate((far_a, far_b)):
-        cols = slice(h * half, h * half + half)
-        total = None
-        for k, w in enumerate((own[cols, :], right[cols, :], far[...], left[cols, :])):
-            term = lax.dot_general(g[:, k * feat : k * feat + feat], w, NT, preferred_element_type=F32)
-            total = term if total is None else total + term
+        to_gate[:, cols] = up * sig * (1.0 + gate * (1.0 - sig))
+        to_up[:, cols] = activ
+        hid_ref[:, cols] = (activ * up).astype(BF16)
+
+    for copy in down_came:
+        copy.wait()
+    for n in range(hidden_units // tile):
+        cols = slice(n * tile, n * tile + tile)
+        total = lax.dot_general(g_ref[...], wd[cols, :], NT, preferred_element_type=F32)
         gp_ref[:, cols] = (total * to_gate[:, cols]).astype(BF16)
-        gp_ref[:, hidden_units + h * half : hidden_units + h * half + half] = (total * to_up[:, cols]).astype(BF16)
-    fetch_up.wait()
-    at = 0
-    for w in (own_up, *ups):
-        rows = w.shape[0]
-        hold[lax.rem(me_ref[0] + at // feat, quarters), :, at % feat : at % feat + rows] = lax.dot_general(
-            gp_ref[...], w[...], NT, preferred_element_type=F32
+        gp_ref[:, hidden_units + n * tile : hidden_units + n * tile + tile] = (total * to_up[:, cols]).astype(BF16)
+    for k in range(quarters):
+        hold[lax.rem(me_ref[0] + k, quarters)] = lax.dot_general(
+            gp_ref[...], w[k * feat : k * feat + feat, :], NT, preferred_element_type=F32
         ).astype(BF16)
-        at += rows
-    rows = 256
-    per = rows // quarters
-    order = order_matrix(rows, quarters)
     copies = []
     for b in range(back_ref.shape[0] // rows):
         here = pl.ds(b * rows, rows)
         stacked = jnp.concatenate([hold[q, b * per : b * per + per, :] for q in range(quarters)], axis=0)
         out[here, :] = lax.dot_general(order, stacked, TN, preferred_element_type=F32).astype(BF16)
-        copies.append(pltpu.make_async_copy(out.at[here, :], back_ref.at[here, :], sems.at[2 + b]))
-        copies[-1].start()
+        copies.append(start(started, out.at[here, :], back_ref.at[here, :], sems))
+    for k, ref in enumerate(blocks):
+        ref[...] = lax.dot_general(
+            hid_ref[...], g_ref[:, k * feat : k * feat + feat], TN, preferred_element_type=F32
+        ).astype(BF16)
     for copy in copies:
         copy.wait()
 
@@ -249,47 +254,30 @@
     )(expert_ids.T, gate_values.T, tokens, out_grad)
     recv = lax.all_to_all(sent, "ep", split_axis=0, concat_axis=0, tiled=True)
 
-    to_gate, to_up, rows_g, *blocks = pl.pallas_call(
-        functools.partial(hidden_kernel, quarters),
-        in_specs=[whole(pltpu.SMEM), whole(), whole(pltpu.HBM)] + [whole()] * 6,
-        out_specs=[whole()] * 7,
-        out_shape=[
-            jax.ShapeDtypeStruct((slots, hidden_units), F32),
-            jax.ShapeDtypeStruct((slots, hidden_units), F32),
-            jax.ShapeDtypeStruct((slots, width), BF16),
-        ]
+    back, *blocks = pl.pallas_call(
+        functools.partial(expert_kernel, quarters),
+        in_specs=[whole(pltpu.SMEM)] + [whole(pl.ANY)] * 11,
+        out_specs=[whole(pl.ANY)] + [whole()] * parts,
+        out_shape=[jax.ShapeDtypeStruct((rows, feat), BF16)]
         + [jax.ShapeDtypeStruct((hidden_units, feat), BF16)] * parts,
         scratch_shapes=[
+            pltpu.VMEM((rows, 2 * feat), BF16),
+            pltpu.VMEM((width, 2 * hidden_units), BF16),
+            pltpu.VMEM((hidden_units, width), BF16),
             pltpu.VMEM((slots, width), BF16),
-            pltpu.VMEM((feat, 2 * hidden_units), BF16),
-            pltpu.SemaphoreType.DMA,
-        ],
-        compiler_params=params,
-        name="hidden_rows",
-    )(me, recv, gate_up_weight[0], *others[:4], *others[5:7])
-    down_grad = scatter_two_steps(blocks, parts)[None]
-
-    back = pl.pallas_call(
-        functools.partial(back_kernel, quarters),
-        in_specs=[whole(pltpu.SMEM)]
-        + [whole()] * 3
-        + [whole(pltpu.HBM)]
-        + [whole()] * 4
-        + [whole(pltpu.HBM)]
-        + [whole()] * 4,
-        out_specs=whole(pltpu.HBM),
-        out_shape=jax.ShapeDtypeStruct((rows, feat), BF16),
-        scratch_shapes=[
+            pltpu.VMEM((slots, width), BF16),
+            pltpu.VMEM((slots, hidden_units), BF16),
+            pltpu.VMEM((slots, hidden_units), F32),
+            pltpu.VMEM((slots, hidden_units), F32),
             pltpu.VMEM((slots, 2 * hidden_units), BF16),
             pltpu.VMEM((quarters, slots, feat), BF16),
-            pltpu.VMEM((feat, 2 * hidden_units), BF16),
-            pltpu.VMEM((hidden_units, feat), BF16),
             pltpu.VMEM((rows, feat), BF16),
-            pltpu.SemaphoreType.DMA((8,)),
+            pltpu.SemaphoreType.DMA((64,)),
         ],
-        compiler_params=params,
-        name="back_rows",
-    )(me, to_gate, to_up, rows_g, gate_up_weight[0], *others[:4], down_weight[0], *others[4:])
+        compiler_params=pltpu.CompilerParams(vmem_limit_bytes=EXPERT_LIMIT),
+        name="expert_rows",
+    )(me, recv, gate_up_weight[0], *others[:4], down_weight[0], *others[4:])
+    down_grad = scatter_two_steps(blocks, parts)[None]
     returned = lax.all_to_all(back, "ep", split_axis=0, concat_axis=0, tiled=True)
     token_grads = pl.pallas_call(
         functools.partial(combine_kernel, toks),

time: 157 us -> 151 us (0.962)
  Pallas kernels: 21.4 us -> 17.4 us
  local copies, waits for them, and re-layouts: 7.67 us -> 3.99 us
  waiting for transfers between devices: 48.3 us -> 51.5 us
    ppermute x2, waiting for transfers between devices: 14.5 us -> 0.01 us  [gather_two_steps(): lax.ppermute(right[half:], 'edp', bwd)]
    ppermute x2, waiting for transfers between devices: 5.28 us -> 17.7 us  [gather_two_steps(): lax.ppermute(left[:half], 'edp', fwd)]
    ppermute x1, waiting for transfers between devices: 0.01 us -> 8.17 us  [gather_two_steps(): lax.ppermute(down, 'edp', fwd)]
    ppermute x1, waiting for transfers between devices: 3.39 us -> 0.01 us  [gather_two_steps(): lax.ppermute(down, 'edp', bwd)]
    pallas_call x2 -> x1, Pallas kernels: 13.2 us -> 10.5 us  [per_device(): pl.pallas_call(functools.partial(expert_kernel, quarters), in_specs=[whol...]
    unnamed x26 -> x12, local copies, waits for them, and re-layouts: 4.14 us -> 1.77 us
  transfers between devices with their start and end apart: 13 -> 13, of which waited for: 7 -> 6; matrix products, arithmetic and copies ran while one was open for 3% -> 2% of each run, Pallas kernels for 8% -> 4%
where the time goes in v7:
time: 151 us; the launch traced here: 150 us
  starting transfers between devices  75.3 us (50%)
  waiting for transfers between devices  51.5 us (34%)
  Pallas kernels  17.4 us (12%)
  local copies, waits for them, and re-layouts  3.99 us (3%)
    all_to_all x1, starting transfers between devices, per_device(): lax.all_to_all(back, 'ep', split_axis=0, concat_axis=0, tiled=True)  21.4 us
    all_to_all x1, starting transfers between devices, per_device(): recv = lax.all_to_all(sent, 'ep', split_axis=0, concat_axis=0, tiled=True)  18.3 us
    ppermute x2, waiting for transfers between devices, gather_two_steps(): lax.ppermute(left[:half], 'edp', fwd)  17.7 us
    ppermute x1, waiting for transfers between devices, scatter_two_steps(): lax.ppermute(left, 'edp', ring(size, -1))  12.7 us
    pallas_call x1, Pallas kernels, per_device(): pl.pallas_call(functools.partial(expert_kernel, quarters), in_specs=[whol...  10.5 us
    ppermute x2, starting transfers between devices, gather_two_steps(): lax.ppermute(right[half:], 'edp', bwd)  9.13 us
    ppermute x1, waiting for transfers between devices, gather_two_steps(): lax.ppermute(down, 'edp', fwd)  8.17 us
    ppermute x1, waiting for transfers between devices, scatter_two_steps(): lax.ppermute(right, 'edp', ring(size, 1))  6.36 us
  transfers between devices with their start and end apart: 13, of which 6 were waited for; matrix products, arithmetic and copies ran while one was open for 2% of the time, Pallas kernels for 4%

profile of v7, /device:TPU:1, one launch (start us, length us, event | category | flops | bytes accessed | tf_op | source)
XLA Modules:
  0.0 150.3 jit_solution(5618738949233139740)
XLA Ops:
  0.6 5.2 %collective-permute-start.1 = (bf16[512,1536]{1,0:T(8,128)(2,1)}, bf16[512,1536]{1,0:T(8,128)(2,1)S(1)}, u32[]{:S(2)}, u32[]{:S(2)}) collective-permute-start(bf16[512,1536]{1,0:T(8,128)(2,1)} %bitcast.13), channel_id=1, source_target_pairs={{0,3},{1,0},{2,1},{3,2},{4,7},{5,4},{6,5},{7,6},{8,11},{9,8},{10,9... | collective-permute-start | bytes 4718600 | tf_op jit(solution)/shard_map/ppermute | solution.py:196
  5.9 1.9 %collective-permute-start = (bf16[512,1536]{1,0:T(8,128)(2,1)}, bf16[512,1536]{1,0:T(8,128)(2,1)S(1)}, u32[]{:S(2)}, u32[]{:S(2)}) collective-permute-start(bf16[512,1536]{1,0:T(8,128)(2,1)} %bitcast.14), channel_id=1, source_target_pairs={{0,1},{1,2},{2,3},{3,0},{4,5},{5,6},{6,7},{7,4},{8,9},{9,10},{10,1... | collective-permute-start | bytes 4718600 | tf_op jit(solution)/shard_map/ppermute | solution.py:196
  7.8 4.6 %send_rows.1 = (bf16[1024,1024]{1,0:T(8,128)(2,1)}, bf16[1024,96]{1,0:T(8,128)(2,1)}) custom-call(s32[8,24]{1,0:T(8,128)} %bitcast.20, f32[8,24]{1,0:T(8,128)} %bitcast.21, bf16[24,2048]{1,0:T(8,128)(2,1)} %tok_ref.1, bf16[24,2048]{1,0:T(8,128)(2,1)} %grad_ref.1), custom_call_target="tpu_custom_call" | custom-call | tf_op jit(solution)/shard_map/send_rows/pallas_call | solution.py:239
  12.4 18.3 %all-to-all-start = ((bf16[128,8,1024]{2,1,0:T(8,128)(2,1)}), bf16[128,8,1024]{2,1,0:T(8,128)(2,1)}, u32[]{:S(2)}, u32[]{:S(2)}) async-start(bf16[128,8,1024]{2,1,0:T(8,128)(2,1)} %bitcast.12), calls=%async_computation | async-start | bytes 4194304 | tf_op jit(solution)/shard_map/all_to_all | solution.py:255
  30.8 2.4 %collective-permute-start.5 = (bf16[768,512]{1,0:T(8,128)(2,1)}, bf16[768,512]{1,0:T(8,128)(2,1)S(1)}, u32[]{:S(2)}, u32[]{:S(2)}) collective-permute-start(bf16[768,512]{1,0:T(8,128)(2,1)} %bitcast.17), channel_id=1, source_target_pairs={{0,1},{1,2},{2,3},{3,0},{4,5},{5,6},{6,7},{7,4},{8,9},{9,10},{10,1... | collective-permute-start | bytes 2359304 | tf_op jit(solution)/shard_map/ppermute | solution.py:197
  33.1 4.4 %collective-permute-start.4 = (bf16[768,512]{1,0:T(8,128)(2,1)}, bf16[768,512]{1,0:T(8,128)(2,1)S(1)}, u32[]{:S(2)}, u32[]{:S(2)}) collective-permute-start(bf16[768,512]{1,0:T(8,128)(2,1)} %bitcast.18), channel_id=1, source_target_pairs={{0,3},{1,0},{2,1},{3,2},{4,7},{5,4},{6,5},{7,6},{8,11},{9,8},{10,9... | collective-permute-start | bytes 2359304 | tf_op jit(solution)/shard_map/ppermute | solution.py:197
  37.5 0.0 collective-permute-done.1.refs_1_
  37.6 4.0 %collective-permute-done.refs_0_ = bf16[512,1536]{1,0:T(8,128)(2,1)S(1)} collective-permute-done((bf16[512,1536]{1,0:T(8,128)(2,1)}, bf16[512,1536]{1,0:T(8,128)(2,1)S(1)}, u32[]{:S(2)}, u32[]{:S(2)}) %collective-permute-start) | collective-permute-done | bytes 1572896 | tf_op jit(solution)/shard_map/ppermute | solution.py:196
  41.6 0.0 copy-start
  41.6 0.0 copy-start.1
  41.6 1.0 slice.13
  42.6 1.2 slice.12
  43.8 0.0 copy-done
  43.8 0.0 copy-done.1
  43.8 1.9 %collective-permute-start.2 = (bf16[256,1536]{1,0:T(8,128)(2,1)}, bf16[256,1536]{1,0:T(8,128)(2,1)}, u32[]{:S(2)}, u32[]{:S(2)}) collective-permute-start(bf16[256,1536]{1,0:T(8,128)(2,1)} %slice.12), channel_id=1, source_target_pairs={{0,1},{1,2},{2,3},{3,0},{4,5},{5,6},{6,7},{7,4},{8,9},{9,10},{10,1... | collective-permute-start | bytes 2359304 | tf_op jit(solution)/shard_map/ppermute | solution.py:201
  45.7 4.6 %collective-permute-start.3 = (bf16[256,1536]{1,0:T(8,128)(2,1)}, bf16[256,1536]{1,0:T(8,128)(2,1)S(1)}, u32[]{:S(2)}, u32[]{:S(2)}) collective-permute-start(bf16[256,1536]{1,0:T(8,128)(2,1)} %slice.13), channel_id=1, source_target_pairs={{0,3},{1,0},{2,1},{3,2},{4,7},{5,4},{6,5},{7,6},{8,11},{9,8},{10,9... | collective-permute-start | bytes 2359304 | tf_op jit(solution)/shard_map/ppermute | solution.py:201
  50.3 8.2 %collective-permute-done.5.refs_9_ = bf16[768,512]{1,0:T(8,128)(2,1)S(1)} collective-permute-done((bf16[768,512]{1,0:T(8,128)(2,1)}, bf16[768,512]{1,0:T(8,128)(2,1)S(1)}, u32[]{:S(2)}, u32[]{:S(2)}) %collective-permute-start.5) | collective-permute-done | bytes 786464 | tf_op jit(solution)/shard_map/ppermute | solution.py:197
  58.4 0.0 copy-start.3
  58.5 1.9 %collective-permute-start.6 = (bf16[384,512]{1,0:T(8,128)(2,1)S(1)}, bf16[384,512]{1,0:T(8,128)(2,1)S(1)}, u32[]{:S(2)}, u32[]{:S(2)}) collective-permute-start(bf16[384,512]{1,0:T(8,128)(2,1)S(1)} %slice.16), channel_id=1, source_target_pairs={{0,1},{1,2},{2,3},{3,0},{4,5},{5,6},{6,7},{7,4},{8,9},{9,10},{10,1... | collective-permute-start | bytes 1179656 | tf_op jit(solution)/shard_map/ppermute | solution.py:201
  60.4 0.0 collective-permute-done.4.refs_6_
  60.4 0.0 copy-done.3
  60.4 0.0 copy-start.4
  60.5 0.9 copy-done.4
  61.4 4.6 %collective-permute-start.7 = (bf16[384,512]{1,0:T(8,128)(2,1)S(1)}, bf16[384,512]{1,0:T(8,128)(2,1)S(1)}, u32[]{:S(2)}, u32[]{:S(2)}) collective-permute-start(bf16[384,512]{1,0:T(8,128)(2,1)S(1)} %slice.17), channel_id=1, source_target_pairs={{0,3},{1,0},{2,1},{3,2},{4,7},{5,4},{6,5},{7,6},{8,11},{9,8},{10,9... | collective-permute-start | bytes 1179656 | tf_op jit(solution)/shard_map/ppermute | solution.py:201
  65.9 17.7 %collective-permute-done.6.refs_7_ = bf16[384,512]{1,0:T(8,128)(2,1)S(1)} collective-permute-done((bf16[384,512]{1,0:T(8,128)(2,1)S(1)}, bf16[384,512]{1,0:T(8,128)(2,1)S(1)}, u32[]{:S(2)}, u32[]{:S(2)}) %collective-permute-start.6) | collective-permute-done | bytes 393248 | tf_op jit(solution)/shard_map/ppermute | solution.py:201
  83.6 0.0 collective-permute-done.7.refs_8_
  83.6 0.0 collective-permute-done.2.refs_2_
  83.6 0.0 collective-permute-done.3.refs_3_
  83.6 0.0 copy-start.5
  83.6 0.0 all-to-all-done
  83.6 0.9 copy-done.5
  84.5 10.5 %expert_rows.1 = (bf16[1024,512]{1,0:T(8,128)(2,1)}, bf16[768,512]{1,0:T(8,128)(2,1)S(1)}, bf16[768,512]{1,0:T(8,128)(2,1)S(1)}, bf16[768,512]{1,0:T(8,128)(2,1)}, bf16[768,512]{1,0:T(8,128)(2,1)S(1)}) custom-call(s32[1]{0:T(128)} %bitcast.2.me_ref, bf16[1024,1024]{1,0:T(8,128)(2,1)} %bitcast.4.recv_ref, bf16[512,1536]{1,0:T(8,128)(2,1)} %bitcast.15, ...), custom_call_target="tpu_custom_call" | custom-call | tf_op jit(solution)/shard_map/expert_rows/pallas_call | solution.py:257
  95.0 1.9 %collective-permute-start.8 = (bf16[768,512]{1,0:T(8,128)(2,1)}, bf16[768,512]{1,0:T(8,128)(2,1)}, u32[]{:S(2)}, u32[]{:S(2)}) collective-permute-start(bf16[768,512]{1,0:T(8,128)(2,1)} %get-tuple-element.18), channel_id=1, source_target_pairs={{0,1},{1,2},{2,3},{3,0},{4,5},{5,6},{6,7},{7,4},{8,9},{9,10},{10,1... | collective-permute-start | bytes 2359304 | tf_op jit(solution)/shard_map/ppermute | solution.py:211
  97.0 21.4 %all-to-all-start.1 = ((bf16[128,8,512]{2,1,0:T(8,128)(2,1)}), bf16[128,8,512]{2,1,0:T(8,128)(2,1)S(1)}, u32[]{:S(2)}, u32[]{:S(2)}) async-start(bf16[128,8,512]{2,1,0:T(8,128)(2,1)} %bitcast.16), calls=%async_computation.1 | async-start | bytes 2097152 | tf_op jit(solution)/shard_map/all_to_all | solution.py:281
  118.4 4.9 %collective-permute-start.10 = (bf16[768,512]{1,0:T(8,128)(2,1)S(1)}, bf16[768,512]{1,0:T(8,128)(2,1)S(1)}, u32[]{:S(2)}, u32[]{:S(2)}) collective-permute-start(bf16[768,512]{1,0:T(8,128)(2,1)S(1)} %get-tuple-element.19), channel_id=1, source_target_pairs={{0,3},{1,0},{2,1},{3,2},{4,7},{5,4},{6,5},{7,6},{8,11},{9,8},{10,9... | collective-permute-start | bytes 2359304 | tf_op jit(solution)/shard_map/ppermute | solution.py:221
  123.3 0.0 collective-permute-done.8.came
  123.3 1.3 add_far.1
  124.6 1.9 %collective-permute-start.9 = (bf16[768,512]{1,0:T(8,128)(2,1)S(1)}, bf16[768,512]{1,0:T(8,128)(2,1)S(1)}, u32[]{:S(2)}, u32[]{:S(2)}) collective-permute-start(bf16[768,512]{1,0:T(8,128)(2,1)S(1)} %add_far.1), channel_id=1, source_target_pairs={{0,1},{1,2},{2,3},{3,0},{4,5},{5,6},{6,7},{7,4},{8,9},{9,10},{10,1... | collective-permute-start | bytes 2359304 | tf_op jit(solution)/shard_map/ppermute | solution.py:221
  126.5 12.7 %collective-permute-done.10 = bf16[768,512]{1,0:T(8,128)(2,1)S(1)} collective-permute-done((bf16[768,512]{1,0:T(8,128)(2,1)S(1)}, bf16[768,512]{1,0:T(8,128)(2,1)S(1)}, u32[]{:S(2)}, u32[]{:S(2)}) %collective-permute-start.10) | collective-permute-done | bytes 786464 | tf_op jit(solution)/shard_map/ppermute | solution.py:221
  139.2 6.4 %collective-permute-done.9 = bf16[768,512]{1,0:T(8,128)(2,1)S(1)} collective-permute-done((bf16[768,512]{1,0:T(8,128)(2,1)S(1)}, bf16[768,512]{1,0:T(8,128)(2,1)S(1)}, u32[]{:S(2)}, u32[]{:S(2)}) %collective-permute-start.9) | collective-permute-done | bytes 786464 | tf_op jit(solution)/shard_map/ppermute | solution.py:221
  145.6 0.0 copy-start.2
  145.6 1.2 fusion
  146.7 2.6 %all-to-all-done.1 = bf16[128,8,512]{2,1,0:T(8,128)(2,1)S(1)} async-done(((bf16[128,8,512]{2,1,0:T(8,128)(2,1)}), bf16[128,8,512]{2,1,0:T(8,128)(2,1)S(1)}, u32[]{:S(2)}, u32[]{:S(2)}) %all-to-all-start.1) | async-done | bytes 1048608 | tf_op jit(solution)/shard_map/all_to_all | solution.py:281
  149.3 0.0 copy-done.2
  149.3 1.0 combine_rows.1
  (3 shorter events, 0.1 us)
Async XLA Ops:
  0.6 36.9 %collective-permute-start.1 = (bf16[512,1536]{1,0:T(8,128)(2,1)}, bf16[512,1536]{1,0:T(8,128)(2,1)S(1)}, u32[]{:S(2)}, u32[]{:S(2)}) collective-permute-start(bf16[512,1536]{1,0:T(8,128)(2,1)} %bitcast.13), channel_id=1, source_target_pairs={{0,3},{1,0},{2,1},{3,2},{4,7},{5,4},{6,5},{7,6},{8,11},{9,8},{10,9... | collective-permute-start | bytes 4718600 | tf_op jit(solution)/shard_map/ppermute | solution.py:196
  5.9 35.7 %collective-permute-start = (bf16[512,1536]{1,0:T(8,128)(2,1)}, bf16[512,1536]{1,0:T(8,128)(2,1)S(1)}, u32[]{:S(2)}, u32[]{:S(2)}) collective-permute-start(bf16[512,1536]{1,0:T(8,128)(2,1)} %bitcast.14), channel_id=1, source_target_pairs={{0,1},{1,2},{2,3},{3,0},{4,5},{5,6},{6,7},{7,4},{8,9},{9,10},{10,1... | collective-permute-start | bytes 4718600 | tf_op jit(solution)/shard_map/ppermute | solution.py:196
  12.4 71.2 %all-to-all-start = ((bf16[128,8,1024]{2,1,0:T(8,128)(2,1)}), bf16[128,8,1024]{2,1,0:T(8,128)(2,1)}, u32[]{:S(2)}, u32[]{:S(2)}) async-start(bf16[128,8,1024]{2,1,0:T(8,128)(2,1)} %bitcast.12), calls=%async_computation | async-start | bytes 4194304 | tf_op jit(solution)/shard_map/all_to_all | solution.py:255
  30.8 27.7 %collective-permute-start.5 = (bf16[768,512]{1,0:T(8,128)(2,1)}, bf16[768,512]{1,0:T(8,128)(2,1)S(1)}, u32[]{:S(2)}, u32[]{:S(2)}) collective-permute-start(bf16[768,512]{1,0:T(8,128)(2,1)} %bitcast.17), channel_id=1, source_target_pairs={{0,1},{1,2},{2,3},{3,0},{4,5},{5,6},{6,7},{7,4},{8,9},{9,10},{10,1... | collective-permute-start | bytes 2359304 | tf_op jit(solution)/shard_map/ppermute | solution.py:197
  33.1 27.3 %collective-permute-start.4 = (bf16[768,512]{1,0:T(8,128)(2,1)}, bf16[768,512]{1,0:T(8,128)(2,1)S(1)}, u32[]{:S(2)}, u32[]{:S(2)}) collective-permute-start(bf16[768,512]{1,0:T(8,128)(2,1)} %bitcast.18), channel_id=1, source_target_pairs={{0,3},{1,0},{2,1},{3,2},{4,7},{5,4},{6,5},{7,6},{8,11},{9,8},{10,9... | collective-permute-start | bytes 2359304 | tf_op jit(solution)/shard_map/ppermute | solution.py:197
  41.6 2.2 %copy-start = (bf16[512,1536]{1,0:T(8,128)(2,1)}, bf16[512,1536]{1,0:T(8,128)(2,1)S(1)}, u32[]{:S(2)}) copy-start(bf16[512,1536]{1,0:T(8,128)(2,1)S(1)} %get-tuple-element.13.refs_1_) | copy-start | bytes 4718596
  41.6 2.2 %copy-start.1 = (bf16[512,1536]{1,0:T(8,128)(2,1)}, bf16[512,1536]{1,0:T(8,128)(2,1)S(1)}, u32[]{:S(2)}) copy-start(bf16[512,1536]{1,0:T(8,128)(2,1)S(1)} %get-tuple-element.14.refs_4_) | copy-start | bytes 4718596
  43.8 39.9 %collective-permute-start.2 = (bf16[256,1536]{1,0:T(8,128)(2,1)}, bf16[256,1536]{1,0:T(8,128)(2,1)}, u32[]{:S(2)}, u32[]{:S(2)}) collective-permute-start(bf16[256,1536]{1,0:T(8,128)(2,1)} %slice.12), channel_id=1, source_target_pairs={{0,1},{1,2},{2,3},{3,0},{4,5},{5,6},{6,7},{7,4},{8,9},{9,10},{10,1... | collective-permute-start | bytes 2359304 | tf_op jit(solution)/shard_map/ppermute | solution.py:201
  45.7 37.9 %collective-permute-start.3 = (bf16[256,1536]{1,0:T(8,128)(2,1)}, bf16[256,1536]{1,0:T(8,128)(2,1)S(1)}, u32[]{:S(2)}, u32[]{:S(2)}) collective-permute-start(bf16[256,1536]{1,0:T(8,128)(2,1)} %slice.13), channel_id=1, source_target_pairs={{0,3},{1,0},{2,1},{3,2},{4,7},{5,4},{6,5},{7,6},{8,11},{9,8},{10,9... | collective-permute-start | bytes 2359304 | tf_op jit(solution)/shard_map/ppermute | solution.py:201
  58.4 2.0 %copy-start.3 = (bf16[768,512]{1,0:T(8,128)(2,1)}, bf16[768,512]{1,0:T(8,128)(2,1)S(1)}, u32[]{:S(2)}) copy-start(bf16[768,512]{1,0:T(8,128)(2,1)S(1)} %collective-permute-done.5.refs_9_) | copy-start | bytes 2359300
  58.5 25.1 %collective-permute-start.6 = (bf16[384,512]{1,0:T(8,128)(2,1)S(1)}, bf16[384,512]{1,0:T(8,128)(2,1)S(1)}, u32[]{:S(2)}, u32[]{:S(2)}) collective-permute-start(bf16[384,512]{1,0:T(8,128)(2,1)S(1)} %slice.16), channel_id=1, source_target_pairs={{0,1},{1,2},{2,3},{3,0},{4,5},{5,6},{6,7},{7,4},{8,9},{9,10},{10,1... | collective-permute-start | bytes 1179656 | tf_op jit(solution)/shard_map/ppermute | solution.py:201
  60.4 0.9 copy-start.4
  61.4 22.3 %collective-permute-start.7 = (bf16[384,512]{1,0:T(8,128)(2,1)S(1)}, bf16[384,512]{1,0:T(8,128)(2,1)S(1)}, u32[]{:S(2)}, u32[]{:S(2)}) collective-permute-start(bf16[384,512]{1,0:T(8,128)(2,1)S(1)} %slice.17), channel_id=1, source_target_pairs={{0,3},{1,0},{2,1},{3,2},{4,7},{5,4},{6,5},{7,6},{8,11},{9,8},{10,9... | collective-permute-start | bytes 1179656 | tf_op jit(solution)/shard_map/ppermute | solution.py:201
  83.6 0.9 copy-start.5
  95.0 28.2 %collective-permute-start.8 = (bf16[768,512]{1,0:T(8,128)(2,1)}, bf16[768,512]{1,0:T(8,128)(2,1)}, u32[]{:S(2)}, u32[]{:S(2)}) collective-permute-start(bf16[768,512]{1,0:T(8,128)(2,1)} %get-tuple-element.18), channel_id=1, source_target_pairs={{0,1},{1,2},{2,3},{3,0},{4,5},{5,6},{6,7},{7,4},{8,9},{9,10},{10,1... | collective-permute-start | bytes 2359304 | tf_op jit(solution)/shard_map/ppermute | solution.py:211
  97.0 52.3 %all-to-all-start.1 = ((bf16[128,8,512]{2,1,0:T(8,128)(2,1)}), bf16[128,8,512]{2,1,0:T(8,128)(2,1)S(1)}, u32[]{:S(2)}, u32[]{:S(2)}) async-start(bf16[128,8,512]{2,1,0:T(8,128)(2,1)} %bitcast.16), calls=%async_computation.1 | async-start | bytes 2097152 | tf_op jit(solution)/shard_map/all_to_all | solution.py:281
  118.4 20.8 %collective-permute-start.10 = (bf16[768,512]{1,0:T(8,128)(2,1)S(1)}, bf16[768,512]{1,0:T(8,128)(2,1)S(1)}, u32[]{:S(2)}, u32[]{:S(2)}) collective-permute-start(bf16[768,512]{1,0:T(8,128)(2,1)S(1)} %get-tuple-element.19), channel_id=1, source_target_pairs={{0,3},{1,0},{2,1},{3,2},{4,7},{5,4},{6,5},{7,6},{8,11},{9,8},{10,9... | collective-permute-start | bytes 2359304 | tf_op jit(solution)/shard_map/ppermute | solution.py:221
  124.6 21.0 %collective-permute-start.9 = (bf16[768,512]{1,0:T(8,128)(2,1)S(1)}, bf16[768,512]{1,0:T(8,128)(2,1)S(1)}, u32[]{:S(2)}, u32[]{:S(2)}) collective-permute-start(bf16[768,512]{1,0:T(8,128)(2,1)S(1)} %add_far.1), channel_id=1, source_target_pairs={{0,1},{1,2},{2,3},{3,0},{4,5},{5,6},{6,7},{7,4},{8,9},{9,10},{10,1... | collective-permute-start | bytes 2359304 | tf_op jit(solution)/shard_map/ppermute | solution.py:221
  145.6 3.8 %copy-start.2 = (bf16[1024,96]{1,0:T(8,128)(2,1)S(1)}, bf16[1024,96]{1,0:T(8,128)(2,1)}, u32[]{:S(2)}) copy-start(bf16[1024,96]{1,0:T(8,128)(2,1)} %get-tuple-element.11.pick_ref) | copy-start | bytes 589828

commit v8 on v7

--- a/solution.py
+++ b/solution.py
@@ -12,9 +12,11 @@
 NT = (((1,), (1,)), ((), ()))
 TN = (((0,), (0,)), ((), ()))
 VMEM_LIMIT = 16 * 1024 * 1024
-EXPERT_LIMIT = 50 * 1024 * 1024
+BACK_LIMIT = 16 * 1024 * 1024
+HIDDEN_LIMIT = 44 * 1024 * 1024
 SEND_LIMIT = 56 * 1024 * 1024
 COST = 20 * 10**9
+ADD_COST = 8 * 10**9
 
 
 def whole(memory_space=pltpu.VMEM):
@@ -93,9 +95,9 @@
     return [(own, 0, 0, rows), (right, 1, 0, rows), (far_a, 2, 0, half), (far_b, 2, half, half), (left, 3, 0, rows)]
 
 
-def expert_kernel(quarters, me_ref, recv_ref, *refs):
-    ups, downs, refs = pieces(refs[0], refs[1:5]), pieces(refs[5], refs[6:10]), refs[10:]
-    back_ref, *blocks, recv, w, wd, x_ref, g_ref, hid_ref, to_gate, to_up, gp_ref, hold, out, sems = refs
+def hidden_kernel(quarters, me_ref, recv_ref, *refs):
+    ups, refs = pieces(refs[0], refs[1:5]), refs[5:]
+    to_gate, to_up, g_ref, *blocks, recv, w, x_ref, hid_ref, sems = refs
     rows = 256
     per = rows // quarters
     feat = recv.shape[1] // 2
@@ -113,9 +115,6 @@
                 to = w.at[pl.ds(block * feat + row, size), pl.ds(at, tile)]
                 some.append(start(started, ref.at[:, pl.ds(at, tile)], to, sems))
         columns.append(some)
-    down_came = [
-        start(started, ref, wd.at[pl.ds(row, size), pl.ds(block * feat, feat)], sems) for ref, block, row, size in downs
-    ]
     order = order_matrix(rows, quarters)
     for b in range(recv.shape[0] // rows):
         came[b].wait()
@@ -125,44 +124,61 @@
             at = pl.multiple_of(lax.rem(q + quarters - me_ref[0], quarters) * feat, feat)
             x_ref[here, pl.ds(at, feat)] = got[q * per : q * per + per, :feat]
             g_ref[here, pl.ds(at, feat)] = got[q * per : q * per + per, feat:]
-
-    def pre(cols):
-        return jnp.dot(x_ref[...], w[:, cols], preferred_element_type=F32)
-
-    tile = 256
     for n in range(hidden_units // tile):
         for copy in columns[n]:
             copy.wait()
         cols = slice(n * tile, n * tile + tile)
-        gate = pre(cols)
-        up = pre(slice(hidden_units + n * tile, hidden_units + n * tile + tile))
+        up_cols = slice(hidden_units + n * tile, hidden_units + n * tile + tile)
+        gate = jnp.dot(x_ref[...], w[:, cols], preferred_element_type=F32)
+        up = jnp.dot(x_ref[...], w[:, up_cols], preferred_element_type=F32)
         sig = jax.nn.sigmoid(gate)
         activ = gate * sig
         to_gate[:, cols] = up * sig * (1.0 + gate * (1.0 - sig))
         to_up[:, cols] = activ
         hid_ref[:, cols] = (activ * up).astype(BF16)
-
-    for copy in down_came:
-        copy.wait()
-    for n in range(hidden_units // tile):
-        cols = slice(n * tile, n * tile + tile)
-        total = lax.dot_general(g_ref[...], wd[cols, :], NT, preferred_element_type=F32)
+    for k, ref in enumerate(blocks):
+        ref[...] = lax.dot_general(
+            hid_ref[...], g_ref[:, k * feat : k * feat + feat], TN, preferred_element_type=F32
+        ).astype(BF16)
+
+
+def back_kernel(quarters, me_ref, to_gate, to_up, g, *refs):
+    ups, (own_ref, right, far_a, far_b, left), (back_ref, gp_ref, hold, out, own, sems) = refs[:5], refs[5:10], refs[10:]
+    started = []
+    fetch = start(started, own_ref, own, sems)
+    hidden_units = to_gate.shape[1]
+    feat = out.shape[1]
+    half = hidden_units // 2
+
+    def product(h, k, w):
+        return lax.dot_general(g[:, k * feat : k * feat + feat], w, NT, preferred_element_type=F32)
+
+    sums = []
+    for h, far in enumerate((far_a, far_b)):
+        cols = slice(h * half, h * half + half)
+        sums.append(product(h, 1, right[cols, :]) + product(h, 2, far[...]) + product(h, 3, left[cols, :]))
+    fetch.wait()
+    for h, total in enumerate(sums):
+        cols = slice(h * half, h * half + half)
+        total = total + product(h, 0, own[cols, :])
         gp_ref[:, cols] = (total * to_gate[:, cols]).astype(BF16)
-        gp_ref[:, hidden_units + n * tile : hidden_units + n * tile + tile] = (total * to_up[:, cols]).astype(BF16)
-    for k in range(quarters):
-        hold[lax.rem(me_ref[0] + k, quarters)] = lax.dot_general(
-            gp_ref[...], w[k * feat : k * feat + feat, :], NT, preferred_element_type=F32
+        gp_ref[:, hidden_units + h * half : hidden_units + h * half + half] = (total * to_up[:, cols]).astype(BF16)
+    at = 0
+    for w in ups:
+        size = w.shape[0]
+        hold[lax.rem(me_ref[0] + at // feat, quarters), :, at % feat : at % feat + size] = lax.dot_general(
+            gp_ref[...], w[...], NT, preferred_element_type=F32
         ).astype(BF16)
+        at += size
+    rows = 256
+    per = rows // quarters
+    order = order_matrix(rows, quarters)
     copies = []
     for b in range(back_ref.shape[0] // rows):
         here = pl.ds(b * rows, rows)
         stacked = jnp.concatenate([hold[q, b * per : b * per + per, :] for q in range(quarters)], axis=0)
         out[here, :] = lax.dot_general(order, stacked, TN, preferred_element_type=F32).astype(BF16)
         copies.append(start(started, out.at[here, :], back_ref.at[here, :], sems))
-    for k, ref in enumerate(blocks):
-        ref[...] = lax.dot_general(
-            hid_ref[...], g_ref[:, k * feat : k * feat + feat], TN, preferred_element_type=F32
-        ).astype(BF16)
     for copy in copies:
         copy.wait()
 
@@ -215,7 +231,7 @@
         out_specs=whole(),
         out_shape=jax.ShapeDtypeStruct(right.shape, BF16),
         compiler_params=pltpu.CompilerParams(vmem_limit_bytes=VMEM_LIMIT),
-        cost_estimate=pl.CostEstimate(flops=COST, bytes_accessed=0, transcendentals=0),
+        cost_estimate=pl.CostEstimate(flops=ADD_COST, bytes_accessed=0, transcendentals=0),
         name="add_far",
     )(right, came)
     from_left, from_right = lax.ppermute(right, "edp", ring(size, 1)), lax.ppermute(left, "edp", ring(size, -1))
@@ -254,30 +270,42 @@
     )(expert_ids.T, gate_values.T, tokens, out_grad)
     recv = lax.all_to_all(sent, "ep", split_axis=0, concat_axis=0, tiled=True)
 
-    back, *blocks = pl.pallas_call(
-        functools.partial(expert_kernel, quarters),
-        in_specs=[whole(pltpu.SMEM)] + [whole(pl.ANY)] * 11,
-        out_specs=[whole(pl.ANY)] + [whole()] * parts,
-        out_shape=[jax.ShapeDtypeStruct((rows, feat), BF16)]
+    large = pltpu.CompilerParams(vmem_limit_bytes=HIDDEN_LIMIT)
+    to_gate, to_up, rows_g, *blocks = pl.pallas_call(
+        functools.partial(hidden_kernel, quarters),
+        in_specs=[whole(pltpu.SMEM)] + [whole(pl.ANY)] * 6,
+        out_specs=[whole()] * (3 + parts),
+        out_shape=[jax.ShapeDtypeStruct((slots, hidden_units), F32)] * 2
+        + [jax.ShapeDtypeStruct((slots, width), BF16)]
         + [jax.ShapeDtypeStruct((hidden_units, feat), BF16)] * parts,
         scratch_shapes=[
             pltpu.VMEM((rows, 2 * feat), BF16),
             pltpu.VMEM((width, 2 * hidden_units), BF16),
-            pltpu.VMEM((hidden_units, width), BF16),
-            pltpu.VMEM((slots, width), BF16),
             pltpu.VMEM((slots, width), BF16),
             pltpu.VMEM((slots, hidden_units), BF16),
-            pltpu.VMEM((slots, hidden_units), F32),
-            pltpu.VMEM((slots, hidden_units), F32),
+            pltpu.SemaphoreType.DMA((48,)),
+        ],
+        compiler_params=large,
+        name="hidden_rows",
+    )(me, recv, gate_up_weight[0], *others[:4])
+    down_grad = scatter_two_steps(blocks, parts)[None]
+
+    back = pl.pallas_call(
+        functools.partial(back_kernel, quarters),
+        in_specs=[whole(pltpu.SMEM)] + [whole()] * 8 + [whole(pl.ANY)] + [whole()] * 4,
+        out_specs=whole(pl.ANY),
+        out_shape=jax.ShapeDtypeStruct((rows, feat), BF16),
+        scratch_shapes=[
             pltpu.VMEM((slots, 2 * hidden_units), BF16),
             pltpu.VMEM((quarters, slots, feat), BF16),
             pltpu.VMEM((rows, feat), BF16),
-            pltpu.SemaphoreType.DMA((64,)),
+            pltpu.VMEM((hidden_units, feat), BF16),
+            pltpu.SemaphoreType.DMA((8,)),
         ],
-        compiler_params=pltpu.CompilerParams(vmem_limit_bytes=EXPERT_LIMIT),
-        name="expert_rows",
-    )(me, recv, gate_up_weight[0], *others[:4], down_weight[0], *others[4:])
-    down_grad = scatter_two_steps(blocks, parts)[None]
+        compiler_params=pltpu.CompilerParams(vmem_limit_bytes=BACK_LIMIT),
+        cost_estimate=pl.CostEstimate(flops=COST, bytes_accessed=0, transcendentals=0),
+        name="back_rows",
+    )(me, to_gate, to_up, rows_g, gate_up_weight[0], *others[:4], down_weight[0], *others[4:])
     returned = lax.all_to_all(back, "ep", split_axis=0, concat_axis=0, tiled=True)
     token_grads = pl.pallas_call(
         functools.partial(combine_kernel, toks),

time: 151 us -> 146 us (0.967)
  waiting for transfers between devices: 51.5 us -> 46.1 us
  starting transfers between devices: 75.3 us -> 71.6 us
  Pallas kernels: 17.4 us -> 19.6 us
  local copies, waits for them, and re-layouts: 3.99 us -> 6 us
    ppermute x2, waiting for transfers between devices: 17.7 us -> 6.4 us  [gather_two_steps(): lax.ppermute(left[:half], 'edp', fwd)]
    all_to_all x1, waiting for transfers between devices: 0.01 us -> 9.83 us  [per_device(): recv = lax.all_to_all(sent, 'ep', split_axis=0, concat_axis=0, tiled=True)]
    ppermute x2, starting transfers between devices: 3.83 us -> 10.7 us  [gather_two_steps(): lax.ppermute(left[:half], 'edp', fwd)]
    all_to_all x1, starting transfers between devices: 21.4 us -> 15.2 us  [per_device(): lax.all_to_all(back, 'ep', split_axis=0, concat_axis=0, tiled=True)]
    ppermute x1, waiting for transfers between devices: 4.03 us -> 0.01 us  [gather_two_steps(): lax.ppermute(up, 'edp', fwd)]
    ppermute x2, starting transfers between devices: 9.13 us -> 6.08 us  [gather_two_steps(): lax.ppermute(right[half:], 'edp', bwd)]
    ppermute x1, waiting for transfers between devices: 8.17 us -> 5.53 us  [gather_two_steps(): lax.ppermute(down, 'edp', fwd)]
    pallas_call x1 -> x2, Pallas kernels: 10.5 us -> 12.7 us  [the longest x1 6.92 us: per_device(): pl.pallas_call(functools.partial(hidden_kernel, quarters), in_specs=[whol...]
  transfers between devices with their start and end apart: 13 -> 13, of which waited for: 6 -> 8; matrix products, arithmetic and copies ran while one was open for 2% -> 3% of each run, Pallas kernels for 4% -> 13%
where the time goes in v8:
time: 146 us; the launch traced here: 145 us
  starting transfers between devices  71.6 us (49%)
  waiting for transfers between devices  46.1 us (32%)
  Pallas kernels  19.6 us (13%)
  local copies, waits for them, and re-layouts  6 us (4%)
    all_to_all x1, starting transfers between devices, per_device(): recv = lax.all_to_all(sent, 'ep', split_axis=0, concat_axis=0, tiled=True)  18.8 us
    all_to_all x1, starting transfers between devices, per_device(): lax.all_to_all(back, 'ep', split_axis=0, concat_axis=0, tiled=True)  15.2 us
    ppermute x1, waiting for transfers between devices, scatter_two_steps(): lax.ppermute(left, 'edp', ring(size, -1))  13.6 us
    ppermute x2, starting transfers between devices, gather_two_steps(): lax.ppermute(left[:half], 'edp', fwd)  10.7 us
    all_to_all x1, waiting for transfers between devices, per_device(): recv = lax.all_to_all(sent, 'ep', split_axis=0, concat_axis=0, tiled=True)  9.83 us
    pallas_call x1, Pallas kernels, per_device(): pl.pallas_call(functools.partial(hidden_kernel, quarters), in_specs=[whol...  6.92 us
    ppermute x2, waiting for transfers between devices, gather_two_steps(): lax.ppermute(left[:half], 'edp', fwd)  6.4 us
    ppermute x2, starting transfers between devices, gather_two_steps(): lax.ppermute(right[half:], 'edp', bwd)  6.08 us
  transfers between devices with their start and end apart: 13, of which 8 were waited for; matrix products, arithmetic and copies ran while one was open for 3% of the time, Pallas kernels for 13%

profile of v8, /device:TPU:1, one launch (start us, length us, event | category | flops | bytes accessed | tf_op | source)
XLA Modules:
  0.0 145.4 jit_solution(7217426879826241756)
XLA Ops:
  0.6 4.0 %collective-permute-start = (bf16[512,1536]{1,0:T(8,128)(2,1)}, bf16[512,1536]{1,0:T(8,128)(2,1)S(1)}, u32[]{:S(2)}, u32[]{:S(2)}) collective-permute-start(bf16[512,1536]{1,0:T(8,128)(2,1)} %bitcast.12), channel_id=1, source_target_pairs={{0,1},{1,2},{2,3},{3,0},{4,5},{5,6},{6,7},{7,4},{8,9},{9,10},{10,1... | collective-permute-start | bytes 4718600 | tf_op jit(solution)/shard_map/ppermute | solution.py:212
  4.6 3.2 %collective-permute-start.1 = (bf16[512,1536]{1,0:T(8,128)(2,1)}, bf16[512,1536]{1,0:T(8,128)(2,1)S(1)}, u32[]{:S(2)}, u32[]{:S(2)}) collective-permute-start(bf16[512,1536]{1,0:T(8,128)(2,1)} %bitcast.13), channel_id=1, source_target_pairs={{0,3},{1,0},{2,1},{3,2},{4,7},{5,4},{6,5},{7,6},{8,11},{9,8},{10,9... | collective-permute-start | bytes 4718600 | tf_op jit(solution)/shard_map/ppermute | solution.py:212
  7.8 4.6 %send_rows.1 = (bf16[1024,1024]{1,0:T(8,128)(2,1)}, bf16[1024,96]{1,0:T(8,128)(2,1)}) custom-call(s32[8,24]{1,0:T(8,128)} %bitcast.20, f32[8,24]{1,0:T(8,128)} %bitcast.21, bf16[24,2048]{1,0:T(8,128)(2,1)} %tok_ref.1, bf16[24,2048]{1,0:T(8,128)(2,1)} %grad_ref.1), custom_call_target="tpu_custom_call" | custom-call | tf_op jit(solution)/shard_map/send_rows/pallas_call | solution.py:255
  12.4 18.8 %all-to-all-start = ((bf16[128,8,1024]{2,1,0:T(8,128)(2,1)}), bf16[128,8,1024]{2,1,0:T(8,128)(2,1)}, u32[]{:S(2)}, u32[]{:S(2)}) async-start(bf16[128,8,1024]{2,1,0:T(8,128)(2,1)} %bitcast.19), calls=%async_computation | async-start | bytes 4194304 | tf_op jit(solution)/shard_map/all_to_all | solution.py:271
  31.2 1.9 %collective-permute-start.5 = (bf16[768,512]{1,0:T(8,128)(2,1)}, bf16[768,512]{1,0:T(8,128)(2,1)S(1)}, u32[]{:S(2)}, u32[]{:S(2)}) collective-permute-start(bf16[768,512]{1,0:T(8,128)(2,1)} %bitcast.16), channel_id=1, source_target_pairs={{0,1},{1,2},{2,3},{3,0},{4,5},{5,6},{6,7},{7,4},{8,9},{9,10},{10,1... | collective-permute-start | bytes 2359304 | tf_op jit(solution)/shard_map/ppermute | solution.py:213
  33.1 4.6 %collective-permute-start.4 = (bf16[768,512]{1,0:T(8,128)(2,1)}, bf16[768,512]{1,0:T(8,128)(2,1)S(1)}, u32[]{:S(2)}, u32[]{:S(2)}) collective-permute-start(bf16[768,512]{1,0:T(8,128)(2,1)} %bitcast.17), channel_id=1, source_target_pairs={{0,3},{1,0},{2,1},{3,2},{4,7},{5,4},{6,5},{7,6},{8,11},{9,8},{10,9... | collective-permute-start | bytes 2359304 | tf_op jit(solution)/shard_map/ppermute | solution.py:213
  37.7 0.0 collective-permute-done.refs_0_
  37.7 0.1 collective-permute-done.1.refs_1_
  37.8 1.0 slice.12
  38.8 7.0 %collective-permute-start.2 = (bf16[256,1536]{1,0:T(8,128)(2,1)}, bf16[256,1536]{1,0:T(8,128)(2,1)}, u32[]{:S(2)}, u32[]{:S(2)}) collective-permute-start(bf16[256,1536]{1,0:T(8,128)(2,1)} %slice.12), channel_id=1, source_target_pairs={{0,1},{1,2},{2,3},{3,0},{4,5},{5,6},{6,7},{7,4},{8,9},{9,10},{10,1... | collective-permute-start | bytes 2359304 | tf_op jit(solution)/shard_map/ppermute | solution.py:217
  45.9 1.0 slice.13
  46.8 0.0 copy-done
  46.8 0.0 copy-done.2
  46.8 1.9 %collective-permute-start.3 = (bf16[256,1536]{1,0:T(8,128)(2,1)}, bf16[256,1536]{1,0:T(8,128)(2,1)}, u32[]{:S(2)}, u32[]{:S(2)}) collective-permute-start(bf16[256,1536]{1,0:T(8,128)(2,1)} %slice.13), channel_id=1, source_target_pairs={{0,3},{1,0},{2,1},{3,2},{4,7},{5,4},{6,5},{7,6},{8,11},{9,8},{10,9... | collective-permute-start | bytes 2359304 | tf_op jit(solution)/shard_map/ppermute | solution.py:217
  48.7 5.5 %collective-permute-done.5.refs_9_ = bf16[768,512]{1,0:T(8,128)(2,1)S(1)} collective-permute-done((bf16[768,512]{1,0:T(8,128)(2,1)}, bf16[768,512]{1,0:T(8,128)(2,1)S(1)}, u32[]{:S(2)}, u32[]{:S(2)}) %collective-permute-start.5) | collective-permute-done | bytes 786464 | tf_op jit(solution)/shard_map/ppermute | solution.py:213
  54.3 0.9 copy-done.6
  55.2 3.6 %collective-permute-start.6 = (bf16[384,512]{1,0:T(8,128)(2,1)S(1)}, bf16[384,512]{1,0:T(8,128)(2,1)S(1)}, u32[]{:S(2)}, u32[]{:S(2)}) collective-permute-start(bf16[384,512]{1,0:T(8,128)(2,1)S(1)} %slice.16), channel_id=1, source_target_pairs={{0,1},{1,2},{2,3},{3,0},{4,5},{5,6},{6,7},{7,4},{8,9},{9,10},{10,1... | collective-permute-start | bytes 1179656 | tf_op jit(solution)/shard_map/ppermute | solution.py:217
  58.8 0.0 collective-permute-done.4.refs_6_
  58.8 0.8 slice.17
  59.6 0.9 copy-done.8
  60.5 4.2 %collective-permute-start.7 = (bf16[384,512]{1,0:T(8,128)(2,1)}, bf16[384,512]{1,0:T(8,128)(2,1)}, u32[]{:S(2)}, u32[]{:S(2)}) collective-permute-start(bf16[384,512]{1,0:T(8,128)(2,1)} %slice.17), channel_id=1, source_target_pairs={{0,3},{1,0},{2,1},{3,2},{4,7},{5,4},{6,5},{7,6},{8,11},{9,8},{10,9... | collective-permute-start | bytes 1179656 | tf_op jit(solution)/shard_map/ppermute | solution.py:217
  64.7 6.4 %collective-permute-done.2.refs_2_ = bf16[256,1536]{1,0:T(8,128)(2,1)} collective-permute-done((bf16[256,1536]{1,0:T(8,128)(2,1)}, bf16[256,1536]{1,0:T(8,128)(2,1)}, u32[]{:S(2)}, u32[]{:S(2)}) %collective-permute-start.2) | collective-permute-done | bytes 786464 | tf_op jit(solution)/shard_map/ppermute | solution.py:217
  71.1 1.2 collective-permute-done.3.refs_3_
  72.3 9.8 %all-to-all-done = bf16[128,8,1024]{2,1,0:T(8,128)(2,1)} async-done(((bf16[128,8,1024]{2,1,0:T(8,128)(2,1)}), bf16[128,8,1024]{2,1,0:T(8,128)(2,1)}, u32[]{:S(2)}, u32[]{:S(2)}) %all-to-all-start) | async-done | bytes 2097184 | tf_op jit(solution)/shard_map/all_to_all | solution.py:271
  82.1 1.4 copy-done.4
  83.6 0.0 copy-start.10
  83.6 6.9 %hidden_rows.1 = (f32[256,768]{1,0:T(8,128)S(1)}, f32[256,768]{1,0:T(8,128)S(1)}, bf16[256,2048]{1,0:T(8,128)(2,1)S(1)}, bf16[768,512]{1,0:T(8,128)(2,1)S(1)}, b...) custom-call(s32[1]{0:T(128)} %bitcast.2.me_ref, ...), custom_call_target="tpu_custom_call" | custom-call | tf_op jit(solution)/shard_map/hidden_rows/pallas_call | solution.py:274
  90.5 1.9 %collective-permute-start.8 = (bf16[768,512]{1,0:T(8,128)(2,1)}, bf16[768,512]{1,0:T(8,128)(2,1)}, u32[]{:S(2)}, u32[]{:S(2)}) collective-permute-start(bf16[768,512]{1,0:T(8,128)(2,1)} %get-tuple-element.22), channel_id=1, source_target_pairs={{0,1},{1,2},{2,3},{3,0},{4,5},{5,6},{6,7},{7,4},{8,9},{9,10},{10,1... | collective-permute-start | bytes 2359304 | tf_op jit(solution)/shard_map/ppermute | solution.py:227
  92.4 0.0 collective-permute-done.6.refs_7_
  92.4 0.0 collective-permute-done.7.refs_8_
  92.5 0.0 copy-done.1
  92.5 0.0 copy-done.3
  92.5 0.0 copy-done.7
  92.5 0.0 copy-done.9
  92.5 0.0 copy-done.10
  92.5 5.8 %back_rows.1 = bf16[1024,512]{1,0:T(8,128)(2,1)} custom-call(s32[1]{0:T(128)} %bitcast.2.me_ref, f32[256,768]{1,0:T(8,128)S(1)} %get-tuple-element.17.to_gate, f32[256,768]{1,0:T(8,128)S(1)} %get-tuple-element.18.to_up, bf16[256,2048]{1,0:T(8,128)(2,1)S(1)} %get-tuple-element.19.g, bf16[512,1536]{1,0:T(8,128)(2,1)S(1)} %bitcast.15, ...), custom_call_target="tpu_custom_call" | custom-call | flops 20000000000 | tf_op jit(solution)/shard_map/back_rows/pallas_call | solution.py:293
  98.3 0.0 copy-done.11
  98.3 0.0 copy-start.12
  98.3 15.2 %all-to-all-start.1 = ((bf16[128,8,512]{2,1,0:T(8,128)(2,1)}), bf16[128,8,512]{2,1,0:T(8,128)(2,1)S(1)}, u32[]{:S(2)}, u32[]{:S(2)}) async-start(bf16[128,8,512]{2,1,0:T(8,128)(2,1)} %bitcast.7), calls=%async_computation.1 | async-start | bytes 2097152 | tf_op jit(solution)/shard_map/all_to_all | solution.py:309
  113.5 3.4 %collective-permute-start.10 = (bf16[768,512]{1,0:T(8,128)(2,1)}, bf16[768,512]{1,0:T(8,128)(2,1)S(1)}, u32[]{:S(2)}, u32[]{:S(2)}) collective-permute-start(bf16[768,512]{1,0:T(8,128)(2,1)} %get-tuple-element.23), channel_id=1, source_target_pairs={{0,3},{1,0},{2,1},{3,2},{4,7},{5,4},{6,5},{7,6},{8,11},{9,8},{10,9... | collective-permute-start | bytes 2359304 | tf_op jit(solution)/shard_map/ppermute | solution.py:237
  116.9 0.0 collective-permute-done.8.came
  116.9 1.3 add_far.1
  118.2 1.9 %collective-permute-start.9 = (bf16[768,512]{1,0:T(8,128)(2,1)S(1)}, bf16[768,512]{1,0:T(8,128)(2,1)S(1)}, u32[]{:S(2)}, u32[]{:S(2)}) collective-permute-start(bf16[768,512]{1,0:T(8,128)(2,1)S(1)} %add_far.1), channel_id=1, source_target_pairs={{0,1},{1,2},{2,3},{3,0},{4,5},{5,6},{6,7},{7,4},{8,9},{9,10},{10,1... | collective-permute-start | bytes 2359304 | tf_op jit(solution)/shard_map/ppermute | solution.py:237
  120.2 13.6 %collective-permute-done.10 = bf16[768,512]{1,0:T(8,128)(2,1)S(1)} collective-permute-done((bf16[768,512]{1,0:T(8,128)(2,1)}, bf16[768,512]{1,0:T(8,128)(2,1)S(1)}, u32[]{:S(2)}, u32[]{:S(2)}) %collective-permute-start.10) | collective-permute-done | bytes 786464 | tf_op jit(solution)/shard_map/ppermute | solution.py:237
  133.8 5.4 %collective-permute-done.9 = bf16[768,512]{1,0:T(8,128)(2,1)S(1)} collective-permute-done((bf16[768,512]{1,0:T(8,128)(2,1)S(1)}, bf16[768,512]{1,0:T(8,128)(2,1)S(1)}, u32[]{:S(2)}, u32[]{:S(2)}) %collective-permute-start.9) | collective-permute-done | bytes 786464 | tf_op jit(solution)/shard_map/ppermute | solution.py:237
  139.2 1.2 fusion
  140.4 4.0 %all-to-all-done.1 = bf16[128,8,512]{2,1,0:T(8,128)(2,1)S(1)} async-done(((bf16[128,8,512]{2,1,0:T(8,128)(2,1)}), bf16[128,8,512]{2,1,0:T(8,128)(2,1)S(1)}, u32[]{:S(2)}, u32[]{:S(2)}) %all-to-all-start.1) | async-done | bytes 1048608 | tf_op jit(solution)/shard_map/all_to_all | solution.py:309
  144.4 1.0 combine_rows.1
  (15 shorter events, 0.0 us)
Async XLA Ops:
  0.6 37.1 %collective-permute-start = (bf16[512,1536]{1,0:T(8,128)(2,1)}, bf16[512,1536]{1,0:T(8,128)(2,1)S(1)}, u32[]{:S(2)}, u32[]{:S(2)}) collective-permute-start(bf16[512,1536]{1,0:T(8,128)(2,1)} %bitcast.12), channel_id=1, source_target_pairs={{0,1},{1,2},{2,3},{3,0},{4,5},{5,6},{6,7},{7,4},{8,9},{9,10},{10,1... | collective-permute-start | bytes 4718600 | tf_op jit(solution)/shard_map/ppermute | solution.py:212
  4.6 33.2 %collective-permute-start.1 = (bf16[512,1536]{1,0:T(8,128)(2,1)}, bf16[512,1536]{1,0:T(8,128)(2,1)S(1)}, u32[]{:S(2)}, u32[]{:S(2)}) collective-permute-start(bf16[512,1536]{1,0:T(8,128)(2,1)} %bitcast.13), channel_id=1, source_target_pairs={{0,3},{1,0},{2,1},{3,2},{4,7},{5,4},{6,5},{7,6},{8,11},{9,8},{10,9... | collective-permute-start | bytes 4718600 | tf_op jit(solution)/shard_map/ppermute | solution.py:212
  12.4 69.7 %all-to-all-start = ((bf16[128,8,1024]{2,1,0:T(8,128)(2,1)}), bf16[128,8,1024]{2,1,0:T(8,128)(2,1)}, u32[]{:S(2)}, u32[]{:S(2)}) async-start(bf16[128,8,1024]{2,1,0:T(8,128)(2,1)} %bitcast.19), calls=%async_computation | async-start | bytes 4194304 | tf_op jit(solution)/shard_map/all_to_all | solution.py:271
  31.2 23.0 %collective-permute-start.5 = (bf16[768,512]{1,0:T(8,128)(2,1)}, bf16[768,512]{1,0:T(8,128)(2,1)S(1)}, u32[]{:S(2)}, u32[]{:S(2)}) collective-permute-start(bf16[768,512]{1,0:T(8,128)(2,1)} %bitcast.16), channel_id=1, source_target_pairs={{0,1},{1,2},{2,3},{3,0},{4,5},{5,6},{6,7},{7,4},{8,9},{9,10},{10,1... | collective-permute-start | bytes 2359304 | tf_op jit(solution)/shard_map/ppermute | solution.py:213
  33.1 25.7 %collective-permute-start.4 = (bf16[768,512]{1,0:T(8,128)(2,1)}, bf16[768,512]{1,0:T(8,128)(2,1)S(1)}, u32[]{:S(2)}, u32[]{:S(2)}) collective-permute-start(bf16[768,512]{1,0:T(8,128)(2,1)} %bitcast.17), channel_id=1, source_target_pairs={{0,3},{1,0},{2,1},{3,2},{4,7},{5,4},{6,5},{7,6},{8,11},{9,8},{10,9... | collective-permute-start | bytes 2359304 | tf_op jit(solution)/shard_map/ppermute | solution.py:213
  37.8 9.0 %copy-start = (bf16[512,1536]{1,0:T(8,128)(2,1)}, bf16[512,1536]{1,0:T(8,128)(2,1)S(1)}, u32[]{:S(2)}) copy-start(bf16[512,1536]{1,0:T(8,128)(2,1)S(1)} %get-tuple-element.16.refs_4_) | copy-start | bytes 4718596
  37.8 9.0 %copy-start.2 = (bf16[512,1536]{1,0:T(8,128)(2,1)}, bf16[512,1536]{1,0:T(8,128)(2,1)S(1)}, u32[]{:S(2)}) copy-start(bf16[512,1536]{1,0:T(8,128)(2,1)S(1)} %get-tuple-element.15.refs_1_) | copy-start | bytes 4718596
  38.8 32.3 %collective-permute-start.2 = (bf16[256,1536]{1,0:T(8,128)(2,1)}, bf16[256,1536]{1,0:T(8,128)(2,1)}, u32[]{:S(2)}, u32[]{:S(2)}) collective-permute-start(bf16[256,1536]{1,0:T(8,128)(2,1)} %slice.12), channel_id=1, source_target_pairs={{0,1},{1,2},{2,3},{3,0},{4,5},{5,6},{6,7},{7,4},{8,9},{9,10},{10,1... | collective-permute-start | bytes 2359304 | tf_op jit(solution)/shard_map/ppermute | solution.py:217
  46.8 25.5 %collective-permute-start.3 = (bf16[256,1536]{1,0:T(8,128)(2,1)}, bf16[256,1536]{1,0:T(8,128)(2,1)}, u32[]{:S(2)}, u32[]{:S(2)}) collective-permute-start(bf16[256,1536]{1,0:T(8,128)(2,1)} %slice.13), channel_id=1, source_target_pairs={{0,3},{1,0},{2,1},{3,2},{4,7},{5,4},{6,5},{7,6},{8,11},{9,8},{10,9... | collective-permute-start | bytes 2359304 | tf_op jit(solution)/shard_map/ppermute | solution.py:217
  54.3 0.9 copy-start.6
  55.2 37.2 %collective-permute-start.6 = (bf16[384,512]{1,0:T(8,128)(2,1)S(1)}, bf16[384,512]{1,0:T(8,128)(2,1)S(1)}, u32[]{:S(2)}, u32[]{:S(2)}) collective-permute-start(bf16[384,512]{1,0:T(8,128)(2,1)S(1)} %slice.16), channel_id=1, source_target_pairs={{0,1},{1,2},{2,3},{3,0},{4,5},{5,6},{6,7},{7,4},{8,9},{9,10},{10,1... | collective-permute-start | bytes 1179656 | tf_op jit(solution)/shard_map/ppermute | solution.py:217
  59.6 0.9 copy-start.8
  60.5 31.9 %collective-permute-start.7 = (bf16[384,512]{1,0:T(8,128)(2,1)}, bf16[384,512]{1,0:T(8,128)(2,1)}, u32[]{:S(2)}, u32[]{:S(2)}) collective-permute-start(bf16[384,512]{1,0:T(8,128)(2,1)} %slice.17), channel_id=1, source_target_pairs={{0,3},{1,0},{2,1},{3,2},{4,7},{5,4},{6,5},{7,6},{8,11},{9,8},{10,9... | collective-permute-start | bytes 1179656 | tf_op jit(solution)/shard_map/ppermute | solution.py:217
  82.1 1.4 copy-start.4
  83.5 8.9 %copy-start.1 = (bf16[512,1536]{1,0:T(8,128)(2,1)S(1)}, bf16[512,1536]{1,0:T(8,128)(2,1)}, u32[]{:S(2)}) copy-start(bf16[512,1536]{1,0:T(8,128)(2,1)} %copy-done) | copy-start | bytes 4718596
  83.5 8.9 %copy-start.3 = (bf16[512,1536]{1,0:T(8,128)(2,1)S(1)}, bf16[512,1536]{1,0:T(8,128)(2,1)}, u32[]{:S(2)}) copy-start(bf16[512,1536]{1,0:T(8,128)(2,1)} %copy-done.2) | copy-start | bytes 4718596
  83.5 8.9 %copy-start.7 = (bf16[768,512]{1,0:T(8,128)(2,1)S(1)}, bf16[768,512]{1,0:T(8,128)(2,1)}, u32[]{:S(2)}) copy-start(bf16[768,512]{1,0:T(8,128)(2,1)} %copy-done.6) | copy-start | bytes 2359300
  83.5 8.9 %copy-start.9 = (bf16[768,512]{1,0:T(8,128)(2,1)S(1)}, bf16[768,512]{1,0:T(8,128)(2,1)}, u32[]{:S(2)}) copy-start(bf16[768,512]{1,0:T(8,128)(2,1)} %copy-done.8) | copy-start | bytes 2359300
  83.6 8.9 %copy-start.10 = (bf16[1,768,512]{2,1,0:T(8,128)(2,1)S(1)}, bf16[1,768,512]{2,1,0:T(8,128)(2,1)}, u32[]{:S(2)}) copy-start(bf16[1,768,512]{2,1,0:T(8,128)(2,1)} %param.11) | copy-start | bytes 2359300
  90.5 7.8 %copy-start.11 = (bf16[768,512]{1,0:T(8,128)(2,1)}, bf16[768,512]{1,0:T(8,128)(2,1)S(1)}, u32[]{:S(2)}) copy-start(bf16[768,512]{1,0:T(8,128)(2,1)S(1)} %get-tuple-element.21.block) | copy-start | bytes 2359300
  90.5 26.4 %collective-permute-start.8 = (bf16[768,512]{1,0:T(8,128)(2,1)}, bf16[768,512]{1,0:T(8,128)(2,1)}, u32[]{:S(2)}, u32[]{:S(2)}) collective-permute-start(bf16[768,512]{1,0:T(8,128)(2,1)} %get-tuple-element.22), channel_id=1, source_target_pairs={{0,1},{1,2},{2,3},{3,0},{4,5},{5,6},{6,7},{7,4},{8,9},{9,10},{10,1... | collective-permute-start | bytes 2359304 | tf_op jit(solution)/shard_map/ppermute | solution.py:227
  98.3 18.6 %copy-start.12 = (bf16[768,512]{1,0:T(8,128)(2,1)S(1)}, bf16[768,512]{1,0:T(8,128)(2,1)}, u32[]{:S(2)}) copy-start(bf16[768,512]{1,0:T(8,128)(2,1)} %copy-done.11) | copy-start | bytes 2359300
  98.3 46.1 %all-to-all-start.1 = ((bf16[128,8,512]{2,1,0:T(8,128)(2,1)}), bf16[128,8,512]{2,1,0:T(8,128)(2,1)S(1)}, u32[]{:S(2)}, u32[]{:S(2)}) async-start(bf16[128,8,512]{2,1,0:T(8,128)(2,1)} %bitcast.7), calls=%async_computation.1 | async-start | bytes 2097152 | tf_op jit(solution)/shard_map/all_to_all | solution.py:309
  113.5 20.3 %collective-permute-start.10 = (bf16[768,512]{1,0:T(8,128)(2,1)}, bf16[768,512]{1,0:T(8,128)(2,1)S(1)}, u32[]{:S(2)}, u32[]{:S(2)}) collective-permute-start(bf16[768,512]{1,0:T(8,128)(2,1)} %get-tuple-element.23), channel_id=1, source_target_pairs={{0,3},{1,0},{2,1},{3,2},{4,7},{5,4},{6,5},{7,6},{8,11},{9,8},{10,9... | collective-permute-start | bytes 2359304 | tf_op jit(solution)/shard_map/ppermute | solution.py:237
  118.2 21.0 %collective-permute-start.9 = (bf16[768,512]{1,0:T(8,128)(2,1)S(1)}, bf16[768,512]{1,0:T(8,128)(2,1)S(1)}, u32[]{:S(2)}, u32[]{:S(2)}) collective-permute-start(bf16[768,512]{1,0:T(8,128)(2,1)S(1)} %add_far.1), channel_id=1, source_target_pairs={{0,1},{1,2},{2,3},{3,0},{4,5},{5,6},{6,7},{7,4},{8,9},{9,10},{10,1... | collective-permute-start | bytes 2359304 | tf_op jit(solution)/shard_map/ppermute | solution.py:237
  139.2 5.2 %copy-start.5 = (bf16[1024,96]{1,0:T(8,128)(2,1)S(1)}, bf16[1024,96]{1,0:T(8,128)(2,1)}, u32[]{:S(2)}) copy-start(bf16[1024,96]{1,0:T(8,128)(2,1)} %get-tuple-element.13.pick_ref) | copy-start | bytes 589828

commit v9 on v8

--- a/solution.py
+++ b/solution.py
@@ -13,7 +13,7 @@
 TN = (((0,), (0,)), ((), ()))
 VMEM_LIMIT = 16 * 1024 * 1024
 BACK_LIMIT = 16 * 1024 * 1024
-HIDDEN_LIMIT = 44 * 1024 * 1024
+HIDDEN_LIMIT = 40 * 1024 * 1024
 SEND_LIMIT = 56 * 1024 * 1024
 COST = 20 * 10**9
 ADD_COST = 8 * 10**9
@@ -194,28 +194,38 @@
     return [(i, (i + step) % size) for i in range(size)]
 
 
-def pass_on(a, b):
+def hand_on_kernel(left, right, left_out, right_out, top, bottom, sems):
+    half = top.shape[0]
+    copies = []
+    start(copies, left.at[pl.ds(0, half), :], top, sems)
+    start(copies, right.at[pl.ds(half, half), :], bottom, sems)
+    for copy in copies:
+        copy.wait()
+
+
+def hand_on(left, right):
+    half = jax.ShapeDtypeStruct((left.shape[0] // 2, left.shape[1]), left.dtype)
     return pl.pallas_call(
-        lambda *refs: None,
+        hand_on_kernel,
         in_specs=[whole(pl.ANY)] * 2,
-        out_specs=[whole(pl.ANY)] * 2,
-        out_shape=[jax.ShapeDtypeStruct(a.shape, a.dtype)] * 2,
+        out_specs=[whole(pl.ANY)] * 2 + [whole()] * 2,
+        out_shape=[jax.ShapeDtypeStruct(left.shape, left.dtype)] * 2 + [half] * 2,
         input_output_aliases={0: 0, 1: 1},
+        scratch_shapes=[pltpu.SemaphoreType.DMA((2,))],
         compiler_params=pltpu.CompilerParams(vmem_limit_bytes=VMEM_LIMIT),
         cost_estimate=pl.CostEstimate(flops=COST, bytes_accessed=0, transcendentals=0),
-        name="pass_on",
-    )(a, b)
+        name="hand_on",
+    )(left, right)
 
 
 def gather_two_steps(up, down, size):
     fwd, bwd = ring(size, 1), ring(size, -1)
-    left_up, right_up = pass_on(lax.ppermute(up, "edp", fwd), lax.ppermute(up, "edp", bwd))
+    left_up, right_up, up_top, up_bottom = hand_on(lax.ppermute(up, "edp", fwd), lax.ppermute(up, "edp", bwd))
     left_down, right_down = lax.ppermute(down, "edp", fwd), lax.ppermute(down, "edp", bwd)
-    out = []
-    for left, right in ((left_up, right_up), (left_down, right_down)):
-        half = left.shape[0] // 2
-        out += [right, lax.ppermute(left[:half], "edp", fwd), lax.ppermute(right[half:], "edp", bwd), left]
-    return out
+    half = down.shape[0] // 2
+    far_up = [lax.ppermute(up_top, "edp", fwd), lax.ppermute(up_bottom, "edp", bwd)]
+    far_down = [lax.ppermute(left_down[:half], "edp", fwd), lax.ppermute(right_down[half:], "edp", bwd)]
+    return [right_up, *far_up, left_up], [right_down, *far_down, left_down]
 
 
 def add_kernel(block, came, out):
@@ -249,7 +259,7 @@
     params = pltpu.CompilerParams(vmem_limit_bytes=VMEM_LIMIT)
     me = lax.axis_index("edp").astype(jnp.int32).reshape(1)
 
-    others = gather_two_steps(gate_up_weight[0], down_weight[0], parts)
+    ups, downs = gather_two_steps(gate_up_weight[0], down_weight[0], parts)
 
     tile = 512
     sent, pick = pl.pallas_call(
@@ -287,7 +297,7 @@
         ],
         compiler_params=large,
         name="hidden_rows",
-    )(me, recv, gate_up_weight[0], *others[:4])
+    )(me, recv, gate_up_weight[0], *ups)
     down_grad = scatter_two_steps(blocks, parts)[None]
 
     back = pl.pallas_call(
@@ -305,7 +315,7 @@
         compiler_params=pltpu.CompilerParams(vmem_limit_bytes=BACK_LIMIT),
         cost_estimate=pl.CostEstimate(flops=COST, bytes_accessed=0, transcendentals=0),
         name="back_rows",
-    )(me, to_gate, to_up, rows_g, gate_up_weight[0], *others[:4], down_weight[0], *others[4:])
+    )(me, to_gate, to_up, rows_g, gate_up_weight[0], *ups, down_weight[0], *downs)
     returned = lax.all_to_all(back, "ep", split_axis=0, concat_axis=0, tiled=True)
     token_grads = pl.pallas_call(
         functools.partial(combine_kernel, toks),

time: 146 us -> 147 us (level)
  Pallas kernels: 19.6 us -> 22.9 us
  waiting for transfers between devices: 46.1 us -> 44.5 us
    pallas_call x1, Pallas kernels: 0.01 us -> 2.53 us  [hand_on(): pl.pallas_call(hand_on_kernel, in_specs=[whole(pl.ANY)] * 2, out_specs=[w...]
    pallas_call x1, Pallas kernels: 5.79 us -> 7.48 us  [per_device(): pl.pallas_call(functools.partial(back_kernel, quarters), in_specs=[whole(...]
    unnamed x26 -> x24, local copies, waits for them, and re-layouts: 3.24 us -> 3.28 us
  transfers between devices with their start and end apart: 13 -> 13, of which waited for: 8 -> 8; matrix products, arithmetic and copies ran while one was open for 3% -> 2% of each run, Pallas kernels for 13% -> 15%
where the time goes in v9:
time: 147 us; the launch traced here: 146 us
  starting transfers between devices  71.7 us (49%)
  waiting for transfers between devices  44.5 us (30%)
  Pallas kernels  22.9 us (16%)
  local copies, waits for them, and re-layouts  4.87 us (3%)
    all_to_all x1, starting transfers between devices, per_device(): recv = lax.all_to_all(sent, 'ep', split_axis=0, concat_axis=0, tiled=True)  18.3 us
    all_to_all x1, starting transfers between devices, per_device(): lax.all_to_all(back, 'ep', split_axis=0, concat_axis=0, tiled=True)  15.3 us
    ppermute x1, waiting for transfers between devices, scatter_two_steps(): lax.ppermute(left, 'edp', ring(size, -1))  13.3 us
    all_to_all x1, waiting for transfers between devices, per_device(): recv = lax.all_to_all(sent, 'ep', split_axis=0, concat_axis=0, tiled=True)  10.2 us
    pallas_call x1, Pallas kernels, per_device(): pl.pallas_call(functools.partial(back_kernel, quarters), in_specs=[whole(...  7.48 us
    ppermute x1, starting transfers between devices, gather_two_steps(): lax.ppermute(up_top, 'edp', fwd)  7.03 us
    pallas_call x1, Pallas kernels, per_device(): pl.pallas_call(functools.partial(hidden_kernel, quarters), in_specs=[whol...  5.87 us
    ppermute x1, waiting for transfers between devices, scatter_two_steps(): lax.ppermute(right, 'edp', ring(size, 1))  5.72 us
  transfers between devices with their start and end apart: 13, of which 8 were waited for; matrix products, arithmetic and copies ran while one was open for 2% of the time, Pallas kernels for 15%

profile of v9, /device:TPU:1, one launch (start us, length us, event | category | flops | bytes accessed | tf_op | source)
XLA Modules:
  0.0 146.0 jit_solution(988829746584099054)
XLA Ops:
  0.6 4.0 %collective-permute-start = (bf16[512,1536]{1,0:T(8,128)(2,1)}, bf16[512,1536]{1,0:T(8,128)(2,1)}, u32[]{:S(2)}, u32[]{:S(2)}) collective-permute-start(bf16[512,1536]{1,0:T(8,128)(2,1)} %bitcast.13), channel_id=1, source_target_pairs={{0,1},{1,2},{2,3},{3,0},{4,5},{5,6},{6,7},{7,4},{8,9},{9,10},{10,1... | collective-permute-start | bytes 4718600 | tf_op jit(solution)/shard_map/ppermute | solution.py:223
  4.6 3.2 %collective-permute-start.1 = (bf16[512,1536]{1,0:T(8,128)(2,1)}, bf16[512,1536]{1,0:T(8,128)(2,1)}, u32[]{:S(2)}, u32[]{:S(2)}) collective-permute-start(bf16[512,1536]{1,0:T(8,128)(2,1)} %bitcast.14), channel_id=1, source_target_pairs={{0,3},{1,0},{2,1},{3,2},{4,7},{5,4},{6,5},{7,6},{8,11},{9,8},{10,9... | collective-permute-start | bytes 4718600 | tf_op jit(solution)/shard_map/ppermute | solution.py:223
  7.8 4.6 %send_rows.1 = (bf16[1024,1024]{1,0:T(8,128)(2,1)}, bf16[1024,96]{1,0:T(8,128)(2,1)}) custom-call(s32[8,24]{1,0:T(8,128)} %bitcast.18, f32[8,24]{1,0:T(8,128)} %bitcast.19, bf16[24,2048]{1,0:T(8,128)(2,1)} %tok_ref.1, bf16[24,2048]{1,0:T(8,128)(2,1)} %grad_ref.1), custom_call_target="tpu_custom_call" | custom-call | tf_op jit(solution)/shard_map/send_rows/pallas_call | solution.py:265
  12.4 18.3 %all-to-all-start = ((bf16[128,8,1024]{2,1,0:T(8,128)(2,1)}), bf16[128,8,1024]{2,1,0:T(8,128)(2,1)S(1)}, u32[]{:S(2)}, u32[]{:S(2)}) async-start(bf16[128,8,1024]{2,1,0:T(8,128)(2,1)} %bitcast.17), calls=%async_computation | async-start | bytes 4194304 | tf_op jit(solution)/shard_map/all_to_all | solution.py:281
  30.7 1.9 %collective-permute-start.5 = (bf16[768,512]{1,0:T(8,128)(2,1)}, bf16[768,512]{1,0:T(8,128)(2,1)S(1)}, u32[]{:S(2)}, u32[]{:S(2)}) collective-permute-start(bf16[768,512]{1,0:T(8,128)(2,1)} %bitcast.6.refs_5_), channel_id=1, source_target_pairs={{0,1},{1,2},{2,3},{3,0},{4,5},{5,6},{6,7},{7,4},{8,9},{9,10},{10,1... | collective-permute-start | bytes 2359304 | tf_op jit(solution)/shard_map/ppermute | solution.py:224
  32.7 4.6 %collective-permute-start.4 = (bf16[768,512]{1,0:T(8,128)(2,1)}, bf16[768,512]{1,0:T(8,128)(2,1)S(1)}, u32[]{:S(2)}, u32[]{:S(2)}) collective-permute-start(bf16[768,512]{1,0:T(8,128)(2,1)} %bitcast.6.refs_5_), channel_id=1, source_target_pairs={{0,3},{1,0},{2,1},{3,2},{4,7},{5,4},{6,5},{7,6},{8,11},{9,8},{10,9... | collective-permute-start | bytes 2359304 | tf_op jit(solution)/shard_map/ppermute | solution.py:224
  37.3 0.0 collective-permute-done.left
  37.3 0.6 collective-permute-done.1.right
  37.8 2.5 %hand_on.1 = (bf16[512,1536]{1,0:T(8,128)(2,1)}, bf16[512,1536]{1,0:T(8,128)(2,1)}, bf16[256,1536]{1,0:T(8,128)(2,1)}, bf16[256,1536]{1,0:T(8,128)(2,1)}) custom-call(bf16[512,1536]{1,0:T(8,128)(2,1)} %collective-permute-done.left, bf16[512,1536]{1,0:T(8,128)(2,1)} %collective-permute-done.1.right), custom_call_target="tpu_custom_call", output_to_operand_aliasing={{0}: (0, {}), {1}: (1, {})} | custom-call | flops 20000000000 | tf_op jit(solution)/shard_map/hand_on/pallas_call | solution.py:208
  40.4 7.0 %collective-permute-start.2 = (bf16[256,1536]{1,0:T(8,128)(2,1)}, bf16[256,1536]{1,0:T(8,128)(2,1)S(1)}, u32[]{:S(2)}, u32[]{:S(2)}) collective-permute-start(bf16[256,1536]{1,0:T(8,128)(2,1)} %get-tuple-element.18), channel_id=1, source_target_pairs={{0,1},{1,2},{2,3},{3,0},{4,5},{5,6},{6,7},{7,4},{8,9},{9,10},{10,1... | collective-permute-start | bytes 2359304 | tf_op jit(solution)/shard_map/ppermute | solution.py:226
  47.4 1.9 %collective-permute-start.3 = (bf16[256,1536]{1,0:T(8,128)(2,1)}, bf16[256,1536]{1,0:T(8,128)(2,1)}, u32[]{:S(2)}, u32[]{:S(2)}) collective-permute-start(bf16[256,1536]{1,0:T(8,128)(2,1)} %get-tuple-element.19), channel_id=1, source_target_pairs={{0,3},{1,0},{2,1},{3,2},{4,7},{5,4},{6,5},{7,6},{8,11},{9,8},{10,9... | collective-permute-start | bytes 2359304 | tf_op jit(solution)/shard_map/ppermute | solution.py:226
  49.3 4.3 %collective-permute-done.5.refs_9_ = bf16[768,512]{1,0:T(8,128)(2,1)S(1)} collective-permute-done((bf16[768,512]{1,0:T(8,128)(2,1)}, bf16[768,512]{1,0:T(8,128)(2,1)S(1)}, u32[]{:S(2)}, u32[]{:S(2)}) %collective-permute-start.5) | collective-permute-done | bytes 786464 | tf_op jit(solution)/shard_map/ppermute | solution.py:224
  53.7 0.8 slice.8
  54.5 1.0 copy-done.4
  55.5 4.2 %collective-permute-start.6 = (bf16[384,512]{1,0:T(8,128)(2,1)}, bf16[384,512]{1,0:T(8,128)(2,1)S(1)}, u32[]{:S(2)}, u32[]{:S(2)}) collective-permute-start(bf16[384,512]{1,0:T(8,128)(2,1)} %slice.8), channel_id=1, source_target_pairs={{0,1},{1,2},{2,3},{3,0},{4,5},{5,6},{6,7},{7,4},{8,9},{9,10},{10,1... | collective-permute-start | bytes 1179656 | tf_op jit(solution)/shard_map/ppermute | solution.py:227
  59.7 0.0 collective-permute-done.4.refs_6_
  59.7 0.8 slice.9
  60.5 0.9 copy-done.6
  61.4 4.1 %collective-permute-start.7 = (bf16[384,512]{1,0:T(8,128)(2,1)}, bf16[384,512]{1,0:T(8,128)(2,1)}, u32[]{:S(2)}, u32[]{:S(2)}) collective-permute-start(bf16[384,512]{1,0:T(8,128)(2,1)} %slice.9), channel_id=1, source_target_pairs={{0,3},{1,0},{2,1},{3,2},{4,7},{5,4},{6,5},{7,6},{8,11},{9,8},{10,9... | collective-permute-start | bytes 1179656 | tf_op jit(solution)/shard_map/ppermute | solution.py:227
  65.4 5.1 %collective-permute-done.2.refs_2_ = bf16[256,1536]{1,0:T(8,128)(2,1)S(1)} collective-permute-done((bf16[256,1536]{1,0:T(8,128)(2,1)}, bf16[256,1536]{1,0:T(8,128)(2,1)S(1)}, u32[]{:S(2)}, u32[]{:S(2)}) %collective-permute-start.2) | collective-permute-done | bytes 786464 | tf_op jit(solution)/shard_map/ppermute | solution.py:226
  70.5 1.3 collective-permute-done.3.refs_3_
  71.8 10.2 %all-to-all-done = bf16[128,8,1024]{2,1,0:T(8,128)(2,1)S(1)} async-done(((bf16[128,8,1024]{2,1,0:T(8,128)(2,1)}), bf16[128,8,1024]{2,1,0:T(8,128)(2,1)S(1)}, u32[]{:S(2)}, u32[]{:S(2)}) %all-to-all-start) | async-done | bytes 2097184 | tf_op jit(solution)/shard_map/all_to_all | solution.py:281
  82.0 1.4 copy-done
  83.4 5.9 %hidden_rows.1 = (f32[256,768]{1,0:T(8,128)S(1)}, f32[256,768]{1,0:T(8,128)S(1)}, bf16[256,2048]{1,0:T(8,128)(2,1)S(1)}, bf16[768,512]{1,0:T(8,128)(2,1)S(1)}, b...) custom-call(s32[1]{0:T(128)} %bitcast.2.me_ref, ...), custom_call_target="tpu_custom_call" | custom-call | tf_op jit(solution)/shard_map/hidden_rows/pallas_call | solution.py:284
  89.3 0.0 copy-start.1
  89.3 0.0 copy-start.8
  89.3 0.0 copy-start.10
  89.3 1.9 %collective-permute-start.8 = (bf16[768,512]{1,0:T(8,128)(2,1)}, bf16[768,512]{1,0:T(8,128)(2,1)}, u32[]{:S(2)}, u32[]{:S(2)}) collective-permute-start(bf16[768,512]{1,0:T(8,128)(2,1)} %get-tuple-element.26), channel_id=1, source_target_pairs={{0,1},{1,2},{2,3},{3,0},{4,5},{5,6},{6,7},{7,4},{8,9},{9,10},{10,1... | collective-permute-start | bytes 2359304 | tf_op jit(solution)/shard_map/ppermute | solution.py:237
  91.3 0.0 collective-permute-done.6.refs_7_
  91.3 0.0 collective-permute-done.7.refs_8_
  91.3 0.0 copy-done.5
  91.3 0.0 copy-done.7
  91.3 7.5 %back_rows.1 = bf16[1024,512]{1,0:T(8,128)(2,1)} custom-call(s32[1]{0:T(128)} %bitcast.2.me_ref, f32[256,768]{1,0:T(8,128)S(1)} %get-tuple-element.21.to_gate, f32[256,768]{1,0:T(8,128)S(1)} %get-tuple-element.22.to_up, bf16[256,2048]{1,0:T(8,128)(2,1)S(1)} %get-tuple-element.23.g, bf16[512,1536]{1,0:T(8,128)(2,1)S(1)} %bitcast.16, ...), custom_call_target="tpu_custom_call" | custom-call | flops 20000000000 | tf_op jit(solution)/shard_map/back_rows/pallas_call | solution.py:303
  98.8 0.0 copy-done.1
  98.8 0.0 copy-done.8
  98.8 0.0 copy-done.10
  98.8 0.0 copy-start.9
  98.8 0.0 copy-start.11
  98.9 15.3 %all-to-all-start.1 = ((bf16[128,8,512]{2,1,0:T(8,128)(2,1)}), bf16[128,8,512]{2,1,0:T(8,128)(2,1)S(1)}, u32[]{:S(2)}, u32[]{:S(2)}) async-start(bf16[128,8,512]{2,1,0:T(8,128)(2,1)} %bitcast.7), calls=%async_computation.1 | async-start | bytes 2097152 | tf_op jit(solution)/shard_map/all_to_all | solution.py:319
  114.2 3.4 %collective-permute-start.10 = (bf16[768,512]{1,0:T(8,128)(2,1)S(1)}, bf16[768,512]{1,0:T(8,128)(2,1)S(1)}, u32[]{:S(2)}, u32[]{:S(2)}) collective-permute-start(bf16[768,512]{1,0:T(8,128)(2,1)S(1)} %copy-done.9), channel_id=1, source_target_pairs={{0,3},{1,0},{2,1},{3,2},{4,7},{5,4},{6,5},{7,6},{8,11},{9,8},{10,9... | collective-permute-start | bytes 2359304 | tf_op jit(solution)/shard_map/ppermute | solution.py:247
  117.6 0.0 collective-permute-done.8.came
  117.6 1.4 add_far.1
  119.0 1.9 %collective-permute-start.9 = (bf16[768,512]{1,0:T(8,128)(2,1)S(1)}, bf16[768,512]{1,0:T(8,128)(2,1)S(1)}, u32[]{:S(2)}, u32[]{:S(2)}) collective-permute-start(bf16[768,512]{1,0:T(8,128)(2,1)S(1)} %add_far.1), channel_id=1, source_target_pairs={{0,1},{1,2},{2,3},{3,0},{4,5},{5,6},{6,7},{7,4},{8,9},{9,10},{10,1... | collective-permute-start | bytes 2359304 | tf_op jit(solution)/shard_map/ppermute | solution.py:247
  120.9 13.3 %collective-permute-done.10 = bf16[768,512]{1,0:T(8,128)(2,1)S(1)} collective-permute-done((bf16[768,512]{1,0:T(8,128)(2,1)S(1)}, bf16[768,512]{1,0:T(8,128)(2,1)S(1)}, u32[]{:S(2)}, u32[]{:S(2)}) %collective-permute-start.10) | collective-permute-done | bytes 786464 | tf_op jit(solution)/shard_map/ppermute | solution.py:247
  134.2 5.7 %collective-permute-done.9 = bf16[768,512]{1,0:T(8,128)(2,1)S(1)} collective-permute-done((bf16[768,512]{1,0:T(8,128)(2,1)S(1)}, bf16[768,512]{1,0:T(8,128)(2,1)S(1)}, u32[]{:S(2)}, u32[]{:S(2)}) %collective-permute-start.9) | collective-permute-done | bytes 786464 | tf_op jit(solution)/shard_map/ppermute | solution.py:247
  140.0 1.2 fusion
  141.2 3.9 %all-to-all-done.1 = bf16[128,8,512]{2,1,0:T(8,128)(2,1)S(1)} async-done(((bf16[128,8,512]{2,1,0:T(8,128)(2,1)}), bf16[128,8,512]{2,1,0:T(8,128)(2,1)S(1)}, u32[]{:S(2)}, u32[]{:S(2)}) %all-to-all-start.1) | async-done | bytes 1048608 | tf_op jit(solution)/shard_map/all_to_all | solution.py:319
  145.1 1.0 combine_rows.1
  (11 shorter events, 0.0 us)
Async XLA Ops:
  0.6 36.6 %collective-permute-start = (bf16[512,1536]{1,0:T(8,128)(2,1)}, bf16[512,1536]{1,0:T(8,128)(2,1)}, u32[]{:S(2)}, u32[]{:S(2)}) collective-permute-start(bf16[512,1536]{1,0:T(8,128)(2,1)} %bitcast.13), channel_id=1, source_target_pairs={{0,1},{1,2},{2,3},{3,0},{4,5},{5,6},{6,7},{7,4},{8,9},{9,10},{10,1... | collective-permute-start | bytes 4718600 | tf_op jit(solution)/shard_map/ppermute | solution.py:223
  4.6 33.3 %collective-permute-start.1 = (bf16[512,1536]{1,0:T(8,128)(2,1)}, bf16[512,1536]{1,0:T(8,128)(2,1)}, u32[]{:S(2)}, u32[]{:S(2)}) collective-permute-start(bf16[512,1536]{1,0:T(8,128)(2,1)} %bitcast.14), channel_id=1, source_target_pairs={{0,3},{1,0},{2,1},{3,2},{4,7},{5,4},{6,5},{7,6},{8,11},{9,8},{10,9... | collective-permute-start | bytes 4718600 | tf_op jit(solution)/shard_map/ppermute | solution.py:223
  12.4 69.6 %all-to-all-start = ((bf16[128,8,1024]{2,1,0:T(8,128)(2,1)}), bf16[128,8,1024]{2,1,0:T(8,128)(2,1)S(1)}, u32[]{:S(2)}, u32[]{:S(2)}) async-start(bf16[128,8,1024]{2,1,0:T(8,128)(2,1)} %bitcast.17), calls=%async_computation | async-start | bytes 4194304 | tf_op jit(solution)/shard_map/all_to_all | solution.py:281
  30.7 22.9 %collective-permute-start.5 = (bf16[768,512]{1,0:T(8,128)(2,1)}, bf16[768,512]{1,0:T(8,128)(2,1)S(1)}, u32[]{:S(2)}, u32[]{:S(2)}) collective-permute-start(bf16[768,512]{1,0:T(8,128)(2,1)} %bitcast.6.refs_5_), channel_id=1, source_target_pairs={{0,1},{1,2},{2,3},{3,0},{4,5},{5,6},{6,7},{7,4},{8,9},{9,10},{10,1... | collective-permute-start | bytes 2359304 | tf_op jit(solution)/shard_map/ppermute | solution.py:224
  32.7 27.0 %collective-permute-start.4 = (bf16[768,512]{1,0:T(8,128)(2,1)}, bf16[768,512]{1,0:T(8,128)(2,1)S(1)}, u32[]{:S(2)}, u32[]{:S(2)}) collective-permute-start(bf16[768,512]{1,0:T(8,128)(2,1)} %bitcast.6.refs_5_), channel_id=1, source_target_pairs={{0,3},{1,0},{2,1},{3,2},{4,7},{5,4},{6,5},{7,6},{8,11},{9,8},{10,9... | collective-permute-start | bytes 2359304 | tf_op jit(solution)/shard_map/ppermute | solution.py:224
  40.4 30.2 %collective-permute-start.2 = (bf16[256,1536]{1,0:T(8,128)(2,1)}, bf16[256,1536]{1,0:T(8,128)(2,1)S(1)}, u32[]{:S(2)}, u32[]{:S(2)}) collective-permute-start(bf16[256,1536]{1,0:T(8,128)(2,1)} %get-tuple-element.18), channel_id=1, source_target_pairs={{0,1},{1,2},{2,3},{3,0},{4,5},{5,6},{6,7},{7,4},{8,9},{9,10},{10,1... | collective-permute-start | bytes 2359304 | tf_op jit(solution)/shard_map/ppermute | solution.py:226
  47.4 24.4 %collective-permute-start.3 = (bf16[256,1536]{1,0:T(8,128)(2,1)}, bf16[256,1536]{1,0:T(8,128)(2,1)}, u32[]{:S(2)}, u32[]{:S(2)}) collective-permute-start(bf16[256,1536]{1,0:T(8,128)(2,1)} %get-tuple-element.19), channel_id=1, source_target_pairs={{0,3},{1,0},{2,1},{3,2},{4,7},{5,4},{6,5},{7,6},{8,11},{9,8},{10,9... | collective-permute-start | bytes 2359304 | tf_op jit(solution)/shard_map/ppermute | solution.py:226
  54.5 1.0 copy-start.4
  55.5 35.8 %collective-permute-start.6 = (bf16[384,512]{1,0:T(8,128)(2,1)}, bf16[384,512]{1,0:T(8,128)(2,1)S(1)}, u32[]{:S(2)}, u32[]{:S(2)}) collective-permute-start(bf16[384,512]{1,0:T(8,128)(2,1)} %slice.8), channel_id=1, source_target_pairs={{0,1},{1,2},{2,3},{3,0},{4,5},{5,6},{6,7},{7,4},{8,9},{9,10},{10,1... | collective-permute-start | bytes 1179656 | tf_op jit(solution)/shard_map/ppermute | solution.py:227
  60.5 0.9 copy-start.6
  61.4 29.9 %collective-permute-start.7 = (bf16[384,512]{1,0:T(8,128)(2,1)}, bf16[384,512]{1,0:T(8,128)(2,1)}, u32[]{:S(2)}, u32[]{:S(2)}) collective-permute-start(bf16[384,512]{1,0:T(8,128)(2,1)} %slice.9), channel_id=1, source_target_pairs={{0,3},{1,0},{2,1},{3,2},{4,7},{5,4},{6,5},{7,6},{8,11},{9,8},{10,9... | collective-permute-start | bytes 1179656 | tf_op jit(solution)/shard_map/ppermute | solution.py:227
  82.0 1.4 copy-start
  83.4 7.9 %copy-start.5 = (bf16[768,512]{1,0:T(8,128)(2,1)S(1)}, bf16[768,512]{1,0:T(8,128)(2,1)}, u32[]{:S(2)}) copy-start(bf16[768,512]{1,0:T(8,128)(2,1)} %copy-done.4) | copy-start | bytes 2359300
  83.4 7.9 %copy-start.7 = (bf16[768,512]{1,0:T(8,128)(2,1)S(1)}, bf16[768,512]{1,0:T(8,128)(2,1)}, u32[]{:S(2)}) copy-start(bf16[768,512]{1,0:T(8,128)(2,1)} %copy-done.6) | copy-start | bytes 2359300
  89.3 9.5 %copy-start.1 = (bf16[768,512]{1,0:T(8,128)(2,1)}, bf16[768,512]{1,0:T(8,128)(2,1)S(1)}, u32[]{:S(2)}) copy-start(bf16[768,512]{1,0:T(8,128)(2,1)S(1)} %get-tuple-element.24) | copy-start | bytes 2359300
  89.3 9.5 %copy-start.8 = (bf16[768,512]{1,0:T(8,128)(2,1)}, bf16[768,512]{1,0:T(8,128)(2,1)S(1)}, u32[]{:S(2)}) copy-start(bf16[768,512]{1,0:T(8,128)(2,1)S(1)} %get-tuple-element.27) | copy-start | bytes 2359300
  89.3 9.5 %copy-start.10 = (bf16[768,512]{1,0:T(8,128)(2,1)}, bf16[768,512]{1,0:T(8,128)(2,1)S(1)}, u32[]{:S(2)}) copy-start(bf16[768,512]{1,0:T(8,128)(2,1)S(1)} %get-tuple-element.25.block) | copy-start | bytes 2359300
  89.3 28.2 %collective-permute-start.8 = (bf16[768,512]{1,0:T(8,128)(2,1)}, bf16[768,512]{1,0:T(8,128)(2,1)}, u32[]{:S(2)}, u32[]{:S(2)}) collective-permute-start(bf16[768,512]{1,0:T(8,128)(2,1)} %get-tuple-element.26), channel_id=1, source_target_pairs={{0,1},{1,2},{2,3},{3,0},{4,5},{5,6},{6,7},{7,4},{8,9},{9,10},{10,1... | collective-permute-start | bytes 2359304 | tf_op jit(solution)/shard_map/ppermute | solution.py:237
  98.8 15.3 %copy-start.9 = (bf16[768,512]{1,0:T(8,128)(2,1)S(1)}, bf16[768,512]{1,0:T(8,128)(2,1)}, u32[]{:S(2)}) copy-start(bf16[768,512]{1,0:T(8,128)(2,1)} %copy-done.8) | copy-start | bytes 2359300
  98.8 18.7 %copy-start.11 = (bf16[768,512]{1,0:T(8,128)(2,1)S(1)}, bf16[768,512]{1,0:T(8,128)(2,1)}, u32[]{:S(2)}) copy-start(bf16[768,512]{1,0:T(8,128)(2,1)} %copy-done.10) | copy-start | bytes 2359300
  98.9 46.2 %all-to-all-start.1 = ((bf16[128,8,512]{2,1,0:T(8,128)(2,1)}), bf16[128,8,512]{2,1,0:T(8,128)(2,1)S(1)}, u32[]{:S(2)}, u32[]{:S(2)}) async-start(bf16[128,8,512]{2,1,0:T(8,128)(2,1)} %bitcast.7), calls=%async_computation.1 | async-start | bytes 2097152 | tf_op jit(solution)/shard_map/all_to_all | solution.py:319
  114.2 20.1 %collective-permute-start.10 = (bf16[768,512]{1,0:T(8,128)(2,1)S(1)}, bf16[768,512]{1,0:T(8,128)(2,1)S(1)}, u32[]{:S(2)}, u32[]{:S(2)}) collective-permute-start(bf16[768,512]{1,0:T(8,128)(2,1)S(1)} %copy-done.9), channel_id=1, source_target_pairs={{0,3},{1,0},{2,1},{3,2},{4,7},{5,4},{6,5},{7,6},{8,11},{9,8},{10,9... | collective-permute-start | bytes 2359304 | tf_op jit(solution)/shard_map/ppermute | solution.py:247
  117.6 22.4 %copy-start.2 = (bf16[768,512]{1,0:T(8,128)(2,1)S(1)}, bf16[768,512]{1,0:T(8,128)(2,1)}, u32[]{:S(2)}) copy-start(bf16[768,512]{1,0:T(8,128)(2,1)} %copy-done.1) | copy-start | bytes 2359300
  119.0 21.0 %collective-permute-start.9 = (bf16[768,512]{1,0:T(8,128)(2,1)S(1)}, bf16[768,512]{1,0:T(8,128)(2,1)S(1)}, u32[]{:S(2)}, u32[]{:S(2)}) collective-permute-start(bf16[768,512]{1,0:T(8,128)(2,1)S(1)} %add_far.1), channel_id=1, source_target_pairs={{0,1},{1,2},{2,3},{3,0},{4,5},{5,6},{6,7},{7,4},{8,9},{9,10},{10,1... | collective-permute-start | bytes 2359304 | tf_op jit(solution)/shard_map/ppermute | solution.py:247
  140.0 5.1 %copy-start.3 = (bf16[1024,96]{1,0:T(8,128)(2,1)S(1)}, bf16[1024,96]{1,0:T(8,128)(2,1)}, u32[]{:S(2)}) copy-start(bf16[1024,96]{1,0:T(8,128)(2,1)} %get-tuple-element.15.pick_ref) | copy-start | bytes 589828

commit v10 on v9

--- a/solution.py
+++ b/solution.py
@@ -13,9 +13,10 @@
 TN = (((0,), (0,)), ((), ()))
 VMEM_LIMIT = 16 * 1024 * 1024
 BACK_LIMIT = 16 * 1024 * 1024
-HIDDEN_LIMIT = 40 * 1024 * 1024
+UNPACK_COST = 7 * 10**9
+HIDDEN_LIMIT = 32 * 1024 * 1024
 SEND_LIMIT = 56 * 1024 * 1024
-COST = 20 * 10**9
+COST = 30 * 10**9
 ADD_COST = 8 * 10**9
 
 
@@ -88,49 +89,44 @@
     return copies[-1]
 
 
-def pieces(own, others):
-    right, far_a, far_b, left = others
-    rows = own.shape[0]
-    half = rows // 2
-    return [(own, 0, 0, rows), (right, 1, 0, rows), (far_a, 2, 0, half), (far_b, 2, half, half), (left, 3, 0, rows)]
-
-
-def hidden_kernel(quarters, me_ref, recv_ref, *refs):
-    ups, refs = pieces(refs[0], refs[1:5]), refs[5:]
-    to_gate, to_up, g_ref, *blocks, recv, w, x_ref, hid_ref, sems = refs
+def unpack_kernel(quarters, me_ref, recv_ref, x_ref, g_ref, recv, sems):
     rows = 256
     per = rows // quarters
     feat = recv.shape[1] // 2
-    hidden_units = hid_ref.shape[1]
-    tile = 256
     started = []
-    came, columns = [], []
     for b in range(recv.shape[0] // rows):
         here = pl.ds(b * rows, rows)
-        came.append(start(started, recv_ref.at[here, :], recv.at[here, :], sems))
-    for n in range(hidden_units // tile):
-        some = []
-        for at in (n * tile, hidden_units + n * tile):
-            for ref, block, row, size in ups:
-                to = w.at[pl.ds(block * feat + row, size), pl.ds(at, tile)]
-                some.append(start(started, ref.at[:, pl.ds(at, tile)], to, sems))
-        columns.append(some)
+        start(started, recv_ref.at[here, :], recv.at[here, :], sems)
     order = order_matrix(rows, quarters)
-    for b in range(recv.shape[0] // rows):
-        came[b].wait()
+    for b, copy in enumerate(started):
+        copy.wait()
         got = jnp.dot(order, recv[b * rows : b * rows + rows, :], preferred_element_type=F32).astype(BF16)
         here = slice(b * per, b * per + per)
         for q in range(quarters):
             at = pl.multiple_of(lax.rem(q + quarters - me_ref[0], quarters) * feat, feat)
             x_ref[here, pl.ds(at, feat)] = got[q * per : q * per + per, :feat]
             g_ref[here, pl.ds(at, feat)] = got[q * per : q * per + per, feat:]
+
+
+def hidden_kernel(x_ref, g_ref, own_up, right, far_a, far_b, left, own_down_ref, *refs):
+    to_gate, to_up, *blocks, own_down, hid_ref, sem = refs
+    own_came = pltpu.make_async_copy(own_down_ref, own_down, sem)
+    own_came.start()
+    feat = g_ref.shape[1] // len(blocks)
+    hidden_units = hid_ref.shape[1]
+    tile = 256
+
+    def pre(cols):
+        total, row = None, 0
+        for w in (own_up, right, far_a, far_b, left):
+            term = jnp.dot(x_ref[:, row : row + w.shape[0]], w[:, cols], preferred_element_type=F32)
+            total, row = term if total is None else total + term, row + w.shape[0]
+        return total
+
     for n in range(hidden_units // tile):
-        for copy in columns[n]:
-            copy.wait()
         cols = slice(n * tile, n * tile + tile)
-        up_cols = slice(hidden_units + n * tile, hidden_units + n * tile + tile)
-        gate = jnp.dot(x_ref[...], w[:, cols], preferred_element_type=F32)
-        up = jnp.dot(x_ref[...], w[:, up_cols], preferred_element_type=F32)
+        gate = pre(cols)
+        up = pre(slice(hidden_units + n * tile, hidden_units + n * tile + tile))
         sig = jax.nn.sigmoid(gate)
         activ = gate * sig
         to_gate[:, cols] = up * sig * (1.0 + gate * (1.0 - sig))
@@ -140,12 +136,12 @@
         ref[...] = lax.dot_general(
             hid_ref[...], g_ref[:, k * feat : k * feat + feat], TN, preferred_element_type=F32
         ).astype(BF16)
+    own_came.wait()
 
 
 def back_kernel(quarters, me_ref, to_gate, to_up, g, *refs):
-    ups, (own_ref, right, far_a, far_b, left), (back_ref, gp_ref, hold, out, own, sems) = refs[:5], refs[5:10], refs[10:]
+    ups, (own, right, far_a, far_b, left), (back_ref, gp_ref, hold, out, sems) = refs[:5], refs[5:10], refs[10:]
     started = []
-    fetch = start(started, own_ref, own, sems)
     hidden_units = to_gate.shape[1]
     feat = out.shape[1]
     half = hidden_units // 2
@@ -153,14 +149,10 @@
     def product(h, k, w):
         return lax.dot_general(g[:, k * feat : k * feat + feat], w, NT, preferred_element_type=F32)
 
-    sums = []
     for h, far in enumerate((far_a, far_b)):
         cols = slice(h * half, h * half + half)
-        sums.append(product(h, 1, right[cols, :]) + product(h, 2, far[...]) + product(h, 3, left[cols, :]))
-    fetch.wait()
-    for h, total in enumerate(sums):
-        cols = slice(h * half, h * half + half)
-        total = total + product(h, 0, own[cols, :])
+        total = product(h, 0, own[cols, :]) + product(h, 1, right[cols, :])
+        total = total + product(h, 2, far[...]) + product(h, 3, left[cols, :])
         gp_ref[:, cols] = (total * to_gate[:, cols]).astype(BF16)
         gp_ref[:, hidden_units + h * half : hidden_units + h * half + half] = (total * to_up[:, cols]).astype(BF16)
     at = 0
@@ -280,42 +272,43 @@
     )(expert_ids.T, gate_values.T, tokens, out_grad)
     recv = lax.all_to_all(sent, "ep", split_axis=0, concat_axis=0, tiled=True)
 
-    large = pltpu.CompilerParams(vmem_limit_bytes=HIDDEN_LIMIT)
-    to_gate, to_up, rows_g, *blocks = pl.pallas_call(
-        functools.partial(hidden_kernel, quarters),
-        in_specs=[whole(pltpu.SMEM)] + [whole(pl.ANY)] * 6,
+    rows_x, rows_g = pl.pallas_call(
+        functools.partial(unpack_kernel, quarters),
+        in_specs=[whole(pltpu.SMEM), whole(pl.ANY)],
+        out_specs=[whole()] * 2,
+        out_shape=[jax.ShapeDtypeStruct((slots, width), BF16)] * 2,
+        scratch_shapes=[pltpu.VMEM((rows, 2 * feat), BF16), pltpu.SemaphoreType.DMA((4,))],
+        compiler_params=params,
+        cost_estimate=pl.CostEstimate(flops=UNPACK_COST, bytes_accessed=0, transcendentals=0),
+        name="unpack_rows",
+    )(me, recv)
+    to_gate, to_up, *blocks, own_down = pl.pallas_call(
+        hidden_kernel,
+        in_specs=[whole()] * 7 + [whole(pl.ANY)],
         out_specs=[whole()] * (3 + parts),
         out_shape=[jax.ShapeDtypeStruct((slots, hidden_units), F32)] * 2
-        + [jax.ShapeDtypeStruct((slots, width), BF16)]
-        + [jax.ShapeDtypeStruct((hidden_units, feat), BF16)] * parts,
-        scratch_shapes=[
-            pltpu.VMEM((rows, 2 * feat), BF16),
-            pltpu.VMEM((width, 2 * hidden_units), BF16),
-            pltpu.VMEM((slots, width), BF16),
-            pltpu.VMEM((slots, hidden_units), BF16),
-            pltpu.SemaphoreType.DMA((48,)),
-        ],
-        compiler_params=large,
+        + [jax.ShapeDtypeStruct((hidden_units, feat), BF16)] * (parts + 1),
+        scratch_shapes=[pltpu.VMEM((slots, hidden_units), BF16), pltpu.SemaphoreType.DMA],
+        compiler_params=pltpu.CompilerParams(vmem_limit_bytes=HIDDEN_LIMIT),
         name="hidden_rows",
-    )(me, recv, gate_up_weight[0], *ups)
+    )(rows_x, rows_g, gate_up_weight[0], *ups, down_weight[0])
     down_grad = scatter_two_steps(blocks, parts)[None]
 
     back = pl.pallas_call(
         functools.partial(back_kernel, quarters),
-        in_specs=[whole(pltpu.SMEM)] + [whole()] * 8 + [whole(pl.ANY)] + [whole()] * 4,
+        in_specs=[whole(pltpu.SMEM)] + [whole()] * 13,
         out_specs=whole(pl.ANY),
         out_shape=jax.ShapeDtypeStruct((rows, feat), BF16),
         scratch_shapes=[
             pltpu.VMEM((slots, 2 * hidden_units), BF16),
             pltpu.VMEM((quarters, slots, feat), BF16),
             pltpu.VMEM((rows, feat), BF16),
-            pltpu.VMEM((hidden_units, feat), BF16),
-            pltpu.SemaphoreType.DMA((8,)),
+            pltpu.SemaphoreType.DMA((4,)),
         ],
         compiler_params=pltpu.CompilerParams(vmem_limit_bytes=BACK_LIMIT),
         cost_estimate=pl.CostEstimate(flops=COST, bytes_accessed=0, transcendentals=0),
         name="back_rows",
-    )(me, to_gate, to_up, rows_g, gate_up_weight[0], *ups, down_weight[0], *downs)
+    )(me, to_gate, to_up, rows_g, gate_up_weight[0], *ups, own_down, *downs)
     returned = lax.all_to_all(back, "ep", split_axis=0, concat_axis=0, tiled=True)
     token_grads = pl.pallas_call(
         functools.partial(combine_kernel, toks),

time: 147 us -> 145 us (0.986)
  starting transfers between devices: 71.7 us -> 70.1 us
    all_to_all x1, waiting for transfers between devices: 10.2 us -> 16.6 us  [per_device(): recv = lax.all_to_all(sent, 'ep', split_axis=0, concat_axis=0, tiled=True)]
    ppermute x1, waiting for transfers between devices: 5.12 us -> 0.01 us  [gather_two_steps(): lax.ppermute(up_top, 'edp', fwd)]
    unnamed x24 -> x14, local copies, waits for them, and re-layouts: 3.28 us -> 0.03 us
    all_to_all x1, starting transfers between devices: 15.3 us -> 13.6 us  [per_device(): lax.all_to_all(back, 'ep', split_axis=0, concat_axis=0, tiled=True)]
    pallas_call x1 -> x2, Pallas kernels: 5.87 us -> 7.44 us  [the longest x1 6 us: per_device(): pl.pallas_call(hidden_kernel, in_specs=[whole()] * 7 + [whole(pl.ANY)], o...]
  transfers between devices with their start and end apart: 13 -> 13, of which waited for: 8 -> 6; matrix products, arithmetic and copies ran while one was open for 2% -> 3% of each run, Pallas kernels for 15% -> 16%
where the time goes in v10:
time: 145 us; the launch traced here: 144 us
  starting transfers between devices  70.1 us (48%)
  waiting for transfers between devices  44.4 us (31%)
  Pallas kernels  24 us (17%)
  local copies, waits for them, and re-layouts  3.6 us (2%)
    all_to_all x1, starting transfers between devices, per_device(): recv = lax.all_to_all(sent, 'ep', split_axis=0, concat_axis=0, tiled=True)  18.5 us
    all_to_all x1, waiting for transfers between devices, per_device(): recv = lax.all_to_all(sent, 'ep', split_axis=0, concat_axis=0, tiled=True)  16.6 us
    all_to_all x1, starting transfers between devices, per_device(): lax.all_to_all(back, 'ep', split_axis=0, concat_axis=0, tiled=True)  13.6 us
    ppermute x1, waiting for transfers between devices, scatter_two_steps(): lax.ppermute(left, 'edp', ring(size, -1))  13.4 us
    pallas_call x1, Pallas kernels, per_device(): pl.pallas_call(functools.partial(back_kernel, quarters), in_specs=[whole(...  7.04 us
    ppermute x1, starting transfers between devices, gather_two_steps(): lax.ppermute(up_top, 'edp', fwd)  7.03 us
    pallas_call x1, Pallas kernels, per_device(): pl.pallas_call(hidden_kernel, in_specs=[whole()] * 7 + [whole(pl.ANY)], o...  6 us
    ppermute x1, waiting for transfers between devices, scatter_two_steps(): lax.ppermute(right, 'edp', ring(size, 1))  5.63 us
  transfers between devices with their start and end apart: 13, of which 6 were waited for; matrix products, arithmetic and copies ran while one was open for 3% of the time, Pallas kernels for 16%

profile of v10, /device:TPU:1, one launch (start us, length us, event | category | flops | bytes accessed | tf_op | source)
XLA Modules:
  0.0 144.3 jit_solution(8911389962609705684)
XLA Ops:
  0.6 4.0 %collective-permute-start = (bf16[512,1536]{1,0:T(8,128)(2,1)}, bf16[512,1536]{1,0:T(8,128)(2,1)}, u32[]{:S(2)}, u32[]{:S(2)}) collective-permute-start(bf16[512,1536]{1,0:T(8,128)(2,1)} %bitcast.13), channel_id=1, source_target_pairs={{0,1},{1,2},{2,3},{3,0},{4,5},{5,6},{6,7},{7,4},{8,9},{9,10},{10,1... | collective-permute-start | bytes 4718600 | tf_op jit(solution)/shard_map/ppermute | solution.py:215
  4.6 3.2 %collective-permute-start.1 = (bf16[512,1536]{1,0:T(8,128)(2,1)}, bf16[512,1536]{1,0:T(8,128)(2,1)}, u32[]{:S(2)}, u32[]{:S(2)}) collective-permute-start(bf16[512,1536]{1,0:T(8,128)(2,1)} %bitcast.14), channel_id=1, source_target_pairs={{0,3},{1,0},{2,1},{3,2},{4,7},{5,4},{6,5},{7,6},{8,11},{9,8},{10,9... | collective-permute-start | bytes 4718600 | tf_op jit(solution)/shard_map/ppermute | solution.py:215
  7.8 4.7 %send_rows.1 = (bf16[1024,1024]{1,0:T(8,128)(2,1)}, bf16[1024,96]{1,0:T(8,128)(2,1)}) custom-call(s32[8,24]{1,0:T(8,128)} %bitcast.21, f32[8,24]{1,0:T(8,128)} %bitcast.22, bf16[24,2048]{1,0:T(8,128)(2,1)} %tok_ref.1, bf16[24,2048]{1,0:T(8,128)(2,1)} %grad_ref.1), custom_call_target="tpu_custom_call" | custom-call | tf_op jit(solution)/shard_map/send_rows/pallas_call | solution.py:257
  12.5 18.5 %all-to-all-start = ((bf16[128,8,1024]{2,1,0:T(8,128)(2,1)}), bf16[128,8,1024]{2,1,0:T(8,128)(2,1)S(1)}, u32[]{:S(2)}, u32[]{:S(2)}) async-start(bf16[128,8,1024]{2,1,0:T(8,128)(2,1)} %bitcast.20), calls=%async_computation | async-start | bytes 4194304 | tf_op jit(solution)/shard_map/all_to_all | solution.py:273
  31.0 0.0 copy-done.1
  31.0 1.9 %collective-permute-start.5 = (bf16[768,512]{1,0:T(8,128)(2,1)S(1)}, bf16[768,512]{1,0:T(8,128)(2,1)}, u32[]{:S(2)}, u32[]{:S(2)}) collective-permute-start(bf16[768,512]{1,0:T(8,128)(2,1)S(1)} %bitcast.17), channel_id=1, source_target_pairs={{0,1},{1,2},{2,3},{3,0},{4,5},{5,6},{6,7},{7,4},{8,9},{9,10},{10,1... | collective-permute-start | bytes 2359304 | tf_op jit(solution)/shard_map/ppermute | solution.py:216
  32.9 4.6 %collective-permute-start.4 = (bf16[768,512]{1,0:T(8,128)(2,1)S(1)}, bf16[768,512]{1,0:T(8,128)(2,1)}, u32[]{:S(2)}, u32[]{:S(2)}) collective-permute-start(bf16[768,512]{1,0:T(8,128)(2,1)S(1)} %bitcast.18), channel_id=1, source_target_pairs={{0,3},{1,0},{2,1},{3,2},{4,7},{5,4},{6,5},{7,6},{8,11},{9,8},{10,9... | collective-permute-start | bytes 2359304 | tf_op jit(solution)/shard_map/ppermute | solution.py:216
  37.5 0.0 collective-permute-done.left
  37.5 0.3 collective-permute-done.1.right
  37.8 2.5 %hand_on.1 = (bf16[512,1536]{1,0:T(8,128)(2,1)}, bf16[512,1536]{1,0:T(8,128)(2,1)}, bf16[256,1536]{1,0:T(8,128)(2,1)}, bf16[256,1536]{1,0:T(8,128)(2,1)}) custom-call(bf16[512,1536]{1,0:T(8,128)(2,1)} %collective-permute-done.left, bf16[512,1536]{1,0:T(8,128)(2,1)} %collective-permute-done.1.right), custom_call_target="tpu_custom_call", output_to_operand_aliasing={{0}: (0, {}), {1}: (1, {})} | custom-call | flops 30000001024 | tf_op jit(solution)/shard_map/hand_on/pallas_call | solution.py:200
  40.4 7.0 %collective-permute-start.2 = (bf16[256,1536]{1,0:T(8,128)(2,1)}, bf16[256,1536]{1,0:T(8,128)(2,1)}, u32[]{:S(2)}, u32[]{:S(2)}) collective-permute-start(bf16[256,1536]{1,0:T(8,128)(2,1)} %get-tuple-element.22), channel_id=1, source_target_pairs={{0,1},{1,2},{2,3},{3,0},{4,5},{5,6},{6,7},{7,4},{8,9},{9,10},{10,1... | collective-permute-start | bytes 2359304 | tf_op jit(solution)/shard_map/ppermute | solution.py:218
  47.4 1.9 %collective-permute-start.3 = (bf16[256,1536]{1,0:T(8,128)(2,1)}, bf16[256,1536]{1,0:T(8,128)(2,1)}, u32[]{:S(2)}, u32[]{:S(2)}) collective-permute-start(bf16[256,1536]{1,0:T(8,128)(2,1)} %get-tuple-element.23), channel_id=1, source_target_pairs={{0,3},{1,0},{2,1},{3,2},{4,7},{5,4},{6,5},{7,6},{8,11},{9,8},{10,9... | collective-permute-start | bytes 2359304 | tf_op jit(solution)/shard_map/ppermute | solution.py:218
  49.4 4.5 %collective-permute-done.5.refs_9_ = bf16[768,512]{1,0:T(8,128)(2,1)} collective-permute-done((bf16[768,512]{1,0:T(8,128)(2,1)S(1)}, bf16[768,512]{1,0:T(8,128)(2,1)}, u32[]{:S(2)}, u32[]{:S(2)}) %collective-permute-start.5) | collective-permute-done | bytes 786464 | tf_op jit(solution)/shard_map/ppermute | solution.py:216
  53.8 1.8 %slice.8 = bf16[384,512]{1,0:T(8,128)(2,1)} slice(bf16[768,512]{1,0:T(8,128)(2,1)} %collective-permute-done.5.refs_9_), slice={[0:384], [0:512]} | slice | bytes 786432 | tf_op jit(solution)/shard_map/slice | solution.py:219
  55.6 4.0 %collective-permute-start.6 = (bf16[384,512]{1,0:T(8,128)(2,1)}, bf16[384,512]{1,0:T(8,128)(2,1)S(1)}, u32[]{:S(2)}, u32[]{:S(2)}) collective-permute-start(bf16[384,512]{1,0:T(8,128)(2,1)} %slice.8), channel_id=1, source_target_pairs={{0,1},{1,2},{2,3},{3,0},{4,5},{5,6},{6,7},{7,4},{8,9},{9,10},{10,1... | collective-permute-start | bytes 1179656 | tf_op jit(solution)/shard_map/ppermute | solution.py:219
  59.6 0.0 collective-permute-done.4.refs_6_
  59.6 1.8 %slice.9 = bf16[384,512]{1,0:T(8,128)(2,1)} slice(bf16[768,512]{1,0:T(8,128)(2,1)} %collective-permute-done.4.refs_6_), slice={[384:768], [0:512]} | slice | bytes 786432 | tf_op jit(solution)/shard_map/slice | solution.py:219
  61.4 4.3 %collective-permute-start.7 = (bf16[384,512]{1,0:T(8,128)(2,1)}, bf16[384,512]{1,0:T(8,128)(2,1)}, u32[]{:S(2)}, u32[]{:S(2)}) collective-permute-start(bf16[384,512]{1,0:T(8,128)(2,1)} %slice.9), channel_id=1, source_target_pairs={{0,3},{1,0},{2,1},{3,2},{4,7},{5,4},{6,5},{7,6},{8,11},{9,8},{10,9... | collective-permute-start | bytes 1179656 | tf_op jit(solution)/shard_map/ppermute | solution.py:219
  65.7 16.6 %all-to-all-done = bf16[128,8,1024]{2,1,0:T(8,128)(2,1)S(1)} async-done(((bf16[128,8,1024]{2,1,0:T(8,128)(2,1)}), bf16[128,8,1024]{2,1,0:T(8,128)(2,1)S(1)}, u32[]{:S(2)}, u32[]{:S(2)}) %all-to-all-start) | async-done | bytes 2097184 | tf_op jit(solution)/shard_map/all_to_all | solution.py:273
  82.2 0.0 copy-start
  82.2 1.4 unpack_rows.1
  83.7 0.0 collective-permute-done.2.far_a.refs_2_
  83.7 0.0 collective-permute-done.3.far_b.refs_3_
  83.7 0.0 copy-done
  83.7 6.0 %hidden_rows.1 = (f32[256,768]{1,0:T(8,128)S(1)}, f32[256,768]{1,0:T(8,128)S(1)}, bf16[768,512]{1,0:T(8,128)(2,1)S(1)}, bf16[768,512]{1,0:T(8,128)(2,1)S(1)}, bf...) custom-call(bf16[256,2048]{1,0:T(8,128)(2,1)S(1)} %get-tuple-element.19.x_ref, ...), custom_call_target="tpu_custom_call" | custom-call | tf_op jit(solution)/shard_map/hidden_rows/pallas_call | solution.py:285
  89.7 0.0 copy-start.3
  89.7 0.0 copy-start.5
  89.8 1.9 %collective-permute-start.8 = (bf16[768,512]{1,0:T(8,128)(2,1)}, bf16[768,512]{1,0:T(8,128)(2,1)}, u32[]{:S(2)}, u32[]{:S(2)}) collective-permute-start(bf16[768,512]{1,0:T(8,128)(2,1)} %get-tuple-element.30), channel_id=1, source_target_pairs={{0,1},{1,2},{2,3},{3,0},{4,5},{5,6},{6,7},{7,4},{8,9},{9,10},{10,1... | collective-permute-start | bytes 2359304 | tf_op jit(solution)/shard_map/ppermute | solution.py:229
  91.7 0.0 collective-permute-done.6.refs_7_
  91.7 0.0 collective-permute-done.7.refs_8_
  91.7 7.0 %back_rows.1 = bf16[1024,512]{1,0:T(8,128)(2,1)} custom-call(s32[1]{0:T(128)} %bitcast.2.me_ref, f32[256,768]{1,0:T(8,128)S(1)} %get-tuple-element.25.to_gate, f32[256,768]{1,0:T(8,128)S(1)} %get-tuple-element.26.to_up, bf16[256,2048]{1,0:T(8,128)(2,1)S(1)} %get-tuple-element.20.g_ref.g, bf16[512,1536]{1,0:T(8,128)(2,1)S(1)} %bitcast.16, ...), custom_call_target="tpu_custom_call" | custom-call | flops 30000001024 | tf_op jit(solution)/shard_map/back_rows/pallas_call | solution.py:297
  98.8 0.0 copy-done.3
  98.8 0.0 copy-done.5
  98.8 0.0 copy-start.4
  98.8 0.0 copy-start.6
  98.8 13.6 %all-to-all-start.1 = ((bf16[128,8,512]{2,1,0:T(8,128)(2,1)}), bf16[128,8,512]{2,1,0:T(8,128)(2,1)S(1)}, u32[]{:S(2)}, u32[]{:S(2)}) async-start(bf16[128,8,512]{2,1,0:T(8,128)(2,1)} %bitcast.7), calls=%async_computation.1 | async-start | bytes 2097152 | tf_op jit(solution)/shard_map/all_to_all | solution.py:312
  112.4 0.0 copy-done.4
  112.4 3.4 %collective-permute-start.10 = (bf16[768,512]{1,0:T(8,128)(2,1)S(1)}, bf16[768,512]{1,0:T(8,128)(2,1)S(1)}, u32[]{:S(2)}, u32[]{:S(2)}) collective-permute-start(bf16[768,512]{1,0:T(8,128)(2,1)S(1)} %copy-done.4), channel_id=1, source_target_pairs={{0,3},{1,0},{2,1},{3,2},{4,7},{5,4},{6,5},{7,6},{8,11},{9,8},{10,9... | collective-permute-start | bytes 2359304 | tf_op jit(solution)/shard_map/ppermute | solution.py:239
  115.8 0.0 collective-permute-done.8.came
  115.8 0.0 copy-done.6
  115.8 1.3 add_far.1
  117.1 1.9 %collective-permute-start.9 = (bf16[768,512]{1,0:T(8,128)(2,1)S(1)}, bf16[768,512]{1,0:T(8,128)(2,1)S(1)}, u32[]{:S(2)}, u32[]{:S(2)}) collective-permute-start(bf16[768,512]{1,0:T(8,128)(2,1)S(1)} %add_far.1), channel_id=1, source_target_pairs={{0,1},{1,2},{2,3},{3,0},{4,5},{5,6},{6,7},{7,4},{8,9},{9,10},{10,1... | collective-permute-start | bytes 2359304 | tf_op jit(solution)/shard_map/ppermute | solution.py:239
  119.1 13.4 %collective-permute-done.10 = bf16[768,512]{1,0:T(8,128)(2,1)S(1)} collective-permute-done((bf16[768,512]{1,0:T(8,128)(2,1)S(1)}, bf16[768,512]{1,0:T(8,128)(2,1)S(1)}, u32[]{:S(2)}, u32[]{:S(2)}) %collective-permute-start.10) | collective-permute-done | bytes 786464 | tf_op jit(solution)/shard_map/ppermute | solution.py:239
  132.5 5.6 %collective-permute-done.9 = bf16[768,512]{1,0:T(8,128)(2,1)S(1)} collective-permute-done((bf16[768,512]{1,0:T(8,128)(2,1)S(1)}, bf16[768,512]{1,0:T(8,128)(2,1)S(1)}, u32[]{:S(2)}, u32[]{:S(2)}) %collective-permute-start.9) | collective-permute-done | bytes 786464 | tf_op jit(solution)/shard_map/ppermute | solution.py:239
  138.1 1.2 fusion
  139.3 4.0 %all-to-all-done.1 = bf16[128,8,512]{2,1,0:T(8,128)(2,1)S(1)} async-done(((bf16[128,8,512]{2,1,0:T(8,128)(2,1)}), bf16[128,8,512]{2,1,0:T(8,128)(2,1)S(1)}, u32[]{:S(2)}, u32[]{:S(2)}) %all-to-all-start.1) | async-done | bytes 1048608 | tf_op jit(solution)/shard_map/all_to_all | solution.py:312
  143.3 0.0 copy-done.2
  143.3 1.0 combine_rows.1
  (2 shorter events, 0.0 us)
Async XLA Ops:
  0.6 36.9 %collective-permute-start = (bf16[512,1536]{1,0:T(8,128)(2,1)}, bf16[512,1536]{1,0:T(8,128)(2,1)}, u32[]{:S(2)}, u32[]{:S(2)}) collective-permute-start(bf16[512,1536]{1,0:T(8,128)(2,1)} %bitcast.13), channel_id=1, source_target_pairs={{0,1},{1,2},{2,3},{3,0},{4,5},{5,6},{6,7},{7,4},{8,9},{9,10},{10,1... | collective-permute-start | bytes 4718600 | tf_op jit(solution)/shard_map/ppermute | solution.py:215
  4.6 33.3 %collective-permute-start.1 = (bf16[512,1536]{1,0:T(8,128)(2,1)}, bf16[512,1536]{1,0:T(8,128)(2,1)}, u32[]{:S(2)}, u32[]{:S(2)}) collective-permute-start(bf16[512,1536]{1,0:T(8,128)(2,1)} %bitcast.14), channel_id=1, source_target_pairs={{0,3},{1,0},{2,1},{3,2},{4,7},{5,4},{6,5},{7,6},{8,11},{9,8},{10,9... | collective-permute-start | bytes 4718600 | tf_op jit(solution)/shard_map/ppermute | solution.py:215
  12.5 18.5 %copy-start.1 = (bf16[1,768,512]{2,1,0:T(8,128)(2,1)S(1)}, bf16[1,768,512]{2,1,0:T(8,128)(2,1)}, u32[]{:S(2)}) copy-start(bf16[1,768,512]{2,1,0:T(8,128)(2,1)} %param.11) | copy-start | bytes 2359300
  12.5 69.7 %all-to-all-start = ((bf16[128,8,1024]{2,1,0:T(8,128)(2,1)}), bf16[128,8,1024]{2,1,0:T(8,128)(2,1)S(1)}, u32[]{:S(2)}, u32[]{:S(2)}) async-start(bf16[128,8,1024]{2,1,0:T(8,128)(2,1)} %bitcast.20), calls=%async_computation | async-start | bytes 4194304 | tf_op jit(solution)/shard_map/all_to_all | solution.py:273
  31.0 22.8 %collective-permute-start.5 = (bf16[768,512]{1,0:T(8,128)(2,1)S(1)}, bf16[768,512]{1,0:T(8,128)(2,1)}, u32[]{:S(2)}, u32[]{:S(2)}) collective-permute-start(bf16[768,512]{1,0:T(8,128)(2,1)S(1)} %bitcast.17), channel_id=1, source_target_pairs={{0,1},{1,2},{2,3},{3,0},{4,5},{5,6},{6,7},{7,4},{8,9},{9,10},{10,1... | collective-permute-start | bytes 2359304 | tf_op jit(solution)/shard_map/ppermute | solution.py:216
  32.9 26.7 %collective-permute-start.4 = (bf16[768,512]{1,0:T(8,128)(2,1)S(1)}, bf16[768,512]{1,0:T(8,128)(2,1)}, u32[]{:S(2)}, u32[]{:S(2)}) collective-permute-start(bf16[768,512]{1,0:T(8,128)(2,1)S(1)} %bitcast.18), channel_id=1, source_target_pairs={{0,3},{1,0},{2,1},{3,2},{4,7},{5,4},{6,5},{7,6},{8,11},{9,8},{10,9... | collective-permute-start | bytes 2359304 | tf_op jit(solution)/shard_map/ppermute | solution.py:216
  40.4 43.3 %collective-permute-start.2 = (bf16[256,1536]{1,0:T(8,128)(2,1)}, bf16[256,1536]{1,0:T(8,128)(2,1)}, u32[]{:S(2)}, u32[]{:S(2)}) collective-permute-start(bf16[256,1536]{1,0:T(8,128)(2,1)} %get-tuple-element.22), channel_id=1, source_target_pairs={{0,1},{1,2},{2,3},{3,0},{4,5},{5,6},{6,7},{7,4},{8,9},{9,10},{10,1... | collective-permute-start | bytes 2359304 | tf_op jit(solution)/shard_map/ppermute | solution.py:218
  47.4 36.3 %collective-permute-start.3 = (bf16[256,1536]{1,0:T(8,128)(2,1)}, bf16[256,1536]{1,0:T(8,128)(2,1)}, u32[]{:S(2)}, u32[]{:S(2)}) collective-permute-start(bf16[256,1536]{1,0:T(8,128)(2,1)} %get-tuple-element.23), channel_id=1, source_target_pairs={{0,3},{1,0},{2,1},{3,2},{4,7},{5,4},{6,5},{7,6},{8,11},{9,8},{10,9... | collective-permute-start | bytes 2359304 | tf_op jit(solution)/shard_map/ppermute | solution.py:218
  55.6 36.1 %collective-permute-start.6 = (bf16[384,512]{1,0:T(8,128)(2,1)}, bf16[384,512]{1,0:T(8,128)(2,1)S(1)}, u32[]{:S(2)}, u32[]{:S(2)}) collective-permute-start(bf16[384,512]{1,0:T(8,128)(2,1)} %slice.8), channel_id=1, source_target_pairs={{0,1},{1,2},{2,3},{3,0},{4,5},{5,6},{6,7},{7,4},{8,9},{9,10},{10,1... | collective-permute-start | bytes 1179656 | tf_op jit(solution)/shard_map/ppermute | solution.py:219
  61.4 30.3 %collective-permute-start.7 = (bf16[384,512]{1,0:T(8,128)(2,1)}, bf16[384,512]{1,0:T(8,128)(2,1)}, u32[]{:S(2)}, u32[]{:S(2)}) collective-permute-start(bf16[384,512]{1,0:T(8,128)(2,1)} %slice.9), channel_id=1, source_target_pairs={{0,3},{1,0},{2,1},{3,2},{4,7},{5,4},{6,5},{7,6},{8,11},{9,8},{10,9... | collective-permute-start | bytes 1179656 | tf_op jit(solution)/shard_map/ppermute | solution.py:219
  82.2 1.5 %copy-start = (bf16[1,512,1536]{2,1,0:T(8,128)(2,1)S(1)}, bf16[1,512,1536]{2,1,0:T(8,128)(2,1)}, u32[]{:S(2)}) copy-start(bf16[1,512,1536]{2,1,0:T(8,128)(2,1)} %param.10) | copy-start | bytes 4718596
  89.7 9.0 %copy-start.3 = (bf16[768,512]{1,0:T(8,128)(2,1)}, bf16[768,512]{1,0:T(8,128)(2,1)S(1)}, u32[]{:S(2)}) copy-start(bf16[768,512]{1,0:T(8,128)(2,1)S(1)} %get-tuple-element.31) | copy-start | bytes 2359300
  89.7 9.0 %copy-start.5 = (bf16[768,512]{1,0:T(8,128)(2,1)}, bf16[768,512]{1,0:T(8,128)(2,1)S(1)}, u32[]{:S(2)}) copy-start(bf16[768,512]{1,0:T(8,128)(2,1)S(1)} %get-tuple-element.29.block) | copy-start | bytes 2359300
  89.8 26.0 %collective-permute-start.8 = (bf16[768,512]{1,0:T(8,128)(2,1)}, bf16[768,512]{1,0:T(8,128)(2,1)}, u32[]{:S(2)}, u32[]{:S(2)}) collective-permute-start(bf16[768,512]{1,0:T(8,128)(2,1)} %get-tuple-element.30), channel_id=1, source_target_pairs={{0,1},{1,2},{2,3},{3,0},{4,5},{5,6},{6,7},{7,4},{8,9},{9,10},{10,1... | collective-permute-start | bytes 2359304 | tf_op jit(solution)/shard_map/ppermute | solution.py:229
  98.8 13.6 %copy-start.4 = (bf16[768,512]{1,0:T(8,128)(2,1)S(1)}, bf16[768,512]{1,0:T(8,128)(2,1)}, u32[]{:S(2)}) copy-start(bf16[768,512]{1,0:T(8,128)(2,1)} %copy-done.3) | copy-start | bytes 2359300
  98.8 17.0 %copy-start.6 = (bf16[768,512]{1,0:T(8,128)(2,1)S(1)}, bf16[768,512]{1,0:T(8,128)(2,1)}, u32[]{:S(2)}) copy-start(bf16[768,512]{1,0:T(8,128)(2,1)} %copy-done.5) | copy-start | bytes 2359300
  98.8 44.5 %all-to-all-start.1 = ((bf16[128,8,512]{2,1,0:T(8,128)(2,1)}), bf16[128,8,512]{2,1,0:T(8,128)(2,1)S(1)}, u32[]{:S(2)}, u32[]{:S(2)}) async-start(bf16[128,8,512]{2,1,0:T(8,128)(2,1)} %bitcast.7), calls=%async_computation.1 | async-start | bytes 2097152 | tf_op jit(solution)/shard_map/all_to_all | solution.py:312
  112.4 20.1 %collective-permute-start.10 = (bf16[768,512]{1,0:T(8,128)(2,1)S(1)}, bf16[768,512]{1,0:T(8,128)(2,1)S(1)}, u32[]{:S(2)}, u32[]{:S(2)}) collective-permute-start(bf16[768,512]{1,0:T(8,128)(2,1)S(1)} %copy-done.4), channel_id=1, source_target_pairs={{0,3},{1,0},{2,1},{3,2},{4,7},{5,4},{6,5},{7,6},{8,11},{9,8},{10,9... | collective-permute-start | bytes 2359304 | tf_op jit(solution)/shard_map/ppermute | solution.py:239
  117.1 21.0 %collective-permute-start.9 = (bf16[768,512]{1,0:T(8,128)(2,1)S(1)}, bf16[768,512]{1,0:T(8,128)(2,1)S(1)}, u32[]{:S(2)}, u32[]{:S(2)}) collective-permute-start(bf16[768,512]{1,0:T(8,128)(2,1)S(1)} %add_far.1), channel_id=1, source_target_pairs={{0,1},{1,2},{2,3},{3,0},{4,5},{5,6},{6,7},{7,4},{8,9},{9,10},{10,1... | collective-permute-start | bytes 2359304 | tf_op jit(solution)/shard_map/ppermute | solution.py:239
  138.1 5.2 %copy-start.2 = (bf16[1024,96]{1,0:T(8,128)(2,1)S(1)}, bf16[1024,96]{1,0:T(8,128)(2,1)}, u32[]{:S(2)}) copy-start(bf16[1024,96]{1,0:T(8,128)(2,1)} %get-tuple-element.17.pick_ref) | copy-start | bytes 589828

commit v11 on v10

--- a/solution.py
+++ b/solution.py
@@ -12,7 +12,7 @@
 NT = (((1,), (1,)), ((), ()))
 TN = (((0,), (0,)), ((), ()))
 VMEM_LIMIT = 16 * 1024 * 1024
-BACK_LIMIT = 16 * 1024 * 1024
+BACK_LIMIT = 24 * 1024 * 1024
 UNPACK_COST = 7 * 10**9
 HIDDEN_LIMIT = 32 * 1024 * 1024
 SEND_LIMIT = 56 * 1024 * 1024
@@ -108,19 +108,36 @@
             g_ref[here, pl.ds(at, feat)] = got[q * per : q * per + per, feat:]
 
 
-def hidden_kernel(x_ref, g_ref, own_up, right, far_a, far_b, left, own_down_ref, *refs):
-    to_gate, to_up, *blocks, own_down, hid_ref, sem = refs
-    own_came = pltpu.make_async_copy(own_down_ref, own_down, sem)
-    own_came.start()
+def fetch(refs, holds, sems):
+    copies = [pltpu.make_async_copy(ref, hold, sems.at[i]) for i, (ref, hold) in enumerate(zip(refs, holds))]
+    for copy in copies:
+        copy.start()
+    waited = set()
+
+    def get(i):
+        if i not in waited:
+            waited.add(i)
+            copies[i].wait()
+        return holds[i]
+
+    return get
+
+
+def hidden_kernel(x_ref, g_ref, own_up, *refs):
+    to_gate, to_up, *blocks, own_down = refs[5:12]
+    hid_ref, *holds, sems = refs[12:]
+    get = fetch(refs[:5], [*holds, own_down], sems)
     feat = g_ref.shape[1] // len(blocks)
     hidden_units = hid_ref.shape[1]
     tile = 256
 
     def pre(cols):
-        total, row = None, 0
-        for w in (own_up, right, far_a, far_b, left):
-            term = jnp.dot(x_ref[:, row : row + w.shape[0]], w[:, cols], preferred_element_type=F32)
-            total, row = term if total is None else total + term, row + w.shape[0]
+        row = own_up.shape[0]
+        total = jnp.dot(x_ref[:, :row], own_up[:, cols], preferred_element_type=F32)
+        for i in range(len(holds)):
+            w = get(i)
+            total = total + jnp.dot(x_ref[:, row : row + w.shape[0]], w[:, cols], preferred_element_type=F32)
+            row += w.shape[0]
         return total
 
     for n in range(hidden_units // tile):
@@ -136,11 +153,12 @@
         ref[...] = lax.dot_general(
             hid_ref[...], g_ref[:, k * feat : k * feat + feat], TN, preferred_element_type=F32
         ).astype(BF16)
-    own_came.wait()
+    get(len(holds))
 
 
 def back_kernel(quarters, me_ref, to_gate, to_up, g, *refs):
-    ups, (own, right, far_a, far_b, left), (back_ref, gp_ref, hold, out, sems) = refs[:5], refs[5:10], refs[10:]
+    own_up, own, others, (back_ref, gp_ref, hold, out, *holds, sems, got_sems) = refs[0], refs[1], refs[2:10], refs[10:]
+    get = fetch(others, holds, got_sems)
     started = []
     hidden_units = to_gate.shape[1]
     feat = out.shape[1]
@@ -149,14 +167,16 @@
     def product(h, k, w):
         return lax.dot_general(g[:, k * feat : k * feat + feat], w, NT, preferred_element_type=F32)
 
-    for h, far in enumerate((far_a, far_b)):
+    sums = [product(h, 0, own[h * half : h * half + half, :]) for h in range(2)]
+    for h in range(2):
         cols = slice(h * half, h * half + half)
-        total = product(h, 0, own[cols, :]) + product(h, 1, right[cols, :])
-        total = total + product(h, 2, far[...]) + product(h, 3, left[cols, :])
+        total = sums[h] + product(h, 1, get(0)[cols, :])
+        total = total + product(h, 2, get(1 + h)[...]) + product(h, 3, get(3)[cols, :])
         gp_ref[:, cols] = (total * to_gate[:, cols]).astype(BF16)
         gp_ref[:, hidden_units + h * half : hidden_units + h * half + half] = (total * to_up[:, cols]).astype(BF16)
     at = 0
-    for w in ups:
+    for i in range(5):
+        w = get(3 + i) if i else own_up
         size = w.shape[0]
         hold[lax.rem(me_ref[0] + at // feat, quarters), :, at % feat : at % feat + size] = lax.dot_general(
             gp_ref[...], w[...], NT, preferred_element_type=F32
@@ -284,11 +304,13 @@
     )(me, recv)
     to_gate, to_up, *blocks, own_down = pl.pallas_call(
         hidden_kernel,
-        in_specs=[whole()] * 7 + [whole(pl.ANY)],
+        in_specs=[whole()] * 3 + [whole(pl.ANY)] * 5,
         out_specs=[whole()] * (3 + parts),
         out_shape=[jax.ShapeDtypeStruct((slots, hidden_units), F32)] * 2
         + [jax.ShapeDtypeStruct((hidden_units, feat), BF16)] * (parts + 1),
-        scratch_shapes=[pltpu.VMEM((slots, hidden_units), BF16), pltpu.SemaphoreType.DMA],
+        scratch_shapes=[pltpu.VMEM((slots, hidden_units), BF16)]
+        + [pltpu.VMEM(x.shape, BF16) for x in ups]
+        + [pltpu.SemaphoreType.DMA((5,))],
         compiler_params=pltpu.CompilerParams(vmem_limit_bytes=HIDDEN_LIMIT),
         name="hidden_rows",
     )(rows_x, rows_g, gate_up_weight[0], *ups, down_weight[0])
@@ -296,19 +318,20 @@
 
     back = pl.pallas_call(
         functools.partial(back_kernel, quarters),
-        in_specs=[whole(pltpu.SMEM)] + [whole()] * 13,
+        in_specs=[whole(pltpu.SMEM)] + [whole()] * 5 + [whole(pl.ANY)] * 8,
         out_specs=whole(pl.ANY),
         out_shape=jax.ShapeDtypeStruct((rows, feat), BF16),
         scratch_shapes=[
             pltpu.VMEM((slots, 2 * hidden_units), BF16),
             pltpu.VMEM((quarters, slots, feat), BF16),
             pltpu.VMEM((rows, feat), BF16),
-            pltpu.SemaphoreType.DMA((4,)),
-        ],
+        ]
+        + [pltpu.VMEM(x.shape, BF16) for x in (*downs, *ups)]
+        + [pltpu.SemaphoreType.DMA((4,)), pltpu.SemaphoreType.DMA((8,))],
         compiler_params=pltpu.CompilerParams(vmem_limit_bytes=BACK_LIMIT),
         cost_estimate=pl.CostEstimate(flops=COST, bytes_accessed=0, transcendentals=0),
         name="back_rows",
-    )(me, to_gate, to_up, rows_g, gate_up_weight[0], *ups, own_down, *downs)
+    )(me, to_gate, to_up, rows_g, gate_up_weight[0], own_down, *downs, *ups)
     returned = lax.all_to_all(back, "ep", split_axis=0, concat_axis=0, tiled=True)
     token_grads = pl.pallas_call(
         functools.partial(combine_kernel, toks),

time: 145 us -> 145 us (level)
  no operation moved by 1% of the time
where the time goes in v11:
time: 145 us; the launch traced here: 144 us
  starting transfers between devices  70.1 us (48%)
  waiting for transfers between devices  44.4 us (31%)
  Pallas kernels  23.7 us (16%)
  local copies, waits for them, and re-layouts  3.6 us (2%)
    all_to_all x1, starting transfers between devices, per_device(): recv = lax.all_to_all(sent, 'ep', split_axis=0, concat_axis=0, tiled=True)  18.5 us
    all_to_all x1, waiting for transfers between devices, per_device(): recv = lax.all_to_all(sent, 'ep', split_axis=0, concat_axis=0, tiled=True)  16.6 us
    all_to_all x1, starting transfers between devices, per_device(): lax.all_to_all(back, 'ep', split_axis=0, concat_axis=0, tiled=True)  13.6 us
    ppermute x1, waiting for transfers between devices, scatter_two_steps(): lax.ppermute(left, 'edp', ring(size, -1))  13.4 us
    ppermute x1, starting transfers between devices, gather_two_steps(): lax.ppermute(up_top, 'edp', fwd)  7.03 us
    pallas_call x1, Pallas kernels, per_device(): pl.pallas_call(functools.partial(back_kernel, quarters), in_specs=[whole(...  6.73 us
    pallas_call x1, Pallas kernels, per_device(): pl.pallas_call(hidden_kernel, in_specs=[whole()] * 3 + [whole(pl.ANY)] *...  5.98 us
    ppermute x1, waiting for transfers between devices, scatter_two_steps(): lax.ppermute(right, 'edp', ring(size, 1))  5.63 us
  transfers between devices with their start and end apart: 13, of which 6 were waited for; matrix products, arithmetic and copies ran while one was open for 3% of the time, Pallas kernels for 16%

profile of v11, /device:TPU:1, one launch (start us, length us, event | category | flops | bytes accessed | tf_op | source)
XLA Modules:
  0.0 143.9 jit_solution(1050006322651560416)
XLA Ops:
  0.6 4.0 %collective-permute-start = (bf16[512,1536]{1,0:T(8,128)(2,1)}, bf16[512,1536]{1,0:T(8,128)(2,1)}, u32[]{:S(2)}, u32[]{:S(2)}) collective-permute-start(bf16[512,1536]{1,0:T(8,128)(2,1)} %bitcast.13), channel_id=1, source_target_pairs={{0,1},{1,2},{2,3},{3,0},{4,5},{5,6},{6,7},{7,4},{8,9},{9,10},{10,1... | collective-permute-start | bytes 4718600 | tf_op jit(solution)/shard_map/ppermute | solution.py:235
  4.6 3.2 %collective-permute-start.1 = (bf16[512,1536]{1,0:T(8,128)(2,1)}, bf16[512,1536]{1,0:T(8,128)(2,1)}, u32[]{:S(2)}, u32[]{:S(2)}) collective-permute-start(bf16[512,1536]{1,0:T(8,128)(2,1)} %bitcast.14), channel_id=1, source_target_pairs={{0,3},{1,0},{2,1},{3,2},{4,7},{5,4},{6,5},{7,6},{8,11},{9,8},{10,9... | collective-permute-start | bytes 4718600 | tf_op jit(solution)/shard_map/ppermute | solution.py:235
  7.8 4.7 %send_rows.1 = (bf16[1024,1024]{1,0:T(8,128)(2,1)}, bf16[1024,96]{1,0:T(8,128)(2,1)}) custom-call(s32[8,24]{1,0:T(8,128)} %bitcast.21, f32[8,24]{1,0:T(8,128)} %bitcast.22, bf16[24,2048]{1,0:T(8,128)(2,1)} %tok_ref.1, bf16[24,2048]{1,0:T(8,128)(2,1)} %grad_ref.1), custom_call_target="tpu_custom_call" | custom-call | tf_op jit(solution)/shard_map/send_rows/pallas_call | solution.py:277
  12.5 18.5 %all-to-all-start = ((bf16[128,8,1024]{2,1,0:T(8,128)(2,1)}), bf16[128,8,1024]{2,1,0:T(8,128)(2,1)S(1)}, u32[]{:S(2)}, u32[]{:S(2)}) async-start(bf16[128,8,1024]{2,1,0:T(8,128)(2,1)} %bitcast.20), calls=%async_computation | async-start | bytes 4194304 | tf_op jit(solution)/shard_map/all_to_all | solution.py:293
  31.0 0.0 copy-done.1
  31.0 1.9 %collective-permute-start.5 = (bf16[768,512]{1,0:T(8,128)(2,1)S(1)}, bf16[768,512]{1,0:T(8,128)(2,1)}, u32[]{:S(2)}, u32[]{:S(2)}) collective-permute-start(bf16[768,512]{1,0:T(8,128)(2,1)S(1)} %bitcast.17), channel_id=1, source_target_pairs={{0,1},{1,2},{2,3},{3,0},{4,5},{5,6},{6,7},{7,4},{8,9},{9,10},{10,1... | collective-permute-start | bytes 2359304 | tf_op jit(solution)/shard_map/ppermute | solution.py:236
  32.9 4.6 %collective-permute-start.4 = (bf16[768,512]{1,0:T(8,128)(2,1)S(1)}, bf16[768,512]{1,0:T(8,128)(2,1)}, u32[]{:S(2)}, u32[]{:S(2)}) collective-permute-start(bf16[768,512]{1,0:T(8,128)(2,1)S(1)} %bitcast.18), channel_id=1, source_target_pairs={{0,3},{1,0},{2,1},{3,2},{4,7},{5,4},{6,5},{7,6},{8,11},{9,8},{10,9... | collective-permute-start | bytes 2359304 | tf_op jit(solution)/shard_map/ppermute | solution.py:236
  37.5 0.0 collective-permute-done.left
  37.5 0.3 collective-permute-done.1.right
  37.8 2.5 %hand_on.1 = (bf16[512,1536]{1,0:T(8,128)(2,1)}, bf16[512,1536]{1,0:T(8,128)(2,1)}, bf16[256,1536]{1,0:T(8,128)(2,1)}, bf16[256,1536]{1,0:T(8,128)(2,1)}) custom-call(bf16[512,1536]{1,0:T(8,128)(2,1)} %collective-permute-done.left, bf16[512,1536]{1,0:T(8,128)(2,1)} %collective-permute-done.1.right), custom_call_target="tpu_custom_call", output_to_operand_aliasing={{0}: (0, {}), {1}: (1, {})} | custom-call | flops 30000001024 | tf_op jit(solution)/shard_map/hand_on/pallas_call | solution.py:220
  40.4 7.0 %collective-permute-start.2 = (bf16[256,1536]{1,0:T(8,128)(2,1)}, bf16[256,1536]{1,0:T(8,128)(2,1)}, u32[]{:S(2)}, u32[]{:S(2)}) collective-permute-start(bf16[256,1536]{1,0:T(8,128)(2,1)} %get-tuple-element.22), channel_id=1, source_target_pairs={{0,1},{1,2},{2,3},{3,0},{4,5},{5,6},{6,7},{7,4},{8,9},{9,10},{10,1... | collective-permute-start | bytes 2359304 | tf_op jit(solution)/shard_map/ppermute | solution.py:238
  47.4 1.9 %collective-permute-start.3 = (bf16[256,1536]{1,0:T(8,128)(2,1)}, bf16[256,1536]{1,0:T(8,128)(2,1)}, u32[]{:S(2)}, u32[]{:S(2)}) collective-permute-start(bf16[256,1536]{1,0:T(8,128)(2,1)} %get-tuple-element.23), channel_id=1, source_target_pairs={{0,3},{1,0},{2,1},{3,2},{4,7},{5,4},{6,5},{7,6},{8,11},{9,8},{10,9... | collective-permute-start | bytes 2359304 | tf_op jit(solution)/shard_map/ppermute | solution.py:238
  49.4 4.5 %collective-permute-done.5.refs_5_ = bf16[768,512]{1,0:T(8,128)(2,1)} collective-permute-done((bf16[768,512]{1,0:T(8,128)(2,1)S(1)}, bf16[768,512]{1,0:T(8,128)(2,1)}, u32[]{:S(2)}, u32[]{:S(2)}) %collective-permute-start.5) | collective-permute-done | bytes 786464 | tf_op jit(solution)/shard_map/ppermute | solution.py:236
  53.8 1.8 %slice.8 = bf16[384,512]{1,0:T(8,128)(2,1)} slice(bf16[768,512]{1,0:T(8,128)(2,1)} %collective-permute-done.5.refs_5_), slice={[0:384], [0:512]} | slice | bytes 786432 | tf_op jit(solution)/shard_map/slice | solution.py:239
  55.6 4.0 %collective-permute-start.6 = (bf16[384,512]{1,0:T(8,128)(2,1)}, bf16[384,512]{1,0:T(8,128)(2,1)S(1)}, u32[]{:S(2)}, u32[]{:S(2)}) collective-permute-start(bf16[384,512]{1,0:T(8,128)(2,1)} %slice.8), channel_id=1, source_target_pairs={{0,1},{1,2},{2,3},{3,0},{4,5},{5,6},{6,7},{7,4},{8,9},{9,10},{10,1... | collective-permute-start | bytes 1179656 | tf_op jit(solution)/shard_map/ppermute | solution.py:239
  59.6 0.0 collective-permute-done.4.refs_2_
  59.6 1.8 %slice.9 = bf16[384,512]{1,0:T(8,128)(2,1)} slice(bf16[768,512]{1,0:T(8,128)(2,1)} %collective-permute-done.4.refs_2_), slice={[384:768], [0:512]} | slice | bytes 786432 | tf_op jit(solution)/shard_map/slice | solution.py:239
  61.4 4.3 %collective-permute-start.7 = (bf16[384,512]{1,0:T(8,128)(2,1)}, bf16[384,512]{1,0:T(8,128)(2,1)}, u32[]{:S(2)}, u32[]{:S(2)}) collective-permute-start(bf16[384,512]{1,0:T(8,128)(2,1)} %slice.9), channel_id=1, source_target_pairs={{0,3},{1,0},{2,1},{3,2},{4,7},{5,4},{6,5},{7,6},{8,11},{9,8},{10,9... | collective-permute-start | bytes 1179656 | tf_op jit(solution)/shard_map/ppermute | solution.py:239
  65.7 16.6 %all-to-all-done = bf16[128,8,1024]{2,1,0:T(8,128)(2,1)S(1)} async-done(((bf16[128,8,1024]{2,1,0:T(8,128)(2,1)}), bf16[128,8,1024]{2,1,0:T(8,128)(2,1)S(1)}, u32[]{:S(2)}, u32[]{:S(2)}) %all-to-all-start) | async-done | bytes 2097184 | tf_op jit(solution)/shard_map/all_to_all | solution.py:293
  82.2 0.0 copy-start
  82.2 1.4 unpack_rows.1
  83.7 0.0 collective-permute-done.2.refs_1_.refs_7_
  83.7 0.0 collective-permute-done.3.refs_2_.refs_8_
  83.7 0.0 copy-done
  83.7 6.0 %hidden_rows.1 = (f32[256,768]{1,0:T(8,128)S(1)}, f32[256,768]{1,0:T(8,128)S(1)}, bf16[768,512]{1,0:T(8,128)(2,1)S(1)}, bf16[768,512]{1,0:T(8,128)(2,1)S(1)}, bf...) custom-call(bf16[256,2048]{1,0:T(8,128)(2,1)S(1)} %get-tuple-element.19.x_ref, ...), custom_call_target="tpu_custom_call" | custom-call | tf_op jit(solution)/shard_map/hidden_rows/pallas_call | solution.py:305
  89.7 0.0 copy-start.3
  89.7 0.0 copy-start.5
  89.7 1.9 %collective-permute-start.8 = (bf16[768,512]{1,0:T(8,128)(2,1)}, bf16[768,512]{1,0:T(8,128)(2,1)}, u32[]{:S(2)}, u32[]{:S(2)}) collective-permute-start(bf16[768,512]{1,0:T(8,128)(2,1)} %get-tuple-element.30), channel_id=1, source_target_pairs={{0,1},{1,2},{2,3},{3,0},{4,5},{5,6},{6,7},{7,4},{8,9},{9,10},{10,1... | collective-permute-start | bytes 2359304 | tf_op jit(solution)/shard_map/ppermute | solution.py:249
  91.7 0.0 collective-permute-done.6.refs_3_
  91.7 0.0 collective-permute-done.7.refs_4_
  91.7 6.7 %back_rows.1 = bf16[1024,512]{1,0:T(8,128)(2,1)} custom-call(s32[1]{0:T(128)} %bitcast.2.me_ref, f32[256,768]{1,0:T(8,128)S(1)} %get-tuple-element.25.to_gate, f32[256,768]{1,0:T(8,128)S(1)} %get-tuple-element.26.to_up, bf16[256,2048]{1,0:T(8,128)(2,1)S(1)} %get-tuple-element.20.g_ref.g, bf16[512,1536]{1,0:T(8,128)(2,1)S(1)} %bitcast.16, ...), custom_call_target="tpu_custom_call" | custom-call | flops 30000001024 | tf_op jit(solution)/shard_map/back_rows/pallas_call | solution.py:319
  98.4 0.0 copy-done.3
  98.4 0.0 copy-done.5
  98.4 0.0 copy-start.4
  98.4 0.0 copy-start.6
  98.5 13.6 %all-to-all-start.1 = ((bf16[128,8,512]{2,1,0:T(8,128)(2,1)}), bf16[128,8,512]{2,1,0:T(8,128)(2,1)S(1)}, u32[]{:S(2)}, u32[]{:S(2)}) async-start(bf16[128,8,512]{2,1,0:T(8,128)(2,1)} %bitcast.7), calls=%async_computation.1 | async-start | bytes 2097152 | tf_op jit(solution)/shard_map/all_to_all | solution.py:335
  112.1 0.0 copy-done.4
  112.1 3.4 %collective-permute-start.10 = (bf16[768,512]{1,0:T(8,128)(2,1)S(1)}, bf16[768,512]{1,0:T(8,128)(2,1)S(1)}, u32[]{:S(2)}, u32[]{:S(2)}) collective-permute-start(bf16[768,512]{1,0:T(8,128)(2,1)S(1)} %copy-done.4), channel_id=1, source_target_pairs={{0,3},{1,0},{2,1},{3,2},{4,7},{5,4},{6,5},{7,6},{8,11},{9,8},{10,9... | collective-permute-start | bytes 2359304 | tf_op jit(solution)/shard_map/ppermute | solution.py:259
  115.5 0.0 collective-permute-done.8.came
  115.5 0.0 copy-done.6
  115.5 1.3 add_far.1
  116.8 1.9 %collective-permute-start.9 = (bf16[768,512]{1,0:T(8,128)(2,1)S(1)}, bf16[768,512]{1,0:T(8,128)(2,1)S(1)}, u32[]{:S(2)}, u32[]{:S(2)}) collective-permute-start(bf16[768,512]{1,0:T(8,128)(2,1)S(1)} %add_far.1), channel_id=1, source_target_pairs={{0,1},{1,2},{2,3},{3,0},{4,5},{5,6},{6,7},{7,4},{8,9},{9,10},{10,1... | collective-permute-start | bytes 2359304 | tf_op jit(solution)/shard_map/ppermute | solution.py:259
  118.7 13.4 %collective-permute-done.10 = bf16[768,512]{1,0:T(8,128)(2,1)S(1)} collective-permute-done((bf16[768,512]{1,0:T(8,128)(2,1)S(1)}, bf16[768,512]{1,0:T(8,128)(2,1)S(1)}, u32[]{:S(2)}, u32[]{:S(2)}) %collective-permute-start.10) | collective-permute-done | bytes 786464 | tf_op jit(solution)/shard_map/ppermute | solution.py:259
  132.1 5.6 %collective-permute-done.9 = bf16[768,512]{1,0:T(8,128)(2,1)S(1)} collective-permute-done((bf16[768,512]{1,0:T(8,128)(2,1)S(1)}, bf16[768,512]{1,0:T(8,128)(2,1)S(1)}, u32[]{:S(2)}, u32[]{:S(2)}) %collective-permute-start.9) | collective-permute-done | bytes 786464 | tf_op jit(solution)/shard_map/ppermute | solution.py:259
  137.8 1.2 fusion
  139.0 4.0 %all-to-all-done.1 = bf16[128,8,512]{2,1,0:T(8,128)(2,1)S(1)} async-done(((bf16[128,8,512]{2,1,0:T(8,128)(2,1)}), bf16[128,8,512]{2,1,0:T(8,128)(2,1)S(1)}, u32[]{:S(2)}, u32[]{:S(2)}) %all-to-all-start.1) | async-done | bytes 1048608 | tf_op jit(solution)/shard_map/all_to_all | solution.py:335
  143.0 0.0 copy-done.2
  143.0 1.0 combine_rows.1
  (2 shorter events, 0.0 us)
Async XLA Ops:
  0.6 36.9 %collective-permute-start = (bf16[512,1536]{1,0:T(8,128)(2,1)}, bf16[512,1536]{1,0:T(8,128)(2,1)}, u32[]{:S(2)}, u32[]{:S(2)}) collective-permute-start(bf16[512,1536]{1,0:T(8,128)(2,1)} %bitcast.13), channel_id=1, source_target_pairs={{0,1},{1,2},{2,3},{3,0},{4,5},{5,6},{6,7},{7,4},{8,9},{9,10},{10,1... | collective-permute-start | bytes 4718600 | tf_op jit(solution)/shard_map/ppermute | solution.py:235
  4.6 33.3 %collective-permute-start.1 = (bf16[512,1536]{1,0:T(8,128)(2,1)}, bf16[512,1536]{1,0:T(8,128)(2,1)}, u32[]{:S(2)}, u32[]{:S(2)}) collective-permute-start(bf16[512,1536]{1,0:T(8,128)(2,1)} %bitcast.14), channel_id=1, source_target_pairs={{0,3},{1,0},{2,1},{3,2},{4,7},{5,4},{6,5},{7,6},{8,11},{9,8},{10,9... | collective-permute-start | bytes 4718600 | tf_op jit(solution)/shard_map/ppermute | solution.py:235
  12.5 18.5 %copy-start.1 = (bf16[1,768,512]{2,1,0:T(8,128)(2,1)S(1)}, bf16[1,768,512]{2,1,0:T(8,128)(2,1)}, u32[]{:S(2)}) copy-start(bf16[1,768,512]{2,1,0:T(8,128)(2,1)} %param.11) | copy-start | bytes 2359300
  12.5 69.7 %all-to-all-start = ((bf16[128,8,1024]{2,1,0:T(8,128)(2,1)}), bf16[128,8,1024]{2,1,0:T(8,128)(2,1)S(1)}, u32[]{:S(2)}, u32[]{:S(2)}) async-start(bf16[128,8,1024]{2,1,0:T(8,128)(2,1)} %bitcast.20), calls=%async_computation | async-start | bytes 4194304 | tf_op jit(solution)/shard_map/all_to_all | solution.py:293
  31.0 22.8 %collective-permute-start.5 = (bf16[768,512]{1,0:T(8,128)(2,1)S(1)}, bf16[768,512]{1,0:T(8,128)(2,1)}, u32[]{:S(2)}, u32[]{:S(2)}) collective-permute-start(bf16[768,512]{1,0:T(8,128)(2,1)S(1)} %bitcast.17), channel_id=1, source_target_pairs={{0,1},{1,2},{2,3},{3,0},{4,5},{5,6},{6,7},{7,4},{8,9},{9,10},{10,1... | collective-permute-start | bytes 2359304 | tf_op jit(solution)/shard_map/ppermute | solution.py:236
  32.9 26.7 %collective-permute-start.4 = (bf16[768,512]{1,0:T(8,128)(2,1)S(1)}, bf16[768,512]{1,0:T(8,128)(2,1)}, u32[]{:S(2)}, u32[]{:S(2)}) collective-permute-start(bf16[768,512]{1,0:T(8,128)(2,1)S(1)} %bitcast.18), channel_id=1, source_target_pairs={{0,3},{1,0},{2,1},{3,2},{4,7},{5,4},{6,5},{7,6},{8,11},{9,8},{10,9... | collective-permute-start | bytes 2359304 | tf_op jit(solution)/shard_map/ppermute | solution.py:236
  40.4 43.3 %collective-permute-start.2 = (bf16[256,1536]{1,0:T(8,128)(2,1)}, bf16[256,1536]{1,0:T(8,128)(2,1)}, u32[]{:S(2)}, u32[]{:S(2)}) collective-permute-start(bf16[256,1536]{1,0:T(8,128)(2,1)} %get-tuple-element.22), channel_id=1, source_target_pairs={{0,1},{1,2},{2,3},{3,0},{4,5},{5,6},{6,7},{7,4},{8,9},{9,10},{10,1... | collective-permute-start | bytes 2359304 | tf_op jit(solution)/shard_map/ppermute | solution.py:238
  47.4 36.3 %collective-permute-start.3 = (bf16[256,1536]{1,0:T(8,128)(2,1)}, bf16[256,1536]{1,0:T(8,128)(2,1)}, u32[]{:S(2)}, u32[]{:S(2)}) collective-permute-start(bf16[256,1536]{1,0:T(8,128)(2,1)} %get-tuple-element.23), channel_id=1, source_target_pairs={{0,3},{1,0},{2,1},{3,2},{4,7},{5,4},{6,5},{7,6},{8,11},{9,8},{10,9... | collective-permute-start | bytes 2359304 | tf_op jit(solution)/shard_map/ppermute | solution.py:238
  55.6 36.1 %collective-permute-start.6 = (bf16[384,512]{1,0:T(8,128)(2,1)}, bf16[384,512]{1,0:T(8,128)(2,1)S(1)}, u32[]{:S(2)}, u32[]{:S(2)}) collective-permute-start(bf16[384,512]{1,0:T(8,128)(2,1)} %slice.8), channel_id=1, source_target_pairs={{0,1},{1,2},{2,3},{3,0},{4,5},{5,6},{6,7},{7,4},{8,9},{9,10},{10,1... | collective-permute-start | bytes 1179656 | tf_op jit(solution)/shard_map/ppermute | solution.py:239
  61.4 30.3 %collective-permute-start.7 = (bf16[384,512]{1,0:T(8,128)(2,1)}, bf16[384,512]{1,0:T(8,128)(2,1)}, u32[]{:S(2)}, u32[]{:S(2)}) collective-permute-start(bf16[384,512]{1,0:T(8,128)(2,1)} %slice.9), channel_id=1, source_target_pairs={{0,3},{1,0},{2,1},{3,2},{4,7},{5,4},{6,5},{7,6},{8,11},{9,8},{10,9... | collective-permute-start | bytes 1179656 | tf_op jit(solution)/shard_map/ppermute | solution.py:239
  82.2 1.5 %copy-start = (bf16[1,512,1536]{2,1,0:T(8,128)(2,1)S(1)}, bf16[1,512,1536]{2,1,0:T(8,128)(2,1)}, u32[]{:S(2)}) copy-start(bf16[1,512,1536]{2,1,0:T(8,128)(2,1)} %param.10) | copy-start | bytes 4718596
  89.7 8.7 %copy-start.3 = (bf16[768,512]{1,0:T(8,128)(2,1)}, bf16[768,512]{1,0:T(8,128)(2,1)S(1)}, u32[]{:S(2)}) copy-start(bf16[768,512]{1,0:T(8,128)(2,1)S(1)} %get-tuple-element.31) | copy-start | bytes 2359300
  89.7 8.7 %copy-start.5 = (bf16[768,512]{1,0:T(8,128)(2,1)}, bf16[768,512]{1,0:T(8,128)(2,1)S(1)}, u32[]{:S(2)}) copy-start(bf16[768,512]{1,0:T(8,128)(2,1)S(1)} %get-tuple-element.29.block) | copy-start | bytes 2359300
  89.7 25.7 %collective-permute-start.8 = (bf16[768,512]{1,0:T(8,128)(2,1)}, bf16[768,512]{1,0:T(8,128)(2,1)}, u32[]{:S(2)}, u32[]{:S(2)}) collective-permute-start(bf16[768,512]{1,0:T(8,128)(2,1)} %get-tuple-element.30), channel_id=1, source_target_pairs={{0,1},{1,2},{2,3},{3,0},{4,5},{5,6},{6,7},{7,4},{8,9},{9,10},{10,1... | collective-permute-start | bytes 2359304 | tf_op jit(solution)/shard_map/ppermute | solution.py:249
  98.4 13.6 %copy-start.4 = (bf16[768,512]{1,0:T(8,128)(2,1)S(1)}, bf16[768,512]{1,0:T(8,128)(2,1)}, u32[]{:S(2)}) copy-start(bf16[768,512]{1,0:T(8,128)(2,1)} %copy-done.3) | copy-start | bytes 2359300
  98.4 17.0 %copy-start.6 = (bf16[768,512]{1,0:T(8,128)(2,1)S(1)}, bf16[768,512]{1,0:T(8,128)(2,1)}, u32[]{:S(2)}) copy-start(bf16[768,512]{1,0:T(8,128)(2,1)} %copy-done.5) | copy-start | bytes 2359300
  98.5 44.5 %all-to-all-start.1 = ((bf16[128,8,512]{2,1,0:T(8,128)(2,1)}), bf16[128,8,512]{2,1,0:T(8,128)(2,1)S(1)}, u32[]{:S(2)}, u32[]{:S(2)}) async-start(bf16[128,8,512]{2,1,0:T(8,128)(2,1)} %bitcast.7), calls=%async_computation.1 | async-start | bytes 2097152 | tf_op jit(solution)/shard_map/all_to_all | solution.py:335
  112.1 20.1 %collective-permute-start.10 = (bf16[768,512]{1,0:T(8,128)(2,1)S(1)}, bf16[768,512]{1,0:T(8,128)(2,1)S(1)}, u32[]{:S(2)}, u32[]{:S(2)}) collective-permute-start(bf16[768,512]{1,0:T(8,128)(2,1)S(1)} %copy-done.4), channel_id=1, source_target_pairs={{0,3},{1,0},{2,1},{3,2},{4,7},{5,4},{6,5},{7,6},{8,11},{9,8},{10,9... | collective-permute-start | bytes 2359304 | tf_op jit(solution)/shard_map/ppermute | solution.py:259
  116.8 21.0 %collective-permute-start.9 = (bf16[768,512]{1,0:T(8,128)(2,1)S(1)}, bf16[768,512]{1,0:T(8,128)(2,1)S(1)}, u32[]{:S(2)}, u32[]{:S(2)}) collective-permute-start(bf16[768,512]{1,0:T(8,128)(2,1)S(1)} %add_far.1), channel_id=1, source_target_pairs={{0,1},{1,2},{2,3},{3,0},{4,5},{5,6},{6,7},{7,4},{8,9},{9,10},{10,1... | collective-permute-start | bytes 2359304 | tf_op jit(solution)/shard_map/ppermute | solution.py:259
  137.8 5.2 %copy-start.2 = (bf16[1024,96]{1,0:T(8,128)(2,1)S(1)}, bf16[1024,96]{1,0:T(8,128)(2,1)}, u32[]{:S(2)}) copy-start(bf16[1024,96]{1,0:T(8,128)(2,1)} %get-tuple-element.17.pick_ref) | copy-start | bytes 589828

commit v12 on v11

--- a/solution.py
+++ b/solution.py
@@ -124,26 +124,25 @@
 
 
 def hidden_kernel(x_ref, g_ref, own_up, *refs):
-    to_gate, to_up, *blocks, own_down = refs[5:12]
-    hid_ref, *holds, sems = refs[12:]
-    get = fetch(refs[:5], [*holds, own_down], sems)
+    given, outs, (pre, hid_ref, sems) = refs[:7], refs[7:20], refs[20:]
+    to_gate, to_up, blocks, holds = outs[0], outs[1], outs[2:6], outs[6:]
+    get = fetch(given, holds, sems)
     feat = g_ref.shape[1] // len(blocks)
     hidden_units = hid_ref.shape[1]
     tile = 256
-
-    def pre(cols):
-        row = own_up.shape[0]
-        total = jnp.dot(x_ref[:, :row], own_up[:, cols], preferred_element_type=F32)
-        for i in range(len(holds)):
-            w = get(i)
-            total = total + jnp.dot(x_ref[:, row : row + w.shape[0]], w[:, cols], preferred_element_type=F32)
-            row += w.shape[0]
-        return total
-
+    row = 0
+    for i in range(5):
+        w = get(i - 1) if i else own_up
+        rows = slice(row, row + w.shape[0])
+        row += w.shape[0]
+        for n in range(w.shape[1] // tile):
+            cols = slice(n * tile, n * tile + tile)
+            term = jnp.dot(x_ref[:, rows], w[:, cols], preferred_element_type=F32)
+            pre[:, cols] = pre[:, cols] + term if i else term
     for n in range(hidden_units // tile):
         cols = slice(n * tile, n * tile + tile)
-        gate = pre(cols)
-        up = pre(slice(hidden_units + n * tile, hidden_units + n * tile + tile))
+        gate = pre[:, cols]
+        up = pre[:, hidden_units + n * tile : hidden_units + n * tile + tile]
         sig = jax.nn.sigmoid(gate)
         activ = gate * sig
         to_gate[:, cols] = up * sig * (1.0 + gate * (1.0 - sig))
@@ -153,12 +152,14 @@
         ref[...] = lax.dot_general(
             hid_ref[...], g_ref[:, k * feat : k * feat + feat], TN, preferred_element_type=F32
         ).astype(BF16)
-    get(len(holds))
+    for i in range(4, len(holds)):
+        get(i)
 
 
 def back_kernel(quarters, me_ref, to_gate, to_up, g, *refs):
-    own_up, own, others, (back_ref, gp_ref, hold, out, *holds, sems, got_sems) = refs[0], refs[1], refs[2:10], refs[10:]
-    get = fetch(others, holds, got_sems)
+    ups, own, right, left, (far_a, far_b), refs = refs[:5], refs[5], refs[6], refs[7], refs[8:10], refs[10:]
+    back_ref, gp_ref, hold, out, *holds, sems, far_sems = refs
+    get = fetch((far_a, far_b), holds, far_sems)
     started = []
     hidden_units = to_gate.shape[1]
     feat = out.shape[1]
@@ -167,16 +168,17 @@
     def product(h, k, w):
         return lax.dot_general(g[:, k * feat : k * feat + feat], w, NT, preferred_element_type=F32)
 
-    sums = [product(h, 0, own[h * half : h * half + half, :]) for h in range(2)]
+    sums = []
     for h in range(2):
         cols = slice(h * half, h * half + half)
-        total = sums[h] + product(h, 1, get(0)[cols, :])
-        total = total + product(h, 2, get(1 + h)[...]) + product(h, 3, get(3)[cols, :])
+        sums.append(product(h, 0, own[cols, :]) + product(h, 1, right[cols, :]) + product(h, 3, left[cols, :]))
+    for h in range(2):
+        cols = slice(h * half, h * half + half)
+        total = sums[h] + product(h, 2, get(h)[...])
         gp_ref[:, cols] = (total * to_gate[:, cols]).astype(BF16)
         gp_ref[:, hidden_units + h * half : hidden_units + h * half + half] = (total * to_up[:, cols]).astype(BF16)
     at = 0
-    for i in range(5):
-        w = get(3 + i) if i else own_up
+    for w in ups:
         size = w.shape[0]
         hold[lax.rem(me_ref[0] + at // feat, quarters), :, at % feat : at % feat + size] = lax.dot_general(
             gp_ref[...], w[...], NT, preferred_element_type=F32
@@ -302,23 +304,28 @@
         cost_estimate=pl.CostEstimate(flops=UNPACK_COST, bytes_accessed=0, transcendentals=0),
         name="unpack_rows",
     )(me, recv)
-    to_gate, to_up, *blocks, own_down = pl.pallas_call(
+    near_downs = (down_weight[0], downs[0], downs[3])
+    to_gate, to_up, *rest = pl.pallas_call(
         hidden_kernel,
-        in_specs=[whole()] * 3 + [whole(pl.ANY)] * 5,
-        out_specs=[whole()] * (3 + parts),
+        in_specs=[whole()] * 3 + [whole(pl.ANY)] * 7,
+        out_specs=[whole()] * 13,
         out_shape=[jax.ShapeDtypeStruct((slots, hidden_units), F32)] * 2
-        + [jax.ShapeDtypeStruct((hidden_units, feat), BF16)] * (parts + 1),
-        scratch_shapes=[pltpu.VMEM((slots, hidden_units), BF16)]
-        + [pltpu.VMEM(x.shape, BF16) for x in ups]
-        + [pltpu.SemaphoreType.DMA((5,))],
+        + [jax.ShapeDtypeStruct((hidden_units, feat), BF16)] * parts
+        + [jax.ShapeDtypeStruct(x.shape, BF16) for x in (*ups, *near_downs)],
+        scratch_shapes=[
+            pltpu.VMEM((slots, 2 * hidden_units), F32),
+            pltpu.VMEM((slots, hidden_units), BF16),
+            pltpu.SemaphoreType.DMA((7,)),
+        ],
         compiler_params=pltpu.CompilerParams(vmem_limit_bytes=HIDDEN_LIMIT),
         name="hidden_rows",
-    )(rows_x, rows_g, gate_up_weight[0], *ups, down_weight[0])
+    )(rows_x, rows_g, gate_up_weight[0], *ups, *near_downs)
+    blocks, held = rest[:parts], rest[parts:]
     down_grad = scatter_two_steps(blocks, parts)[None]
 
     back = pl.pallas_call(
         functools.partial(back_kernel, quarters),
-        in_specs=[whole(pltpu.SMEM)] + [whole()] * 5 + [whole(pl.ANY)] * 8,
+        in_specs=[whole(pltpu.SMEM)] + [whole()] * 11 + [whole(pl.ANY)] * 2,
         out_specs=whole(pl.ANY),
         out_shape=jax.ShapeDtypeStruct((rows, feat), BF16),
         scratch_shapes=[
@@ -326,12 +333,12 @@
             pltpu.VMEM((quarters, slots, feat), BF16),
             pltpu.VMEM((rows, feat), BF16),
         ]
-        + [pltpu.VMEM(x.shape, BF16) for x in (*downs, *ups)]
-        + [pltpu.SemaphoreType.DMA((4,)), pltpu.SemaphoreType.DMA((8,))],
+        + [pltpu.VMEM(x.shape, BF16) for x in downs[1:3]]
+        + [pltpu.SemaphoreType.DMA((4,)), pltpu.SemaphoreType.DMA((2,))],
         compiler_params=pltpu.CompilerParams(vmem_limit_bytes=BACK_LIMIT),
         cost_estimate=pl.CostEstimate(flops=COST, bytes_accessed=0, transcendentals=0),
         name="back_rows",
-    )(me, to_gate, to_up, rows_g, gate_up_weight[0], own_down, *downs, *ups)
+    )(me, to_gate, to_up, rows_g, gate_up_weight[0], *held, *downs[1:3])
     returned = lax.all_to_all(back, "ep", split_axis=0, concat_axis=0, tiled=True)
     token_grads = pl.pallas_call(
         functools.partial(combine_kernel, toks),

time: 145 us -> 142 us (0.979)
  waiting for transfers between devices: 44.4 us -> 49.2 us
  starting transfers between devices: 70.1 us -> 67.1 us
  Pallas kernels: 23.7 us -> 21.1 us
  local copies, waits for them, and re-layouts: 3.6 us -> 1.94 us
    ppermute x1, waiting for transfers between devices: 4.47 us -> 7.65 us  [gather_two_steps(): lax.ppermute(down, 'edp', fwd)]
    ppermute x1, starting transfers between devices: 3.98 us -> 1.92 us  [gather_two_steps(): lax.ppermute(left_down[:half], 'edp', fwd)]
  transfers between devices with their start and end apart: 13 -> 13, of which waited for: 6 -> 6; matrix products, arithmetic and copies ran while one was open for 3% -> 2% of each run, Pallas kernels for 16% -> 14%
where the time goes in v12:
time: 142 us; the launch traced here: 141 us
  starting transfers between devices  67.1 us (47%)
  waiting for transfers between devices  49.2 us (35%)
  Pallas kernels  21.1 us (15%)
  local copies, waits for them, and re-layouts  1.94 us (1%)
    all_to_all x1, starting transfers between devices, per_device(): recv = lax.all_to_all(sent, 'ep', split_axis=0, concat_axis=0, tiled=True)  18.3 us
    all_to_all x1, waiting for transfers between devices, per_device(): recv = lax.all_to_all(sent, 'ep', split_axis=0, concat_axis=0, tiled=True)  16.7 us
    all_to_all x1, starting transfers between devices, per_device(): lax.all_to_all(back, 'ep', split_axis=0, concat_axis=0, tiled=True)  13.7 us
    ppermute x1, waiting for transfers between devices, scatter_two_steps(): lax.ppermute(left, 'edp', ring(size, -1))  13.4 us
    ppermute x1, waiting for transfers between devices, gather_two_steps(): lax.ppermute(down, 'edp', fwd)  7.65 us
    ppermute x1, starting transfers between devices, gather_two_steps(): lax.ppermute(up_top, 'edp', fwd)  7.03 us
    ppermute x1, waiting for transfers between devices, scatter_two_steps(): lax.ppermute(right, 'edp', ring(size, 1))  5.63 us
    pallas_call x1, Pallas kernels, per_device(): pl.pallas_call(functools.partial(back_kernel, quarters), in_specs=[whole(...  5.34 us
  transfers between devices with their start and end apart: 13, of which 6 were waited for; matrix products, arithmetic and copies ran while one was open for 2% of the time, Pallas kernels for 14%

profile of v12, /device:TPU:1, one launch (start us, length us, event | category | flops | bytes accessed | tf_op | source)
XLA Modules:
  0.0 141.5 jit_solution(12792855692844041829)
XLA Ops:
  0.6 4.0 %collective-permute-start = (bf16[512,1536]{1,0:T(8,128)(2,1)}, bf16[512,1536]{1,0:T(8,128)(2,1)}, u32[]{:S(2)}, u32[]{:S(2)}) collective-permute-start(bf16[512,1536]{1,0:T(8,128)(2,1)} %bitcast.13), channel_id=1, source_target_pairs={{0,1},{1,2},{2,3},{3,0},{4,5},{5,6},{6,7},{7,4},{8,9},{9,10},{10,1... | collective-permute-start | bytes 4718600 | tf_op jit(solution)/shard_map/ppermute | solution.py:237
  4.6 3.2 %collective-permute-start.1 = (bf16[512,1536]{1,0:T(8,128)(2,1)}, bf16[512,1536]{1,0:T(8,128)(2,1)}, u32[]{:S(2)}, u32[]{:S(2)}) collective-permute-start(bf16[512,1536]{1,0:T(8,128)(2,1)} %bitcast.14), channel_id=1, source_target_pairs={{0,3},{1,0},{2,1},{3,2},{4,7},{5,4},{6,5},{7,6},{8,11},{9,8},{10,9... | collective-permute-start | bytes 4718600 | tf_op jit(solution)/shard_map/ppermute | solution.py:237
  7.8 4.6 %send_rows.1 = (bf16[1024,1024]{1,0:T(8,128)(2,1)}, bf16[1024,96]{1,0:T(8,128)(2,1)}) custom-call(s32[8,24]{1,0:T(8,128)} %bitcast.21, f32[8,24]{1,0:T(8,128)} %bitcast.22, bf16[24,2048]{1,0:T(8,128)(2,1)} %tok_ref.1, bf16[24,2048]{1,0:T(8,128)(2,1)} %grad_ref.1), custom_call_target="tpu_custom_call" | custom-call | tf_op jit(solution)/shard_map/send_rows/pallas_call | solution.py:279
  12.4 18.3 %all-to-all-start = ((bf16[128,8,1024]{2,1,0:T(8,128)(2,1)}), bf16[128,8,1024]{2,1,0:T(8,128)(2,1)S(1)}, u32[]{:S(2)}, u32[]{:S(2)}) async-start(bf16[128,8,1024]{2,1,0:T(8,128)(2,1)} %bitcast.20), calls=%async_computation | async-start | bytes 4194304 | tf_op jit(solution)/shard_map/all_to_all | solution.py:295
  30.8 3.2 %collective-permute-start.4 = (bf16[768,512]{1,0:T(8,128)(2,1)}, bf16[768,512]{1,0:T(8,128)(2,1)S(1)}, u32[]{:S(2)}, u32[]{:S(2)}) collective-permute-start(bf16[768,512]{1,0:T(8,128)(2,1)} %bitcast.17), channel_id=1, source_target_pairs={{0,3},{1,0},{2,1},{3,2},{4,7},{5,4},{6,5},{7,6},{8,11},{9,8},{10,9... | collective-permute-start | bytes 2359304 | tf_op jit(solution)/shard_map/ppermute | solution.py:238
  34.0 2.1 %collective-permute-start.5 = (bf16[768,512]{1,0:T(8,128)(2,1)}, bf16[768,512]{1,0:T(8,128)(2,1)}, u32[]{:S(2)}, u32[]{:S(2)}) collective-permute-start(bf16[768,512]{1,0:T(8,128)(2,1)} %bitcast.18), channel_id=1, source_target_pairs={{0,1},{1,2},{2,3},{3,0},{4,5},{5,6},{6,7},{7,4},{8,9},{9,10},{10,1... | collective-permute-start | bytes 2359304 | tf_op jit(solution)/shard_map/ppermute | solution.py:238
  36.1 0.0 collective-permute-done.left
  36.1 1.8 %collective-permute-done.1.right = bf16[512,1536]{1,0:T(8,128)(2,1)} collective-permute-done((bf16[512,1536]{1,0:T(8,128)(2,1)}, bf16[512,1536]{1,0:T(8,128)(2,1)}, u32[]{:S(2)}, u32[]{:S(2)}) %collective-permute-start.1) | collective-permute-done | bytes 1572896 | tf_op jit(solution)/shard_map/ppermute | solution.py:237
  37.8 2.5 %hand_on.1 = (bf16[512,1536]{1,0:T(8,128)(2,1)}, bf16[512,1536]{1,0:T(8,128)(2,1)}, bf16[256,1536]{1,0:T(8,128)(2,1)}, bf16[256,1536]{1,0:T(8,128)(2,1)}) custom-call(bf16[512,1536]{1,0:T(8,128)(2,1)} %collective-permute-done.left, bf16[512,1536]{1,0:T(8,128)(2,1)} %collective-permute-done.1.right), custom_call_target="tpu_custom_call", output_to_operand_aliasing={{0}: (0, {}), {1}: (1, {})} | custom-call | flops 30000001024 | tf_op jit(solution)/shard_map/hand_on/pallas_call | solution.py:222
  40.4 7.0 %collective-permute-start.2 = (bf16[256,1536]{1,0:T(8,128)(2,1)}, bf16[256,1536]{1,0:T(8,128)(2,1)}, u32[]{:S(2)}, u32[]{:S(2)}) collective-permute-start(bf16[256,1536]{1,0:T(8,128)(2,1)} %get-tuple-element.28), channel_id=1, source_target_pairs={{0,1},{1,2},{2,3},{3,0},{4,5},{5,6},{6,7},{7,4},{8,9},{9,10},{10,1... | collective-permute-start | bytes 2359304 | tf_op jit(solution)/shard_map/ppermute | solution.py:240
  47.4 1.9 %collective-permute-start.3 = (bf16[256,1536]{1,0:T(8,128)(2,1)}, bf16[256,1536]{1,0:T(8,128)(2,1)}, u32[]{:S(2)}, u32[]{:S(2)}) collective-permute-start(bf16[256,1536]{1,0:T(8,128)(2,1)} %get-tuple-element.29), channel_id=1, source_target_pairs={{0,3},{1,0},{2,1},{3,2},{4,7},{5,4},{6,5},{7,6},{8,11},{9,8},{10,9... | collective-permute-start | bytes 2359304 | tf_op jit(solution)/shard_map/ppermute | solution.py:240
  49.4 7.7 %collective-permute-done.5.refs_6_ = bf16[768,512]{1,0:T(8,128)(2,1)} collective-permute-done((bf16[768,512]{1,0:T(8,128)(2,1)}, bf16[768,512]{1,0:T(8,128)(2,1)}, u32[]{:S(2)}, u32[]{:S(2)}) %collective-permute-start.5) | collective-permute-done | bytes 786464 | tf_op jit(solution)/shard_map/ppermute | solution.py:238
  57.0 1.0 slice.8
  58.0 1.9 %collective-permute-start.6 = (bf16[384,512]{1,0:T(8,128)(2,1)S(1)}, bf16[384,512]{1,0:T(8,128)(2,1)}, u32[]{:S(2)}, u32[]{:S(2)}) collective-permute-start(bf16[384,512]{1,0:T(8,128)(2,1)S(1)} %slice.8), channel_id=1, source_target_pairs={{0,1},{1,2},{2,3},{3,0},{4,5},{5,6},{6,7},{7,4},{8,9},{9,10},{10,1... | collective-permute-start | bytes 1179656 | tf_op jit(solution)/shard_map/ppermute | solution.py:241
  60.0 0.0 collective-permute-done.4.refs_5_
  60.0 0.8 slice.9
  60.7 4.6 %collective-permute-start.7 = (bf16[384,512]{1,0:T(8,128)(2,1)}, bf16[384,512]{1,0:T(8,128)(2,1)}, u32[]{:S(2)}, u32[]{:S(2)}) collective-permute-start(bf16[384,512]{1,0:T(8,128)(2,1)} %slice.9), channel_id=1, source_target_pairs={{0,3},{1,0},{2,1},{3,2},{4,7},{5,4},{6,5},{7,6},{8,11},{9,8},{10,9... | collective-permute-start | bytes 1179656 | tf_op jit(solution)/shard_map/ppermute | solution.py:241
  65.3 16.7 %all-to-all-done = bf16[128,8,1024]{2,1,0:T(8,128)(2,1)S(1)} async-done(((bf16[128,8,1024]{2,1,0:T(8,128)(2,1)}), bf16[128,8,1024]{2,1,0:T(8,128)(2,1)S(1)}, u32[]{:S(2)}, u32[]{:S(2)}) %all-to-all-start) | async-done | bytes 2097184 | tf_op jit(solution)/shard_map/all_to_all | solution.py:295
  82.0 0.0 copy-start
  82.0 0.0 copy-start.1
  82.0 1.4 %unpack_rows.1 = (bf16[256,2048]{1,0:T(8,128)(2,1)S(1)}, bf16[256,2048]{1,0:T(8,128)(2,1)S(1)}) custom-call(s32[1]{0:T(128)} %bitcast.2.me_ref, bf16[1024,1024]{1,0:T(8,128)(2,1)S(1)} %bitcast.12), custom_call_target="tpu_custom_call" | custom-call | flops 7000000000 | tf_op jit(solution)/shard_map/unpack_rows/pallas_call | solution.py:297
  83.5 0.0 collective-permute-done.2.refs_1_
  83.5 0.0 collective-permute-done.3.refs_2_
  83.5 0.0 copy-done
  83.5 0.1 copy-done.1
  83.6 4.9 %hidden_rows.1 = (f32[256,768]{1,0:T(8,128)S(1)}, f32[256,768]{1,0:T(8,128)S(1)}, bf16[768,512]{1,0:T(8,128)(2,1)S(1)}, bf16[768,512]{1,0:T(8,128)(2,1)S(1)}, bf...) custom-call(bf16[256,2048]{1,0:T(8,128)(2,1)S(1)} %get-tuple-element, ...), custom_call_target="tpu_custom_call" | custom-call | tf_op jit(solution)/shard_map/hidden_rows/pallas_call | solution.py:308
  88.6 0.0 copy-start.3
  88.6 1.9 %collective-permute-start.8 = (bf16[768,512]{1,0:T(8,128)(2,1)}, bf16[768,512]{1,0:T(8,128)(2,1)}, u32[]{:S(2)}, u32[]{:S(2)}) collective-permute-start(bf16[768,512]{1,0:T(8,128)(2,1)} %get-tuple-element.42), channel_id=1, source_target_pairs={{0,1},{1,2},{2,3},{3,0},{4,5},{5,6},{6,7},{7,4},{8,9},{9,10},{10,1... | collective-permute-start | bytes 2359304 | tf_op jit(solution)/shard_map/ppermute | solution.py:251
  90.5 0.0 collective-permute-done.6.refs_8_
  90.5 0.0 collective-permute-done.7.refs_9_
  90.5 5.3 %back_rows.1 = bf16[1024,512]{1,0:T(8,128)(2,1)} custom-call(s32[1]{0:T(128)} %bitcast.2.me_ref, f32[256,768]{1,0:T(8,128)S(1)} %get-tuple-element.31.to_gate, f32[256,768]{1,0:T(8,128)S(1)} %get-tuple-element.32.to_up, bf16[256,2048]{1,0:T(8,128)(2,1)S(1)} %get-tuple-element.26.g_ref.g, bf16[512,1536]{1,0:T(8,128)(2,1)S(1)} %bitcast.16, ...), custom_call_target="tpu_custom_call" | custom-call | flops 30000001024 | tf_op jit(solution)/shard_map/back_rows/pallas_call | solution.py:326
  95.9 0.0 copy-done.3
  95.9 0.0 copy-start.4
  95.9 13.7 %all-to-all-start.1 = ((bf16[128,8,512]{2,1,0:T(8,128)(2,1)}), bf16[128,8,512]{2,1,0:T(8,128)(2,1)S(1)}, u32[]{:S(2)}, u32[]{:S(2)}) async-start(bf16[128,8,512]{2,1,0:T(8,128)(2,1)} %bitcast.7), calls=%async_computation.1 | async-start | bytes 2097152 | tf_op jit(solution)/shard_map/all_to_all | solution.py:342
  109.6 3.4 %collective-permute-start.10 = (bf16[768,512]{1,0:T(8,128)(2,1)S(1)}, bf16[768,512]{1,0:T(8,128)(2,1)S(1)}, u32[]{:S(2)}, u32[]{:S(2)}) collective-permute-start(bf16[768,512]{1,0:T(8,128)(2,1)S(1)} %get-tuple-element.43), channel_id=1, source_target_pairs={{0,3},{1,0},{2,1},{3,2},{4,7},{5,4},{6,5},{7,6},{8,11},{9,8},{10,9... | collective-permute-start | bytes 2359304 | tf_op jit(solution)/shard_map/ppermute | solution.py:261
  113.0 0.0 collective-permute-done.8.came
  113.0 0.0 copy-done.4
  113.0 1.3 add_far.1
  114.3 1.9 %collective-permute-start.9 = (bf16[768,512]{1,0:T(8,128)(2,1)S(1)}, bf16[768,512]{1,0:T(8,128)(2,1)S(1)}, u32[]{:S(2)}, u32[]{:S(2)}) collective-permute-start(bf16[768,512]{1,0:T(8,128)(2,1)S(1)} %add_far.1), channel_id=1, source_target_pairs={{0,1},{1,2},{2,3},{3,0},{4,5},{5,6},{6,7},{7,4},{8,9},{9,10},{10,1... | collective-permute-start | bytes 2359304 | tf_op jit(solution)/shard_map/ppermute | solution.py:261
  116.3 13.4 %collective-permute-done.10 = bf16[768,512]{1,0:T(8,128)(2,1)S(1)} collective-permute-done((bf16[768,512]{1,0:T(8,128)(2,1)S(1)}, bf16[768,512]{1,0:T(8,128)(2,1)S(1)}, u32[]{:S(2)}, u32[]{:S(2)}) %collective-permute-start.10) | collective-permute-done | bytes 786464 | tf_op jit(solution)/shard_map/ppermute | solution.py:261
  129.7 5.6 %collective-permute-done.9 = bf16[768,512]{1,0:T(8,128)(2,1)S(1)} collective-permute-done((bf16[768,512]{1,0:T(8,128)(2,1)S(1)}, bf16[768,512]{1,0:T(8,128)(2,1)S(1)}, u32[]{:S(2)}, u32[]{:S(2)}) %collective-permute-start.9) | collective-permute-done | bytes 786464 | tf_op jit(solution)/shard_map/ppermute | solution.py:261
  135.3 0.0 copy-start.2
  135.3 1.2 fusion
  136.5 4.0 %all-to-all-done.1 = bf16[128,8,512]{2,1,0:T(8,128)(2,1)S(1)} async-done(((bf16[128,8,512]{2,1,0:T(8,128)(2,1)}), bf16[128,8,512]{2,1,0:T(8,128)(2,1)S(1)}, u32[]{:S(2)}, u32[]{:S(2)}) %all-to-all-start.1) | async-done | bytes 1048608 | tf_op jit(solution)/shard_map/all_to_all | solution.py:342
  140.5 0.0 copy-done.2
  140.5 1.0 combine_rows.1
Async XLA Ops:
  0.6 35.4 %collective-permute-start = (bf16[512,1536]{1,0:T(8,128)(2,1)}, bf16[512,1536]{1,0:T(8,128)(2,1)}, u32[]{:S(2)}, u32[]{:S(2)}) collective-permute-start(bf16[512,1536]{1,0:T(8,128)(2,1)} %bitcast.13), channel_id=1, source_target_pairs={{0,1},{1,2},{2,3},{3,0},{4,5},{5,6},{6,7},{7,4},{8,9},{9,10},{10,1... | collective-permute-start | bytes 4718600 | tf_op jit(solution)/shard_map/ppermute | solution.py:237
  4.6 33.3 %collective-permute-start.1 = (bf16[512,1536]{1,0:T(8,128)(2,1)}, bf16[512,1536]{1,0:T(8,128)(2,1)}, u32[]{:S(2)}, u32[]{:S(2)}) collective-permute-start(bf16[512,1536]{1,0:T(8,128)(2,1)} %bitcast.14), channel_id=1, source_target_pairs={{0,3},{1,0},{2,1},{3,2},{4,7},{5,4},{6,5},{7,6},{8,11},{9,8},{10,9... | collective-permute-start | bytes 4718600 | tf_op jit(solution)/shard_map/ppermute | solution.py:237
  12.4 69.6 %all-to-all-start = ((bf16[128,8,1024]{2,1,0:T(8,128)(2,1)}), bf16[128,8,1024]{2,1,0:T(8,128)(2,1)S(1)}, u32[]{:S(2)}, u32[]{:S(2)}) async-start(bf16[128,8,1024]{2,1,0:T(8,128)(2,1)} %bitcast.20), calls=%async_computation | async-start | bytes 4194304 | tf_op jit(solution)/shard_map/all_to_all | solution.py:295
  30.8 29.2 %collective-permute-start.4 = (bf16[768,512]{1,0:T(8,128)(2,1)}, bf16[768,512]{1,0:T(8,128)(2,1)S(1)}, u32[]{:S(2)}, u32[]{:S(2)}) collective-permute-start(bf16[768,512]{1,0:T(8,128)(2,1)} %bitcast.17), channel_id=1, source_target_pairs={{0,3},{1,0},{2,1},{3,2},{4,7},{5,4},{6,5},{7,6},{8,11},{9,8},{10,9... | collective-permute-start | bytes 2359304 | tf_op jit(solution)/shard_map/ppermute | solution.py:238
  34.0 23.0 %collective-permute-start.5 = (bf16[768,512]{1,0:T(8,128)(2,1)}, bf16[768,512]{1,0:T(8,128)(2,1)}, u32[]{:S(2)}, u32[]{:S(2)}) collective-permute-start(bf16[768,512]{1,0:T(8,128)(2,1)} %bitcast.18), channel_id=1, source_target_pairs={{0,1},{1,2},{2,3},{3,0},{4,5},{5,6},{6,7},{7,4},{8,9},{9,10},{10,1... | collective-permute-start | bytes 2359304 | tf_op jit(solution)/shard_map/ppermute | solution.py:238
  40.4 43.1 %collective-permute-start.2 = (bf16[256,1536]{1,0:T(8,128)(2,1)}, bf16[256,1536]{1,0:T(8,128)(2,1)}, u32[]{:S(2)}, u32[]{:S(2)}) collective-permute-start(bf16[256,1536]{1,0:T(8,128)(2,1)} %get-tuple-element.28), channel_id=1, source_target_pairs={{0,1},{1,2},{2,3},{3,0},{4,5},{5,6},{6,7},{7,4},{8,9},{9,10},{10,1... | collective-permute-start | bytes 2359304 | tf_op jit(solution)/shard_map/ppermute | solution.py:240
  47.4 36.1 %collective-permute-start.3 = (bf16[256,1536]{1,0:T(8,128)(2,1)}, bf16[256,1536]{1,0:T(8,128)(2,1)}, u32[]{:S(2)}, u32[]{:S(2)}) collective-permute-start(bf16[256,1536]{1,0:T(8,128)(2,1)} %get-tuple-element.29), channel_id=1, source_target_pairs={{0,3},{1,0},{2,1},{3,2},{4,7},{5,4},{6,5},{7,6},{8,11},{9,8},{10,9... | collective-permute-start | bytes 2359304 | tf_op jit(solution)/shard_map/ppermute | solution.py:240
  58.0 32.5 %collective-permute-start.6 = (bf16[384,512]{1,0:T(8,128)(2,1)S(1)}, bf16[384,512]{1,0:T(8,128)(2,1)}, u32[]{:S(2)}, u32[]{:S(2)}) collective-permute-start(bf16[384,512]{1,0:T(8,128)(2,1)S(1)} %slice.8), channel_id=1, source_target_pairs={{0,1},{1,2},{2,3},{3,0},{4,5},{5,6},{6,7},{7,4},{8,9},{9,10},{10,1... | collective-permute-start | bytes 1179656 | tf_op jit(solution)/shard_map/ppermute | solution.py:241
  60.7 29.8 %collective-permute-start.7 = (bf16[384,512]{1,0:T(8,128)(2,1)}, bf16[384,512]{1,0:T(8,128)(2,1)}, u32[]{:S(2)}, u32[]{:S(2)}) collective-permute-start(bf16[384,512]{1,0:T(8,128)(2,1)} %slice.9), channel_id=1, source_target_pairs={{0,3},{1,0},{2,1},{3,2},{4,7},{5,4},{6,5},{7,6},{8,11},{9,8},{10,9... | collective-permute-start | bytes 1179656 | tf_op jit(solution)/shard_map/ppermute | solution.py:241
  82.0 1.5 %copy-start = (bf16[1,512,1536]{2,1,0:T(8,128)(2,1)S(1)}, bf16[1,512,1536]{2,1,0:T(8,128)(2,1)}, u32[]{:S(2)}) copy-start(bf16[1,512,1536]{2,1,0:T(8,128)(2,1)} %param.10) | copy-start | bytes 4718596
  82.0 1.6 %copy-start.1 = (bf16[1,768,512]{2,1,0:T(8,128)(2,1)S(1)}, bf16[1,768,512]{2,1,0:T(8,128)(2,1)}, u32[]{:S(2)}) copy-start(bf16[1,768,512]{2,1,0:T(8,128)(2,1)} %param.11) | copy-start | bytes 2359300
  88.6 7.3 %copy-start.3 = (bf16[768,512]{1,0:T(8,128)(2,1)}, bf16[768,512]{1,0:T(8,128)(2,1)S(1)}, u32[]{:S(2)}) copy-start(bf16[768,512]{1,0:T(8,128)(2,1)S(1)} %get-tuple-element.41.block) | copy-start | bytes 2359300
  88.6 24.4 %collective-permute-start.8 = (bf16[768,512]{1,0:T(8,128)(2,1)}, bf16[768,512]{1,0:T(8,128)(2,1)}, u32[]{:S(2)}, u32[]{:S(2)}) collective-permute-start(bf16[768,512]{1,0:T(8,128)(2,1)} %get-tuple-element.42), channel_id=1, source_target_pairs={{0,1},{1,2},{2,3},{3,0},{4,5},{5,6},{6,7},{7,4},{8,9},{9,10},{10,1... | collective-permute-start | bytes 2359304 | tf_op jit(solution)/shard_map/ppermute | solution.py:251
  95.9 17.1 %copy-start.4 = (bf16[768,512]{1,0:T(8,128)(2,1)S(1)}, bf16[768,512]{1,0:T(8,128)(2,1)}, u32[]{:S(2)}) copy-start(bf16[768,512]{1,0:T(8,128)(2,1)} %copy-done.3) | copy-start | bytes 2359300
  95.9 44.6 %all-to-all-start.1 = ((bf16[128,8,512]{2,1,0:T(8,128)(2,1)}), bf16[128,8,512]{2,1,0:T(8,128)(2,1)S(1)}, u32[]{:S(2)}, u32[]{:S(2)}) async-start(bf16[128,8,512]{2,1,0:T(8,128)(2,1)} %bitcast.7), calls=%async_computation.1 | async-start | bytes 2097152 | tf_op jit(solution)/shard_map/all_to_all | solution.py:342
  109.6 20.1 %collective-permute-start.10 = (bf16[768,512]{1,0:T(8,128)(2,1)S(1)}, bf16[768,512]{1,0:T(8,128)(2,1)S(1)}, u32[]{:S(2)}, u32[]{:S(2)}) collective-permute-start(bf16[768,512]{1,0:T(8,128)(2,1)S(1)} %get-tuple-element.43), channel_id=1, source_target_pairs={{0,3},{1,0},{2,1},{3,2},{4,7},{5,4},{6,5},{7,6},{8,11},{9,8},{10,9... | collective-permute-start | bytes 2359304 | tf_op jit(solution)/shard_map/ppermute | solution.py:261
  114.3 21.0 %collective-permute-start.9 = (bf16[768,512]{1,0:T(8,128)(2,1)S(1)}, bf16[768,512]{1,0:T(8,128)(2,1)S(1)}, u32[]{:S(2)}, u32[]{:S(2)}) collective-permute-start(bf16[768,512]{1,0:T(8,128)(2,1)S(1)} %add_far.1), channel_id=1, source_target_pairs={{0,1},{1,2},{2,3},{3,0},{4,5},{5,6},{6,7},{7,4},{8,9},{9,10},{10,1... | collective-permute-start | bytes 2359304 | tf_op jit(solution)/shard_map/ppermute | solution.py:261
  135.3 5.2 %copy-start.2 = (bf16[1024,96]{1,0:T(8,128)(2,1)S(1)}, bf16[1024,96]{1,0:T(8,128)(2,1)}, u32[]{:S(2)}) copy-start(bf16[1024,96]{1,0:T(8,128)(2,1)} %get-tuple-element.23.pick_ref) | copy-start | bytes 589828

commit v13 on v12

--- a/solution.py
+++ b/solution.py
@@ -17,6 +17,8 @@
 HIDDEN_LIMIT = 32 * 1024 * 1024
 SEND_LIMIT = 56 * 1024 * 1024
 COST = 30 * 10**9
+LEFT_COST = 1 * 10**9
+RIGHT_COST = 30 * 10**9
 ADD_COST = 8 * 10**9
 
 
@@ -208,33 +210,31 @@
     return [(i, (i + step) % size) for i in range(size)]
 
 
-def hand_on_kernel(left, right, left_out, right_out, top, bottom, sems):
-    half = top.shape[0]
-    copies = []
-    start(copies, left.at[pl.ds(0, half), :], top, sems)
-    start(copies, right.at[pl.ds(half, half), :], bottom, sems)
-    for copy in copies:
-        copy.wait()
-
-
-def hand_on(left, right):
-    half = jax.ShapeDtypeStruct((left.shape[0] // 2, left.shape[1]), left.dtype)
+def hand_on_kernel(first, block, block_out, going, sem):
+    copy = pltpu.make_async_copy(block.at[pl.ds(first, going.shape[0]), :], going, sem)
+    copy.start()
+    copy.wait()
+
+
+def hand_on(block, first, cost):
+    half = jax.ShapeDtypeStruct((block.shape[0] // 2, block.shape[1]), block.dtype)
     return pl.pallas_call(
-        hand_on_kernel,
-        in_specs=[whole(pl.ANY)] * 2,
-        out_specs=[whole(pl.ANY)] * 2 + [whole()] * 2,
-        out_shape=[jax.ShapeDtypeStruct(left.shape, left.dtype)] * 2 + [half] * 2,
-        input_output_aliases={0: 0, 1: 1},
-        scratch_shapes=[pltpu.SemaphoreType.DMA((2,))],
+        functools.partial(hand_on_kernel, first),
+        in_specs=[whole(pl.ANY)],
+        out_specs=[whole(pl.ANY), whole()],
+        out_shape=[jax.ShapeDtypeStruct(block.shape, block.dtype), half],
+        input_output_aliases={0: 0},
+        scratch_shapes=[pltpu.SemaphoreType.DMA],
         compiler_params=pltpu.CompilerParams(vmem_limit_bytes=VMEM_LIMIT),
-        cost_estimate=pl.CostEstimate(flops=COST, bytes_accessed=0, transcendentals=0),
+        cost_estimate=pl.CostEstimate(flops=cost, bytes_accessed=0, transcendentals=0),
         name="hand_on",
-    )(left, right)
+    )(block)
 
 
 def gather_two_steps(up, down, size):
     fwd, bwd = ring(size, 1), ring(size, -1)
-    left_up, right_up, up_top, up_bottom = hand_on(lax.ppermute(up, "edp", fwd), lax.ppermute(up, "edp", bwd))
+    left_up, up_top = hand_on(lax.ppermute(up, "edp", fwd), 0, LEFT_COST)
+    right_up, up_bottom = hand_on(lax.ppermute(up, "edp", bwd), up.shape[0] // 2, RIGHT_COST)
     left_down, right_down = lax.ppermute(down, "edp", fwd), lax.ppermute(down, "edp", bwd)
     half = down.shape[0] // 2
     far_up = [lax.ppermute(up_top, "edp", fwd), lax.ppermute(up_bottom, "edp", bwd)]

time: 142 us -> 142 us (level)
  waiting for transfers between devices: 49.2 us -> 47.5 us
  Pallas kernels: 21.1 us -> 22.7 us
    ppermute x1, starting transfers between devices: 1.92 us -> 4.18 us  [gather_two_steps(): lax.ppermute(up_bottom, 'edp', bwd)]
    ppermute x1, starting transfers between devices: 7.03 us -> 4.99 us  [gather_two_steps(): lax.ppermute(up_top, 'edp', fwd)]
    ppermute x1, waiting for transfers between devices: 1.77 us -> 0.01 us  [gather_two_steps(): lax.ppermute(up, 'edp', bwd)]
    pallas_call x1 -> x2, Pallas kernels: 2.53 us -> 4.06 us  [hand_on(): pl.pallas_call(functools.partial(hand_on_kernel, first), in_specs=[whole(...]
  transfers between devices with their start and end apart: 13 -> 13, of which waited for: 6 -> 5; matrix products, arithmetic and copies ran while one was open for 2% -> 2% of each run, Pallas kernels for 14% -> 15%
where the time goes in v13:
time: 142 us; the launch traced here: 141 us
  starting transfers between devices  67.3 us (47%)
  waiting for transfers between devices  47.5 us (33%)
  Pallas kernels  22.7 us (16%)
  local copies, waits for them, and re-layouts  1.94 us (1%)
    all_to_all x1, starting transfers between devices, per_device(): recv = lax.all_to_all(sent, 'ep', split_axis=0, concat_axis=0, tiled=True)  18.3 us
    all_to_all x1, waiting for transfers between devices, per_device(): recv = lax.all_to_all(sent, 'ep', split_axis=0, concat_axis=0, tiled=True)  16.7 us
    all_to_all x1, starting transfers between devices, per_device(): lax.all_to_all(back, 'ep', split_axis=0, concat_axis=0, tiled=True)  13.7 us
    ppermute x1, waiting for transfers between devices, scatter_two_steps(): lax.ppermute(left, 'edp', ring(size, -1))  13.4 us
    ppermute x1, waiting for transfers between devices, gather_two_steps(): lax.ppermute(down, 'edp', fwd)  7.65 us
    ppermute x1, waiting for transfers between devices, scatter_two_steps(): lax.ppermute(right, 'edp', ring(size, 1))  5.63 us
    pallas_call x1, Pallas kernels, per_device(): pl.pallas_call(functools.partial(back_kernel, quarters), in_specs=[whole(...  5.33 us
    ppermute x1, starting transfers between devices, gather_two_steps(): lax.ppermute(up_top, 'edp', fwd)  4.99 us
  transfers between devices with their start and end apart: 13, of which 5 were waited for; matrix products, arithmetic and copies ran while one was open for 2% of the time, Pallas kernels for 15%

profile of v13, /device:TPU:1, one launch (start us, length us, event | category | flops | bytes accessed | tf_op | source)
XLA Modules:
  0.0 141.5 jit_solution(10581488371339443717)
XLA Ops:
  0.6 4.0 %collective-permute-start.1 = (bf16[512,1536]{1,0:T(8,128)(2,1)}, bf16[512,1536]{1,0:T(8,128)(2,1)}, u32[]{:S(2)}, u32[]{:S(2)}) collective-permute-start(bf16[512,1536]{1,0:T(8,128)(2,1)} %bitcast.13), channel_id=1, source_target_pairs={{0,1},{1,2},{2,3},{3,0},{4,5},{5,6},{6,7},{7,4},{8,9},{9,10},{10,1... | collective-permute-start | bytes 4718600 | tf_op jit(solution)/shard_map/ppermute | solution.py:236
  4.6 3.2 %collective-permute-start = (bf16[512,1536]{1,0:T(8,128)(2,1)}, bf16[512,1536]{1,0:T(8,128)(2,1)}, u32[]{:S(2)}, u32[]{:S(2)}) collective-permute-start(bf16[512,1536]{1,0:T(8,128)(2,1)} %bitcast.14), channel_id=1, source_target_pairs={{0,3},{1,0},{2,1},{3,2},{4,7},{5,4},{6,5},{7,6},{8,11},{9,8},{10,9... | collective-permute-start | bytes 4718600 | tf_op jit(solution)/shard_map/ppermute | solution.py:237
  7.8 4.6 %send_rows.1 = (bf16[1024,1024]{1,0:T(8,128)(2,1)}, bf16[1024,96]{1,0:T(8,128)(2,1)}) custom-call(s32[8,24]{1,0:T(8,128)} %bitcast.21, f32[8,24]{1,0:T(8,128)} %bitcast.22, bf16[24,2048]{1,0:T(8,128)(2,1)} %tok_ref.1, bf16[24,2048]{1,0:T(8,128)(2,1)} %grad_ref.1), custom_call_target="tpu_custom_call" | custom-call | tf_op jit(solution)/shard_map/send_rows/pallas_call | solution.py:279
  12.4 18.3 %all-to-all-start = ((bf16[128,8,1024]{2,1,0:T(8,128)(2,1)}), bf16[128,8,1024]{2,1,0:T(8,128)(2,1)S(1)}, u32[]{:S(2)}, u32[]{:S(2)}) async-start(bf16[128,8,1024]{2,1,0:T(8,128)(2,1)} %bitcast.20), calls=%async_computation | async-start | bytes 4194304 | tf_op jit(solution)/shard_map/all_to_all | solution.py:295
  30.8 3.2 %collective-permute-start.4 = (bf16[768,512]{1,0:T(8,128)(2,1)}, bf16[768,512]{1,0:T(8,128)(2,1)S(1)}, u32[]{:S(2)}, u32[]{:S(2)}) collective-permute-start(bf16[768,512]{1,0:T(8,128)(2,1)} %bitcast.17), channel_id=1, source_target_pairs={{0,3},{1,0},{2,1},{3,2},{4,7},{5,4},{6,5},{7,6},{8,11},{9,8},{10,9... | collective-permute-start | bytes 2359304 | tf_op jit(solution)/shard_map/ppermute | solution.py:238
  34.0 2.1 %collective-permute-start.5 = (bf16[768,512]{1,0:T(8,128)(2,1)}, bf16[768,512]{1,0:T(8,128)(2,1)}, u32[]{:S(2)}, u32[]{:S(2)}) collective-permute-start(bf16[768,512]{1,0:T(8,128)(2,1)} %bitcast.18), channel_id=1, source_target_pairs={{0,1},{1,2},{2,3},{3,0},{4,5},{5,6},{6,7},{7,4},{8,9},{9,10},{10,1... | collective-permute-start | bytes 2359304 | tf_op jit(solution)/shard_map/ppermute | solution.py:238
  36.1 0.0 collective-permute-done.1.block
  36.1 2.0 %hand_on.3 = (bf16[512,1536]{1,0:T(8,128)(2,1)}, bf16[256,1536]{1,0:T(8,128)(2,1)}) custom-call(bf16[512,1536]{1,0:T(8,128)(2,1)} %collective-permute-done.1.block), custom_call_target="tpu_custom_call", output_to_operand_aliasing={{0}: (0, {})} | custom-call | flops 1000000000 | tf_op jit(solution)/shard_map/hand_on/pallas_call | solution.py:221
  38.1 5.0 %collective-permute-start.2 = (bf16[256,1536]{1,0:T(8,128)(2,1)}, bf16[256,1536]{1,0:T(8,128)(2,1)}, u32[]{:S(2)}, u32[]{:S(2)}) collective-permute-start(bf16[256,1536]{1,0:T(8,128)(2,1)} %get-tuple-element.28), channel_id=1, source_target_pairs={{0,1},{1,2},{2,3},{3,0},{4,5},{5,6},{6,7},{7,4},{8,9},{9,10},{10,1... | collective-permute-start | bytes 2359304 | tf_op jit(solution)/shard_map/ppermute | solution.py:240
  43.1 0.0 collective-permute-done.block
  43.1 2.0 %hand_on.2 = (bf16[512,1536]{1,0:T(8,128)(2,1)}, bf16[256,1536]{1,0:T(8,128)(2,1)}) custom-call(bf16[512,1536]{1,0:T(8,128)(2,1)} %collective-permute-done.block), custom_call_target="tpu_custom_call", output_to_operand_aliasing={{0}: (0, {})} | custom-call | flops 30000001024 | tf_op jit(solution)/shard_map/hand_on/pallas_call | solution.py:221
  45.2 4.2 %collective-permute-start.3 = (bf16[256,1536]{1,0:T(8,128)(2,1)}, bf16[256,1536]{1,0:T(8,128)(2,1)}, u32[]{:S(2)}, u32[]{:S(2)}) collective-permute-start(bf16[256,1536]{1,0:T(8,128)(2,1)} %get-tuple-element.29), channel_id=1, source_target_pairs={{0,3},{1,0},{2,1},{3,2},{4,7},{5,4},{6,5},{7,6},{8,11},{9,8},{10,9... | collective-permute-start | bytes 2359304 | tf_op jit(solution)/shard_map/ppermute | solution.py:240
  49.4 7.7 %collective-permute-done.5.refs_6_ = bf16[768,512]{1,0:T(8,128)(2,1)} collective-permute-done((bf16[768,512]{1,0:T(8,128)(2,1)}, bf16[768,512]{1,0:T(8,128)(2,1)}, u32[]{:S(2)}, u32[]{:S(2)}) %collective-permute-start.5) | collective-permute-done | bytes 786464 | tf_op jit(solution)/shard_map/ppermute | solution.py:238
  57.0 1.0 slice.8
  58.0 1.9 %collective-permute-start.6 = (bf16[384,512]{1,0:T(8,128)(2,1)S(1)}, bf16[384,512]{1,0:T(8,128)(2,1)}, u32[]{:S(2)}, u32[]{:S(2)}) collective-permute-start(bf16[384,512]{1,0:T(8,128)(2,1)S(1)} %slice.8), channel_id=1, source_target_pairs={{0,1},{1,2},{2,3},{3,0},{4,5},{5,6},{6,7},{7,4},{8,9},{9,10},{10,1... | collective-permute-start | bytes 1179656 | tf_op jit(solution)/shard_map/ppermute | solution.py:241
  60.0 0.0 collective-permute-done.4.refs_5_
  60.0 0.8 slice.9
  60.7 4.6 %collective-permute-start.7 = (bf16[384,512]{1,0:T(8,128)(2,1)}, bf16[384,512]{1,0:T(8,128)(2,1)}, u32[]{:S(2)}, u32[]{:S(2)}) collective-permute-start(bf16[384,512]{1,0:T(8,128)(2,1)} %slice.9), channel_id=1, source_target_pairs={{0,3},{1,0},{2,1},{3,2},{4,7},{5,4},{6,5},{7,6},{8,11},{9,8},{10,9... | collective-permute-start | bytes 1179656 | tf_op jit(solution)/shard_map/ppermute | solution.py:241
  65.3 16.7 %all-to-all-done = bf16[128,8,1024]{2,1,0:T(8,128)(2,1)S(1)} async-done(((bf16[128,8,1024]{2,1,0:T(8,128)(2,1)}), bf16[128,8,1024]{2,1,0:T(8,128)(2,1)S(1)}, u32[]{:S(2)}, u32[]{:S(2)}) %all-to-all-start) | async-done | bytes 2097184 | tf_op jit(solution)/shard_map/all_to_all | solution.py:295
  82.0 0.0 copy-start
  82.0 0.0 copy-start.1
  82.0 1.4 %unpack_rows.1 = (bf16[256,2048]{1,0:T(8,128)(2,1)S(1)}, bf16[256,2048]{1,0:T(8,128)(2,1)S(1)}) custom-call(s32[1]{0:T(128)} %bitcast.2.me_ref, bf16[1024,1024]{1,0:T(8,128)(2,1)S(1)} %bitcast.12), custom_call_target="tpu_custom_call" | custom-call | flops 7000000000 | tf_op jit(solution)/shard_map/unpack_rows/pallas_call | solution.py:297
  83.5 0.0 collective-permute-done.2.refs_1_
  83.5 0.0 collective-permute-done.3.refs_2_
  83.5 0.0 copy-done
  83.5 0.1 copy-done.1
  83.6 4.9 %hidden_rows.1 = (f32[256,768]{1,0:T(8,128)S(1)}, f32[256,768]{1,0:T(8,128)S(1)}, bf16[768,512]{1,0:T(8,128)(2,1)S(1)}, bf16[768,512]{1,0:T(8,128)(2,1)S(1)}, bf...) custom-call(bf16[256,2048]{1,0:T(8,128)(2,1)S(1)} %get-tuple-element, ...), custom_call_target="tpu_custom_call" | custom-call | tf_op jit(solution)/shard_map/hidden_rows/pallas_call | solution.py:308
  88.6 0.0 copy-start.3
  88.6 1.9 %collective-permute-start.8 = (bf16[768,512]{1,0:T(8,128)(2,1)}, bf16[768,512]{1,0:T(8,128)(2,1)}, u32[]{:S(2)}, u32[]{:S(2)}) collective-permute-start(bf16[768,512]{1,0:T(8,128)(2,1)} %get-tuple-element.42), channel_id=1, source_target_pairs={{0,1},{1,2},{2,3},{3,0},{4,5},{5,6},{6,7},{7,4},{8,9},{9,10},{10,1... | collective-permute-start | bytes 2359304 | tf_op jit(solution)/shard_map/ppermute | solution.py:251
  90.5 0.0 collective-permute-done.6.refs_8_
  90.5 0.0 collective-permute-done.7.refs_9_
  90.5 5.3 %back_rows.1 = bf16[1024,512]{1,0:T(8,128)(2,1)} custom-call(s32[1]{0:T(128)} %bitcast.2.me_ref, f32[256,768]{1,0:T(8,128)S(1)} %get-tuple-element.31.to_gate, f32[256,768]{1,0:T(8,128)S(1)} %get-tuple-element.32.to_up, bf16[256,2048]{1,0:T(8,128)(2,1)S(1)} %get-tuple-element.26.g_ref.g, bf16[512,1536]{1,0:T(8,128)(2,1)S(1)} %bitcast.16, ...), custom_call_target="tpu_custom_call" | custom-call | flops 30000001024 | tf_op jit(solution)/shard_map/back_rows/pallas_call | solution.py:326
  95.9 0.0 copy-done.3
  95.9 0.0 copy-start.4
  95.9 13.7 %all-to-all-start.1 = ((bf16[128,8,512]{2,1,0:T(8,128)(2,1)}), bf16[128,8,512]{2,1,0:T(8,128)(2,1)S(1)}, u32[]{:S(2)}, u32[]{:S(2)}) async-start(bf16[128,8,512]{2,1,0:T(8,128)(2,1)} %bitcast.7), calls=%async_computation.1 | async-start | bytes 2097152 | tf_op jit(solution)/shard_map/all_to_all | solution.py:342
  109.6 3.4 %collective-permute-start.10 = (bf16[768,512]{1,0:T(8,128)(2,1)S(1)}, bf16[768,512]{1,0:T(8,128)(2,1)S(1)}, u32[]{:S(2)}, u32[]{:S(2)}) collective-permute-start(bf16[768,512]{1,0:T(8,128)(2,1)S(1)} %get-tuple-element.43), channel_id=1, source_target_pairs={{0,3},{1,0},{2,1},{3,2},{4,7},{5,4},{6,5},{7,6},{8,11},{9,8},{10,9... | collective-permute-start | bytes 2359304 | tf_op jit(solution)/shard_map/ppermute | solution.py:261
  113.0 0.0 collective-permute-done.8.came
  113.0 0.0 copy-done.4
  113.0 1.3 add_far.1
  114.3 1.9 %collective-permute-start.9 = (bf16[768,512]{1,0:T(8,128)(2,1)S(1)}, bf16[768,512]{1,0:T(8,128)(2,1)S(1)}, u32[]{:S(2)}, u32[]{:S(2)}) collective-permute-start(bf16[768,512]{1,0:T(8,128)(2,1)S(1)} %add_far.1), channel_id=1, source_target_pairs={{0,1},{1,2},{2,3},{3,0},{4,5},{5,6},{6,7},{7,4},{8,9},{9,10},{10,1... | collective-permute-start | bytes 2359304 | tf_op jit(solution)/shard_map/ppermute | solution.py:261
  116.2 13.4 %collective-permute-done.10 = bf16[768,512]{1,0:T(8,128)(2,1)S(1)} collective-permute-done((bf16[768,512]{1,0:T(8,128)(2,1)S(1)}, bf16[768,512]{1,0:T(8,128)(2,1)S(1)}, u32[]{:S(2)}, u32[]{:S(2)}) %collective-permute-start.10) | collective-permute-done | bytes 786464 | tf_op jit(solution)/shard_map/ppermute | solution.py:261
  129.7 5.6 %collective-permute-done.9 = bf16[768,512]{1,0:T(8,128)(2,1)S(1)} collective-permute-done((bf16[768,512]{1,0:T(8,128)(2,1)S(1)}, bf16[768,512]{1,0:T(8,128)(2,1)S(1)}, u32[]{:S(2)}, u32[]{:S(2)}) %collective-permute-start.9) | collective-permute-done | bytes 786464 | tf_op jit(solution)/shard_map/ppermute | solution.py:261
  135.3 0.0 copy-start.2
  135.3 1.2 fusion
  136.5 4.0 %all-to-all-done.1 = bf16[128,8,512]{2,1,0:T(8,128)(2,1)S(1)} async-done(((bf16[128,8,512]{2,1,0:T(8,128)(2,1)}), bf16[128,8,512]{2,1,0:T(8,128)(2,1)S(1)}, u32[]{:S(2)}, u32[]{:S(2)}) %all-to-all-start.1) | async-done | bytes 1048608 | tf_op jit(solution)/shard_map/all_to_all | solution.py:342
  140.5 0.0 copy-done.2
  140.5 1.0 combine_rows.1
Async XLA Ops:
  0.6 35.4 %collective-permute-start.1 = (bf16[512,1536]{1,0:T(8,128)(2,1)}, bf16[512,1536]{1,0:T(8,128)(2,1)}, u32[]{:S(2)}, u32[]{:S(2)}) collective-permute-start(bf16[512,1536]{1,0:T(8,128)(2,1)} %bitcast.13), channel_id=1, source_target_pairs={{0,1},{1,2},{2,3},{3,0},{4,5},{5,6},{6,7},{7,4},{8,9},{9,10},{10,1... | collective-permute-start | bytes 4718600 | tf_op jit(solution)/shard_map/ppermute | solution.py:236
  4.6 38.5 %collective-permute-start = (bf16[512,1536]{1,0:T(8,128)(2,1)}, bf16[512,1536]{1,0:T(8,128)(2,1)}, u32[]{:S(2)}, u32[]{:S(2)}) collective-permute-start(bf16[512,1536]{1,0:T(8,128)(2,1)} %bitcast.14), channel_id=1, source_target_pairs={{0,3},{1,0},{2,1},{3,2},{4,7},{5,4},{6,5},{7,6},{8,11},{9,8},{10,9... | collective-permute-start | bytes 4718600 | tf_op jit(solution)/shard_map/ppermute | solution.py:237
  12.4 69.6 %all-to-all-start = ((bf16[128,8,1024]{2,1,0:T(8,128)(2,1)}), bf16[128,8,1024]{2,1,0:T(8,128)(2,1)S(1)}, u32[]{:S(2)}, u32[]{:S(2)}) async-start(bf16[128,8,1024]{2,1,0:T(8,128)(2,1)} %bitcast.20), calls=%async_computation | async-start | bytes 4194304 | tf_op jit(solution)/shard_map/all_to_all | solution.py:295
  30.8 29.2 %collective-permute-start.4 = (bf16[768,512]{1,0:T(8,128)(2,1)}, bf16[768,512]{1,0:T(8,128)(2,1)S(1)}, u32[]{:S(2)}, u32[]{:S(2)}) collective-permute-start(bf16[768,512]{1,0:T(8,128)(2,1)} %bitcast.17), channel_id=1, source_target_pairs={{0,3},{1,0},{2,1},{3,2},{4,7},{5,4},{6,5},{7,6},{8,11},{9,8},{10,9... | collective-permute-start | bytes 2359304 | tf_op jit(solution)/shard_map/ppermute | solution.py:238
  34.0 23.0 %collective-permute-start.5 = (bf16[768,512]{1,0:T(8,128)(2,1)}, bf16[768,512]{1,0:T(8,128)(2,1)}, u32[]{:S(2)}, u32[]{:S(2)}) collective-permute-start(bf16[768,512]{1,0:T(8,128)(2,1)} %bitcast.18), channel_id=1, source_target_pairs={{0,1},{1,2},{2,3},{3,0},{4,5},{5,6},{6,7},{7,4},{8,9},{9,10},{10,1... | collective-permute-start | bytes 2359304 | tf_op jit(solution)/shard_map/ppermute | solution.py:238
  38.1 45.4 %collective-permute-start.2 = (bf16[256,1536]{1,0:T(8,128)(2,1)}, bf16[256,1536]{1,0:T(8,128)(2,1)}, u32[]{:S(2)}, u32[]{:S(2)}) collective-permute-start(bf16[256,1536]{1,0:T(8,128)(2,1)} %get-tuple-element.28), channel_id=1, source_target_pairs={{0,1},{1,2},{2,3},{3,0},{4,5},{5,6},{6,7},{7,4},{8,9},{9,10},{10,1... | collective-permute-start | bytes 2359304 | tf_op jit(solution)/shard_map/ppermute | solution.py:240
  45.2 38.3 %collective-permute-start.3 = (bf16[256,1536]{1,0:T(8,128)(2,1)}, bf16[256,1536]{1,0:T(8,128)(2,1)}, u32[]{:S(2)}, u32[]{:S(2)}) collective-permute-start(bf16[256,1536]{1,0:T(8,128)(2,1)} %get-tuple-element.29), channel_id=1, source_target_pairs={{0,3},{1,0},{2,1},{3,2},{4,7},{5,4},{6,5},{7,6},{8,11},{9,8},{10,9... | collective-permute-start | bytes 2359304 | tf_op jit(solution)/shard_map/ppermute | solution.py:240
  58.0 32.5 %collective-permute-start.6 = (bf16[384,512]{1,0:T(8,128)(2,1)S(1)}, bf16[384,512]{1,0:T(8,128)(2,1)}, u32[]{:S(2)}, u32[]{:S(2)}) collective-permute-start(bf16[384,512]{1,0:T(8,128)(2,1)S(1)} %slice.8), channel_id=1, source_target_pairs={{0,1},{1,2},{2,3},{3,0},{4,5},{5,6},{6,7},{7,4},{8,9},{9,10},{10,1... | collective-permute-start | bytes 1179656 | tf_op jit(solution)/shard_map/ppermute | solution.py:241
  60.7 29.8 %collective-permute-start.7 = (bf16[384,512]{1,0:T(8,128)(2,1)}, bf16[384,512]{1,0:T(8,128)(2,1)}, u32[]{:S(2)}, u32[]{:S(2)}) collective-permute-start(bf16[384,512]{1,0:T(8,128)(2,1)} %slice.9), channel_id=1, source_target_pairs={{0,3},{1,0},{2,1},{3,2},{4,7},{5,4},{6,5},{7,6},{8,11},{9,8},{10,9... | collective-permute-start | bytes 1179656 | tf_op jit(solution)/shard_map/ppermute | solution.py:241
  82.0 1.5 %copy-start = (bf16[1,512,1536]{2,1,0:T(8,128)(2,1)S(1)}, bf16[1,512,1536]{2,1,0:T(8,128)(2,1)}, u32[]{:S(2)}) copy-start(bf16[1,512,1536]{2,1,0:T(8,128)(2,1)} %param.10) | copy-start | bytes 4718596
  82.0 1.6 %copy-start.1 = (bf16[1,768,512]{2,1,0:T(8,128)(2,1)S(1)}, bf16[1,768,512]{2,1,0:T(8,128)(2,1)}, u32[]{:S(2)}) copy-start(bf16[1,768,512]{2,1,0:T(8,128)(2,1)} %param.11) | copy-start | bytes 2359300
  88.6 7.3 %copy-start.3 = (bf16[768,512]{1,0:T(8,128)(2,1)}, bf16[768,512]{1,0:T(8,128)(2,1)S(1)}, u32[]{:S(2)}) copy-start(bf16[768,512]{1,0:T(8,128)(2,1)S(1)} %get-tuple-element.41.block) | copy-start | bytes 2359300
  88.6 24.4 %collective-permute-start.8 = (bf16[768,512]{1,0:T(8,128)(2,1)}, bf16[768,512]{1,0:T(8,128)(2,1)}, u32[]{:S(2)}, u32[]{:S(2)}) collective-permute-start(bf16[768,512]{1,0:T(8,128)(2,1)} %get-tuple-element.42), channel_id=1, source_target_pairs={{0,1},{1,2},{2,3},{3,0},{4,5},{5,6},{6,7},{7,4},{8,9},{9,10},{10,1... | collective-permute-start | bytes 2359304 | tf_op jit(solution)/shard_map/ppermute | solution.py:251
  95.9 17.1 %copy-start.4 = (bf16[768,512]{1,0:T(8,128)(2,1)S(1)}, bf16[768,512]{1,0:T(8,128)(2,1)}, u32[]{:S(2)}) copy-start(bf16[768,512]{1,0:T(8,128)(2,1)} %copy-done.3) | copy-start | bytes 2359300
  95.9 44.6 %all-to-all-start.1 = ((bf16[128,8,512]{2,1,0:T(8,128)(2,1)}), bf16[128,8,512]{2,1,0:T(8,128)(2,1)S(1)}, u32[]{:S(2)}, u32[]{:S(2)}) async-start(bf16[128,8,512]{2,1,0:T(8,128)(2,1)} %bitcast.7), calls=%async_computation.1 | async-start | bytes 2097152 | tf_op jit(solution)/shard_map/all_to_all | solution.py:342
  109.6 20.1 %collective-permute-start.10 = (bf16[768,512]{1,0:T(8,128)(2,1)S(1)}, bf16[768,512]{1,0:T(8,128)(2,1)S(1)}, u32[]{:S(2)}, u32[]{:S(2)}) collective-permute-start(bf16[768,512]{1,0:T(8,128)(2,1)S(1)} %get-tuple-element.43), channel_id=1, source_target_pairs={{0,3},{1,0},{2,1},{3,2},{4,7},{5,4},{6,5},{7,6},{8,11},{9,8},{10,9... | collective-permute-start | bytes 2359304 | tf_op jit(solution)/shard_map/ppermute | solution.py:261
  114.3 21.0 %collective-permute-start.9 = (bf16[768,512]{1,0:T(8,128)(2,1)S(1)}, bf16[768,512]{1,0:T(8,128)(2,1)S(1)}, u32[]{:S(2)}, u32[]{:S(2)}) collective-permute-start(bf16[768,512]{1,0:T(8,128)(2,1)S(1)} %add_far.1), channel_id=1, source_target_pairs={{0,1},{1,2},{2,3},{3,0},{4,5},{5,6},{6,7},{7,4},{8,9},{9,10},{10,1... | collective-permute-start | bytes 2359304 | tf_op jit(solution)/shard_map/ppermute | solution.py:261
  135.3 5.2 %copy-start.2 = (bf16[1024,96]{1,0:T(8,128)(2,1)S(1)}, bf16[1024,96]{1,0:T(8,128)(2,1)}, u32[]{:S(2)}) copy-start(bf16[1024,96]{1,0:T(8,128)(2,1)} %get-tuple-element.23.pick_ref) | copy-start | bytes 589828
